TPU v7x, 32 devices: a whole 2x2x4 slice. The times are simulated.
32 devices in a mesh: pipe: 4 (over y, core), dp: 8 (over z, x).
Axes of the slice: x: 2, y: 2, z: 4, core: 2. Of those that a mesh axis runs over, the one named last changes fastest.
Arguments:
- weights: bfloat16 [4, 2, 7168, 256], P('pipe'), may hold values from -0.375 to 0.375
- gain_model: bfloat16 [4, 7168], P('pipe'), may hold values from 0.099609375 to 1.8984375
- gain_latent: bfloat16 [4, 256], P('pipe'), may hold values from 0.099609375 to 1.8984375
- saved_down: bfloat16 [4, 2, 256, 7168], P('pipe', None, 'dp'), may hold values from -6 to 6
- saved_up: bfloat16 [4, 2, 256, 7168], P('pipe', None, 'dp'), may hold values from -6 to 6
- grad_start: bfloat16 [2, 4, 256, 7168], P(None, 'pipe', 'dp'), may hold values from -0.119628906 to 0.119628906
Outputs:
- section_grads: bfloat16 [4, 2, 7168, 256], P('pipe', None, 'dp')
All inputs are finite; a program needn't handle non-finite values.
Results may differ from a plain program's by a relative error of at most 0.024.
Values may be sent and summed in bfloat16 or wider, within the bound.
No kernel may reach another device: no remote copies, remote signals or barrier semaphores. Data moves between devices by JAX's collectives and lax.ppermute only.
A program may use at most 128 MiB of HBM per device.

v0:
```python
import jax
import jax.numpy as jnp
from jax import lax
from jax.sharding import PartitionSpec as P

EPS = 1e-06


def from_partner(block, axis, apart):
    count = lax.axis_size(axis)
    route = []
    for low in range(count):
        high = low | 1 << apart
        if high != low and high < count:
            route += [(low, high), (high, low)]
    return lax.ppermute(block, axis, route)


def from_behind(block, axis, distance):
    devices = range(lax.axis_size(axis))
    route = [(i - distance, i) for i in devices if i - distance in devices]
    return lax.ppermute(block, axis, route)


def contract(left, right):
    return lax.dot_general(
        left, right, (((0,), (0,)), ((), ())), preferred_element_type=jnp.float32
    )


def micro(inputs, incoming, pair, gain_in, gain_lat, need_input):
    xf = inputs.astype(jnp.float32)
    inv_in = lax.rsqrt(jnp.mean(xf * xf, axis=-1, keepdims=True) + EPS)
    normed = (xf * inv_in * gain_in.astype(jnp.float32)).astype(jnp.bfloat16)
    latent = jnp.dot(normed, pair[0], preferred_element_type=jnp.float32)
    inv_lat = lax.rsqrt(jnp.mean(latent * latent, axis=-1, keepdims=True) + EPS)
    keyed = (latent * inv_lat * gain_lat.astype(jnp.float32)).astype(jnp.bfloat16)
    dkey = jnp.dot(incoming, pair[1], preferred_element_type=jnp.float32)
    scaled = dkey * gain_lat.astype(jnp.float32)
    dlat = (
        inv_lat
        * (scaled - latent * inv_lat * inv_lat * jnp.mean(scaled * latent, axis=-1, keepdims=True))
    ).astype(jnp.bfloat16)
    terms = jnp.stack([contract(normed, dlat), contract(incoming, keyed)])
    result = None
    if need_input:
        dnorm = lax.dot_general(
            dlat, pair[0], (((1,), (1,)), ((), ())), preferred_element_type=jnp.float32
        )
        vgrad = dnorm * gain_in.astype(jnp.float32)
        result = (
            incoming.astype(jnp.float32)
            + inv_in * (vgrad - xf * inv_in * inv_in * jnp.mean(vgrad * xf, axis=-1, keepdims=True))
        ).astype(jnp.bfloat16)
    return (result, terms)


def per_device(weights, gain_model, gain_latent, saved_down, saved_up, grad_start):
    bits = lax.axis_size("pipe").bit_length() - 1
    replicas = lax.axis_size("dp")
    replica = lax.axis_index("dp")
    own = weights[0]
    own_in = gain_model[0]
    own_lat = gain_latent[0]
    share = own.shape[1] // replicas
    carried = (lax.dynamic_slice_in_dim(own, replica * share, share, 1), own_in, own_lat)
    for bit in range(bits):
        carried = from_partner((carried[0], carried[1], carried[2]), "pipe", bit)
    other_piece, other_in, other_lat = carried
    other = lax.all_gather(other_piece, "dp", axis=1, tiled=True)
    down_grad, down_first = micro(saved_down[0, 0], grad_start[0, 0], own, own_in, own_lat, True)
    up_grad, up_first = micro(saved_up[0, 0], grad_start[1, 0], other, other_in, other_lat, True)
    from_above = from_behind(down_grad, "pipe", -1)
    from_below = from_behind(up_grad, "pipe", 1)
    unused_down, down_second = micro(saved_down[0, 1], from_above, own, own_in, own_lat, False)
    unused_up, up_second = micro(saved_up[0, 1], from_below, other, other_in, other_lat, False)
    own_part, other_part = (
        lax.psum_scatter(
            (down_first + down_second).astype(jnp.bfloat16), "dp", scatter_dimension=1, tiled=True
        ).astype(jnp.float32),
        lax.psum_scatter(
            (up_first + up_second).astype(jnp.bfloat16), "dp", scatter_dimension=1, tiled=True
        ).astype(jnp.float32),
    )
    returned = other_part
    for bit in range(bits):
        returned = from_partner(returned.astype(jnp.bfloat16), "pipe", bit).astype(returned.dtype)
    total = own_part + returned
    return total.astype(jnp.bfloat16)[None]


def solution(mesh):
    placed = (
        P("pipe", None, None, None),
        P("pipe", None),
        P("pipe", None),
        P("pipe", None, "dp", None),
        P("pipe", None, "dp", None),
        P(None, "pipe", "dp", None),
    )
    return jax.shard_map(
        per_device,
        mesh=mesh,
        in_specs=placed,
        out_specs=P("pipe", None, "dp", None),
        check_vma=False,
    )
```

profile of v0, /device:TPU:0, one launch (start us, length us, event | category | flops | bytes accessed | tf_op | source)
XLA Modules:
  0.0 450.4 jit_solution(15813962192803437237)
XLA Ops:
  6.5 1.4 dynamic-slice_bitcast_fusion
  7.9 0.5 collective-permute-start.3
  8.4 2.1 collective-permute-done.3
  10.5 2.9 collective-permute-start.4
  13.4 20.6 %collective-permute-done.4 = bf16[2,896,256]{2,1,0:T(8,128)(2,1)S(1)} collective-permute-done((bf16[2,896,256]{2,1,0:T(8,128)(2,1)S(1)}, bf16[2,896,256]{2,1,0:T(8,128)(2,1)S(1)}, u32[]{:S(2)}, u32[]{:S(2)}) %collective-permute-start.4) | collective-permute-done | bytes 917536 | tf_op jit(solution)/shard_map/ppermute | solution.py:16
  34.1 0.9 copy-done.3
  35.0 0.0 all-gather.2.cloned.1.call-update
  35.0 0.0 reduce-scatter.5.cloned.1.call-start
  35.1 0.8 reduce
  35.9 0.1 collective-permute-start.1
  36.0 0.7 reduce.1
  36.7 0.6 collective-permute-start.5
  37.2 1.5 fusion.64
  38.7 1.4 fusion.55
  40.1 0.0 copy-start
  40.1 3.0 fusion.9
  43.2 0.0 copy-done.2
  43.2 3.3 multiply_reduce_fusion.6
  46.5 0.1 multiply_convert_fusion.7
  46.6 0.0 copy-done.1
  46.6 2.2 fusion.59
  48.9 0.0 collective-permute-done.5
  48.9 1.8 collective-permute-start.6
  50.7 0.0 collective-permute-done.1
  50.7 0.3 collective-permute-start.2
  51.0 1.5 collective-permute-done.6
  52.5 1.9 collective-permute-done.2
  54.4 94.2 %all-gather.2.cloned.1.call-done = bf16[2,7168,256]{2,1,0:T(8,128)(2,1)} async-done(((bf16[2,896,256]{2,1,0:T(8,128)(2,1)}), bf16[2,7168,256]{2,1,0:T(8,128)(2,1)}) %all-gather.2.cloned.1.call-update) | async-done | bytes 7340048 | tf_op jit(solution)/shard_map/all_gather | solution.py:70
  148.7 3.0 fusion.16
  151.6 0.0 slice-start.3
  151.6 3.0 multiply_reduce_fusion.2
  154.7 0.1 multiply_convert_fusion.3
  154.8 1.3 convolution_bitcast_fusion.3
  156.1 1.3 fusion.68
  157.4 0.6 fusion.54
  158.0 1.3 collective-permute-start.7
  159.4 1.2 convolution_bitcast_fusion.2
  160.6 0.8 fusion.15
  161.4 0.0 collective-permute-done.7
  161.4 0.8 multiply_reduce_fusion
  162.3 1.3 convolution_bitcast_fusion.1
  163.5 1.2 convolution_bitcast_fusion
  164.7 4.0 fusion.1
  168.7 0.0 reduce-scatter.5.cloned.1.call-update
  168.7 0.2 reduce-scatter.3.cloned.1.call-start
  169.0 0.0 slice-start
  169.0 1.3 convolution_bitcast_fusion.7
  170.2 0.0 slice-start.1
  170.3 1.6 collective-permute-start
  171.8 1.2 convolution_bitcast_fusion.6
  173.0 2.8 fusion.7
  175.8 3.5 collective-permute-done
  179.3 0.8 multiply_reduce_fusion.4
  180.1 1.2 convolution_bitcast_fusion.4
  181.3 1.3 convolution_bitcast_fusion.5
  182.6 4.0 fusion
  186.6 0.0 reduce-scatter.3.cloned.1.call-update
  186.6 119.6 %reduce-scatter.5.cloned.1.call-done = bf16[2,896,256]{2,1,0:T(8,128)(2,1)} async-done(((bf16[2,7168,256]{2,1,0:T(8,128)(2,1)}), bf16[2,896,256]{2,1,0:T(8,128)(2,1)}) %reduce-scatter.5.cloned.1.call-update) | async-done | bytes 917520 | tf_op jit(solution)/shard_map/reduce_scatter | solution.py:81
  306.2 0.0 collective-permute-start.8
  306.2 2.7 collective-permute-done.8
  308.9 1.5 collective-permute-start.9
  310.4 131.2 %reduce-scatter.3.cloned.1.call-done = bf16[2,896,256]{2,1,0:T(8,128)(2,1)} async-done(((bf16[2,7168,256]{2,1,0:T(8,128)(2,1)}), bf16[2,896,256]{2,1,0:T(8,128)(2,1)}) %reduce-scatter.3.cloned.1.call-update) | async-done | bytes 917520 | tf_op jit(solution)/shard_map/reduce_scatter | solution.py:78
  441.6 0.0 collective-permute-done.9
  441.6 2.3 fusion.73
  (32 shorter events, 0.1 us)
Async XLA Ops:
  6.5 40.1 %copy-start.1 = (bf16[1,2,32,7168]{3,2,1,0:T(8,128)(2,1)S(1)}, bf16[1,2,32,7168]{3,2,1,0:T(8,128)(2,1)}, u32[]{:S(2)}) copy-start(bf16[1,2,32,7168]{3,2,1,0:T(8,128)(2,1)} %param.9) | copy-start | bytes 2752516
  6.5 36.6 %copy-start.2 = (bf16[2,1,32,7168]{3,2,1,0:T(8,128)(2,1)S(1)}, bf16[2,1,32,7168]{3,2,1,0:T(8,128)(2,1)}, u32[]{:S(2)}) copy-start(bf16[2,1,32,7168]{3,2,1,0:T(8,128)(2,1)} %param.11) | copy-start | bytes 2752516
  6.5 142.1 %all-gather.2.cloned.1.call-start = ((), (), s32[]{:S(2)}) async-start(), calls=%async_computation.3 | async-start | bytes 8257536 | tf_op jit(solution)/shard_map/all_gather | solution.py:70
  7.9 2.6 collective-permute-start.3
  10.5 23.5 %collective-permute-start.4 = (bf16[2,896,256]{2,1,0:T(8,128)(2,1)S(1)}, bf16[2,896,256]{2,1,0:T(8,128)(2,1)S(1)}, u32[]{:S(2)}, u32[]{:S(2)}) collective-permute-start(bf16[2,896,256]{2,1,0:T(8,128)(2,1)S(1)} %collective-permute-done.3), channel_id=1, source_target_pairs={{0,16},{16,0},{8,24},{24,8},{1,17},{17,1},{9,25},{25,9},{2,18},{18... | collective-permute-start | bytes 2752520 | tf_op jit(solution)/shard_map/ppermute | solution.py:16
  34.1 0.9 copy-start.3
  35.0 271.2 %reduce-scatter.5.cloned.1.call-start = ((), (), s32[]{:S(2)}) async-start(), calls=%async_computation.4 | async-start | bytes 8257536 | tf_op jit(solution)/shard_map/reduce_scatter | solution.py:81
  35.9 14.8 %collective-permute-start.1 = (bf16[7168]{0:T(1024)(128)(2,1)S(1)}, bf16[7168]{0:T(1024)(128)(2,1)S(1)}, u32[]{:S(2)}, u32[]{:S(2)}) collective-permute-start(bf16[7168]{0:T(1024)(128)(2,1)S(1)} %reduce), channel_id=1, source_target_pairs={{0,8},{8,0},{16,24},{24,16},{1,9},{9,1},{17,25},{25,17},{2,10},{10... | collective-permute-start | bytes 43016 | tf_op jit(solution)/shard_map/ppermute | solution.py:16
  36.7 9.9 %copy-start.5 = (bf16[1,2,7168,256]{3,2,1,0:T(8,128)(2,1)S(1)}, bf16[1,2,7168,256]{3,2,1,0:T(8,128)(2,1)}, u32[]{:S(2)}) copy-start(bf16[1,2,7168,256]{3,2,1,0:T(8,128)(2,1)} %param.6) | copy-start | bytes 22020100
  36.7 12.2 %collective-permute-start.5 = (bf16[256]{0:T(256)(128)(2,1)S(1)}, bf16[256]{0:T(256)(128)(2,1)S(1)}, u32[]{:S(2)}, u32[]{:S(2)}) collective-permute-start(bf16[256]{0:T(256)(128)(2,1)S(1)} %reduce.1), channel_id=1, source_target_pairs={{0,8},{8,0},{16,24},{24,16},{1,9},{9,1},{17,25},{25,17},{2,10},{10... | collective-permute-start | bytes 1544 | tf_op jit(solution)/shard_map/ppermute | solution.py:16
  40.1 108.5 %copy-start = (bf16[1,2,32,7168]{3,2,1,0:T(8,128)(2,1)S(1)}, bf16[1,2,32,7168]{3,2,1,0:T(8,128)(2,1)}, u32[]{:S(2)}) copy-start(bf16[1,2,32,7168]{3,2,1,0:T(8,128)(2,1)} %param.10) | copy-start | bytes 2752516
  48.9 3.6 collective-permute-start.6
  50.7 3.7 collective-permute-start.2
  148.7 7.4 %slice-start.2 = ((s8[7340032]{0:T(1024)(128)(4,1)}), s8[4194304]{0:T(1024)(128)(4,1)S(1)}, s32[]{:S(2)}) async-start(s8[7340032]{0:T(1024)(128)(4,1)} %bitcast.191), calls=%async_computation.7 | async-start | bytes 8388608
  151.6 4.4 slice-start.3
  154.7 2.7 copy-start.4
  158.0 3.3 collective-permute-start.7
  168.7 272.9 %reduce-scatter.3.cloned.1.call-start = ((), (), s32[]{:S(2)}) async-start(), calls=%async_computation.2 | async-start | bytes 8257536 | tf_op jit(solution)/shard_map/reduce_scatter | solution.py:78
  169.0 10.3 %slice-start = ((s8[7340032]{0:T(1024)(128)(4,1)}), s8[4194304]{0:T(1024)(128)(4,1)S(1)}, s32[]{:S(2)}) async-start(s8[7340032]{0:T(1024)(128)(4,1)} %bitcast.189), calls=%async_computation.5 | async-start | bytes 8388608
  170.2 9.0 %slice-start.1 = ((s8[7340032]{0:T(1024)(128)(4,1)}), s8[3145728]{0:T(1024)(128)(4,1)S(1)}, s32[]{:S(2)}) async-start(s8[7340032]{0:T(1024)(128)(4,1)} %bitcast.189), calls=%async_computation.6 | async-start | bytes 6291456
  170.3 9.0 %collective-permute-start = (bf16[32,7168]{1,0:T(8,128)(2,1)S(1)}, bf16[32,7168]{1,0:T(8,128)(2,1)S(1)}, u32[]{:S(2)}, u32[]{:S(2)}) collective-permute-start(bf16[32,7168]{1,0:T(8,128)(2,1)S(1)} %get-tuple-element.17), channel_id=1, source_target_pairs={{8,0},{16,8},{24,16},{9,1},{17,9},{25,17},{10,2},{18,10},{26,18},{... | collective-permute-start | bytes 1376264 | tf_op jit(solution)/shard_map/ppermute | solution.py:22
  306.2 2.7 collective-permute-start.8
  308.9 132.7 %collective-permute-start.9 = (bf16[2,896,256]{2,1,0:T(8,128)(2,1)S(1)}, bf16[2,896,256]{2,1,0:T(8,128)(2,1)S(1)}, u32[]{:S(2)}, u32[]{:S(2)}) collective-permute-start(bf16[2,896,256]{2,1,0:T(8,128)(2,1)S(1)} %collective-permute-done.8), channel_id=1, source_target_pairs={{0,16},{16,0},{8,24},{24,8},{1,17},{17,1},{9,25},{25,9},{2,18},{18... | collective-permute-start | bytes 2752520 | tf_op jit(solution)/shard_map/ppermute | solution.py:16
Sparse Core Ops, SparseCore 0:
  35.1 113.4 all-gather.1
  168.8 137.2 reduce-scatter.4
  309.8 131.7 reduce-scatter.2
where the time goes:
time: 451 us; the launch traced here: 450 us
  waiting for transfers between devices  377 us (84%)
  matrix products  30.9 us (7%)
  other arithmetic  15.5 us (3%)
  between operations  13.4 us (3%)
  starting transfers between devices  10.8 us (2%)
    reduce_scatter x1, waiting for transfers between devices, per_device(): lax.psum_scatter((down_first + down_second).astype(jnp.bfloat16), 'dp', s...  131 us
    reduce_scatter x1, waiting for transfers between devices, per_device(): lax.psum_scatter((up_first + up_second).astype(jnp.bfloat16), 'dp', scatt...  120 us
    all_gather x1, waiting for transfers between devices, per_device(): other = lax.all_gather(other_piece, 'dp', axis=1, tiled=True)  94.2 us
    ppermute x8, waiting for transfers between devices, from_partner(): return lax.ppermute(block, axis, route)  28.9 us
    dot_general x8, matrix products, contract(): lax.dot_general(left, right, (((0,), (0,)), ((), ())), preferred_element_...  9.73 us
    dot_general x4, matrix products, micro(): latent = jnp.dot(normed, pair[0], preferred_element_type=jnp.float32)  9.62 us
  transfers between devices with their start and end apart: 13, of which 9 were waited for; matrix products, arithmetic and copies ran while one was open for 6% of the time, Pallas kernels for 0%

commit v1 on v0

v1 whole, which is shorter than its diff:
```python
import jax
import jax.numpy as jnp
from jax import lax
from jax.sharding import PartitionSpec as P

EPS = 1e-06


def rows_dot(left, right):
    return lax.dot_general(left, right, (((0,), (0,)), ((), ())), preferred_element_type=jnp.float32)


def dot_t(left, right):
    return lax.dot_general(left, right, (((1,), (1,)), ((), ())), preferred_element_type=jnp.float32)


def dot(left, right):
    return jnp.dot(left, right, preferred_element_type=jnp.float32)


def latent_side(x, down, g, h):
    xf = x.astype(jnp.float32)
    a = lax.rsqrt(jnp.mean(xf * xf, axis=-1, keepdims=True) + EPS)
    c = dot((xf * a * g).astype(jnp.bfloat16), down)
    b = lax.rsqrt(jnp.mean(c * c, axis=-1, keepdims=True) + EPS)
    k = (c * b * h).astype(jnp.bfloat16)
    return a, c, b, k


def gradient_side(y, up, a, c, b, h):
    u = dot(y, up) * h
    q = b * (u - c * b * b * jnp.mean(u * c, axis=-1, keepdims=True))
    return (q * a).astype(jnp.bfloat16)


def input_gradient(x, y, aq, s, down, g):
    return (y.astype(jnp.float32) + dot_t(aq, down) * g - x.astype(jnp.float32) * s).astype(jnp.bfloat16)


def per_device(weights, gain_model, gain_latent, saved_down, saved_up, grad_start):
    ranks = lax.axis_size("pipe")
    replicas = lax.axis_size("dp")
    j = lax.axis_index("dp")
    down, up = weights[0, 0], weights[0, 1]
    width = down.shape[0]
    share = width // replicas
    g = gain_model[0].astype(jnp.float32)
    h = gain_latent[0].astype(jnp.float32)
    own_down = lax.dynamic_slice_in_dim(down, j * share, share, 0)
    own_g = lax.dynamic_slice_in_dim(g, j * share, share, 0)

    def mirror(block):
        return lax.ppermute(block, "pipe", [(i, ranks - 1 - i) for i in range(ranks)])

    def to_before(block):
        return lax.ppermute(block, "pipe", [(i + 1, i) for i in range(ranks - 1)])

    def across(block, apart):
        return lax.ppermute(block, "dp", [(i, i ^ apart) for i in range(replicas)])

    def exchange(blocks):
        out = []
        for apart in range(replicas):
            at = (j ^ apart) * share
            piece = jnp.stack([lax.dynamic_slice_in_dim(b, at, share, 1) for b in blocks])
            out.append(across(piece, apart) if apart else piece)
        return jnp.stack(out, 1)

    def gather(block):
        return jnp.stack([across(block, apart) if apart else block for apart in range(replicas)])

    x0u = mirror(saved_up[0, 0])
    y0u = mirror(grad_start[1, 0])
    x1u = mirror(saved_up[0, 1])
    x0d, x1d, y0d = saved_down[0, 0], saved_down[0, 1], grad_start[0, 0]

    x0d_s, y0d_s = exchange([x0d, y0d])

    def first(x, y):
        a, c, b, k = latent_side(x, down, g, h)
        aq = gradient_side(y, up, a, c, b, h)
        s = a * jnp.sum(aq.astype(jnp.float32) * c, axis=-1, keepdims=True) / width
        z = input_gradient(x, y, aq, s, down, g)
        return aq, k, s, to_before(z)

    def pack(aq, s):
        high = s.astype(jnp.bfloat16)
        low = (s - high.astype(jnp.float32)).astype(jnp.bfloat16)
        pad = jnp.zeros((aq.shape[0], 126), jnp.bfloat16)
        return jnp.concatenate([aq, high, low, pad], 1)

    aq0d, k0d, s0d, y1d = first(x0d, y0d)
    a1d, c1d, b1d, k1d = latent_side(x1d, down, g, h)
    aq1d = gradient_side(y1d, up, a1d, c1d, b1d, h)

    aq0u, k0u, s0u, y1u = first(x0u, y0u)
    x0u_s, y0u_s = exchange([x0u, y0u])
    a1u, c1u, b1u, k1u = latent_side(x1u, down, g, h)
    x1d_s, x1u_s = exchange([x1d, x1u])

    packed = gather(jnp.stack([pack(aq0d, s0d), pack(aq0u, s0u)]))
    aq1u = gradient_side(y1u, up, a1u, c1u, b1u, h)
    late = gather(jnp.stack([jnp.concatenate([k0d, k1d, aq1d], 1), jnp.concatenate([k0u, k1u, aq1u], 1)]))
    lat = h.shape[0]

    x0_s = jnp.stack([x0d_s, x0u_s], 1)
    y0_s = jnp.stack([y0d_s, y0u_s], 1)
    x1_s = jnp.stack([x1d_s, x1u_s], 1)
    flat = lambda v: v.reshape(-1, v.shape[-1])
    x0_s, y0_s, x1_s = flat(x0_s), flat(y0_s), flat(x1_s)
    packed, late = flat(packed), flat(late)
    aq0_all = packed[:, :lat]
    s_all = packed[:, lat : lat + 1].astype(jnp.float32) + packed[:, lat + 1 : lat + 2].astype(jnp.float32)
    k0_all, k1_all, aq1_all = late[:, :lat], late[:, lat : 2 * lat], late[:, 2 * lat :]
    y1_s = to_before(input_gradient(x0_s, y0_s, aq0_all, s_all, own_down, own_g))
    first_term = (rows_dot(x0_s, aq0_all) + rows_dot(x1_s, aq1_all)) * own_g[:, None]
    second_term = rows_dot(y0_s, k0_all) + rows_dot(y1_s, k1_all)
    return jnp.stack([first_term, second_term]).astype(jnp.bfloat16)[None]


def solution(mesh):
    placed = (
        P("pipe", None, None, None),
        P("pipe", None),
        P("pipe", None),
        P("pipe", None, "dp", None),
        P("pipe", None, "dp", None),
        P(None, "pipe", "dp", None),
    )
    return jax.shard_map(
        per_device,
        mesh=mesh,
        in_specs=placed,
        out_specs=P("pipe", None, "dp", None),
        check_vma=False,
    )
```

time: 451 us -> 217 us (0.48)
  waiting for transfers between devices: 377 us -> 59 us
  starting transfers between devices: 10.8 us -> 71.4 us
  local copies, waits for them, and re-layouts: 2.35 us -> 28 us
  other arithmetic: 15.5 us -> 28.2 us
  between operations: 13.4 us -> 1.02 us
    reduce_scatter x2 -> x0, waiting for transfers between devices: 251 us -> none  [the longest x1 131 us: per_device(): lax.psum_scatter((down_first + down_second).astype(jnp.bfloat16), 'dp', s...]
    all_gather x1 -> x0, waiting for transfers between devices: 94.2 us -> none  [per_device(): other = lax.all_gather(other_piece, 'dp', axis=1, tiled=True)]
    ppermute x10 -> x41, starting transfers between devices: 10.5 us -> 71.4 us  [the longest x35 61.1 us: across(): return lax.ppermute(block, 'dp', [(i, i ^ apart) for i in range(replicas)])]
    ppermute x10 -> x41, waiting for transfers between devices: 32.3 us -> 59 us  [the longest x35 59 us: across(): return lax.ppermute(block, 'dp', [(i, i ^ apart) for i in range(replicas)])]
    another operation x0 -> x30, other arithmetic: none -> 17.7 us  [the longest x21 15.5 us: exchange(): jnp.stack([lax.dynamic_slice_in_dim(b, at, share, 1) for b in blocks])]
    unnamed x20 -> x102, local copies, waits for them, and re-layouts: 0.98 us -> 12.1 us
    another operation x0 -> x16, local copies, waits for them, and re-layouts: none -> 9.72 us  [the longest x6 6.43 us: exchange(): jnp.stack([lax.dynamic_slice_in_dim(b, at, share, 1) for b in blocks])]
    convert_element_type x7 -> x5, other arithmetic: 8.74 us -> 0.13 us  [the longest x1 0.1 us: latent_side(): k = (c * b * h).astype(jnp.bfloat16)]
  transfers between devices with their start and end apart: 13 -> 41, of which waited for: 9 -> 12; matrix products, arithmetic and copies ran while one was open for 6% -> 32% of each run, Pallas kernels for 0% -> 0%
where the time goes in v1:
time: 217 us; the launch traced here: 216 us
  starting transfers between devices  71.4 us (33%)
  waiting for transfers between devices  59 us (27%)
  other arithmetic  28.2 us (13%)
  matrix products  28.1 us (13%)
  local copies, waits for them, and re-layouts  28 us (13%)
    ppermute x35, starting transfers between devices, across(): return lax.ppermute(block, 'dp', [(i, i ^ apart) for i in range(replicas)])  61.1 us
    ppermute x35, waiting for transfers between devices, across(): return lax.ppermute(block, 'dp', [(i, i ^ apart) for i in range(replicas)])  59 us
    dot_general x8, matrix products, dot(): return jnp.dot(left, right, preferred_element_type=jnp.float32)  20.6 us
    another operation x21, other arithmetic, exchange(): jnp.stack([lax.dynamic_slice_in_dim(b, at, share, 1) for b in blocks])  15.5 us
    unnamed x102, local copies, waits for them, and re-layouts  12.1 us
    another operation x6, local copies, waits for them, and re-layouts, exchange(): jnp.stack([lax.dynamic_slice_in_dim(b, at, share, 1) for b in blocks])  6.43 us
    ppermute x3, starting transfers between devices, mirror(): lax.ppermute(block, 'pipe', [(i, ranks - 1 - i) for i in range(ranks)])  6.2 us
    dot_general x3, matrix products, dot_t(): lax.dot_general(left, right, (((1,), (1,)), ((), ())), preferred_element_...  5.69 us
  transfers between devices with their start and end apart: 41, of which 12 were waited for; matrix products, arithmetic and copies ran while one was open for 32% of the time, Pallas kernels for 0%

profile of v1, /device:TPU:0, one launch (start us, length us, event | category | flops | bytes accessed | tf_op | source)
XLA Modules:
  0.0 215.8 jit_solution(13307998391504132369)
XLA Ops:
  0.0 1.3 fusion.44
  2.8 3.1 %fusion.32 = f32[32,256]{1,0:T(8,128)S(1)} fusion(bf16[1,2,7168,256]{3,2,1,0:T(8,128)(2,1)} %param.6, f32[256]{0:T(256)S(1)} %bitcast.337, bf16[2,1,32,7168]{3,2,1,0:T(8,128)(2,1)} %param.11), kind=kOutput, calls=%fused_computation.46 | convolution fusion | flops 117448704 | bytes 4162560 | tf_op jit(solution)/shard_map/dot_general | solution.py:18
  5.9 3.4 %multiply_reduce_fusion.9 = (f32[32]{0:T(128)S(1)}, f32[32]{0:T(128)S(1)}, f32[32,256]{1,0:T(8,128)S(1)}) fusion(f32[32,256]{1,0:T(8,128)S(1)} %fusion.32, bf16[1,2,7168,256]{3,2,1,0:T(8,128)(2,1)} %param.6, f32[7168]{0:T(1024)S(1)} %bitcast.331, f32[32]{0:T(128)S(1)} %add_rsqrt_fusion.7, bf16[1,2,32,7168]{3,2,1,0:T(8,128)(2,1)S(1)} %copy-done.1), kind=kOutput, calls=%fused_computation.230 | convolution fusion | flops 118390720 | bytes 4223744 | tf_op jit(solution)/shard_map/dot_general | solution.py:18
  10.2 2.0 fusion.2
  12.1 1.3 collective-permute-start.31
  14.4 4.5 %collective-permute-start.23 = (bf16[32,7168]{1,0:T(8,128)(2,1)}, bf16[32,7168]{1,0:T(8,128)(2,1)}, u32[]{:S(2)}, u32[]{:S(2)}) collective-permute-start(bf16[32,7168]{1,0:T(8,128)(2,1)} %get-tuple-element.25), channel_id=1, source_target_pairs={{0,24},{8,16},{16,8},{24,0},{1,25},{9,17},{17,9},{25,1},{2,26},{10... | collective-permute-start | bytes 1376264 | tf_op jit(solution)/shard_map/ppermute | solution.py:53
  19.8 1.7 collective-permute-start.8
  24.5 1.5 collective-permute-start
  28.2 1.7 dynamic-slice_bitcast_fusion.1
  34.2 1.1 pad_maximum_fusion.6
  37.1 1.6 collective-permute-start.1
  39.6 2.3 %collective-permute-done.1 = bf16[2,32,896]{2,1,0:T(8,128)(2,1)S(1)} collective-permute-done((bf16[2,32,896]{2,1,0:T(8,128)(2,1)S(1)}, bf16[2,32,896]{2,1,0:T(8,128)(2,1)S(1)}, u32[]{:S(2)}, u32[]{:S(2)}) %collective-permute-start.1) | collective-permute-done | bytes 114720 | tf_op jit(solution)/shard_map/ppermute | solution.py:59
  41.9 1.6 collective-permute-start.2
  43.5 4.1 %collective-permute-done.2 = bf16[2,32,896]{2,1,0:T(8,128)(2,1)S(1)} collective-permute-done((bf16[2,32,896]{2,1,0:T(8,128)(2,1)S(1)}, bf16[2,32,896]{2,1,0:T(8,128)(2,1)S(1)}, u32[]{:S(2)}, u32[]{:S(2)}) %collective-permute-start.2) | collective-permute-done | bytes 114720 | tf_op jit(solution)/shard_map/ppermute | solution.py:59
  47.6 3.1 %collective-permute-start.3 = (bf16[2,32,896]{2,1,0:T(8,128)(2,1)S(1)}, bf16[2,32,896]{2,1,0:T(8,128)(2,1)S(1)}, u32[]{:S(2)}, u32[]{:S(2)}) collective-permute-start(bf16[2,32,896]{2,1,0:T(8,128)(2,1)S(1)} %pad_maximum_fusion.7), channel_id=1, source_target_pairs={{0,4},{1,5},{2,6},{3,7},{4,0},{5,1},{6,2},{7,3},{8,12},{9,13},{10,... | collective-permute-start | bytes 344072 | tf_op jit(solution)/shard_map/ppermute | solution.py:59
  50.7 5.8 %collective-permute-done.3 = bf16[2,32,896]{2,1,0:T(8,128)(2,1)S(1)} collective-permute-done((bf16[2,32,896]{2,1,0:T(8,128)(2,1)S(1)}, bf16[2,32,896]{2,1,0:T(8,128)(2,1)S(1)}, u32[]{:S(2)}, u32[]{:S(2)}) %collective-permute-start.3) | collective-permute-done | bytes 114720 | tf_op jit(solution)/shard_map/ppermute | solution.py:59
  56.5 9.7 %collective-permute-done.4 = bf16[2,32,896]{2,1,0:T(8,128)(2,1)S(1)} collective-permute-done((bf16[2,32,896]{2,1,0:T(8,128)(2,1)S(1)}, bf16[2,32,896]{2,1,0:T(8,128)(2,1)S(1)}, u32[]{:S(2)}, u32[]{:S(2)}) %collective-permute-start.4) | collective-permute-done | bytes 114720 | tf_op jit(solution)/shard_map/ppermute | solution.py:59
  66.2 2.4 %collective-permute-start.5 = (bf16[2,32,896]{2,1,0:T(8,128)(2,1)S(1)}, bf16[2,32,896]{2,1,0:T(8,128)(2,1)S(1)}, u32[]{:S(2)}, u32[]{:S(2)}) collective-permute-start(bf16[2,32,896]{2,1,0:T(8,128)(2,1)S(1)} %pad_maximum_fusion.9), channel_id=1, source_target_pairs={{0,6},{1,7},{2,4},{3,5},{4,2},{5,3},{6,0},{7,1},{8,14},{9,15},{10,... | collective-permute-start | bytes 344072 | tf_op jit(solution)/shard_map/ppermute | solution.py:59
  68.6 4.2 %collective-permute-done.5 = bf16[2,32,896]{2,1,0:T(8,128)(2,1)S(1)} collective-permute-done((bf16[2,32,896]{2,1,0:T(8,128)(2,1)S(1)}, bf16[2,32,896]{2,1,0:T(8,128)(2,1)S(1)}, u32[]{:S(2)}, u32[]{:S(2)}) %collective-permute-start.5) | collective-permute-done | bytes 114720 | tf_op jit(solution)/shard_map/ppermute | solution.py:59
  72.8 2.3 %collective-permute-start.6 = (bf16[2,32,896]{2,1,0:T(8,128)(2,1)S(1)}, bf16[2,32,896]{2,1,0:T(8,128)(2,1)S(1)}, u32[]{:S(2)}, u32[]{:S(2)}) collective-permute-start(bf16[2,32,896]{2,1,0:T(8,128)(2,1)S(1)} %pad_maximum_fusion.10), channel_id=1, source_target_pairs={{0,7},{1,6},{2,5},{3,4},{4,3},{5,2},{6,1},{7,0},{8,15},{9,14},{10,... | collective-permute-start | bytes 344072 | tf_op jit(solution)/shard_map/ppermute | solution.py:59
  75.2 5.1 %collective-permute-done.6 = bf16[2,32,896]{2,1,0:T(8,128)(2,1)S(1)} collective-permute-done((bf16[2,32,896]{2,1,0:T(8,128)(2,1)S(1)}, bf16[2,32,896]{2,1,0:T(8,128)(2,1)S(1)}, u32[]{:S(2)}, u32[]{:S(2)}) %collective-permute-start.6) | collective-permute-done | bytes 114720 | tf_op jit(solution)/shard_map/ppermute | solution.py:59
  81.3 1.2 fusion.53
  82.6 2.9 %fusion.35 = f32[32,256]{1,0:T(8,128)S(1)} fusion(bf16[32,7168]{1,0:T(8,128)(2,1)} %collective-permute-done.8, bf16[1,2,7168,256]{3,2,1,0:T(8,128)(2,1)} %param.6, f32[256]{0:T(256)} %bitcast.339), kind=kOutput, calls=%fused_computation.47 | convolution fusion | flops 117448704 | bytes 4162560 | tf_op jit(solution)/shard_map/dot_general | solution.py:18
  85.5 1.9 multiply_reduce_fusion.6
  89.3 2.5 %collective-permute-start.21 = (bf16[2,32,384]{2,1,0:T(8,128)(2,1)S(1)}, bf16[2,32,384]{2,1,0:T(8,128)(2,1)S(1)}, u32[]{:S(2)}, u32[]{:S(2)}) collective-permute-start(bf16[2,32,384]{2,1,0:T(8,128)(2,1)S(1)} %pad_maximum_fusion.26), channel_id=1, source_target_pairs={{0,6},{1,7},{2,4},{3,5},{4,2},{5,3},{6,0},{7,1},{8,14},{9,15},{10,... | collective-permute-start | bytes 147464 | tf_op jit(solution)/shard_map/ppermute | solution.py:59
  91.8 3.0 %collective-permute-start.19 = (bf16[2,32,384]{2,1,0:T(8,128)(2,1)S(1)}, bf16[2,32,384]{2,1,0:T(8,128)(2,1)S(1)}, u32[]{:S(2)}, u32[]{:S(2)}) collective-permute-start(bf16[2,32,384]{2,1,0:T(8,128)(2,1)S(1)} %pad_maximum_fusion.26), channel_id=1, source_target_pairs={{0,4},{1,5},{2,6},{3,7},{4,0},{5,1},{6,2},{7,3},{8,12},{9,13},{10,... | collective-permute-start | bytes 147464 | tf_op jit(solution)/shard_map/ppermute | solution.py:59
  94.7 3.0 %fusion.38 = f32[32,256]{1,0:T(8,128)S(1)} fusion(bf16[32,7168]{1,0:T(8,128)(2,1)} %collective-permute-done.31, bf16[1,2,7168,256]{3,2,1,0:T(8,128)(2,1)} %param.6, f32[256]{0:T(256)} %bitcast.340), kind=kOutput, calls=%fused_computation.48 | convolution fusion | flops 117448704 | bytes 4162560 | tf_op jit(solution)/shard_map/dot_general | solution.py:18
  97.8 3.7 %multiply_reduce_fusion.3 = (f32[32]{0:T(128)S(1)}, f32[32]{0:T(128)S(1)}, f32[32,256]{1,0:T(8,128)}) fusion(f32[32,256]{1,0:T(8,128)S(1)} %fusion.38, bf16[1,2,7168,256]{3,2,1,0:T(8,128)(2,1)} %param.6, f32[32]{0:T(128)S(1)} %copy-done.26, f32[7168]{0:T(1024)S(1)} %bitcast.334, bf16[1,2,32,7168]{3,2,1,0:T(8,128)(2,1)S(1)} %copy-done.2), kind=kOutput, calls=%fused_computation.221 | convolution fusion | flops 118390720 | bytes 4223744 | tf_op jit(solution)/shard_map/dot_general | solution.py:18
  101.5 1.5 collective-permute-start.16
  103.0 1.2 fusion.50
  104.9 1.1 dynamic-slice_bitcast_fusion.17
  105.9 1.1 dynamic-slice_bitcast_fusion.16
  118.7 3.1 %fusion.57 = bf16[32,7168]{1,0:T(8,128)(2,1)} fusion(bf16[32,7168]{1,0:T(8,128)(2,1)} %collective-permute-done.7, bf16[32,7168]{1,0:T(8,128)(2,1)} %collective-permute-done.8, f32[32]{0:T(128)S(1)} %get-tuple-element.18, f32[7168]{0:T(1024)S(1)} %bitcast.335, bf16[32,256]{1,0:T(8,128)(2,1)S(1)} %get-tuple-element.20, bf16[1,2,7168,256]{3,2,1,0:T(8,128)(2,1)S(1)} %bitcast.317), kind=kOutput, calls=%fused_computation.63 | convolution fusion | flops 119046144 | bytes 5091840 | tf_op jit(solution)/shard_map/dot_general | solution.py:14
  121.9 2.1 collective-permute-start.17
  124.0 2.1 collective-permute-done.17
  126.1 2.3 %collective-permute-start.22 = (bf16[2,32,384]{2,1,0:T(8,128)(2,1)S(1)}, bf16[2,32,384]{2,1,0:T(8,128)(2,1)S(1)}, u32[]{:S(2)}, u32[]{:S(2)}) collective-permute-start(bf16[2,32,384]{2,1,0:T(8,128)(2,1)S(1)} %pad_maximum_fusion.26), channel_id=1, source_target_pairs={{0,7},{1,6},{2,5},{3,4},{4,3},{5,2},{6,1},{7,0},{8,15},{9,14},{10,... | collective-permute-start | bytes 147464 | tf_op jit(solution)/shard_map/ppermute | solution.py:59
  130.0 2.1 collective-permute-start.11
  132.1 2.5 %collective-permute-start.12 = (bf16[2,32,896]{2,1,0:T(8,128)(2,1)}, bf16[2,32,896]{2,1,0:T(8,128)(2,1)}, u32[]{:S(2)}, u32[]{:S(2)}) collective-permute-start(bf16[2,32,896]{2,1,0:T(8,128)(2,1)} %pad_maximum_fusion.14), channel_id=1, source_target_pairs={{0,4},{1,5},{2,6},{3,7},{4,0},{5,1},{6,2},{7,3},{8,12},{9,13},{10,... | collective-permute-start | bytes 344072 | tf_op jit(solution)/shard_map/ppermute | solution.py:59
  136.0 1.3 copy.31
  138.4 3.3 %collective-permute-start.14 = (bf16[2,32,896]{2,1,0:T(8,128)(2,1)}, bf16[2,32,896]{2,1,0:T(8,128)(2,1)S(1)}, u32[]{:S(2)}, u32[]{:S(2)}) collective-permute-start(bf16[2,32,896]{2,1,0:T(8,128)(2,1)} %pad_maximum_fusion.16), channel_id=1, source_target_pairs={{0,6},{1,7},{2,4},{3,5},{4,2},{5,3},{6,0},{7,1},{8,14},{9,15},{10,... | collective-permute-start | bytes 344072 | tf_op jit(solution)/shard_map/ppermute | solution.py:59
  141.7 1.6 bitcast_dynamic-update-slice_fusion.13
  143.2 1.5 collective-permute-start.15
  144.8 1.6 bitcast_dynamic-update-slice_fusion.12
  146.3 1.3 collective-permute-start.32
  147.6 1.6 bitcast_dynamic-update-slice_fusion.11
  149.7 1.6 bitcast_dynamic-update-slice_fusion.10
  151.5 1.6 bitcast_dynamic-update-slice_fusion.9
  153.1 2.7 %collective-permute-start.26 = (bf16[2,32,896]{2,1,0:T(8,128)(2,1)}, bf16[2,32,896]{2,1,0:T(8,128)(2,1)S(1)}, u32[]{:S(2)}, u32[]{:S(2)}) collective-permute-start(bf16[2,32,896]{2,1,0:T(8,128)(2,1)} %pad_maximum_fusion.20), channel_id=1, source_target_pairs={{0,3},{1,2},{2,1},{3,0},{4,7},{5,6},{6,5},{7,4},{8,11},{9,10},{10,... | collective-permute-start | bytes 344072 | tf_op jit(solution)/shard_map/ppermute | solution.py:59
  156.4 2.3 %collective-permute-start.27 = (bf16[2,32,896]{2,1,0:T(8,128)(2,1)}, bf16[2,32,896]{2,1,0:T(8,128)(2,1)S(1)}, u32[]{:S(2)}, u32[]{:S(2)}) collective-permute-start(bf16[2,32,896]{2,1,0:T(8,128)(2,1)} %pad_maximum_fusion.21), channel_id=1, source_target_pairs={{0,4},{1,5},{2,6},{3,7},{4,0},{5,1},{6,2},{7,3},{8,12},{9,13},{10,... | collective-permute-start | bytes 344072 | tf_op jit(solution)/shard_map/ppermute | solution.py:59
  159.4 1.4 slice_bitcast_fusion
  163.0 3.3 %collective-permute-start.29 = (bf16[2,32,896]{2,1,0:T(8,128)(2,1)S(1)}, bf16[2,32,896]{2,1,0:T(8,128)(2,1)S(1)}, u32[]{:S(2)}, u32[]{:S(2)}) collective-permute-start(bf16[2,32,896]{2,1,0:T(8,128)(2,1)S(1)} %copy-done.10), channel_id=1, source_target_pairs={{0,6},{1,7},{2,4},{3,5},{4,2},{5,3},{6,0},{7,1},{8,14},{9,15},{10,... | collective-permute-start | bytes 344072 | tf_op jit(solution)/shard_map/ppermute | solution.py:59
  166.4 1.6 collective-permute-start.30
  168.0 1.5 collective-permute-start.40
  169.5 8.0 %collective-permute-done.28 = bf16[2,32,896]{2,1,0:T(8,128)(2,1)S(1)} collective-permute-done((bf16[2,32,896]{2,1,0:T(8,128)(2,1)S(1)}, bf16[2,32,896]{2,1,0:T(8,128)(2,1)S(1)}, u32[]{:S(2)}, u32[]{:S(2)}) %collective-permute-start.28) | collective-permute-done | bytes 114720 | tf_op jit(solution)/shard_map/ppermute | solution.py:59
  178.7 1.9 multiply_reduce_fusion.1
  180.8 1.2 collective-permute-start.38
  182.0 5.1 %collective-permute-start.37 = (bf16[2,32,768]{2,1,0:T(8,128)(2,1)S(1)}, bf16[2,32,768]{2,1,0:T(8,128)(2,1)S(1)}, u32[]{:S(2)}, u32[]{:S(2)}) collective-permute-start(bf16[2,32,768]{2,1,0:T(8,128)(2,1)S(1)} %pad_maximum_fusion.25), channel_id=1, source_target_pairs={{0,5},{1,4},{2,7},{3,6},{4,1},{5,0},{6,3},{7,2},{8,13},{9,12},{10,... | collective-permute-start | bytes 294920 | tf_op jit(solution)/shard_map/ppermute | solution.py:59
  187.2 1.5 collective-permute-start.33
  188.6 3.2 %collective-permute-done.33 = bf16[2,32,768]{2,1,0:T(8,128)(2,1)S(1)} collective-permute-done((bf16[2,32,768]{2,1,0:T(8,128)(2,1)S(1)}, bf16[2,32,768]{2,1,0:T(8,128)(2,1)S(1)}, u32[]{:S(2)}, u32[]{:S(2)}) %collective-permute-start.33) | collective-permute-done | bytes 98336 | tf_op jit(solution)/shard_map/ppermute | solution.py:59
  191.9 3.3 %collective-permute-start.34 = (bf16[2,32,768]{2,1,0:T(8,128)(2,1)S(1)}, bf16[2,32,768]{2,1,0:T(8,128)(2,1)S(1)}, u32[]{:S(2)}, u32[]{:S(2)}) collective-permute-start(bf16[2,32,768]{2,1,0:T(8,128)(2,1)S(1)} %pad_maximum_fusion.25), channel_id=1, source_target_pairs={{0,2},{1,3},{2,0},{3,1},{4,6},{5,7},{6,4},{7,5},{8,10},{9,11},{10,... | collective-permute-start | bytes 294920 | tf_op jit(solution)/shard_map/ppermute | solution.py:59
  195.2 4.7 %collective-permute-done.34 = bf16[2,32,768]{2,1,0:T(8,128)(2,1)S(1)} collective-permute-done((bf16[2,32,768]{2,1,0:T(8,128)(2,1)S(1)}, bf16[2,32,768]{2,1,0:T(8,128)(2,1)S(1)}, u32[]{:S(2)}, u32[]{:S(2)}) %collective-permute-start.34) | collective-permute-done | bytes 98336 | tf_op jit(solution)/shard_map/ppermute | solution.py:59
  200.5 5.1 %collective-permute-done.35 = bf16[2,32,768]{2,1,0:T(8,128)(2,1)S(1)} collective-permute-done((bf16[2,32,768]{2,1,0:T(8,128)(2,1)S(1)}, bf16[2,32,768]{2,1,0:T(8,128)(2,1)S(1)}, u32[]{:S(2)}, u32[]{:S(2)}) %collective-permute-start.35) | collective-permute-done | bytes 98336 | tf_op jit(solution)/shard_map/ppermute | solution.py:59
  205.6 2.7 %collective-permute-start.39 = (bf16[2,32,768]{2,1,0:T(8,128)(2,1)S(1)}, bf16[2,32,768]{2,1,0:T(8,128)(2,1)S(1)}, u32[]{:S(2)}, u32[]{:S(2)}) collective-permute-start(bf16[2,32,768]{2,1,0:T(8,128)(2,1)S(1)} %pad_maximum_fusion.25), channel_id=1, source_target_pairs={{0,7},{1,6},{2,5},{3,4},{4,3},{5,2},{6,1},{7,0},{8,15},{9,14},{10,... | collective-permute-start | bytes 294920 | tf_op jit(solution)/shard_map/ppermute | solution.py:59
  208.3 4.6 %collective-permute-done.39 = bf16[2,32,768]{2,1,0:T(8,128)(2,1)S(1)} collective-permute-done((bf16[2,32,768]{2,1,0:T(8,128)(2,1)S(1)}, bf16[2,32,768]{2,1,0:T(8,128)(2,1)S(1)}, u32[]{:S(2)}, u32[]{:S(2)}) %collective-permute-start.39) | collective-permute-done | bytes 98336 | tf_op jit(solution)/shard_map/ppermute | solution.py:59
  (225 shorter events, 44.6 us)
Async XLA Ops:
  0.0 5.9 %copy-start.1 = (bf16[1,2,32,7168]{3,2,1,0:T(8,128)(2,1)S(1)}, bf16[1,2,32,7168]{3,2,1,0:T(8,128)(2,1)}, u32[]{:S(2)}) copy-start(bf16[1,2,32,7168]{3,2,1,0:T(8,128)(2,1)} %param.9) | copy-start | bytes 2752516
  2.0 7.3 %copy-start.22 = (f32[1,256]{1,0:T(1,128)}, f32[1,256]{1,0:T(1,128)S(1)}, u32[]{:S(2)}) copy-start(f32[1,256]{1,0:T(1,128)S(1)} %mul.563) | copy-start | bytes 3076
  2.8 23.5 %copy-start.15 = (f32[1,7168]{1,0:T(1,128)}, f32[1,7168]{1,0:T(1,128)S(1)}, u32[]{:S(2)}) copy-start(f32[1,7168]{1,0:T(1,128)S(1)} %mul.562) | copy-start | bytes 86020
  2.8 7.4 %copy-start = (bf16[1,2,7168,256]{3,2,1,0:T(8,128)(2,1)S(1)}, bf16[1,2,7168,256]{3,2,1,0:T(8,128)(2,1)}, u32[]{:S(2)}) copy-start(bf16[1,2,7168,256]{3,2,1,0:T(8,128)(2,1)} %param.6) | copy-start | bytes 22020100
  2.8 7.4 %copy-start.7 = (bf16[2,1,32,7168]{3,2,1,0:T(8,128)(2,1)S(1)}, bf16[2,1,32,7168]{3,2,1,0:T(8,128)(2,1)}, u32[]{:S(2)}) copy-start(bf16[2,1,32,7168]{3,2,1,0:T(8,128)(2,1)} %param.11) | copy-start | bytes 2752516
  9.3 4.1 %copy-start.6 = (bf16[1,2,32,7168]{3,2,1,0:T(8,128)(2,1)S(1)}, bf16[1,2,32,7168]{3,2,1,0:T(8,128)(2,1)}, u32[]{:S(2)}) copy-start(bf16[1,2,32,7168]{3,2,1,0:T(8,128)(2,1)} %param.10) | copy-start | bytes 2752516
  10.1 4.3 %copy-start.12 = (bf16[32,256]{1,0:T(8,128)(2,1)}, bf16[32,256]{1,0:T(8,128)(2,1)S(1)}, u32[]{:S(2)}) copy-start(bf16[32,256]{1,0:T(8,128)(2,1)S(1)} %get-tuple-element.16) | copy-start | bytes 49156
  12.1 82.6 %collective-permute-start.31 = (bf16[32,7168]{1,0:T(8,128)(2,1)}, bf16[32,7168]{1,0:T(8,128)(2,1)}, u32[]{:S(2)}, u32[]{:S(2)}) collective-permute-start(bf16[32,7168]{1,0:T(8,128)(2,1)} %fusion.2), channel_id=1, source_target_pairs={{8,0},{16,8},{24,16},{9,1},{17,9},{25,17},{10,2},{18,10},{26,18},{... | collective-permute-start | bytes 1376264 | tf_op jit(solution)/shard_map/ppermute | solution.py:56
  14.4 87.1 %collective-permute-start.23 = (bf16[32,7168]{1,0:T(8,128)(2,1)}, bf16[32,7168]{1,0:T(8,128)(2,1)}, u32[]{:S(2)}, u32[]{:S(2)}) collective-permute-start(bf16[32,7168]{1,0:T(8,128)(2,1)} %get-tuple-element.25), channel_id=1, source_target_pairs={{0,24},{8,16},{16,8},{24,0},{1,25},{9,17},{17,9},{25,1},{2,26},{10... | collective-permute-start | bytes 1376264 | tf_op jit(solution)/shard_map/ppermute | solution.py:53
  18.9 62.4 %collective-permute-start.7 = (bf16[32,7168]{1,0:T(8,128)(2,1)}, bf16[32,7168]{1,0:T(8,128)(2,1)}, u32[]{:S(2)}, u32[]{:S(2)}) collective-permute-start(bf16[32,7168]{1,0:T(8,128)(2,1)} %get-tuple-element.26), channel_id=1, source_target_pairs={{0,24},{8,16},{16,8},{24,0},{1,25},{9,17},{17,9},{25,1},{2,26},{10... | collective-permute-start | bytes 1376264 | tf_op jit(solution)/shard_map/ppermute | solution.py:53
  19.8 62.8 %collective-permute-start.8 = (bf16[32,7168]{1,0:T(8,128)(2,1)}, bf16[32,7168]{1,0:T(8,128)(2,1)}, u32[]{:S(2)}, u32[]{:S(2)}) collective-permute-start(bf16[32,7168]{1,0:T(8,128)(2,1)} %get-tuple-element.32), channel_id=1, source_target_pairs={{0,24},{8,16},{16,8},{24,0},{1,25},{9,17},{17,9},{25,1},{2,26},{10... | collective-permute-start | bytes 1376264 | tf_op jit(solution)/shard_map/ppermute | solution.py:53
  24.5 12.5 %collective-permute-start = (bf16[2,32,896]{2,1,0:T(8,128)(2,1)}, bf16[2,32,896]{2,1,0:T(8,128)(2,1)}, u32[]{:S(2)}, u32[]{:S(2)}) collective-permute-start(bf16[2,32,896]{2,1,0:T(8,128)(2,1)} %pad_maximum_fusion.4), channel_id=1, source_target_pairs={{0,1},{1,0},{2,3},{3,2},{4,5},{5,4},{6,7},{7,6},{8,9},{9,8},{10,11... | collective-permute-start | bytes 344072 | tf_op jit(solution)/shard_map/ppermute | solution.py:59
  26.9 58.6 %slice-start = ((s8[7340032]{0:T(1024)(128)(4,1)}), s8[3145728]{0:T(1024)(128)(4,1)S(1)}, s32[]{:S(2)}) async-start(s8[7340032]{0:T(1024)(128)(4,1)} %bitcast.314), calls=%async_computation | async-start | bytes 6291456
  33.2 52.3 %slice-start.1 = ((s8[7340032]{0:T(1024)(128)(4,1)}), s8[4194304]{0:T(1024)(128)(4,1)S(1)}, s32[]{:S(2)}) async-start(s8[7340032]{0:T(1024)(128)(4,1)} %bitcast.314), calls=%async_computation.1 | async-start | bytes 8388608
  37.1 4.9 %collective-permute-start.1 = (bf16[2,32,896]{2,1,0:T(8,128)(2,1)S(1)}, bf16[2,32,896]{2,1,0:T(8,128)(2,1)S(1)}, u32[]{:S(2)}, u32[]{:S(2)}) collective-permute-start(bf16[2,32,896]{2,1,0:T(8,128)(2,1)S(1)} %pad_maximum_fusion.5), channel_id=1, source_target_pairs={{0,2},{1,3},{2,0},{3,1},{4,6},{5,7},{6,4},{7,5},{8,10},{9,11},{10,... | collective-permute-start | bytes 344072 | tf_op jit(solution)/shard_map/ppermute | solution.py:59
  41.9 5.7 %collective-permute-start.2 = (bf16[2,32,896]{2,1,0:T(8,128)(2,1)S(1)}, bf16[2,32,896]{2,1,0:T(8,128)(2,1)S(1)}, u32[]{:S(2)}, u32[]{:S(2)}) collective-permute-start(bf16[2,32,896]{2,1,0:T(8,128)(2,1)S(1)} %pad_maximum_fusion.6), channel_id=1, source_target_pairs={{0,3},{1,2},{2,1},{3,0},{4,7},{5,6},{6,5},{7,4},{8,11},{9,10},{10,... | collective-permute-start | bytes 344072 | tf_op jit(solution)/shard_map/ppermute | solution.py:59
  47.6 8.9 %collective-permute-start.3 = (bf16[2,32,896]{2,1,0:T(8,128)(2,1)S(1)}, bf16[2,32,896]{2,1,0:T(8,128)(2,1)S(1)}, u32[]{:S(2)}, u32[]{:S(2)}) collective-permute-start(bf16[2,32,896]{2,1,0:T(8,128)(2,1)S(1)} %pad_maximum_fusion.7), channel_id=1, source_target_pairs={{0,4},{1,5},{2,6},{3,7},{4,0},{5,1},{6,2},{7,3},{8,12},{9,13},{10,... | collective-permute-start | bytes 344072 | tf_op jit(solution)/shard_map/ppermute | solution.py:59
  50.7 34.8 %copy-start.16 = (f32[1,7168]{1,0:T(1,128)S(1)}, f32[1,7168]{1,0:T(1,128)}, u32[]{:S(2)}) copy-start(f32[1,7168]{1,0:T(1,128)} %copy-done.15) | copy-start | bytes 86020
  56.5 9.7 %collective-permute-start.4 = (bf16[2,32,896]{2,1,0:T(8,128)(2,1)S(1)}, bf16[2,32,896]{2,1,0:T(8,128)(2,1)S(1)}, u32[]{:S(2)}, u32[]{:S(2)}) collective-permute-start(bf16[2,32,896]{2,1,0:T(8,128)(2,1)S(1)} %pad_maximum_fusion.8), channel_id=1, source_target_pairs={{0,5},{1,4},{2,7},{3,6},{4,1},{5,0},{6,3},{7,2},{8,13},{9,12},{10,... | collective-permute-start | bytes 344072 | tf_op jit(solution)/shard_map/ppermute | solution.py:59
  66.2 6.6 %collective-permute-start.5 = (bf16[2,32,896]{2,1,0:T(8,128)(2,1)S(1)}, bf16[2,32,896]{2,1,0:T(8,128)(2,1)S(1)}, u32[]{:S(2)}, u32[]{:S(2)}) collective-permute-start(bf16[2,32,896]{2,1,0:T(8,128)(2,1)S(1)} %pad_maximum_fusion.9), channel_id=1, source_target_pairs={{0,6},{1,7},{2,4},{3,5},{4,2},{5,3},{6,0},{7,1},{8,14},{9,15},{10,... | collective-permute-start | bytes 344072 | tf_op jit(solution)/shard_map/ppermute | solution.py:59
  72.8 7.5 %collective-permute-start.6 = (bf16[2,32,896]{2,1,0:T(8,128)(2,1)S(1)}, bf16[2,32,896]{2,1,0:T(8,128)(2,1)S(1)}, u32[]{:S(2)}, u32[]{:S(2)}) collective-permute-start(bf16[2,32,896]{2,1,0:T(8,128)(2,1)S(1)} %pad_maximum_fusion.10), channel_id=1, source_target_pairs={{0,7},{1,6},{2,5},{3,4},{4,3},{5,2},{6,1},{7,0},{8,15},{9,14},{10,... | collective-permute-start | bytes 344072 | tf_op jit(solution)/shard_map/ppermute | solution.py:59
  82.6 4.9 %copy-start.23 = (f32[1,256]{1,0:T(1,128)S(1)}, f32[1,256]{1,0:T(1,128)}, u32[]{:S(2)}) copy-start(f32[1,256]{1,0:T(1,128)} %copy-done.22) | copy-start | bytes 3076
  87.4 10.3 %copy-start.2 = (bf16[1,2,32,7168]{3,2,1,0:T(8,128)(2,1)S(1)}, bf16[1,2,32,7168]{3,2,1,0:T(8,128)(2,1)}, u32[]{:S(2)}) copy-start(bf16[1,2,32,7168]{3,2,1,0:T(8,128)(2,1)} %param.9) | copy-start | bytes 2752516
  87.4 10.3 %copy-start.17 = (f32[1,7168]{1,0:T(1,128)S(1)}, f32[1,7168]{1,0:T(1,128)}, u32[]{:S(2)}) copy-start(f32[1,7168]{1,0:T(1,128)} %copy-done.15) | copy-start | bytes 86020
  87.4 10.3 %copy-start.26 = (f32[32]{0:T(128)S(1)}, f32[32]{0:T(128)}, u32[]{:S(2)}) copy-start(f32[32]{0:T(128)} %add_rsqrt_fusion.3) | copy-start | bytes 388
  89.3 42.8 %collective-permute-start.21 = (bf16[2,32,384]{2,1,0:T(8,128)(2,1)S(1)}, bf16[2,32,384]{2,1,0:T(8,128)(2,1)S(1)}, u32[]{:S(2)}, u32[]{:S(2)}) collective-permute-start(bf16[2,32,384]{2,1,0:T(8,128)(2,1)S(1)} %pad_maximum_fusion.26), channel_id=1, source_target_pairs={{0,6},{1,7},{2,4},{3,5},{4,2},{5,3},{6,0},{7,1},{8,14},{9,15},{10,... | collective-permute-start | bytes 147464 | tf_op jit(solution)/shard_map/ppermute | solution.py:59
  91.8 38.2 %collective-permute-start.20 = (bf16[2,32,384]{2,1,0:T(8,128)(2,1)S(1)}, bf16[2,32,384]{2,1,0:T(8,128)(2,1)S(1)}, u32[]{:S(2)}, u32[]{:S(2)}) collective-permute-start(bf16[2,32,384]{2,1,0:T(8,128)(2,1)S(1)} %pad_maximum_fusion.26), channel_id=1, source_target_pairs={{0,5},{1,4},{2,7},{3,6},{4,1},{5,0},{6,3},{7,2},{8,13},{9,12},{10,... | collective-permute-start | bytes 147464 | tf_op jit(solution)/shard_map/ppermute | solution.py:59
  91.8 37.3 %collective-permute-start.19 = (bf16[2,32,384]{2,1,0:T(8,128)(2,1)S(1)}, bf16[2,32,384]{2,1,0:T(8,128)(2,1)S(1)}, u32[]{:S(2)}, u32[]{:S(2)}) collective-permute-start(bf16[2,32,384]{2,1,0:T(8,128)(2,1)S(1)} %pad_maximum_fusion.26), channel_id=1, source_target_pairs={{0,4},{1,5},{2,6},{3,7},{4,0},{5,1},{6,2},{7,3},{8,12},{9,13},{10,... | collective-permute-start | bytes 147464 | tf_op jit(solution)/shard_map/ppermute | solution.py:59
  94.7 33.7 %collective-permute-start.18 = (bf16[2,32,384]{2,1,0:T(8,128)(2,1)S(1)}, bf16[2,32,384]{2,1,0:T(8,128)(2,1)S(1)}, u32[]{:S(2)}, u32[]{:S(2)}) collective-permute-start(bf16[2,32,384]{2,1,0:T(8,128)(2,1)S(1)} %pad_maximum_fusion.26), channel_id=1, source_target_pairs={{0,3},{1,2},{2,1},{3,0},{4,7},{5,6},{6,5},{7,4},{8,11},{9,10},{10,... | collective-permute-start | bytes 147464 | tf_op jit(solution)/shard_map/ppermute | solution.py:59
  94.7 24.0 %slice-start.2 = ((s8[7340032]{0:T(1024)(128)(4,1)}), s8[4194304]{0:T(1024)(128)(4,1)S(1)}, s32[]{:S(2)}) async-start(s8[7340032]{0:T(1024)(128)(4,1)} %bitcast.316), calls=%async_computation.2 | async-start | bytes 8388608
  97.8 20.9 %slice-start.3 = ((s8[7340032]{0:T(1024)(128)(4,1)}), s8[3145728]{0:T(1024)(128)(4,1)S(1)}, s32[]{:S(2)}) async-start(s8[7340032]{0:T(1024)(128)(4,1)} %bitcast.316), calls=%async_computation.3 | async-start | bytes 6291456
  101.5 11.9 %copy-start.8 = (bf16[1,32,896]{2,1,0:T(8,128)(2,1)S(1)}, bf16[1,32,896]{2,1,0:T(8,128)(2,1)}, u32[]{:S(2)}) copy-start(bf16[1,32,896]{2,1,0:T(8,128)(2,1)} %get-tuple-element.33) | copy-start | bytes 172036
  101.5 20.3 %collective-permute-start.16 = (bf16[2,32,384]{2,1,0:T(8,128)(2,1)S(1)}, bf16[2,32,384]{2,1,0:T(8,128)(2,1)S(1)}, u32[]{:S(2)}, u32[]{:S(2)}) collective-permute-start(bf16[2,32,384]{2,1,0:T(8,128)(2,1)S(1)} %pad_maximum_fusion.26), channel_id=1, source_target_pairs={{0,1},{1,0},{2,3},{3,2},{4,5},{5,4},{6,7},{7,6},{8,9},{9,8},{10,11... | collective-permute-start | bytes 147464 | tf_op jit(solution)/shard_map/ppermute | solution.py:59
  121.9 4.2 %collective-permute-start.17 = (bf16[2,32,384]{2,1,0:T(8,128)(2,1)S(1)}, bf16[2,32,384]{2,1,0:T(8,128)(2,1)S(1)}, u32[]{:S(2)}, u32[]{:S(2)}) collective-permute-start(bf16[2,32,384]{2,1,0:T(8,128)(2,1)S(1)} %pad_maximum_fusion.26), channel_id=1, source_target_pairs={{0,2},{1,3},{2,0},{3,1},{4,6},{5,7},{6,4},{7,5},{8,10},{9,11},{10,... | collective-permute-start | bytes 147464 | tf_op jit(solution)/shard_map/ppermute | solution.py:59
  126.1 8.6 %collective-permute-start.22 = (bf16[2,32,384]{2,1,0:T(8,128)(2,1)S(1)}, bf16[2,32,384]{2,1,0:T(8,128)(2,1)S(1)}, u32[]{:S(2)}, u32[]{:S(2)}) collective-permute-start(bf16[2,32,384]{2,1,0:T(8,128)(2,1)S(1)} %pad_maximum_fusion.26), channel_id=1, source_target_pairs={{0,7},{1,6},{2,5},{3,4},{4,3},{5,2},{6,1},{7,0},{8,15},{9,14},{10,... | collective-permute-start | bytes 147464 | tf_op jit(solution)/shard_map/ppermute | solution.py:59
  128.4 9.9 %collective-permute-start.9 = (bf16[2,32,896]{2,1,0:T(8,128)(2,1)}, bf16[2,32,896]{2,1,0:T(8,128)(2,1)}, u32[]{:S(2)}, u32[]{:S(2)}) collective-permute-start(bf16[2,32,896]{2,1,0:T(8,128)(2,1)} %pad_maximum_fusion.11), channel_id=1, source_target_pairs={{0,1},{1,0},{2,3},{3,2},{4,5},{5,4},{6,7},{7,6},{8,9},{9,8},{10,11... | collective-permute-start | bytes 344072 | tf_op jit(solution)/shard_map/ppermute | solution.py:59
  129.1 14.2 %collective-permute-start.10 = (bf16[2,32,896]{2,1,0:T(8,128)(2,1)}, bf16[2,32,896]{2,1,0:T(8,128)(2,1)}, u32[]{:S(2)}, u32[]{:S(2)}) collective-permute-start(bf16[2,32,896]{2,1,0:T(8,128)(2,1)} %pad_maximum_fusion.12), channel_id=1, source_target_pairs={{0,2},{1,3},{2,0},{3,1},{4,6},{5,7},{6,4},{7,5},{8,10},{9,11},{10,... | collective-permute-start | bytes 344072 | tf_op jit(solution)/shard_map/ppermute | solution.py:59
  130.0 16.3 %collective-permute-start.11 = (bf16[2,32,896]{2,1,0:T(8,128)(2,1)}, bf16[2,32,896]{2,1,0:T(8,128)(2,1)}, u32[]{:S(2)}, u32[]{:S(2)}) collective-permute-start(bf16[2,32,896]{2,1,0:T(8,128)(2,1)} %pad_maximum_fusion.13), channel_id=1, source_target_pairs={{0,3},{1,2},{2,1},{3,0},{4,7},{5,6},{6,5},{7,4},{8,11},{9,10},{10,... | collective-permute-start | bytes 344072 | tf_op jit(solution)/shard_map/ppermute | solution.py:59
  132.1 17.0 %collective-permute-start.12 = (bf16[2,32,896]{2,1,0:T(8,128)(2,1)}, bf16[2,32,896]{2,1,0:T(8,128)(2,1)}, u32[]{:S(2)}, u32[]{:S(2)}) collective-permute-start(bf16[2,32,896]{2,1,0:T(8,128)(2,1)} %pad_maximum_fusion.14), channel_id=1, source_target_pairs={{0,4},{1,5},{2,6},{3,7},{4,0},{5,1},{6,2},{7,3},{8,12},{9,13},{10,... | collective-permute-start | bytes 344072 | tf_op jit(solution)/shard_map/ppermute | solution.py:59
  134.7 16.6 %collective-permute-start.13 = (bf16[2,32,896]{2,1,0:T(8,128)(2,1)}, bf16[2,32,896]{2,1,0:T(8,128)(2,1)}, u32[]{:S(2)}, u32[]{:S(2)}) collective-permute-start(bf16[2,32,896]{2,1,0:T(8,128)(2,1)} %pad_maximum_fusion.15), channel_id=1, source_target_pairs={{0,5},{1,4},{2,7},{3,6},{4,1},{5,0},{6,3},{7,2},{8,13},{9,12},{10,... | collective-permute-start | bytes 344072 | tf_op jit(solution)/shard_map/ppermute | solution.py:59
  135.3 42.6 %slice-start.4 = ((s8[7340032]{0:T(1024)(128)(4,1)}), s8[3145728]{0:T(1024)(128)(4,1)S(1)}, s32[]{:S(2)}) async-start(s8[7340032]{0:T(1024)(128)(4,1)} %bitcast.318), calls=%async_computation.4 | async-start | bytes 6291456
  138.3 22.5 %copy-start.4 = (bf16[8,1,32,896]{3,2,0,1:T(8,128)(2,1)S(1)}, bf16[8,1,32,896]{3,2,0,1:T(8,128)(2,1)}, u32[]{:S(2)}) copy-start(bf16[8,1,32,896]{3,2,0,1:T(8,128)(2,1)} %get-tuple-element.27) | copy-start | bytes 1376260
  138.3 22.7 %copy-start.3 = (bf16[8,1,32,896]{3,2,1,0:T(8,128)(2,1)S(1)}, bf16[8,1,32,896]{3,2,1,0:T(8,128)(2,1)}, u32[]{:S(2)}) copy-start(bf16[8,1,32,896]{3,2,1,0:T(8,128)(2,1)} %get-tuple-element.28) | copy-start | bytes 1376260
  138.4 14.7 %collective-permute-start.14 = (bf16[2,32,896]{2,1,0:T(8,128)(2,1)}, bf16[2,32,896]{2,1,0:T(8,128)(2,1)S(1)}, u32[]{:S(2)}, u32[]{:S(2)}) collective-permute-start(bf16[2,32,896]{2,1,0:T(8,128)(2,1)} %pad_maximum_fusion.16), channel_id=1, source_target_pairs={{0,6},{1,7},{2,4},{3,5},{4,2},{5,3},{6,0},{7,1},{8,14},{9,15},{10,... | collective-permute-start | bytes 344072 | tf_op jit(solution)/shard_map/ppermute | solution.py:59
  143.2 13.2 %collective-permute-start.15 = (bf16[2,32,896]{2,1,0:T(8,128)(2,1)}, bf16[2,32,896]{2,1,0:T(8,128)(2,1)S(1)}, u32[]{:S(2)}, u32[]{:S(2)}) collective-permute-start(bf16[2,32,896]{2,1,0:T(8,128)(2,1)} %pad_maximum_fusion.17), channel_id=1, source_target_pairs={{0,7},{1,6},{2,5},{3,4},{4,3},{5,2},{6,1},{7,0},{8,15},{9,14},{10,... | collective-permute-start | bytes 344072 | tf_op jit(solution)/shard_map/ppermute | solution.py:59
  146.3 31.6 %collective-permute-start.32 = (bf16[32,7168]{1,0:T(8,128)(2,1)}, bf16[32,7168]{1,0:T(8,128)(2,1)S(1)}, u32[]{:S(2)}, u32[]{:S(2)}) collective-permute-start(bf16[32,7168]{1,0:T(8,128)(2,1)} %fusion.57), channel_id=1, source_target_pairs={{8,0},{16,8},{24,16},{9,1},{17,9},{25,17},{10,2},{18,10},{26,18},{... | collective-permute-start | bytes 1376264 | tf_op jit(solution)/shard_map/ppermute | solution.py:56
  149.2 13.1 %collective-permute-start.24 = (bf16[2,32,896]{2,1,0:T(8,128)(2,1)}, bf16[2,32,896]{2,1,0:T(8,128)(2,1)S(1)}, u32[]{:S(2)}, u32[]{:S(2)}) collective-permute-start(bf16[2,32,896]{2,1,0:T(8,128)(2,1)} %pad_maximum_fusion.18), channel_id=1, source_target_pairs={{0,1},{1,0},{2,3},{3,2},{4,5},{5,4},{6,7},{7,6},{8,9},{9,8},{10,11... | collective-permute-start | bytes 344072 | tf_op jit(solution)/shard_map/ppermute | solution.py:59
  151.2 11.8 %collective-permute-start.25 = (bf16[2,32,896]{2,1,0:T(8,128)(2,1)}, bf16[2,32,896]{2,1,0:T(8,128)(2,1)S(1)}, u32[]{:S(2)}, u32[]{:S(2)}) collective-permute-start(bf16[2,32,896]{2,1,0:T(8,128)(2,1)} %pad_maximum_fusion.19), channel_id=1, source_target_pairs={{0,2},{1,3},{2,0},{3,1},{4,6},{5,7},{6,4},{7,5},{8,10},{9,11},{10,... | collective-permute-start | bytes 344072 | tf_op jit(solution)/shard_map/ppermute | solution.py:59
  153.1 13.3 %collective-permute-start.26 = (bf16[2,32,896]{2,1,0:T(8,128)(2,1)}, bf16[2,32,896]{2,1,0:T(8,128)(2,1)S(1)}, u32[]{:S(2)}, u32[]{:S(2)}) collective-permute-start(bf16[2,32,896]{2,1,0:T(8,128)(2,1)} %pad_maximum_fusion.20), channel_id=1, source_target_pairs={{0,3},{1,2},{2,1},{3,0},{4,7},{5,6},{6,5},{7,4},{8,11},{9,10},{10,... | collective-permute-start | bytes 344072 | tf_op jit(solution)/shard_map/ppermute | solution.py:59
  156.4 11.6 %collective-permute-start.27 = (bf16[2,32,896]{2,1,0:T(8,128)(2,1)}, bf16[2,32,896]{2,1,0:T(8,128)(2,1)S(1)}, u32[]{:S(2)}, u32[]{:S(2)}) collective-permute-start(bf16[2,32,896]{2,1,0:T(8,128)(2,1)} %pad_maximum_fusion.21), channel_id=1, source_target_pairs={{0,4},{1,5},{2,6},{3,7},{4,0},{5,1},{6,2},{7,3},{8,12},{9,13},{10,... | collective-permute-start | bytes 344072 | tf_op jit(solution)/shard_map/ppermute | solution.py:59
  160.9 5.5 %copy-start.9 = (bf16[2,32,896]{2,1,0:T(8,128)(2,1)S(1)}, bf16[2,32,896]{2,1,0:T(8,128)(2,1)}, u32[]{:S(2)}) copy-start(bf16[2,32,896]{2,1,0:T(8,128)(2,1)} %pad_maximum_fusion.24) | copy-start | bytes 344068
  161.0 16.9 %slice-start.5 = ((s8[7340032]{0:T(1024)(128)(4,1)}), s8[4194304]{0:T(1024)(128)(4,1)S(1)}, s32[]{:S(2)}) async-start(s8[7340032]{0:T(1024)(128)(4,1)} %bitcast.318), calls=%async_computation.5 | async-start | bytes 8388608
  161.7 16.2 %copy-start.24 = (f32[1,256]{1,0:T(1,128)S(1)}, f32[1,256]{1,0:T(1,128)}, u32[]{:S(2)}) copy-start(f32[1,256]{1,0:T(1,128)} %copy-done.22) | copy-start | bytes 3076
  162.3 15.2 %collective-permute-start.28 = (bf16[2,32,896]{2,1,0:T(8,128)(2,1)S(1)}, bf16[2,32,896]{2,1,0:T(8,128)(2,1)S(1)}, u32[]{:S(2)}, u32[]{:S(2)}) collective-permute-start(bf16[2,32,896]{2,1,0:T(8,128)(2,1)S(1)} %copy-done.11), channel_id=1, source_target_pairs={{0,5},{1,4},{2,7},{3,6},{4,1},{5,0},{6,3},{7,2},{8,13},{9,12},{10,... | collective-permute-start | bytes 344072 | tf_op jit(solution)/shard_map/ppermute | solution.py:59
  163.0 14.5 %collective-permute-start.29 = (bf16[2,32,896]{2,1,0:T(8,128)(2,1)S(1)}, bf16[2,32,896]{2,1,0:T(8,128)(2,1)S(1)}, u32[]{:S(2)}, u32[]{:S(2)}) collective-permute-start(bf16[2,32,896]{2,1,0:T(8,128)(2,1)S(1)} %copy-done.10), channel_id=1, source_target_pairs={{0,6},{1,7},{2,4},{3,5},{4,2},{5,3},{6,0},{7,1},{8,14},{9,15},{10,... | collective-permute-start | bytes 344072 | tf_op jit(solution)/shard_map/ppermute | solution.py:59
  166.4 11.2 %collective-permute-start.30 = (bf16[2,32,896]{2,1,0:T(8,128)(2,1)S(1)}, bf16[2,32,896]{2,1,0:T(8,128)(2,1)S(1)}, u32[]{:S(2)}, u32[]{:S(2)}) collective-permute-start(bf16[2,32,896]{2,1,0:T(8,128)(2,1)S(1)} %copy-done.9), channel_id=1, source_target_pairs={{0,7},{1,6},{2,5},{3,4},{4,3},{5,2},{6,1},{7,0},{8,15},{9,14},{10,... | collective-permute-start | bytes 344072 | tf_op jit(solution)/shard_map/ppermute | solution.py:59
  168.0 45.8 %collective-permute-start.40 = (bf16[512,896]{1,0:T(8,128)(2,1)S(1)}, bf16[512,896]{1,0:T(8,128)(2,1)S(1)}, u32[]{:S(2)}, u32[]{:S(2)}) collective-permute-start(bf16[512,896]{1,0:T(8,128)(2,1)S(1)} %subtract_convert_fusion), channel_id=1, source_target_pairs={{8,0},{16,8},{24,16},{9,1},{17,9},{25,17},{10,2},{18,10},{26,18},{... | collective-permute-start | bytes 2752520 | tf_op jit(solution)/shard_map/ppermute | solution.py:56
  180.8 27.5 %collective-permute-start.38 = (bf16[2,32,768]{2,1,0:T(8,128)(2,1)S(1)}, bf16[2,32,768]{2,1,0:T(8,128)(2,1)S(1)}, u32[]{:S(2)}, u32[]{:S(2)}) collective-permute-start(bf16[2,32,768]{2,1,0:T(8,128)(2,1)S(1)} %pad_maximum_fusion.25), channel_id=1, source_target_pairs={{0,6},{1,7},{2,4},{3,5},{4,2},{5,3},{6,0},{7,1},{8,14},{9,15},{10,... | collective-permute-start | bytes 294920 | tf_op jit(solution)/shard_map/ppermute | solution.py:59
  182.0 26.2 %collective-permute-start.37 = (bf16[2,32,768]{2,1,0:T(8,128)(2,1)S(1)}, bf16[2,32,768]{2,1,0:T(8,128)(2,1)S(1)}, u32[]{:S(2)}, u32[]{:S(2)}) collective-permute-start(bf16[2,32,768]{2,1,0:T(8,128)(2,1)S(1)} %pad_maximum_fusion.25), channel_id=1, source_target_pairs={{0,5},{1,4},{2,7},{3,6},{4,1},{5,0},{6,3},{7,2},{8,13},{9,12},{10,... | collective-permute-start | bytes 294920 | tf_op jit(solution)/shard_map/ppermute | solution.py:59
  187.1 21.1 %collective-permute-start.36 = (bf16[2,32,768]{2,1,0:T(8,128)(2,1)S(1)}, bf16[2,32,768]{2,1,0:T(8,128)(2,1)S(1)}, u32[]{:S(2)}, u32[]{:S(2)}) collective-permute-start(bf16[2,32,768]{2,1,0:T(8,128)(2,1)S(1)} %pad_maximum_fusion.25), channel_id=1, source_target_pairs={{0,4},{1,5},{2,6},{3,7},{4,0},{5,1},{6,2},{7,3},{8,12},{9,13},{10,... | collective-permute-start | bytes 294920 | tf_op jit(solution)/shard_map/ppermute | solution.py:59
  187.2 4.7 %collective-permute-start.33 = (bf16[2,32,768]{2,1,0:T(8,128)(2,1)S(1)}, bf16[2,32,768]{2,1,0:T(8,128)(2,1)S(1)}, u32[]{:S(2)}, u32[]{:S(2)}) collective-permute-start(bf16[2,32,768]{2,1,0:T(8,128)(2,1)S(1)} %pad_maximum_fusion.25), channel_id=1, source_target_pairs={{0,1},{1,0},{2,3},{3,2},{4,5},{5,4},{6,7},{7,6},{8,9},{9,8},{10,11... | collective-permute-start | bytes 294920 | tf_op jit(solution)/shard_map/ppermute | solution.py:59
  191.9 8.1 %collective-permute-start.34 = (bf16[2,32,768]{2,1,0:T(8,128)(2,1)S(1)}, bf16[2,32,768]{2,1,0:T(8,128)(2,1)S(1)}, u32[]{:S(2)}, u32[]{:S(2)}) collective-permute-start(bf16[2,32,768]{2,1,0:T(8,128)(2,1)S(1)} %pad_maximum_fusion.25), channel_id=1, source_target_pairs={{0,2},{1,3},{2,0},{3,1},{4,6},{5,7},{6,4},{7,5},{8,10},{9,11},{10,... | collective-permute-start | bytes 294920 | tf_op jit(solution)/shard_map/ppermute | solution.py:59
  200.0 5.6 %collective-permute-start.35 = (bf16[2,32,768]{2,1,0:T(8,128)(2,1)S(1)}, bf16[2,32,768]{2,1,0:T(8,128)(2,1)S(1)}, u32[]{:S(2)}, u32[]{:S(2)}) collective-permute-start(bf16[2,32,768]{2,1,0:T(8,128)(2,1)S(1)} %pad_maximum_fusion.25), channel_id=1, source_target_pairs={{0,3},{1,2},{2,1},{3,0},{4,7},{5,6},{6,5},{7,4},{8,11},{9,10},{10,... | collective-permute-start | bytes 294920 | tf_op jit(solution)/shard_map/ppermute | solution.py:59
  205.6 7.3 %collective-permute-start.39 = (bf16[2,32,768]{2,1,0:T(8,128)(2,1)S(1)}, bf16[2,32,768]{2,1,0:T(8,128)(2,1)S(1)}, u32[]{:S(2)}, u32[]{:S(2)}) collective-permute-start(bf16[2,32,768]{2,1,0:T(8,128)(2,1)S(1)} %pad_maximum_fusion.25), channel_id=1, source_target_pairs={{0,7},{1,6},{2,5},{3,4},{4,3},{5,2},{6,1},{7,0},{8,15},{9,14},{10,... | collective-permute-start | bytes 294920 | tf_op jit(solution)/shard_map/ppermute | solution.py:59
  (13 other events, 30.3 us)

commit v2 on v1

v2 whole, which is shorter than its diff:
```python
import functools

import jax
import jax.numpy as jnp
from jax import lax
from jax.experimental import pallas as pl
from jax.experimental.pallas import tpu as pltpu
from jax.sharding import PartitionSpec as P

EPS = 1e-06
LANES = 128
LIMIT = 48 * 1024 * 1024
F32 = jnp.float32
BF16 = jnp.bfloat16


def rows_dot(left, right):
    return lax.dot_general(left, right, (((0,), (0,)), ((), ())), preferred_element_type=F32)


def dot_t(left, right):
    return lax.dot_general(left, right, (((1,), (1,)), ((), ())), preferred_element_type=F32)


def dot(left, right):
    return jnp.dot(left, right, preferred_element_type=F32)


def norm_scale(v):
    return lax.rsqrt(jnp.mean(v * v, axis=-1, keepdims=True) + EPS)


def with_scalar(aq, s):
    high = s.astype(BF16).astype(F32)
    at = lax.broadcasted_iota(jnp.int32, (aq.shape[0], LANES), 1)
    tail = jnp.where(at == 0, high, jnp.where(at == 1, s - high, 0.0)).astype(BF16)
    return jnp.concatenate([aq, tail], 1)


def pack_kernel(parts, share, *refs):
    count = len(refs) - 2
    sources, out, sems = refs[:count], refs[count], refs[count + 1]
    copies = []
    for i, source in enumerate(sources):
        for d in range(parts):
            copies.append(
                pltpu.make_async_copy(
                    source.at[:, pl.ds(d * share, share)], out.at[d, i], sems.at[i * parts + d]
                )
            )
    for copy in copies:
        copy.start()
    for copy in copies:
        copy.wait()


def pack(blocks, parts):
    rows, width = blocks[0].shape
    share = width // parts
    if share % LANES:
        return jnp.stack([b.reshape(rows, parts, share).swapaxes(0, 1) for b in blocks], 1)
    count = len(blocks)
    return pl.pallas_call(
        functools.partial(pack_kernel, parts, share),
        out_shape=jax.ShapeDtypeStruct((parts, count, rows, share), BF16),
        in_specs=[pl.BlockSpec(memory_space=pl.ANY)] * count,
        out_specs=pl.BlockSpec(memory_space=pl.ANY),
        scratch_shapes=[pltpu.SemaphoreType.DMA((count * parts,))],
        name="pack",
    )(*blocks)


CHUNKS = 7


def load_chunks(source, buffer, sems, chunk):
    copies = []
    for i in range(CHUNKS):
        part = pl.ds(i * chunk, chunk)
        copies.append(pltpu.make_async_copy(source.at[part], buffer.at[part], sems.at[i]))
    for copy in copies:
        copy.start()
    return copies


def chunked_dot(left, copies, buffer, chunk):
    total = None
    for i, copy in enumerate(copies):
        copy.wait()
        part = dot(left[:, i * chunk : (i + 1) * chunk], buffer[i * chunk : (i + 1) * chunk, :])
        total = part if total is None else total + part
    return total


def latent_gradient(u, c, a, b):
    q = b * (u - c * b * b * jnp.mean(u * c, axis=-1, keepdims=True))
    return (q * a).astype(BF16)


def first_kernel(with_next, x_ref, y_ref, *rest):
    if with_next:
        x1_ref, w_ref, g_ref, h_ref, z_ref, aq_ref, k_ref, k1_ref, c1_ref, ab1_ref, down, up, sem0, sem1 = rest
    else:
        w_ref, g_ref, h_ref, z_ref, aq_ref, k_ref, down, up, sem0, sem1 = rest
    rows, width = x_ref.shape
    chunk = width // CHUNKS
    copies0 = load_chunks(w_ref.at[0, 0], down, sem0, chunk)
    copies1 = load_chunks(w_ref.at[0, 1], up, sem1, chunk)
    g = g_ref[...].astype(F32)
    h = h_ref[...].astype(F32)
    x = x_ref[...].astype(F32)
    a = norm_scale(x)
    normed = (x * a * g).astype(BF16)
    if with_next:
        x1 = x1_ref[...].astype(F32)
        a1 = norm_scale(x1)
        normed = jnp.concatenate([normed, (x1 * a1 * g).astype(BF16)], 0)
    c = chunked_dot(normed, copies0, down, chunk)
    if with_next:
        c1 = c[rows:]
        c = c[:rows]
        b1 = norm_scale(c1)
        k1_ref[...] = (c1 * b1 * h).astype(BF16)
        c1_ref[...] = c1
        at = lax.broadcasted_iota(jnp.int32, (rows, LANES), 1)
        ab1_ref[...] = jnp.where(at == 0, a1, b1)
    b = norm_scale(c)
    k_ref[...] = (c * b * h).astype(BF16)
    u = chunked_dot(y_ref[...], copies1, up, chunk) * h
    aq = latent_gradient(u, c, a, b)
    s = a * jnp.sum(aq.astype(F32) * c, axis=-1, keepdims=True) / width
    aq_ref[...] = with_scalar(aq, s)
    for i in range(CHUNKS):
        cols = slice(i * chunk, (i + 1) * chunk)
        m = dot_t(aq, down[cols, :])
        z = y_ref[:, cols].astype(F32) + m * g[:, cols] - x_ref[:, cols].astype(F32) * s
        z_ref[:, cols] = z.astype(BF16)


ANY = pl.BlockSpec(memory_space=pl.ANY)
VMEM = pl.BlockSpec(memory_space=pltpu.VMEM)


def shape(*dims, dtype=BF16):
    return jax.ShapeDtypeStruct(dims, dtype)


def first_step(x, y, weights, g, h, x1=None):
    rows, width = x.shape
    lat = h.shape[1]
    outs = [shape(rows, width), shape(rows, lat + LANES), shape(rows, lat)]
    if x1 is not None:
        outs += [shape(rows, lat), shape(rows, lat, dtype=F32), shape(rows, LANES, dtype=F32)]
    wide = [x, y] if x1 is None else [x, y, x1]
    return pl.pallas_call(
        functools.partial(first_kernel, x1 is not None),
        out_shape=outs,
        in_specs=[VMEM] * len(wide) + [ANY, VMEM, VMEM],
        out_specs=[VMEM] * len(outs),
        scratch_shapes=[
            pltpu.VMEM((width, lat), BF16),
            pltpu.VMEM((width, lat), BF16),
            pltpu.SemaphoreType.DMA((CHUNKS,)),
            pltpu.SemaphoreType.DMA((CHUNKS,)),
        ],
        compiler_params=pltpu.CompilerParams(vmem_limit_bytes=LIMIT),
        cost_estimate=pl.CostEstimate(flops=6 * rows * width * lat, bytes_accessed=4 * width * lat + 6 * rows * width, transcendentals=0),
        name="first_step",
    )(*wide, weights, g, h)


def latent_kernel(x_ref, w_ref, g_ref, h_ref, k_ref, c_ref, ab_ref, down, sem):
    rows, width = x_ref.shape
    chunk = width // CHUNKS
    copies = load_chunks(w_ref.at[0, 0], down, sem, chunk)
    h = h_ref[...].astype(F32)
    x = x_ref[...].astype(F32)
    a = norm_scale(x)
    c = chunked_dot((x * a * g_ref[...].astype(F32)).astype(BF16), copies, down, chunk)
    b = norm_scale(c)
    k_ref[...] = (c * b * h).astype(BF16)
    c_ref[...] = c
    at = lax.broadcasted_iota(jnp.int32, (rows, LANES), 1)
    ab_ref[...] = jnp.where(at == 0, a, b)


def latent_side(x, weights, g, h):
    rows, width = x.shape
    lat = h.shape[1]
    outs = [shape(rows, lat), shape(rows, lat, dtype=F32), shape(rows, LANES, dtype=F32)]
    return pl.pallas_call(
        latent_kernel,
        out_shape=outs,
        in_specs=[VMEM, ANY, VMEM, VMEM],
        out_specs=[VMEM] * 3,
        scratch_shapes=[pltpu.VMEM((width, lat), BF16), pltpu.SemaphoreType.DMA((CHUNKS,))],
        compiler_params=pltpu.CompilerParams(vmem_limit_bytes=LIMIT),
        cost_estimate=pl.CostEstimate(flops=2 * rows * width * lat, bytes_accessed=2 * width * lat + 2 * rows * width, transcendentals=0),
        name="latent_side",
    )(x, weights, g, h)


def second_kernel(y0_ref, y1_ref, w_ref, h_ref, c0_ref, c1_ref, ab0_ref, ab1_ref, aq_ref, up, sem):
    rows, width = y0_ref.shape
    chunk = width // CHUNKS
    copies = load_chunks(w_ref.at[0, 1], up, sem, chunk)
    y = jnp.concatenate([y0_ref[...], y1_ref[...]], 0)
    u = chunked_dot(y, copies, up, chunk) * h_ref[...].astype(F32)
    aq_ref[:rows] = latent_gradient(u[:rows], c0_ref[...], ab0_ref[:, 0:1], ab0_ref[:, 1:2])
    aq_ref[rows:] = latent_gradient(u[rows:], c1_ref[...], ab1_ref[:, 0:1], ab1_ref[:, 1:2])


def second_step(y0, y1, weights, h, c0, c1, ab0, ab1):
    rows, width = y0.shape
    lat = h.shape[1]
    return pl.pallas_call(
        second_kernel,
        out_shape=shape(2 * rows, lat),
        in_specs=[VMEM, VMEM, ANY, VMEM, VMEM, VMEM, VMEM, VMEM],
        out_specs=VMEM,
        scratch_shapes=[pltpu.VMEM((width, lat), BF16), pltpu.SemaphoreType.DMA((CHUNKS,))],
        compiler_params=pltpu.CompilerParams(vmem_limit_bytes=LIMIT),
        cost_estimate=pl.CostEstimate(flops=4 * rows * width * lat, bytes_accessed=2 * width * lat + 4 * rows * width, transcendentals=0),
        name="second_step",
    )(y0, y1, weights, h, c0, c1, ab0, ab1)


def columns_kernel(lat, d_ref, u_ref, aq_ref, down_ref, g_ref, z_ref):
    parts, two, rows, share = d_ref.shape
    g = g_ref[...].astype(F32)
    down = down_ref[...]
    for i, ref in enumerate((d_ref, u_ref)):
        narrow = aq_ref[:, i * rows : (i + 1) * rows, :].reshape(parts * rows, lat + LANES)
        s = narrow[:, lat : lat + 1].astype(F32) + narrow[:, lat + 1 : lat + 2].astype(F32)
        m = dot_t(narrow[:, :lat], down)
        x = ref[:, 0].reshape(parts * rows, share).astype(F32)
        y = ref[:, 1].reshape(parts * rows, share).astype(F32)
        z_ref[i] = (y + m * g - x * s).astype(BF16)


def columns_step(d, u, aq, down, g):
    parts, two, rows, share = d.shape
    lat = down.shape[1]
    return pl.pallas_call(
        functools.partial(columns_kernel, lat),
        out_shape=shape(2, parts * rows, share),
        in_specs=[VMEM] * 5,
        out_specs=VMEM,
        compiler_params=pltpu.CompilerParams(vmem_limit_bytes=LIMIT),
        cost_estimate=pl.CostEstimate(flops=4 * parts * rows * share * lat, bytes_accessed=12 * parts * rows * share, transcendentals=0),
        name="columns_step",
    )(d, u, aq, down, g)


def terms_kernel(d_ref, u_ref, x1_ref, y1_ref, aq0_ref, aq1_ref, k_ref, g_ref, out_ref):
    parts, two, rows, share = d_ref.shape
    lat = aq1_ref.shape[2]
    total = parts * rows

    def half(ref, i, start=0):
        return ref[:, i * rows : (i + 1) * rows, start : start + lat].reshape(total, lat)

    def wide(ref, i):
        return ref[:, i].reshape(total, share)

    first = rows_dot(wide(d_ref, 0), half(aq0_ref, 0))
    first += rows_dot(wide(u_ref, 0), half(aq0_ref, 1))
    first += rows_dot(wide(x1_ref, 0), half(aq1_ref, 0))
    first += rows_dot(wide(x1_ref, 1), half(aq1_ref, 1))
    out_ref[0, 0] = (first * g_ref[...].astype(F32)).astype(BF16)
    second = rows_dot(wide(d_ref, 1), half(k_ref, 0))
    second += rows_dot(wide(u_ref, 1), half(k_ref, 1))
    second += rows_dot(y1_ref[0], half(k_ref, 0, lat))
    second += rows_dot(y1_ref[1], half(k_ref, 1, lat))
    out_ref[0, 1] = second.astype(BF16)


def terms(d, u, x1, y1, aq0, aq1, k, g):
    parts, two, rows, share = d.shape
    lat = aq1.shape[2]
    return pl.pallas_call(
        terms_kernel,
        out_shape=shape(1, 2, share, lat),
        in_specs=[VMEM] * 8,
        out_specs=VMEM,
        compiler_params=pltpu.CompilerParams(vmem_limit_bytes=LIMIT),
        cost_estimate=pl.CostEstimate(flops=16 * parts * rows * share * lat, bytes_accessed=16 * parts * rows * share, transcendentals=0),
        name="terms",
    )(d, u, x1, y1, aq0, aq1, k, g)


def per_device(weights, gain_model, gain_latent, saved_down, saved_up, grad_start):
    ranks = lax.axis_size("pipe")
    replicas = lax.axis_size("dp")
    j = lax.axis_index("dp")
    share = weights.shape[2] // replicas
    own_down = lax.dynamic_slice_in_dim(weights[0, 0], j * share, share, 0)
    own_g = lax.dynamic_slice_in_dim(gain_model, j * share, share, 1)

    def mirror(block):
        return lax.ppermute(block, "pipe", [(i, ranks - 1 - i) for i in range(ranks)])

    def to_before(block):
        return lax.ppermute(block, "pipe", [(i + 1, i) for i in range(ranks - 1)])

    def exchange(blocks):
        return lax.all_to_all(pack(blocks, replicas), "dp", 0, 0, tiled=True)

    def spread(block):
        return lax.all_to_all(jnp.broadcast_to(block[None], (replicas,) + block.shape), "dp", 0, 0, tiled=True)

    x0u = mirror(saved_up[0, 0])
    y0u = mirror(grad_start[1, 0])
    x1u = mirror(saved_up[0, 1])
    x0d, x1d, y0d = saved_down[0, 0], saved_down[0, 1], grad_start[0, 0]

    d_s = exchange([x0d, y0d])
    z0d, aq0d, k0d, k1d, c1d, ab1d = first_step(x0d, y0d, weights, gain_model, gain_latent, x1d)
    y1d = to_before(z0d)
    z0u, aq0u, k0u = first_step(x0u, y0u, weights, gain_model, gain_latent)
    y1u = to_before(z0u)
    u_s = exchange([x0u, y0u])
    aq0 = spread(jnp.concatenate([aq0d, aq0u], 0))
    k1u, c1u, ab1u = latent_side(x1u, weights, gain_model, gain_latent)
    k = lax.all_gather(jnp.concatenate([jnp.concatenate([k0d, k1d], 1), jnp.concatenate([k0u, k1u], 1)], 0), "dp")
    aq1 = spread(second_step(y1d, y1u, weights, gain_latent, c1d, c1u, ab1d, ab1u))
    x1_s = exchange([x1d, x1u])
    y1_s = to_before(columns_step(d_s, u_s, aq0, own_down, own_g))
    return terms(d_s, u_s, x1_s, y1_s, aq0, aq1, k, own_g.reshape(share, 1))


def solution(mesh):
    placed = (
        P("pipe", None, None, None),
        P("pipe", None),
        P("pipe", None),
        P("pipe", None, "dp", None),
        P("pipe", None, "dp", None),
        P(None, "pipe", "dp", None),
    )
    return jax.shard_map(
        per_device,
        mesh=mesh,
        in_specs=placed,
        out_specs=P("pipe", None, "dp", None),
        check_vma=False,
    )
```

time: 217 us -> 222 us (1.023)
  Pallas kernels: 0 us -> 109 us
  blocking collectives: 0 us -> 37.2 us
  waiting for transfers between devices: 59 us -> 22.3 us
  starting transfers between devices: 71.4 us -> 38.1 us
  other arithmetic: 28.2 us -> 0.01 us
  matrix products: 28.1 us -> 0 us
  local copies, waits for them, and re-layouts: 28 us -> 12.1 us
    pallas_call x0 -> x9, Pallas kernels: none -> 109 us  [the longest x3 87.1 us: pack(): pl.pallas_call(functools.partial(pack_kernel, parts, share), out_shape=ja...]
    ppermute x35 -> x0, starting transfers between devices: 61.1 us -> none  [across(): return lax.ppermute(block, 'dp', [(i, i ^ apart) for i in range(replicas)])]
    ppermute x35 -> x0, waiting for transfers between devices: 59 us -> none  [across(): return lax.ppermute(block, 'dp', [(i, i ^ apart) for i in range(replicas)])]
    all_gather x0 -> x1, blocking collectives: none -> 37.2 us  [per_device(): lax.all_gather(jnp.concatenate([jnp.concatenate([k0d, k1d], 1), jnp.conca...]
    all_to_all x0 -> x5, starting transfers between devices: none -> 30.7 us  [the longest x3 18 us: exchange(): return lax.all_to_all(pack(blocks, replicas), 'dp', 0, 0, tiled=True)]
    dot_general x15 -> x0, matrix products: 28.1 us -> none  [the longest x8 20.6 us: dot(): return jnp.dot(left, right, preferred_element_type=jnp.float32)]
    ppermute x3, waiting for transfers between devices: 0.01 us -> 22.3 us  [mirror(): lax.ppermute(block, 'pipe', [(i, ranks - 1 - i) for i in range(ranks)])]
    another operation x30 -> x0, other arithmetic: 17.7 us -> none  [the longest x21 15.5 us: exchange(): jnp.stack([lax.dynamic_slice_in_dim(b, at, share, 1) for b in blocks])]
  transfers between devices with their start and end apart: 41 -> 11, of which waited for: 12 -> 3; matrix products, arithmetic and copies ran while one was open for 32% -> 3% of each run, Pallas kernels for 0% -> 46%
where the time goes in v2:
time: 222 us; the launch traced here: 219 us
  Pallas kernels  109 us (49%)
  starting transfers between devices  38.1 us (17%)
  blocking collectives  37.2 us (17%)
  waiting for transfers between devices  22.3 us (10%)
  local copies, waits for them, and re-layouts  12.1 us (5%)
    pallas_call x3, Pallas kernels, pack(): pl.pallas_call(functools.partial(pack_kernel, parts, share), out_shape=ja...  87.1 us
    all_gather x1, blocking collectives, per_device(): lax.all_gather(jnp.concatenate([jnp.concatenate([k0d, k1d], 1), jnp.conca...  37.2 us
    ppermute x3, waiting for transfers between devices, mirror(): lax.ppermute(block, 'pipe', [(i, ranks - 1 - i) for i in range(ranks)])  22.3 us
    all_to_all x3, starting transfers between devices, exchange(): return lax.all_to_all(pack(blocks, replicas), 'dp', 0, 0, tiled=True)  18 us
    all_to_all x2, starting transfers between devices, spread(): lax.all_to_all(jnp.broadcast_to(block[None], (replicas,) + block.shape),...  12.7 us
    pallas_call x2, Pallas kernels, first_step(): pl.pallas_call(functools.partial(first_kernel, x1 is not None), out_shape...  12 us
  transfers between devices with their start and end apart: 11, of which 3 were waited for; matrix products, arithmetic and copies ran while one was open for 3% of the time, Pallas kernels for 46%

profile of v2, /device:TPU:0, one launch (start us, length us, event | category | flops | bytes accessed | tf_op | source)
XLA Modules:
  0.0 219.3 jit_solution(11108192744726894720)
XLA Ops:
  0.0 0.0 copy-start.10
  0.0 0.0 copy-start.8
  0.0 0.0 copy-start.9
  0.0 1.3 slice_bitcast_fusion
  1.3 2.5 %collective-permute-start = (bf16[32,7168]{1,0:T(8,128)(2,1)S(1)}, bf16[32,7168]{1,0:T(8,128)(2,1)S(1)}, u32[]{:S(2)}, u32[]{:S(2)}) collective-permute-start(bf16[32,7168]{1,0:T(8,128)(2,1)S(1)} %get-tuple-element.30), channel_id=1, source_target_pairs={{0,24},{8,16},{16,8},{24,0},{1,25},{9,17},{17,9},{25,1},{2,26},{10... | collective-permute-start | bytes 1376264 | tf_op jit(solution)/shard_map/ppermute | solution.py:301
  3.8 1.2 slice_bitcast_fusion.2
  5.0 0.0 copy-start.1
  5.0 0.1 collective-permute-start.1
  5.1 0.0 copy-done.10
  5.1 0.1 slice_bitcast_fusion.1
  5.2 0.0 copy-start
  5.2 0.0 copy-start.2
  5.2 0.0 copy-done.8
  5.2 0.0 copy-done.9
  5.2 6.1 %first_step.2 = (bf16[32,7168]{1,0:T(8,128)(2,1)S(1)}, bf16[32,384]{1,0:T(8,128)(2,1)S(1)}, bf16[32,256]{1,0:T(8,128)(2,1)S(1)}, bf16[32,256]{1,0:T(8,128)(2,1)S...) custom-call(bf16[32,7168]{1,0:T(8,128)(2,1)S(1)} %get-tuple-element.32.refs_0_.x_ref, ...), custom_call_target="tpu_custom_call" | custom-call | flops 352321536 | bytes 8716288 | tf_op jit(solution)/shard_map/first_step/pallas_call | solution.py:155
  11.3 0.0 copy-done.1
  11.3 0.0 copy-done
  11.3 0.0 copy-done.2
  11.3 3.4 %collective-permute-done.refs_0_.x_ref = bf16[32,7168]{1,0:T(8,128)(2,1)S(1)} collective-permute-done((bf16[32,7168]{1,0:T(8,128)(2,1)S(1)}, bf16[32,7168]{1,0:T(8,128)(2,1)S(1)}, u32[]{:S(2)}, u32[]{:S(2)}) %collective-permute-start) | collective-permute-done | bytes 458784 | tf_op jit(solution)/shard_map/ppermute | solution.py:301
  14.7 0.0 copy-start.4
  14.7 9.8 %collective-permute-done.1.refs_1_.y_ref = bf16[32,7168]{1,0:T(8,128)(2,1)S(1)} collective-permute-done((bf16[32,7168]{1,0:T(8,128)(2,1)S(1)}, bf16[32,7168]{1,0:T(8,128)(2,1)S(1)}, u32[]{:S(2)}, u32[]{:S(2)}) %collective-permute-start.1) | collective-permute-done | bytes 458784 | tf_op jit(solution)/shard_map/ppermute | solution.py:301
  24.5 0.0 copy-start.5
  24.5 5.9 %first_step.3 = (bf16[32,7168]{1,0:T(8,128)(2,1)S(1)}, bf16[32,384]{1,0:T(8,128)(2,1)S(1)}, bf16[32,256]{1,0:T(8,128)(2,1)S(1)}) custom-call(bf16[32,7168]{1,0:T(8,128)(2,1)S(1)} %collective-permute-done.refs_0_.x_ref, bf16[32,7168]{1,0:T(8,128)(2,1)S(1)} %collective-permute-done.1.refs_1_.y_ref, bf16[1,2,7168,256]{3,2,1,0:T(8,128)(2,1)} %w_ref.3, ...), custom_call_target="tpu_custom_call" | custom-call | flops 352321536 | bytes 8716288 | tf_op jit(solution)/shard_map/first_step/pallas_call | solution.py:155
  30.5 0.0 copy-done.4
  30.5 0.0 copy-done.5
  30.5 0.8 broadcast_in_dim.4
  31.3 6.7 %all-to-all-start.3 = ((bf16[8,64,384]{2,1,0:T(8,128)(2,1)}), bf16[8,64,384]{2,1,0:T(8,128)(2,1)S(1)}, u32[]{:S(2)}, u32[]{:S(2)}) async-start(bf16[8,64,384]{2,1,0:T(8,128)(2,1)} %broadcast_in_dim.4), calls=%async_computation.3 | async-start | bytes 786432 | tf_op jit(solution)/shard_map/all_to_all | solution.py:310
  38.0 1.0 collective-permute-start.2
  39.0 1.3 collective-permute-start.4
  40.3 1.3 collective-permute-start.5
  41.6 9.1 %collective-permute-done.2.refs_1_.x_ref = bf16[32,7168]{1,0:T(8,128)(2,1)S(1)} collective-permute-done((bf16[32,7168]{1,0:T(8,128)(2,1)S(1)}, bf16[32,7168]{1,0:T(8,128)(2,1)S(1)}, u32[]{:S(2)}, u32[]{:S(2)}) %collective-permute-start.2) | collective-permute-done | bytes 458784 | tf_op jit(solution)/shard_map/ppermute | solution.py:301
  50.6 0.0 copy-start.6
  50.6 2.7 %latent_side.1 = (bf16[32,256]{1,0:T(8,128)(2,1)S(1)}, f32[32,256]{1,0:T(8,128)S(1)}, f32[32,128]{1,0:T(8,128)S(1)}) custom-call(bf16[32,7168]{1,0:T(8,128)(2,1)S(1)} %collective-permute-done.2.refs_1_.x_ref, bf16[1,2,7168,256]{3,2,1,0:T(8,128)(2,1)} %w_ref.3, bf16[1,7168]{1,0:T(2,128)(2,1)S(1)} %copy-done.8, bf16[1,256]{1,0:T(2,128)(2,1)S(1)} %copy-done.9), custom_call_target="tpu_custom_call" | custom-call | flops 117440512 | bytes 4128768 | tf_op jit(solution)/shard_map/latent_side/pallas_call | solution.py:191
  53.3 0.0 copy-done.6
  53.3 0.0 collective-permute-done.4.y0_ref
  53.4 0.0 collective-permute-done.5.y1_ref
  53.4 2.6 %second_step.1 = bf16[64,256]{1,0:T(8,128)(2,1)S(1)} custom-call(bf16[32,7168]{1,0:T(8,128)(2,1)S(1)} %collective-permute-done.4.y0_ref, bf16[32,7168]{1,0:T(8,128)(2,1)S(1)} %collective-permute-done.5.y1_ref, bf16[1,2,7168,256]{3,2,1,0:T(8,128)(2,1)} %w_ref.3, bf16[1,256]{1,0:T(2,128)(2,1)S(1)} %copy-done.9, f32[32,256]{1,0:T(8,128)S(1)} %get-tuple-element.21.c0_ref, ...), custom_call_target="tpu_custom_call" | custom-call | flops 234881024 | bytes 4587520 | tf_op jit(solution)/shard_map/second_step/pallas_call | solution.py:216
  56.0 0.0 all-to-all-done.3.aq_ref.aq0_ref
  56.0 0.7 broadcast_in_dim.5
  56.7 6.0 %all-to-all-start.4 = ((bf16[8,64,256]{2,1,0:T(8,128)(2,1)}), bf16[8,64,256]{2,1,0:T(8,128)(2,1)S(1)}, u32[]{:S(2)}, u32[]{:S(2)}) async-start(bf16[8,64,256]{2,1,0:T(8,128)(2,1)} %broadcast_in_dim.5), calls=%async_computation.4 | async-start | bytes 524288 | tf_op jit(solution)/shard_map/all_to_all | solution.py:310
  62.7 29.0 %pack.3 = bf16[8,2,32,896]{3,2,1,0:T(8,128)(2,1)} custom-call(bf16[32,7168]{1,0:T(8,128)(2,1)} %copy-done.2, bf16[32,7168]{1,0:T(8,128)(2,1)} %copy-done.1), custom_call_target="tpu_custom_call" | custom-call | tf_op jit(solution)/shard_map/pack/pallas_call | solution.py:63
  91.8 0.0 all-to-all-done.4.aq1_ref
  91.8 6.0 %all-to-all-start = ((bf16[8,2,32,896]{3,2,1,0:T(8,128)(2,1)}), bf16[8,2,32,896]{3,2,1,0:T(8,128)(2,1)S(1)}, u32[]{:S(2)}, u32[]{:S(2)}) async-start(bf16[8,2,32,896]{3,2,1,0:T(8,128)(2,1)} %pack.3), calls=%async_computation | async-start | bytes 1835008 | tf_op jit(solution)/shard_map/all_to_all | solution.py:307
  97.8 29.0 %pack.4 = bf16[8,2,32,896]{3,2,1,0:T(8,128)(2,1)} custom-call(bf16[32,7168]{1,0:T(8,128)(2,1)} %copy-done.4, bf16[32,7168]{1,0:T(8,128)(2,1)} %copy-done.5), custom_call_target="tpu_custom_call" | custom-call | tf_op jit(solution)/shard_map/pack/pallas_call | solution.py:63
  126.9 0.0 all-to-all-done.d_ref
  126.9 6.0 %all-to-all-start.1 = ((bf16[8,2,32,896]{3,2,1,0:T(8,128)(2,1)}), bf16[8,2,32,896]{3,2,1,0:T(8,128)(2,1)S(1)}, u32[]{:S(2)}, u32[]{:S(2)}) async-start(bf16[8,2,32,896]{3,2,1,0:T(8,128)(2,1)} %pack.4), calls=%async_computation.1 | async-start | bytes 1835008 | tf_op jit(solution)/shard_map/all_to_all | solution.py:307
  132.9 29.0 %pack.5 = bf16[8,2,32,896]{3,2,1,0:T(8,128)(2,1)} custom-call(bf16[32,7168]{1,0:T(8,128)(2,1)} %copy-done, bf16[32,7168]{1,0:T(8,128)(2,1)} %copy-done.6), custom_call_target="tpu_custom_call" | custom-call | tf_op jit(solution)/shard_map/pack/pallas_call | solution.py:63
  161.9 0.0 all-to-all-done.1.u_ref
  161.9 6.0 %all-to-all-start.2 = ((bf16[8,2,32,896]{3,2,1,0:T(8,128)(2,1)}), bf16[8,2,32,896]{3,2,1,0:T(8,128)(2,1)S(1)}, u32[]{:S(2)}, u32[]{:S(2)}) async-start(bf16[8,2,32,896]{3,2,1,0:T(8,128)(2,1)} %pack.5), calls=%async_computation.2 | async-start | bytes 1835008 | tf_op jit(solution)/shard_map/all_to_all | solution.py:307
  167.9 4.1 %slice.27 = bf16[1,1,7168,256]{3,2,1,0:T(8,128)(2,1)} slice(bf16[1,2,7168,256]{3,2,1,0:T(8,128)(2,1)} %w_ref.3), slice={[0:1], [0:1], [0:7168], [0:256]} | slice | bytes 7340032 | tf_op jit(solution)/shard_map/slice | solution.py:297
  172.0 1.0 dynamic-slice_bitcast_fusion.down_ref
  173.1 1.6 columns_step.1
  174.6 1.3 collective-permute-start.3
  175.9 0.9 copy.7.g_ref
  176.8 37.2 %all-gather = bf16[512,512]{1,0:T(8,128)(2,1)} all-gather(bf16[64,512]{1,0:T(8,128)(2,1)S(1)} %maximum_maximum_fusion), channel_id=2, replica_groups=mesh['pipe'=4,'dp'=8] {'dp'}, dimensions={0}, use_global_device_ids=true | all-gather | bytes 589824 | tf_op jit(solution)/shard_map/all_gather | solution.py:325
  214.0 0.0 all-to-all-done.2.x1_ref
  214.0 0.0 collective-permute-done.3.y1_ref
  214.0 0.0 copy-start.3
  214.0 1.0 copy-done.3
  215.1 0.0 copy-start.7
  215.1 0.9 copy-done.7
  216.0 3.4 %terms.1 = bf16[1,2,896,256]{3,2,1,0:T(8,128)(2,1)} custom-call(bf16[8,2,32,896]{3,2,1,0:T(8,128)(2,1)S(1)} %all-to-all-done.d_ref, bf16[8,2,32,896]{3,2,1,0:T(8,128)(2,1)S(1)} %all-to-all-done.1.u_ref, bf16[8,2,32,896]{3,2,1,0:T(8,128)(2,1)S(1)} %all-to-all-done.2.x1_ref, bf16[2,256,896]{2,1,0:T(8,128)(2,1)} %collective-permute-done.3.y1_ref, ...), custom_call_target="tpu_custom_call" | custom-call | flops 939524096 | bytes 3670016 | tf_op jit(solution)/shard_map/terms/pallas_call | solution.py:281
  (4 shorter events, 0.0 us)
Async XLA Ops:
  0.0 5.1 %copy-start.10 = (bf16[1,2,32,7168]{3,2,1,0:T(8,128)(2,1)S(1)}, bf16[1,2,32,7168]{3,2,1,0:T(8,128)(2,1)}, u32[]{:S(2)}) copy-start(bf16[1,2,32,7168]{3,2,1,0:T(8,128)(2,1)} %param.9) | copy-start | bytes 2752516
  0.0 5.2 %copy-start.8 = (bf16[1,7168]{1,0:T(2,128)(2,1)S(1)}, bf16[1,7168]{1,0:T(2,128)(2,1)}, u32[]{:S(2)}) copy-start(bf16[1,7168]{1,0:T(2,128)(2,1)} %g_ref.1) | copy-start | bytes 43012
  0.0 5.2 %copy-start.9 = (bf16[1,256]{1,0:T(2,128)(2,1)S(1)}, bf16[1,256]{1,0:T(2,128)(2,1)}, u32[]{:S(2)}) copy-start(bf16[1,256]{1,0:T(2,128)(2,1)} %h_ref.3) | copy-start | bytes 1540
  1.3 13.4 %collective-permute-start = (bf16[32,7168]{1,0:T(8,128)(2,1)S(1)}, bf16[32,7168]{1,0:T(8,128)(2,1)S(1)}, u32[]{:S(2)}, u32[]{:S(2)}) collective-permute-start(bf16[32,7168]{1,0:T(8,128)(2,1)S(1)} %get-tuple-element.30), channel_id=1, source_target_pairs={{0,24},{8,16},{16,8},{24,0},{1,25},{9,17},{17,9},{25,1},{2,26},{10... | collective-permute-start | bytes 1376264 | tf_op jit(solution)/shard_map/ppermute | solution.py:301
  5.0 6.3 %copy-start.1 = (bf16[32,7168]{1,0:T(8,128)(2,1)}, bf16[32,7168]{1,0:T(8,128)(2,1)S(1)}, u32[]{:S(2)}) copy-start(bf16[32,7168]{1,0:T(8,128)(2,1)S(1)} %get-tuple-element.34.refs_1_.y_ref) | copy-start | bytes 1376260
  5.0 19.5 %collective-permute-start.1 = (bf16[32,7168]{1,0:T(8,128)(2,1)S(1)}, bf16[32,7168]{1,0:T(8,128)(2,1)S(1)}, u32[]{:S(2)}, u32[]{:S(2)}) collective-permute-start(bf16[32,7168]{1,0:T(8,128)(2,1)S(1)} %get-tuple-element.33), channel_id=1, source_target_pairs={{0,24},{8,16},{16,8},{24,0},{1,25},{9,17},{17,9},{25,1},{2,26},{10... | collective-permute-start | bytes 1376264 | tf_op jit(solution)/shard_map/ppermute | solution.py:301
  5.2 6.1 %copy-start = (bf16[32,7168]{1,0:T(8,128)(2,1)}, bf16[32,7168]{1,0:T(8,128)(2,1)S(1)}, u32[]{:S(2)}) copy-start(bf16[32,7168]{1,0:T(8,128)(2,1)S(1)} %get-tuple-element.31.refs_0_.rest_0_) | copy-start | bytes 1376260
  5.2 6.1 %copy-start.2 = (bf16[32,7168]{1,0:T(8,128)(2,1)}, bf16[32,7168]{1,0:T(8,128)(2,1)S(1)}, u32[]{:S(2)}) copy-start(bf16[32,7168]{1,0:T(8,128)(2,1)S(1)} %get-tuple-element.32.refs_0_.x_ref) | copy-start | bytes 1376260
  14.7 15.8 %copy-start.4 = (bf16[32,7168]{1,0:T(8,128)(2,1)}, bf16[32,7168]{1,0:T(8,128)(2,1)S(1)}, u32[]{:S(2)}) copy-start(bf16[32,7168]{1,0:T(8,128)(2,1)S(1)} %collective-permute-done.refs_0_.x_ref) | copy-start | bytes 1376260
  24.5 5.9 %copy-start.5 = (bf16[32,7168]{1,0:T(8,128)(2,1)}, bf16[32,7168]{1,0:T(8,128)(2,1)S(1)}, u32[]{:S(2)}) copy-start(bf16[32,7168]{1,0:T(8,128)(2,1)S(1)} %collective-permute-done.1.refs_1_.y_ref) | copy-start | bytes 1376260
  31.3 24.7 %all-to-all-start.3 = ((bf16[8,64,384]{2,1,0:T(8,128)(2,1)}), bf16[8,64,384]{2,1,0:T(8,128)(2,1)S(1)}, u32[]{:S(2)}, u32[]{:S(2)}) async-start(bf16[8,64,384]{2,1,0:T(8,128)(2,1)} %broadcast_in_dim.4), calls=%async_computation.3 | async-start | bytes 786432 | tf_op jit(solution)/shard_map/all_to_all | solution.py:310
  38.0 12.7 %collective-permute-start.2 = (bf16[32,7168]{1,0:T(8,128)(2,1)S(1)}, bf16[32,7168]{1,0:T(8,128)(2,1)S(1)}, u32[]{:S(2)}, u32[]{:S(2)}) collective-permute-start(bf16[32,7168]{1,0:T(8,128)(2,1)S(1)} %get-tuple-element.29), channel_id=1, source_target_pairs={{0,24},{8,16},{16,8},{24,0},{1,25},{9,17},{17,9},{25,1},{2,26},{10... | collective-permute-start | bytes 1376264 | tf_op jit(solution)/shard_map/ppermute | solution.py:301
  39.0 14.4 %collective-permute-start.4 = (bf16[32,7168]{1,0:T(8,128)(2,1)S(1)}, bf16[32,7168]{1,0:T(8,128)(2,1)S(1)}, u32[]{:S(2)}, u32[]{:S(2)}) collective-permute-start(bf16[32,7168]{1,0:T(8,128)(2,1)S(1)} %get-tuple-element.19), channel_id=1, source_target_pairs={{8,0},{16,8},{24,16},{9,1},{17,9},{25,17},{10,2},{18,10},{26,18},{... | collective-permute-start | bytes 1376264 | tf_op jit(solution)/shard_map/ppermute | solution.py:304
  40.3 13.1 %collective-permute-start.5 = (bf16[32,7168]{1,0:T(8,128)(2,1)S(1)}, bf16[32,7168]{1,0:T(8,128)(2,1)S(1)}, u32[]{:S(2)}, u32[]{:S(2)}) collective-permute-start(bf16[32,7168]{1,0:T(8,128)(2,1)S(1)} %get-tuple-element.20), channel_id=1, source_target_pairs={{8,0},{16,8},{24,16},{9,1},{17,9},{25,17},{10,2},{18,10},{26,18},{... | collective-permute-start | bytes 1376264 | tf_op jit(solution)/shard_map/ppermute | solution.py:304
  50.6 2.7 %copy-start.6 = (bf16[32,7168]{1,0:T(8,128)(2,1)}, bf16[32,7168]{1,0:T(8,128)(2,1)S(1)}, u32[]{:S(2)}) copy-start(bf16[32,7168]{1,0:T(8,128)(2,1)S(1)} %collective-permute-done.2.refs_1_.x_ref) | copy-start | bytes 1376260
  56.7 35.0 %all-to-all-start.4 = ((bf16[8,64,256]{2,1,0:T(8,128)(2,1)}), bf16[8,64,256]{2,1,0:T(8,128)(2,1)S(1)}, u32[]{:S(2)}, u32[]{:S(2)}) async-start(bf16[8,64,256]{2,1,0:T(8,128)(2,1)} %broadcast_in_dim.5), calls=%async_computation.4 | async-start | bytes 524288 | tf_op jit(solution)/shard_map/all_to_all | solution.py:310
  91.8 35.1 %all-to-all-start = ((bf16[8,2,32,896]{3,2,1,0:T(8,128)(2,1)}), bf16[8,2,32,896]{3,2,1,0:T(8,128)(2,1)S(1)}, u32[]{:S(2)}, u32[]{:S(2)}) async-start(bf16[8,2,32,896]{3,2,1,0:T(8,128)(2,1)} %pack.3), calls=%async_computation | async-start | bytes 1835008 | tf_op jit(solution)/shard_map/all_to_all | solution.py:307
  126.9 35.1 %all-to-all-start.1 = ((bf16[8,2,32,896]{3,2,1,0:T(8,128)(2,1)}), bf16[8,2,32,896]{3,2,1,0:T(8,128)(2,1)S(1)}, u32[]{:S(2)}, u32[]{:S(2)}) async-start(bf16[8,2,32,896]{3,2,1,0:T(8,128)(2,1)} %pack.4), calls=%async_computation.1 | async-start | bytes 1835008 | tf_op jit(solution)/shard_map/all_to_all | solution.py:307
  161.9 52.1 %all-to-all-start.2 = ((bf16[8,2,32,896]{3,2,1,0:T(8,128)(2,1)}), bf16[8,2,32,896]{3,2,1,0:T(8,128)(2,1)S(1)}, u32[]{:S(2)}, u32[]{:S(2)}) async-start(bf16[8,2,32,896]{3,2,1,0:T(8,128)(2,1)} %pack.5), calls=%async_computation.2 | async-start | bytes 1835008 | tf_op jit(solution)/shard_map/all_to_all | solution.py:307
  174.6 39.4 %collective-permute-start.3 = (bf16[2,256,896]{2,1,0:T(8,128)(2,1)}, bf16[2,256,896]{2,1,0:T(8,128)(2,1)}, u32[]{:S(2)}, u32[]{:S(2)}) collective-permute-start(bf16[2,256,896]{2,1,0:T(8,128)(2,1)} %columns_step.1), channel_id=1, source_target_pairs={{8,0},{16,8},{24,16},{9,1},{17,9},{25,17},{10,2},{18,10},{26,18},{... | collective-permute-start | bytes 2752520 | tf_op jit(solution)/shard_map/ppermute | solution.py:304
  214.0 1.0 copy-start.3
  215.1 0.9 copy-start.7

commit v3 on v2

--- a/solution.py
+++ b/solution.py
@@ -9,6 +9,9 @@
 
 EPS = 1e-06
 LANES = 128
+ANY = pl.BlockSpec(memory_space=pl.ANY)
+VMEM = pl.BlockSpec(memory_space=pltpu.VMEM)
+SMEM = pl.BlockSpec(memory_space=pltpu.SMEM)
 LIMIT = 48 * 1024 * 1024
 F32 = jnp.float32
 BF16 = jnp.bfloat16
@@ -38,34 +41,23 @@
 
 
 def pack_kernel(parts, share, *refs):
-    count = len(refs) - 2
-    sources, out, sems = refs[:count], refs[count], refs[count + 1]
-    copies = []
-    for i, source in enumerate(sources):
+    out = refs[-1]
+    for i, source in enumerate(refs[:-1]):
         for d in range(parts):
-            copies.append(
-                pltpu.make_async_copy(
-                    source.at[:, pl.ds(d * share, share)], out.at[d, i], sems.at[i * parts + d]
-                )
-            )
-    for copy in copies:
-        copy.start()
-    for copy in copies:
-        copy.wait()
+            out[d, i] = source[:, d * share : (d + 1) * share]
 
 
 def pack(blocks, parts):
     rows, width = blocks[0].shape
     share = width // parts
-    if share % LANES:
-        return jnp.stack([b.reshape(rows, parts, share).swapaxes(0, 1) for b in blocks], 1)
     count = len(blocks)
     return pl.pallas_call(
         functools.partial(pack_kernel, parts, share),
         out_shape=jax.ShapeDtypeStruct((parts, count, rows, share), BF16),
-        in_specs=[pl.BlockSpec(memory_space=pl.ANY)] * count,
-        out_specs=pl.BlockSpec(memory_space=pl.ANY),
-        scratch_shapes=[pltpu.SemaphoreType.DMA((count * parts,))],
+        in_specs=[VMEM] * count,
+        out_specs=VMEM,
+        compiler_params=pltpu.CompilerParams(vmem_limit_bytes=LIMIT),
+        cost_estimate=pl.CostEstimate(flops=0, bytes_accessed=4 * count * rows * width, transcendentals=0),
         name="pack",
     )(*blocks)
 
@@ -99,10 +91,11 @@
 
 def first_kernel(with_next, x_ref, y_ref, *rest):
     if with_next:
-        x1_ref, w_ref, g_ref, h_ref, z_ref, aq_ref, k_ref, k1_ref, c1_ref, ab1_ref, down, up, sem0, sem1 = rest
+        x1_ref, w_ref, g_ref, h_ref, z_ref, narrow_ref, k1_ref, c1_ref, ab1_ref, down, up, sem0, sem1 = rest
     else:
-        w_ref, g_ref, h_ref, z_ref, aq_ref, k_ref, down, up, sem0, sem1 = rest
+        before_ref, w_ref, g_ref, h_ref, z_ref, narrow_ref, down, up, sem0, sem1 = rest
     rows, width = x_ref.shape
+    lat = h_ref.shape[1]
     chunk = width // CHUNKS
     copies0 = load_chunks(w_ref.at[0, 0], down, sem0, chunk)
     copies1 = load_chunks(w_ref.at[0, 1], up, sem1, chunk)
@@ -116,6 +109,7 @@
         a1 = norm_scale(x1)
         normed = jnp.concatenate([normed, (x1 * a1 * g).astype(BF16)], 0)
     c = chunked_dot(normed, copies0, down, chunk)
+    mine = slice(0, rows)
     if with_next:
         c1 = c[rows:]
         c = c[:rows]
@@ -124,12 +118,15 @@
         c1_ref[...] = c1
         at = lax.broadcasted_iota(jnp.int32, (rows, LANES), 1)
         ab1_ref[...] = jnp.where(at == 0, a1, b1)
+    else:
+        narrow_ref[:rows] = before_ref[...]
+        mine = slice(rows, 2 * rows)
     b = norm_scale(c)
-    k_ref[...] = (c * b * h).astype(BF16)
+    narrow_ref[mine, lat + LANES :] = (c * b * h).astype(BF16)
     u = chunked_dot(y_ref[...], copies1, up, chunk) * h
     aq = latent_gradient(u, c, a, b)
     s = a * jnp.sum(aq.astype(F32) * c, axis=-1, keepdims=True) / width
-    aq_ref[...] = with_scalar(aq, s)
+    narrow_ref[mine, : lat + LANES] = with_scalar(aq, s)
     for i in range(CHUNKS):
         cols = slice(i * chunk, (i + 1) * chunk)
         m = dot_t(aq, down[cols, :])
@@ -137,23 +134,22 @@
         z_ref[:, cols] = z.astype(BF16)
 
 
-ANY = pl.BlockSpec(memory_space=pl.ANY)
-VMEM = pl.BlockSpec(memory_space=pltpu.VMEM)
-
-
 def shape(*dims, dtype=BF16):
     return jax.ShapeDtypeStruct(dims, dtype)
 
 
-def first_step(x, y, weights, g, h, x1=None):
+def first_step(x, y, weights, g, h, x1=None, before=None):
     rows, width = x.shape
     lat = h.shape[1]
-    outs = [shape(rows, width), shape(rows, lat + LANES), shape(rows, lat)]
-    if x1 is not None:
-        outs += [shape(rows, lat), shape(rows, lat, dtype=F32), shape(rows, LANES, dtype=F32)]
-    wide = [x, y] if x1 is None else [x, y, x1]
-    return pl.pallas_call(
-        functools.partial(first_kernel, x1 is not None),
+    narrow = 2 * lat + LANES
+    if before is None:
+        outs = [shape(rows, width), shape(rows, narrow), shape(rows, lat), shape(rows, lat, dtype=F32), shape(rows, LANES, dtype=F32)]
+        wide = [x, y, x1]
+    else:
+        outs = [shape(rows, width), shape(2 * rows, narrow)]
+        wide = [x, y, before]
+    return pl.pallas_call(
+        functools.partial(first_kernel, before is None),
         out_shape=outs,
         in_specs=[VMEM] * len(wide) + [ANY, VMEM, VMEM],
         out_specs=[VMEM] * len(outs),
@@ -200,37 +196,76 @@
     )(x, weights, g, h)
 
 
-def second_kernel(y0_ref, y1_ref, w_ref, h_ref, c0_ref, c1_ref, ab0_ref, ab1_ref, aq_ref, up, sem):
+def second_kernel(y0_ref, y1_ref, w_ref, h_ref, c0_ref, c1_ref, ab0_ref, ab1_ref, k0_ref, k1_ref, out_ref, up, sem):
     rows, width = y0_ref.shape
+    lat = h_ref.shape[1]
     chunk = width // CHUNKS
     copies = load_chunks(w_ref.at[0, 1], up, sem, chunk)
+    out_ref[:rows, lat:] = k0_ref[...]
+    out_ref[rows:, lat:] = k1_ref[...]
     y = jnp.concatenate([y0_ref[...], y1_ref[...]], 0)
     u = chunked_dot(y, copies, up, chunk) * h_ref[...].astype(F32)
-    aq_ref[:rows] = latent_gradient(u[:rows], c0_ref[...], ab0_ref[:, 0:1], ab0_ref[:, 1:2])
-    aq_ref[rows:] = latent_gradient(u[rows:], c1_ref[...], ab1_ref[:, 0:1], ab1_ref[:, 1:2])
-
-
-def second_step(y0, y1, weights, h, c0, c1, ab0, ab1):
+    out_ref[:rows, :lat] = latent_gradient(u[:rows], c0_ref[...], ab0_ref[:, 0:1], ab0_ref[:, 1:2])
+    out_ref[rows:, :lat] = latent_gradient(u[rows:], c1_ref[...], ab1_ref[:, 0:1], ab1_ref[:, 1:2])
+
+
+def second_step(y0, y1, weights, h, c0, c1, ab0, ab1, k0, k1):
     rows, width = y0.shape
     lat = h.shape[1]
     return pl.pallas_call(
         second_kernel,
-        out_shape=shape(2 * rows, lat),
-        in_specs=[VMEM, VMEM, ANY, VMEM, VMEM, VMEM, VMEM, VMEM],
+        out_shape=shape(2 * rows, 2 * lat),
+        in_specs=[VMEM, VMEM, ANY] + [VMEM] * 7,
         out_specs=VMEM,
         scratch_shapes=[pltpu.VMEM((width, lat), BF16), pltpu.SemaphoreType.DMA((CHUNKS,))],
         compiler_params=pltpu.CompilerParams(vmem_limit_bytes=LIMIT),
         cost_estimate=pl.CostEstimate(flops=4 * rows * width * lat, bytes_accessed=2 * width * lat + 4 * rows * width, transcendentals=0),
         name="second_step",
-    )(y0, y1, weights, h, c0, c1, ab0, ab1)
-
-
-def columns_kernel(lat, d_ref, u_ref, aq_ref, down_ref, g_ref, z_ref):
+    )(y0, y1, weights, h, c0, c1, ab0, ab1, k0, k1)
+
+
+def far_bits(parts):
+    bits, at = [], parts // 2
+    while at:
+        bits.append(at)
+        at //= 2
+    return bits
+
+
+def held_order(parts):
+    order = [0]
+    for bit in far_bits(parts):
+        order += [p ^ bit for p in order]
+    return order
+
+
+def gather_pieces(block, axis):
+    parts = lax.axis_size(axis)
+    pieces, held = [block], block
+    for bit in far_bits(parts):
+        pieces.append(lax.ppermute(held, axis, [(i, i ^ bit) for i in range(parts)]))
+        if bit > 1:
+            held = jnp.concatenate([held, pieces[-1]], 0)
+    return pieces
+
+
+def restore(j, pieces, out):
+    parts, rows = out.shape[:2]
+    order, at = held_order(parts), 0
+    for piece in pieces:
+        for i in range(piece.shape[0] // rows):
+            out[j ^ order[at]] = piece[i * rows : (i + 1) * rows, :]
+            at += 1
+
+
+def columns_kernel(lat, j_ref, d_ref, u_ref, down_ref, g_ref, *rest):
+    pieces, z_ref, narrow_ref = rest[:-2], rest[-2], rest[-1]
     parts, two, rows, share = d_ref.shape
+    restore(j_ref[0], pieces, narrow_ref)
     g = g_ref[...].astype(F32)
     down = down_ref[...]
     for i, ref in enumerate((d_ref, u_ref)):
-        narrow = aq_ref[:, i * rows : (i + 1) * rows, :].reshape(parts * rows, lat + LANES)
+        narrow = narrow_ref[:, i * rows : (i + 1) * rows, :].reshape(parts * rows, narrow_ref.shape[2])
         s = narrow[:, lat : lat + 1].astype(F32) + narrow[:, lat + 1 : lat + 2].astype(F32)
         m = dot_t(narrow[:, :lat], down)
         x = ref[:, 0].reshape(parts * rows, share).astype(F32)
@@ -238,55 +273,60 @@
         z_ref[i] = (y + m * g - x * s).astype(BF16)
 
 
-def columns_step(d, u, aq, down, g):
+def columns_step(j, d, u, down, g, pieces):
     parts, two, rows, share = d.shape
     lat = down.shape[1]
+    narrow = pieces[0].shape
     return pl.pallas_call(
         functools.partial(columns_kernel, lat),
-        out_shape=shape(2, parts * rows, share),
-        in_specs=[VMEM] * 5,
-        out_specs=VMEM,
+        out_shape=[shape(2, parts * rows, share), shape(parts, *narrow)],
+        in_specs=[SMEM] + [VMEM] * (4 + len(pieces)),
+        out_specs=[VMEM, VMEM],
         compiler_params=pltpu.CompilerParams(vmem_limit_bytes=LIMIT),
         cost_estimate=pl.CostEstimate(flops=4 * parts * rows * share * lat, bytes_accessed=12 * parts * rows * share, transcendentals=0),
         name="columns_step",
-    )(d, u, aq, down, g)
-
-
-def terms_kernel(d_ref, u_ref, x1_ref, y1_ref, aq0_ref, aq1_ref, k_ref, g_ref, out_ref):
+    )(j, d, u, down, g, *pieces)
+
+
+def terms_kernel(j_ref, d_ref, u_ref, x1_ref, y1_ref, first_ref, g_ref, *rest):
+    pieces, out_ref, second_ref = rest[:-2], rest[-2], rest[-1]
     parts, two, rows, share = d_ref.shape
-    lat = aq1_ref.shape[2]
+    lat = second_ref.shape[2] // 2
     total = parts * rows
-
-    def half(ref, i, start=0):
+    restore(j_ref[0], pieces, second_ref)
+
+    def half(ref, i, start):
         return ref[:, i * rows : (i + 1) * rows, start : start + lat].reshape(total, lat)
 
     def wide(ref, i):
         return ref[:, i].reshape(total, share)
 
-    first = rows_dot(wide(d_ref, 0), half(aq0_ref, 0))
-    first += rows_dot(wide(u_ref, 0), half(aq0_ref, 1))
-    first += rows_dot(wide(x1_ref, 0), half(aq1_ref, 0))
-    first += rows_dot(wide(x1_ref, 1), half(aq1_ref, 1))
+    first = rows_dot(wide(d_ref, 0), half(first_ref, 0, 0))
+    first += rows_dot(wide(u_ref, 0), half(first_ref, 1, 0))
+    first += rows_dot(wide(x1_ref, 0), half(second_ref, 0, 0))
+    first += rows_dot(wide(x1_ref, 1), half(second_ref, 1, 0))
     out_ref[0, 0] = (first * g_ref[...].astype(F32)).astype(BF16)
-    second = rows_dot(wide(d_ref, 1), half(k_ref, 0))
-    second += rows_dot(wide(u_ref, 1), half(k_ref, 1))
-    second += rows_dot(y1_ref[0], half(k_ref, 0, lat))
-    second += rows_dot(y1_ref[1], half(k_ref, 1, lat))
+    second = rows_dot(wide(d_ref, 1), half(first_ref, 0, lat + LANES))
+    second += rows_dot(wide(u_ref, 1), half(first_ref, 1, lat + LANES))
+    second += rows_dot(y1_ref[0], half(second_ref, 0, lat))
+    second += rows_dot(y1_ref[1], half(second_ref, 1, lat))
     out_ref[0, 1] = second.astype(BF16)
 
 
-def terms(d, u, x1, y1, aq0, aq1, k, g):
+def terms(j, d, u, x1, y1, first, g, pieces):
     parts, two, rows, share = d.shape
-    lat = aq1.shape[2]
+    narrow = pieces[0].shape
+    lat = narrow[1] // 2
     return pl.pallas_call(
         terms_kernel,
         out_shape=shape(1, 2, share, lat),
-        in_specs=[VMEM] * 8,
+        in_specs=[SMEM] + [VMEM] * (6 + len(pieces)),
         out_specs=VMEM,
+        scratch_shapes=[pltpu.VMEM((parts,) + narrow, BF16)],
         compiler_params=pltpu.CompilerParams(vmem_limit_bytes=LIMIT),
         cost_estimate=pl.CostEstimate(flops=16 * parts * rows * share * lat, bytes_accessed=16 * parts * rows * share, transcendentals=0),
         name="terms",
-    )(d, u, x1, y1, aq0, aq1, k, g)
+    )(j, d, u, x1, y1, first, g, *pieces)
 
 
 def per_device(weights, gain_model, gain_latent, saved_down, saved_up, grad_start):
@@ -304,29 +344,29 @@
         return lax.ppermute(block, "pipe", [(i + 1, i) for i in range(ranks - 1)])
 
     def exchange(blocks):
-        return lax.all_to_all(pack(blocks, replicas), "dp", 0, 0, tiled=True)
-
-    def spread(block):
-        return lax.all_to_all(jnp.broadcast_to(block[None], (replicas,) + block.shape), "dp", 0, 0, tiled=True)
+        return lax.all_to_all(blocks, "dp", 0, 0, tiled=True)
 
     x0u = mirror(saved_up[0, 0])
     y0u = mirror(grad_start[1, 0])
     x1u = mirror(saved_up[0, 1])
     x0d, x1d, y0d = saved_down[0, 0], saved_down[0, 1], grad_start[0, 0]
 
-    d_s = exchange([x0d, y0d])
-    z0d, aq0d, k0d, k1d, c1d, ab1d = first_step(x0d, y0d, weights, gain_model, gain_latent, x1d)
+    d_packed, x0d, y0d, x1d = lax.optimization_barrier((pack([x0d, y0d], replicas), x0d, y0d, x1d))
+    d_s = exchange(d_packed)
+    z0d, before, k1d, c1d, ab1d = first_step(x0d, y0d, weights, gain_model, gain_latent, x1d)
     y1d = to_before(z0d)
-    z0u, aq0u, k0u = first_step(x0u, y0u, weights, gain_model, gain_latent)
+    u_packed, x0u, y0u = lax.optimization_barrier((pack([x0u, y0u], replicas), x0u, y0u))
+    u_s = exchange(u_packed)
+    z0u, narrow = first_step(x0u, y0u, weights, gain_model, gain_latent, before=before)
     y1u = to_before(z0u)
-    u_s = exchange([x0u, y0u])
-    aq0 = spread(jnp.concatenate([aq0d, aq0u], 0))
+    first_pieces = gather_pieces(narrow, "dp")
     k1u, c1u, ab1u = latent_side(x1u, weights, gain_model, gain_latent)
-    k = lax.all_gather(jnp.concatenate([jnp.concatenate([k0d, k1d], 1), jnp.concatenate([k0u, k1u], 1)], 0), "dp")
-    aq1 = spread(second_step(y1d, y1u, weights, gain_latent, c1d, c1u, ab1d, ab1u))
-    x1_s = exchange([x1d, x1u])
-    y1_s = to_before(columns_step(d_s, u_s, aq0, own_down, own_g))
-    return terms(d_s, u_s, x1_s, y1_s, aq0, aq1, k, own_g.reshape(share, 1))
+    second = second_step(y1d, y1u, weights, gain_latent, c1d, c1u, ab1d, ab1u, k1d, k1u)
+    x1_s = exchange(pack([x1d, x1u], replicas))
+    second_pieces = gather_pieces(second, "dp")
+    z0_s, first = columns_step(j[None], d_s, u_s, own_down, own_g, first_pieces)
+    y1_s = to_before(z0_s)
+    return terms(j[None], d_s, u_s, x1_s, y1_s, first, own_g.reshape(share, 1), second_pieces)
 
 
 def solution(mesh):

time: 222 us -> 137 us (0.62)
  Pallas kernels: 109 us -> 25.2 us
  blocking collectives: 37.2 us -> 0 us
  waiting for transfers between devices: 22.3 us -> 58.8 us
  starting transfers between devices: 38.1 us -> 32.6 us
  local copies, waits for them, and re-layouts: 12.1 us -> 16.7 us
    pallas_call x3, Pallas kernels: 87.1 us -> 1.13 us  [pack(): pl.pallas_call(functools.partial(pack_kernel, parts, share), out_shape=ja...]
    all_gather x1 -> x0, blocking collectives: 37.2 us -> none  [per_device(): lax.all_gather(jnp.concatenate([jnp.concatenate([k0d, k1d], 1), jnp.conca...]
    ppermute x0 -> x6, waiting for transfers between devices: none -> 31.9 us  [gather_pieces(): lax.ppermute(held, axis, [(i, i ^ bit) for i in range(parts)])]
    all_to_all x5 -> x3, starting transfers between devices: 30.7 us -> 13.1 us  [exchange(): return lax.all_to_all(blocks, 'dp', 0, 0, tiled=True)]
    all_to_all x5 -> x3, waiting for transfers between devices: 0.01 us -> 15.8 us  [exchange(): return lax.all_to_all(blocks, 'dp', 0, 0, tiled=True)]
    ppermute x0 -> x6, starting transfers between devices: none -> 12.4 us  [gather_pieces(): lax.ppermute(held, axis, [(i, i ^ bit) for i in range(parts)])]
    ppermute x3, waiting for transfers between devices: 22.3 us -> 11 us  [mirror(): lax.ppermute(block, 'pipe', [(i, ranks - 1 - i) for i in range(ranks)])]
    unnamed x22 -> x42, local copies, waits for them, and re-layouts: 2.01 us -> 6.33 us
  transfers between devices with their start and end apart: 11 -> 15, of which waited for: 3 -> 8; matrix products, arithmetic and copies ran while one was open for 3% -> 7% of each run, Pallas kernels for 46% -> 16%
where the time goes in v3:
time: 137 us; the launch traced here: 135 us
  waiting for transfers between devices  58.8 us (43%)
  starting transfers between devices  32.6 us (24%)
  Pallas kernels  25.2 us (18%)
  local copies, waits for them, and re-layouts  16.7 us (12%)
  other arithmetic  1.52 us (1%)
    ppermute x6, waiting for transfers between devices, gather_pieces(): lax.ppermute(held, axis, [(i, i ^ bit) for i in range(parts)])  31.9 us
    all_to_all x3, waiting for transfers between devices, exchange(): return lax.all_to_all(blocks, 'dp', 0, 0, tiled=True)  15.8 us
    all_to_all x3, starting transfers between devices, exchange(): return lax.all_to_all(blocks, 'dp', 0, 0, tiled=True)  13.1 us
    ppermute x6, starting transfers between devices, gather_pieces(): lax.ppermute(held, axis, [(i, i ^ bit) for i in range(parts)])  12.4 us
    pallas_call x2, Pallas kernels, first_step(): pl.pallas_call(functools.partial(first_kernel, before is None), out_shape...  11.9 us
    ppermute x3, waiting for transfers between devices, mirror(): lax.ppermute(block, 'pipe', [(i, ranks - 1 - i) for i in range(ranks)])  11 us
    unnamed x42, local copies, waits for them, and re-layouts  6.33 us
    ppermute x3, starting transfers between devices, to_before(): return lax.ppermute(block, 'pipe', [(i + 1, i) for i in range(ranks - 1)])  4.1 us
  transfers between devices with their start and end apart: 15, of which 8 were waited for; matrix products, arithmetic and copies ran while one was open for 7% of the time, Pallas kernels for 16%

profile of v3, /device:TPU:0, one launch (start us, length us, event | category | flops | bytes accessed | tf_op | source)
XLA Modules:
  0.0 135.0 jit_solution(2955330077349362846)
XLA Ops:
  0.0 2.3 %slice_bitcast_fusion.1 = (bf16[32,7168]{1,0:T(8,128)(2,1)}, bf16[32,7168]{1,0:T(8,128)(2,1)S(1)}, bf16[32,7168]{1,0:T(8,128)(2,1)S(1)}, bf16[32,7168]{1,0:T(8,128)(2,1)S(1)}) fusion(bf16[2,1,32,7168]{3,2,1,0:T(8,128)(2,1)} %param.11, bf16[1,2,32,7168]{3,2,1,0:T(8,128)(2,1)} %param.9), kind=kLoop, calls=%fused_computation.2 | loop fusion | bytes 3670016 | tf_op jit(solution)/shard_map/squeeze | solution.py:350
  2.3 2.4 %collective-permute-start.1 = (bf16[32,7168]{1,0:T(8,128)(2,1)}, bf16[32,7168]{1,0:T(8,128)(2,1)S(1)}, u32[]{:S(2)}, u32[]{:S(2)}) collective-permute-start(bf16[32,7168]{1,0:T(8,128)(2,1)} %get-tuple-element.45), channel_id=1, source_target_pairs={{0,24},{8,16},{16,8},{24,0},{1,25},{9,17},{17,9},{25,1},{2,26},{10... | collective-permute-start | bytes 1376264 | tf_op jit(solution)/shard_map/ppermute | solution.py:341
  4.7 1.0 pack.3
  5.7 5.9 %all-to-all-start = ((bf16[8,2,32,896]{3,2,1,0:T(8,128)(2,1)}), bf16[8,2,32,896]{3,2,1,0:T(8,128)(2,1)S(1)}, u32[]{:S(2)}, u32[]{:S(2)}) async-start(bf16[8,2,32,896]{3,2,1,0:T(8,128)(2,1)} %pack.3), calls=%async_computation | async-start | bytes 1835008 | tf_op jit(solution)/shard_map/all_to_all | solution.py:347
  11.7 2.0 %slice_bitcast_fusion = (bf16[32,7168]{1,0:T(8,128)(2,1)}, bf16[32,7168]{1,0:T(8,128)(2,1)S(1)}) fusion(bf16[1,2,32,7168]{3,2,1,0:T(8,128)(2,1)} %param.10), kind=kLoop, calls=%fused_computation.1 | loop fusion | bytes 1835008 | tf_op jit(solution)/shard_map/squeeze | solution.py:351
  13.6 0.5 collective-permute-start
  14.2 1.8 %collective-permute-done.1.refs_1_.y_ref = bf16[32,7168]{1,0:T(8,128)(2,1)S(1)} collective-permute-done((bf16[32,7168]{1,0:T(8,128)(2,1)}, bf16[32,7168]{1,0:T(8,128)(2,1)S(1)}, u32[]{:S(2)}, u32[]{:S(2)}) %collective-permute-start.1) | collective-permute-done | bytes 458784 | tf_op jit(solution)/shard_map/ppermute | solution.py:341
  16.0 0.8 copy-done.4
  16.7 9.2 %collective-permute-done.refs_0_.x_ref = bf16[32,7168]{1,0:T(8,128)(2,1)S(1)} collective-permute-done((bf16[32,7168]{1,0:T(8,128)(2,1)S(1)}, bf16[32,7168]{1,0:T(8,128)(2,1)S(1)}, u32[]{:S(2)}, u32[]{:S(2)}) %collective-permute-start) | collective-permute-done | bytes 458784 | tf_op jit(solution)/shard_map/ppermute | solution.py:341
  25.9 1.0 copy-done.5
  26.9 0.1 pack.4
  27.0 0.0 copy-start.1
  27.0 0.9 copy-done.1
  27.9 0.8 copy-done.7
  28.7 6.8 %all-to-all-done.d_ref = bf16[8,2,32,896]{3,2,1,0:T(8,128)(2,1)S(1)} async-done(((bf16[8,2,32,896]{3,2,1,0:T(8,128)(2,1)}), bf16[8,2,32,896]{3,2,1,0:T(8,128)(2,1)S(1)}, u32[]{:S(2)}, u32[]{:S(2)}) %all-to-all-start) | async-done | bytes 917536 | tf_op jit(solution)/shard_map/all_to_all | solution.py:347
  35.5 3.6 %all-to-all-start.1 = ((bf16[8,2,32,896]{3,2,1,0:T(8,128)(2,1)}), bf16[8,2,32,896]{3,2,1,0:T(8,128)(2,1)S(1)}, u32[]{:S(2)}, u32[]{:S(2)}) async-start(bf16[8,2,32,896]{3,2,1,0:T(8,128)(2,1)} %copy-done.1), calls=%async_computation.1 | async-start | bytes 1835008 | tf_op jit(solution)/shard_map/all_to_all | solution.py:347
  39.1 0.0 copy-start.8
  39.1 0.1 collective-permute-start.2
  39.2 0.0 copy-done.11
  39.2 0.0 copy-done.17
  39.2 6.0 %first_step.2 = (bf16[32,7168]{1,0:T(8,128)(2,1)S(1)}, bf16[32,640]{1,0:T(8,128)(2,1)S(1)}, bf16[32,256]{1,0:T(8,128)(2,1)S(1)}, f32[32,256]{1,0:T(8,128)S(1)}, f32[32,128]{1,0:T(8,128)S(1)}) custom-call(bf16[32,7168]{1,0:T(8,128)(2,1)S(1)} %get-tuple-element.29.refs_0_.x_ref, bf16[32,7168]{1,0:T(8,128)(2,1)S(1)} %get-tuple-element.30.refs_1_.y_ref, ...), custom_call_target="tpu_custom_call" | custom-call | flops 352321536 | bytes 8716288 | tf_op jit(solution)/shard_map/first_step/pallas_call | solution.py:151
  45.2 0.0 copy-start.13
  45.2 0.0 copy-start.15
  45.2 0.0 copy-start.19
  45.3 0.0 copy-done.6
  45.3 0.0 copy-done.8
  45.3 5.9 %first_step.3 = (bf16[32,7168]{1,0:T(8,128)(2,1)S(1)}, bf16[64,640]{1,0:T(8,128)(2,1)S(1)}) custom-call(bf16[32,7168]{1,0:T(8,128)(2,1)S(1)} %copy-done.8, bf16[32,7168]{1,0:T(8,128)(2,1)S(1)} %copy-done.6, bf16[32,640]{1,0:T(8,128)(2,1)S(1)} %get-tuple-element.31.rest_0_, bf16[1,2,7168,256]{3,2,1,0:T(8,128)(2,1)} %w_ref.3, bf16[1,7168]{1,0:T(2,128)(2,1)S(1)} %copy-done.11, ...), custom_call_target="tpu_custom_call" | custom-call | flops 352321536 | bytes 8716288 | tf_op jit(solution)/shard_map/first_step/pallas_call | solution.py:151
  51.2 2.9 %collective-permute-start.3 = (bf16[64,640]{1,0:T(8,128)(2,1)S(1)}, bf16[64,640]{1,0:T(8,128)(2,1)S(1)}, u32[]{:S(2)}, u32[]{:S(2)}) collective-permute-start(bf16[64,640]{1,0:T(8,128)(2,1)S(1)} %get-tuple-element.32.rest_0_), channel_id=1, source_target_pairs={{0,4},{1,5},{2,6},{3,7},{4,0},{5,1},{6,2},{7,3},{8,12},{9,13},{10,... | collective-permute-start | bytes 245768 | tf_op jit(solution)/shard_map/ppermute | solution.py:246
  54.1 0.0 collective-permute-done.2.refs_1_.x_ref
  54.1 0.1 pack.5
  54.2 0.0 copy-start
  54.2 0.9 copy-done
  55.1 0.8 copy-done.2
  55.9 9.0 %all-to-all-done.1.u_ref = bf16[8,2,32,896]{3,2,1,0:T(8,128)(2,1)S(1)} async-done(((bf16[8,2,32,896]{3,2,1,0:T(8,128)(2,1)}), bf16[8,2,32,896]{3,2,1,0:T(8,128)(2,1)S(1)}, u32[]{:S(2)}, u32[]{:S(2)}) %all-to-all-start.1) | async-done | bytes 917536 | tf_op jit(solution)/shard_map/all_to_all | solution.py:347
  65.0 3.6 %all-to-all-start.2 = ((bf16[8,2,32,896]{3,2,1,0:T(8,128)(2,1)}), bf16[8,2,32,896]{3,2,1,0:T(8,128)(2,1)S(1)}, u32[]{:S(2)}, u32[]{:S(2)}) async-start(bf16[8,2,32,896]{3,2,1,0:T(8,128)(2,1)} %copy-done), calls=%async_computation.2 | async-start | bytes 1835008 | tf_op jit(solution)/shard_map/all_to_all | solution.py:347
  68.5 0.0 collective-permute-done.3.rest_1_
  68.5 2.0 %collective-permute-start.4 = (bf16[128,640]{1,0:T(8,128)(2,1)S(1)}, bf16[128,640]{1,0:T(8,128)(2,1)S(1)}, u32[]{:S(2)}, u32[]{:S(2)}) collective-permute-start(bf16[128,640]{1,0:T(8,128)(2,1)S(1)} %pad_maximum_fusion.2), channel_id=1, source_target_pairs={{0,2},{1,3},{2,0},{3,1},{4,6},{5,7},{6,4},{7,5},{8,10},{9,11},{10,... | collective-permute-start | bytes 491528 | tf_op jit(solution)/shard_map/ppermute | solution.py:246
  70.5 15.9 %collective-permute-done.4.rest_2_ = bf16[128,640]{1,0:T(8,128)(2,1)S(1)} collective-permute-done((bf16[128,640]{1,0:T(8,128)(2,1)S(1)}, bf16[128,640]{1,0:T(8,128)(2,1)S(1)}, u32[]{:S(2)}, u32[]{:S(2)}) %collective-permute-start.4) | collective-permute-done | bytes 163872 | tf_op jit(solution)/shard_map/ppermute | solution.py:246
  86.4 0.8 pad_maximum_fusion
  87.2 1.7 %collective-permute-start.5 = (bf16[256,640]{1,0:T(8,128)(2,1)}, bf16[256,640]{1,0:T(8,128)(2,1)}, u32[]{:S(2)}, u32[]{:S(2)}) collective-permute-start(bf16[256,640]{1,0:T(8,128)(2,1)} %pad_maximum_fusion), channel_id=1, source_target_pairs={{0,1},{1,0},{2,3},{3,2},{4,5},{5,4},{6,7},{7,6},{8,9},{9,8},{10,11... | collective-permute-start | bytes 983048 | tf_op jit(solution)/shard_map/ppermute | solution.py:246
  88.9 1.3 collective-permute-start.7
  90.2 4.1 %slice.27 = bf16[1,1,7168,256]{3,2,1,0:T(8,128)(2,1)} slice(bf16[1,2,7168,256]{3,2,1,0:T(8,128)(2,1)} %w_ref.3), slice={[0:1], [0:1], [0:7168], [0:256]} | slice | bytes 7340032 | tf_op jit(solution)/shard_map/slice | solution.py:337
  94.3 1.4 %collective-permute-start.8 = (bf16[32,7168]{1,0:T(8,128)(2,1)}, bf16[32,7168]{1,0:T(8,128)(2,1)S(1)}, u32[]{:S(2)}, u32[]{:S(2)}) collective-permute-start(bf16[32,7168]{1,0:T(8,128)(2,1)} %copy-done.20), channel_id=1, source_target_pairs={{8,0},{16,8},{24,16},{9,1},{17,9},{25,17},{10,2},{18,10},{26,18},{... | collective-permute-start | bytes 1376264 | tf_op jit(solution)/shard_map/ppermute | solution.py:344
  95.7 0.7 constant_dynamic-slice_fusion.g_ref
  96.4 1.0 dynamic-slice_bitcast_fusion.down_ref
  97.4 0.0 collective-permute-done.5.rest_3_
  97.5 2.5 %columns_step.1 = (bf16[2,256,896]{2,1,0:T(8,128)(2,1)}, bf16[8,64,640]{2,1,0:T(8,128)(2,1)S(1)}) custom-call(s32[1]{0:T(128)} %bitcast.j_ref, bf16[8,2,32,896]{3,2,1,0:T(8,128)(2,1)S(1)} %all-to-all-done.d_ref, bf16[8,2,32,896]{3,2,1,0:T(8,128)(2,1)S(1)} %all-to-all-done.1.u_ref, bf16[896,256]{1,0:T(8,128)(2,1)S(1)} %dynamic-slice_bitcast_fusion.down_ref, ...), custom_call_target="tpu_custom_call" | custom-call | flops 234881024 | bytes 2752512 | tf_op jit(solution)/shard_map/columns_step/pallas_call | solution.py:280
  100.0 1.4 %collective-permute-start.6 = (bf16[2,256,896]{2,1,0:T(8,128)(2,1)}, bf16[2,256,896]{2,1,0:T(8,128)(2,1)}, u32[]{:S(2)}, u32[]{:S(2)}) collective-permute-start(bf16[2,256,896]{2,1,0:T(8,128)(2,1)} %get-tuple-element.33), channel_id=1, source_target_pairs={{8,0},{16,8},{24,16},{9,1},{17,9},{25,17},{10,2},{18,10},{26,18},{... | collective-permute-start | bytes 2752520 | tf_op jit(solution)/shard_map/ppermute | solution.py:344
  101.5 2.6 %latent_side.1 = (bf16[32,256]{1,0:T(8,128)(2,1)S(1)}, f32[32,256]{1,0:T(8,128)S(1)}, f32[32,128]{1,0:T(8,128)S(1)}) custom-call(bf16[32,7168]{1,0:T(8,128)(2,1)S(1)} %copy-done.3, bf16[1,2,7168,256]{3,2,1,0:T(8,128)(2,1)} %w_ref.3, bf16[1,7168]{1,0:T(2,128)(2,1)S(1)} %copy-done.12, bf16[1,256]{1,0:T(2,128)(2,1)S(1)} %copy-done.18), custom_call_target="tpu_custom_call" | custom-call | flops 117440512 | bytes 4128768 | tf_op jit(solution)/shard_map/latent_side/pallas_call | solution.py:187
  104.1 0.0 collective-permute-done.7.y0_ref
  104.1 0.0 collective-permute-done.8.y1_ref
  104.1 3.7 %second_step.1.rest_0_ = bf16[64,512]{1,0:T(8,128)(2,1)S(1)} custom-call(bf16[32,7168]{1,0:T(8,128)(2,1)} %collective-permute-done.7.y0_ref, bf16[32,7168]{1,0:T(8,128)(2,1)S(1)} %collective-permute-done.8.y1_ref, bf16[1,2,7168,256]{3,2,1,0:T(8,128)(2,1)} %w_ref.3, bf16[1,256]{1,0:T(2,128)(2,1)S(1)} %copy-done.18, f32[32,256]{1,0:T(8,128)S(1)} %copy-done.14, ...), custom_call_target="tpu_custom_call" | custom-call | flops 234881024 | bytes 4587520 | tf_op jit(solution)/shard_map/second_step/pallas_call | solution.py:215
  107.8 4.4 %collective-permute-start.9 = (bf16[64,512]{1,0:T(8,128)(2,1)S(1)}, bf16[64,512]{1,0:T(8,128)(2,1)S(1)}, u32[]{:S(2)}, u32[]{:S(2)}) collective-permute-start(bf16[64,512]{1,0:T(8,128)(2,1)S(1)} %second_step.1.rest_0_), channel_id=1, source_target_pairs={{0,4},{1,5},{2,6},{3,7},{4,0},{5,1},{6,2},{7,3},{8,12},{9,13},{10,... | collective-permute-start | bytes 196616 | tf_op jit(solution)/shard_map/ppermute | solution.py:246
  112.2 2.9 %collective-permute-done.9.rest_1_ = bf16[64,512]{1,0:T(8,128)(2,1)S(1)} collective-permute-done((bf16[64,512]{1,0:T(8,128)(2,1)S(1)}, bf16[64,512]{1,0:T(8,128)(2,1)S(1)}, u32[]{:S(2)}, u32[]{:S(2)}) %collective-permute-start.9) | collective-permute-done | bytes 65568 | tf_op jit(solution)/shard_map/ppermute | solution.py:246
  115.2 0.5 collective-permute-start.10
  115.7 5.4 %collective-permute-done.10.rest_2_ = bf16[128,512]{1,0:T(8,128)(2,1)S(1)} collective-permute-done((bf16[128,512]{1,0:T(8,128)(2,1)S(1)}, bf16[128,512]{1,0:T(8,128)(2,1)S(1)}, u32[]{:S(2)}, u32[]{:S(2)}) %collective-permute-start.10) | collective-permute-done | bytes 131104 | tf_op jit(solution)/shard_map/ppermute | solution.py:246
  121.1 0.7 pad_maximum_fusion.1
  121.8 0.8 collective-permute-start.11
  122.7 0.2 copy.7.g_ref
  122.9 7.7 %collective-permute-done.11.rest_3_ = bf16[256,512]{1,0:T(8,128)(2,1)S(1)} collective-permute-done((bf16[256,512]{1,0:T(8,128)(2,1)}, bf16[256,512]{1,0:T(8,128)(2,1)S(1)}, u32[]{:S(2)}, u32[]{:S(2)}) %collective-permute-start.11) | collective-permute-done | bytes 262176 | tf_op jit(solution)/shard_map/ppermute | solution.py:246
  130.6 0.0 all-to-all-done.2.x1_ref
  130.6 0.0 collective-permute-done.6.y1_ref
  130.6 1.1 copy-done.10
  131.7 3.4 %terms.1 = bf16[1,2,896,256]{3,2,1,0:T(8,128)(2,1)} custom-call(s32[1]{0:T(128)} %bitcast.j_ref, bf16[8,2,32,896]{3,2,1,0:T(8,128)(2,1)S(1)} %all-to-all-done.d_ref, bf16[8,2,32,896]{3,2,1,0:T(8,128)(2,1)S(1)} %all-to-all-done.1.u_ref, bf16[8,2,32,896]{3,2,1,0:T(8,128)(2,1)S(1)} %all-to-all-done.2.x1_ref, ...), custom_call_target="tpu_custom_call" | custom-call | flops 939524096 | bytes 3670016 | tf_op jit(solution)/shard_map/terms/pallas_call | solution.py:320
  (28 shorter events, 0.1 us)
Async XLA Ops:
  2.3 13.6 %collective-permute-start.1 = (bf16[32,7168]{1,0:T(8,128)(2,1)}, bf16[32,7168]{1,0:T(8,128)(2,1)S(1)}, u32[]{:S(2)}, u32[]{:S(2)}) collective-permute-start(bf16[32,7168]{1,0:T(8,128)(2,1)} %get-tuple-element.45), channel_id=1, source_target_pairs={{0,24},{8,16},{16,8},{24,0},{1,25},{9,17},{17,9},{25,1},{2,26},{10... | collective-permute-start | bytes 1376264 | tf_op jit(solution)/shard_map/ppermute | solution.py:341
  5.7 33.5 %copy-start.11 = (bf16[1,7168]{1,0:T(2,128)(2,1)S(1)}, bf16[1,7168]{1,0:T(2,128)(2,1)}, u32[]{:S(2)}) copy-start(bf16[1,7168]{1,0:T(2,128)(2,1)} %g_ref.1) | copy-start | bytes 43012
  5.7 33.5 %copy-start.17 = (bf16[1,256]{1,0:T(2,128)(2,1)S(1)}, bf16[1,256]{1,0:T(2,128)(2,1)}, u32[]{:S(2)}) copy-start(bf16[1,256]{1,0:T(2,128)(2,1)} %h_ref.3) | copy-start | bytes 1540
  5.7 29.8 %all-to-all-start = ((bf16[8,2,32,896]{3,2,1,0:T(8,128)(2,1)}), bf16[8,2,32,896]{3,2,1,0:T(8,128)(2,1)S(1)}, u32[]{:S(2)}, u32[]{:S(2)}) async-start(bf16[8,2,32,896]{3,2,1,0:T(8,128)(2,1)} %pack.3), calls=%async_computation | async-start | bytes 1835008 | tf_op jit(solution)/shard_map/all_to_all | solution.py:347
  13.6 12.3 %collective-permute-start = (bf16[32,7168]{1,0:T(8,128)(2,1)S(1)}, bf16[32,7168]{1,0:T(8,128)(2,1)S(1)}, u32[]{:S(2)}, u32[]{:S(2)}) collective-permute-start(bf16[32,7168]{1,0:T(8,128)(2,1)S(1)} %get-tuple-element.44), channel_id=1, source_target_pairs={{0,24},{8,16},{16,8},{24,0},{1,25},{9,17},{17,9},{25,1},{2,26},{10... | collective-permute-start | bytes 1376264 | tf_op jit(solution)/shard_map/ppermute | solution.py:341
  15.9 0.8 copy-start.4
  25.9 1.0 copy-start.5
  27.0 0.9 copy-start.1
  27.9 0.8 copy-start.7
  35.5 29.4 %all-to-all-start.1 = ((bf16[8,2,32,896]{3,2,1,0:T(8,128)(2,1)}), bf16[8,2,32,896]{3,2,1,0:T(8,128)(2,1)S(1)}, u32[]{:S(2)}, u32[]{:S(2)}) async-start(bf16[8,2,32,896]{3,2,1,0:T(8,128)(2,1)} %copy-done.1), calls=%async_computation.1 | async-start | bytes 1835008 | tf_op jit(solution)/shard_map/all_to_all | solution.py:347
  39.1 6.1 %copy-start.6 = (bf16[32,7168]{1,0:T(8,128)(2,1)S(1)}, bf16[32,7168]{1,0:T(8,128)(2,1)}, u32[]{:S(2)}) copy-start(bf16[32,7168]{1,0:T(8,128)(2,1)} %copy-done.4) | copy-start | bytes 1376260
  39.1 6.1 %copy-start.8 = (bf16[32,7168]{1,0:T(8,128)(2,1)S(1)}, bf16[32,7168]{1,0:T(8,128)(2,1)}, u32[]{:S(2)}) copy-start(bf16[32,7168]{1,0:T(8,128)(2,1)} %copy-done.7) | copy-start | bytes 1376260
  39.1 15.0 %collective-permute-start.2 = (bf16[32,7168]{1,0:T(8,128)(2,1)}, bf16[32,7168]{1,0:T(8,128)(2,1)S(1)}, u32[]{:S(2)}, u32[]{:S(2)}) collective-permute-start(bf16[32,7168]{1,0:T(8,128)(2,1)} %get-tuple-element.43), channel_id=1, source_target_pairs={{0,24},{8,16},{16,8},{24,0},{1,25},{9,17},{17,9},{25,1},{2,26},{10... | collective-permute-start | bytes 1376264 | tf_op jit(solution)/shard_map/ppermute | solution.py:341
  45.2 6.0 %copy-start.13 = (f32[32,256]{1,0:T(8,128)}, f32[32,256]{1,0:T(8,128)S(1)}, u32[]{:S(2)}) copy-start(f32[32,256]{1,0:T(8,128)S(1)} %get-tuple-element.37.c0_ref) | copy-start | bytes 98308
  45.2 6.0 %copy-start.15 = (f32[32,128]{1,0:T(8,128)}, f32[32,128]{1,0:T(8,128)S(1)}, u32[]{:S(2)}) copy-start(f32[32,128]{1,0:T(8,128)S(1)} %get-tuple-element.39.ab0_ref) | copy-start | bytes 49156
  45.2 8.9 %copy-start.19 = (bf16[32,7168]{1,0:T(8,128)(2,1)}, bf16[32,7168]{1,0:T(8,128)(2,1)S(1)}, u32[]{:S(2)}) copy-start(bf16[32,7168]{1,0:T(8,128)(2,1)S(1)} %get-tuple-element.35) | copy-start | bytes 1376260
  51.2 13.8 %copy-start.20 = (bf16[32,7168]{1,0:T(8,128)(2,1)}, bf16[32,7168]{1,0:T(8,128)(2,1)S(1)}, u32[]{:S(2)}) copy-start(bf16[32,7168]{1,0:T(8,128)(2,1)S(1)} %get-tuple-element.36) | copy-start | bytes 1376260
  51.2 17.3 %collective-permute-start.3 = (bf16[64,640]{1,0:T(8,128)(2,1)S(1)}, bf16[64,640]{1,0:T(8,128)(2,1)S(1)}, u32[]{:S(2)}, u32[]{:S(2)}) collective-permute-start(bf16[64,640]{1,0:T(8,128)(2,1)S(1)} %get-tuple-element.32.rest_0_), channel_id=1, source_target_pairs={{0,4},{1,5},{2,6},{3,7},{4,0},{5,1},{6,2},{7,3},{8,12},{9,13},{10,... | collective-permute-start | bytes 245768 | tf_op jit(solution)/shard_map/ppermute | solution.py:246
  54.2 0.9 copy-start
  55.1 0.8 copy-start.2
  65.0 65.6 %all-to-all-start.2 = ((bf16[8,2,32,896]{3,2,1,0:T(8,128)(2,1)}), bf16[8,2,32,896]{3,2,1,0:T(8,128)(2,1)S(1)}, u32[]{:S(2)}, u32[]{:S(2)}) async-start(bf16[8,2,32,896]{3,2,1,0:T(8,128)(2,1)} %copy-done), calls=%async_computation.2 | async-start | bytes 1835008 | tf_op jit(solution)/shard_map/all_to_all | solution.py:347
  68.5 17.8 %collective-permute-start.4 = (bf16[128,640]{1,0:T(8,128)(2,1)S(1)}, bf16[128,640]{1,0:T(8,128)(2,1)S(1)}, u32[]{:S(2)}, u32[]{:S(2)}) collective-permute-start(bf16[128,640]{1,0:T(8,128)(2,1)S(1)} %pad_maximum_fusion.2), channel_id=1, source_target_pairs={{0,2},{1,3},{2,0},{3,1},{4,6},{5,7},{6,4},{7,5},{8,10},{9,11},{10,... | collective-permute-start | bytes 491528 | tf_op jit(solution)/shard_map/ppermute | solution.py:246
  87.2 10.3 %collective-permute-start.5 = (bf16[256,640]{1,0:T(8,128)(2,1)}, bf16[256,640]{1,0:T(8,128)(2,1)}, u32[]{:S(2)}, u32[]{:S(2)}) collective-permute-start(bf16[256,640]{1,0:T(8,128)(2,1)} %pad_maximum_fusion), channel_id=1, source_target_pairs={{0,1},{1,0},{2,3},{3,2},{4,5},{5,4},{6,7},{7,6},{8,9},{9,8},{10,11... | collective-permute-start | bytes 983048 | tf_op jit(solution)/shard_map/ppermute | solution.py:246
  88.9 15.2 %collective-permute-start.7 = (bf16[32,7168]{1,0:T(8,128)(2,1)}, bf16[32,7168]{1,0:T(8,128)(2,1)}, u32[]{:S(2)}, u32[]{:S(2)}) collective-permute-start(bf16[32,7168]{1,0:T(8,128)(2,1)} %copy-done.19), channel_id=1, source_target_pairs={{8,0},{16,8},{24,16},{9,1},{17,9},{25,17},{10,2},{18,10},{26,18},{... | collective-permute-start | bytes 1376264 | tf_op jit(solution)/shard_map/ppermute | solution.py:344
  94.3 7.2 %copy-start.3 = (bf16[32,7168]{1,0:T(8,128)(2,1)S(1)}, bf16[32,7168]{1,0:T(8,128)(2,1)}, u32[]{:S(2)}) copy-start(bf16[32,7168]{1,0:T(8,128)(2,1)} %copy-done.2) | copy-start | bytes 1376260
  94.3 7.2 %copy-start.12 = (bf16[1,7168]{1,0:T(2,128)(2,1)S(1)}, bf16[1,7168]{1,0:T(2,128)(2,1)}, u32[]{:S(2)}) copy-start(bf16[1,7168]{1,0:T(2,128)(2,1)} %g_ref.1) | copy-start | bytes 43012
  94.3 7.2 %copy-start.18 = (bf16[1,256]{1,0:T(2,128)(2,1)S(1)}, bf16[1,256]{1,0:T(2,128)(2,1)}, u32[]{:S(2)}) copy-start(bf16[1,256]{1,0:T(2,128)(2,1)} %h_ref.3) | copy-start | bytes 1540
  94.3 9.8 %collective-permute-start.8 = (bf16[32,7168]{1,0:T(8,128)(2,1)}, bf16[32,7168]{1,0:T(8,128)(2,1)S(1)}, u32[]{:S(2)}, u32[]{:S(2)}) collective-permute-start(bf16[32,7168]{1,0:T(8,128)(2,1)} %copy-done.20), channel_id=1, source_target_pairs={{8,0},{16,8},{24,16},{9,1},{17,9},{25,17},{10,2},{18,10},{26,18},{... | collective-permute-start | bytes 1376264 | tf_op jit(solution)/shard_map/ppermute | solution.py:344
  100.0 4.1 %copy-start.9 = (bf16[8,64,640]{2,1,0:T(8,128)(2,1)}, bf16[8,64,640]{2,1,0:T(8,128)(2,1)S(1)}, u32[]{:S(2)}) copy-start(bf16[8,64,640]{2,1,0:T(8,128)(2,1)S(1)} %get-tuple-element.34.first_ref) | copy-start | bytes 1966084
  100.0 4.1 %copy-start.14 = (f32[32,256]{1,0:T(8,128)S(1)}, f32[32,256]{1,0:T(8,128)}, u32[]{:S(2)}) copy-start(f32[32,256]{1,0:T(8,128)} %copy-done.13) | copy-start | bytes 98308
  100.0 4.1 %copy-start.16 = (f32[32,128]{1,0:T(8,128)S(1)}, f32[32,128]{1,0:T(8,128)}, u32[]{:S(2)}) copy-start(f32[32,128]{1,0:T(8,128)} %copy-done.15) | copy-start | bytes 49156
  100.0 30.6 %collective-permute-start.6 = (bf16[2,256,896]{2,1,0:T(8,128)(2,1)}, bf16[2,256,896]{2,1,0:T(8,128)(2,1)}, u32[]{:S(2)}, u32[]{:S(2)}) collective-permute-start(bf16[2,256,896]{2,1,0:T(8,128)(2,1)} %get-tuple-element.33), channel_id=1, source_target_pairs={{8,0},{16,8},{24,16},{9,1},{17,9},{25,17},{10,2},{18,10},{26,18},{... | collective-permute-start | bytes 2752520 | tf_op jit(solution)/shard_map/ppermute | solution.py:344
  107.8 7.3 %collective-permute-start.9 = (bf16[64,512]{1,0:T(8,128)(2,1)S(1)}, bf16[64,512]{1,0:T(8,128)(2,1)S(1)}, u32[]{:S(2)}, u32[]{:S(2)}) collective-permute-start(bf16[64,512]{1,0:T(8,128)(2,1)S(1)} %second_step.1.rest_0_), channel_id=1, source_target_pairs={{0,4},{1,5},{2,6},{3,7},{4,0},{5,1},{6,2},{7,3},{8,12},{9,13},{10,... | collective-permute-start | bytes 196616 | tf_op jit(solution)/shard_map/ppermute | solution.py:246
  115.2 6.0 %collective-permute-start.10 = (bf16[128,512]{1,0:T(8,128)(2,1)S(1)}, bf16[128,512]{1,0:T(8,128)(2,1)S(1)}, u32[]{:S(2)}, u32[]{:S(2)}) collective-permute-start(bf16[128,512]{1,0:T(8,128)(2,1)S(1)} %pad_maximum_fusion.3), channel_id=1, source_target_pairs={{0,2},{1,3},{2,0},{3,1},{4,6},{5,7},{6,4},{7,5},{8,10},{9,11},{10,... | collective-permute-start | bytes 393224 | tf_op jit(solution)/shard_map/ppermute | solution.py:246
  121.8 8.7 %collective-permute-start.11 = (bf16[256,512]{1,0:T(8,128)(2,1)}, bf16[256,512]{1,0:T(8,128)(2,1)S(1)}, u32[]{:S(2)}, u32[]{:S(2)}) collective-permute-start(bf16[256,512]{1,0:T(8,128)(2,1)} %pad_maximum_fusion.1), channel_id=1, source_target_pairs={{0,1},{1,0},{2,3},{3,2},{4,5},{5,4},{6,7},{7,6},{8,9},{9,8},{10,11... | collective-permute-start | bytes 786440 | tf_op jit(solution)/shard_map/ppermute | solution.py:246
  130.6 1.1 copy-start.10

commit v4 on v3

v4 whole, which is shorter than its diff:
```python
import functools

import jax
import jax.numpy as jnp
from jax import lax
from jax.experimental import pallas as pl
from jax.experimental.pallas import tpu as pltpu
from jax.sharding import PartitionSpec as P

EPS = 1e-06
LANES = 128
ANY = pl.BlockSpec(memory_space=pl.ANY)
VMEM = pl.BlockSpec(memory_space=pltpu.VMEM)
SMEM = pl.BlockSpec(memory_space=pltpu.SMEM)
LIMIT = 62 * 1024 * 1024
COST = pl.CostEstimate(flops=1, bytes_accessed=1, transcendentals=0)
F32 = jnp.float32
BF16 = jnp.bfloat16


def rows_dot(left, right):
    return lax.dot_general(left, right, (((0,), (0,)), ((), ())), preferred_element_type=F32)


def dot_t(left, right):
    return lax.dot_general(left, right, (((1,), (1,)), ((), ())), preferred_element_type=F32)


def dot(left, right):
    return jnp.dot(left, right, preferred_element_type=F32)


def norm_scale(v):
    return lax.rsqrt(jnp.mean(v * v, axis=-1, keepdims=True) + EPS)


def with_scalar(aq, s):
    high = s.astype(BF16).astype(F32)
    at = lax.broadcasted_iota(jnp.int32, (aq.shape[0], LANES), 1)
    tail = jnp.where(at == 0, high, jnp.where(at == 1, s - high, 0.0)).astype(BF16)
    return jnp.concatenate([aq, tail], 1)


def pack_into(out, sources):
    parts, share = out.shape[0], out.shape[3]
    for i, source in enumerate(sources):
        for d in range(parts):
            out[d, i] = source[:, d * share : (d + 1) * share]


def pack_kernel(*refs):
    pack_into(refs[-1], refs[:-1])


def pack(blocks, parts):
    rows, width = blocks[0].shape
    count = len(blocks)
    return pl.pallas_call(
        pack_kernel,
        out_shape=shape(parts, count, rows, width // parts),
        in_specs=[VMEM] * count,
        out_specs=VMEM,
        compiler_params=pltpu.CompilerParams(vmem_limit_bytes=LIMIT),
        cost_estimate=COST,
        name="pack",
    )(*blocks)


def run_copies(pairs, sems):
    copies = [pltpu.make_async_copy(source, target, sems.at[i]) for i, (source, target) in enumerate(pairs)]
    for copy in copies:
        copy.start()
    for copy in copies:
        copy.wait()


def prepare_kernel(down_ref, up_ref, start_ref, packed_ref, x0_ref, y0_ref, x1_ref, sems):
    parts, three, rows, share = packed_ref.shape
    pairs = []
    for i, source in enumerate((down_ref.at[0, 0], start_ref.at[0, 0], down_ref.at[0, 1])):
        for d in range(parts):
            pairs.append((source.at[:, pl.ds(d * share, share)], packed_ref.at[d, i]))
    pairs += [(up_ref.at[0, 0], x0_ref), (start_ref.at[1, 0], y0_ref), (up_ref.at[0, 1], x1_ref)]
    run_copies(pairs, sems)


def prepare(saved_down, saved_up, grad_start, parts):
    rows, width = saved_down.shape[2:]
    share = width // parts
    if share % LANES:
        x0, y0, x1 = saved_up[0, 0], grad_start[1, 0], saved_up[0, 1]
        return pack([saved_down[0, 0], grad_start[0, 0], saved_down[0, 1]], parts), x0, y0, x1
    return pl.pallas_call(
        prepare_kernel,
        out_shape=[shape(parts, 3, rows, share)] + [shape(rows, width)] * 3,
        in_specs=[ANY] * 3,
        out_specs=[VMEM] * 4,
        scratch_shapes=[pltpu.SemaphoreType.DMA((3 * parts + 3,))],
        compiler_params=pltpu.CompilerParams(vmem_limit_bytes=LIMIT),
        cost_estimate=COST,
        name="prepare",
    )(saved_down, saved_up, grad_start)


def shape(*dims, dtype=BF16):
    return jax.ShapeDtypeStruct(dims, dtype)


CHUNKS = 4


def load_chunks(source, buffer, sems):
    chunk = buffer.shape[0] // CHUNKS
    copies = []
    for i in range(CHUNKS):
        part = pl.ds(i * chunk, chunk)
        copies.append(pltpu.make_async_copy(source.at[part], buffer.at[part], sems.at[i]))
    for copy in copies:
        copy.start()
    return copies


def chunked_dot(left, copies, buffer):
    chunk = buffer.shape[0] // CHUNKS
    total = None
    for i, copy in enumerate(copies):
        copy.wait()
        part = dot(left[:, i * chunk : (i + 1) * chunk], buffer[i * chunk : (i + 1) * chunk, :])
        total = part if total is None else total + part
    return total


def latent_gradient(u, c, a, b):
    q = b * (u - c * b * b * jnp.mean(u * c, axis=-1, keepdims=True))
    return (q * a).astype(BF16)


def next_latent(c, a, h, k_ref, c_ref, ab_ref):
    b = norm_scale(c)
    k_ref[...] = (c * b * h).astype(BF16)
    c_ref[...] = c
    at = lax.broadcasted_iota(jnp.int32, (c.shape[0], LANES), 1)
    ab_ref[...] = jnp.where(at == 0, a, b)


def first_kernel(stacked, x_ref, y_ref, w_ref, g_ref, h_ref, *rest):
    rest, (down, up, sem0, sem1) = rest[:-4], rest[-4:]
    copies0 = load_chunks(w_ref.at[0, 0], down, sem0)
    copies1 = load_chunks(w_ref.at[0, 1], up, sem1)
    if stacked:
        x_ref, x1_ref, y_ref = x_ref.at[0, 0], x_ref.at[0, 1], y_ref.at[0, 0]
        z_ref, narrow_ref, k1_ref, c1_ref, ab1_ref = rest
        mine = slice(0, x_ref.shape[0])
    else:
        before_ref, z_ref, narrow_ref = rest
        narrow_ref[: x_ref.shape[0]] = before_ref[...]
        mine = slice(x_ref.shape[0], 2 * x_ref.shape[0])
    rows, width = x_ref.shape
    lat = h_ref.shape[1]
    chunk = width // CHUNKS
    g = g_ref[...].astype(F32)
    h = h_ref[...].astype(F32)
    x = x_ref[...].astype(F32)
    a = norm_scale(x)
    normed = (x * a * g).astype(BF16)
    if stacked:
        x1 = x1_ref[...].astype(F32)
        a1 = norm_scale(x1)
        normed = jnp.concatenate([normed, (x1 * a1 * g).astype(BF16)], 0)
    c = chunked_dot(normed, copies0, down)
    u = chunked_dot(y_ref[...], copies1, up) * h
    if stacked:
        c1 = c[rows:]
        c = c[:rows]
        next_latent(c1, a1, h, k1_ref, c1_ref, ab1_ref)
    b = norm_scale(c)
    narrow_ref[mine, lat + LANES :] = (c * b * h).astype(BF16)
    aq = latent_gradient(u, c, a, b)
    s = a * jnp.sum(aq.astype(F32) * c, axis=-1, keepdims=True) / width
    narrow_ref[mine, : lat + LANES] = with_scalar(aq, s)
    for i in range(CHUNKS):
        cols = slice(i * chunk, (i + 1) * chunk)
        m = dot_t(aq, down[cols, :])
        z = y_ref[:, cols].astype(F32) + m * g[:, cols] - x_ref[:, cols].astype(F32) * s
        z_ref[:, cols] = z.astype(BF16)


def first_step(x, y, weights, g, h, before=None):
    rows, width = x.shape[-2:]
    lat = h.shape[1]
    operands = [x, y, weights, g, h]
    outs = [shape(rows, width)]
    if before is None:
        outs += [shape(rows, 2 * lat + LANES), shape(rows, lat), shape(rows, lat, dtype=F32), shape(rows, LANES, dtype=F32)]
    else:
        outs += [shape(2 * rows, 2 * lat + LANES)]
        operands += [before]
    return pl.pallas_call(
        functools.partial(first_kernel, before is None),
        out_shape=outs,
        in_specs=[VMEM] * 2 + [ANY] + [VMEM] * (len(operands) - 3),
        out_specs=[VMEM] * len(outs),
        scratch_shapes=[pltpu.VMEM((width, lat), BF16)] * 2 + [pltpu.SemaphoreType.DMA((CHUNKS,))] * 2,
        compiler_params=pltpu.CompilerParams(vmem_limit_bytes=LIMIT),
        cost_estimate=COST,
        name="first_step",
    )(*operands)


def latent_kernel(x_ref, w_ref, g_ref, h_ref, k_ref, c_ref, ab_ref, down, sem):
    copies = load_chunks(w_ref.at[0, 0], down, sem)
    x = x_ref[...].astype(F32)
    a = norm_scale(x)
    c = chunked_dot((x * a * g_ref[...].astype(F32)).astype(BF16), copies, down)
    next_latent(c, a, h_ref[...].astype(F32), k_ref, c_ref, ab_ref)


def latent_side(x, weights, g, h):
    rows, width = x.shape
    lat = h.shape[1]
    outs = [shape(rows, lat), shape(rows, lat, dtype=F32), shape(rows, LANES, dtype=F32)]
    return pl.pallas_call(
        latent_kernel,
        out_shape=outs,
        in_specs=[VMEM, ANY, VMEM, VMEM],
        out_specs=[VMEM] * 3,
        scratch_shapes=[pltpu.VMEM((width, lat), BF16), pltpu.SemaphoreType.DMA((CHUNKS,))],
        compiler_params=pltpu.CompilerParams(vmem_limit_bytes=LIMIT),
        cost_estimate=COST,
        name="latent_side",
    )(x, weights, g, h)


def gradient_kernel(x_ref, y_ref, w_ref, g_ref, h_ref, k_ref, c_ref, ab_ref, before_ref, z_ref, narrow_ref, down, up, sem0, sem1):
    copies1 = load_chunks(w_ref.at[0, 1], up, sem1)
    copies0 = load_chunks(w_ref.at[0, 0], down, sem0)
    rows, width = x_ref.shape
    lat = h_ref.shape[1]
    chunk = width // CHUNKS
    c, a, b = c_ref[...], ab_ref[:, 0:1], ab_ref[:, 1:2]
    narrow_ref[:rows] = before_ref[...]
    narrow_ref[rows:, lat + LANES :] = k_ref[...]
    aq = latent_gradient(chunked_dot(y_ref[...], copies1, up) * h_ref[...].astype(F32), c, a, b)
    s = a * jnp.sum(aq.astype(F32) * c, axis=-1, keepdims=True) / width
    narrow_ref[rows:, : lat + LANES] = with_scalar(aq, s)
    for i, copy in enumerate(copies0):
        copy.wait()
        cols = slice(i * chunk, (i + 1) * chunk)
        m = dot_t(aq, down[cols, :])
        z = y_ref[:, cols].astype(F32) + m * g_ref[:, cols].astype(F32) - x_ref[:, cols].astype(F32) * s
        z_ref[:, cols] = z.astype(BF16)


def gradient_step(x, y, weights, g, h, k, c, ab, before):
    rows, width = x.shape
    lat = h.shape[1]
    return pl.pallas_call(
        gradient_kernel,
        out_shape=[shape(rows, width), shape(2 * rows, 2 * lat + LANES)],
        in_specs=[VMEM] * 2 + [ANY] + [VMEM] * 6,
        out_specs=[VMEM] * 2,
        scratch_shapes=[pltpu.VMEM((width, lat), BF16)] * 2 + [pltpu.SemaphoreType.DMA((CHUNKS,))] * 2,
        compiler_params=pltpu.CompilerParams(vmem_limit_bytes=LIMIT),
        cost_estimate=COST,
        name="gradient_step",
    )(x, y, weights, g, h, k, c, ab, before)


def second_kernel(y0_ref, y1_ref, w_ref, h_ref, c0_ref, c1_ref, ab0_ref, ab1_ref, k0_ref, k1_ref, out_ref, up, sem):
    copies = load_chunks(w_ref.at[0, 1], up, sem)
    rows, width = y0_ref.shape
    lat = h_ref.shape[1]
    out_ref[:rows, lat:] = k0_ref[...]
    out_ref[rows:, lat:] = k1_ref[...]
    y = jnp.concatenate([y0_ref[...], y1_ref[...]], 0)
    u = chunked_dot(y, copies, up) * h_ref[...].astype(F32)
    out_ref[:rows, :lat] = latent_gradient(u[:rows], c0_ref[...], ab0_ref[:, 0:1], ab0_ref[:, 1:2])
    out_ref[rows:, :lat] = latent_gradient(u[rows:], c1_ref[...], ab1_ref[:, 0:1], ab1_ref[:, 1:2])


def second_step(y0, y1, weights, h, c0, c1, ab0, ab1, k0, k1):
    rows, width = y0.shape
    lat = h.shape[1]
    return pl.pallas_call(
        second_kernel,
        out_shape=shape(2 * rows, 2 * lat),
        in_specs=[VMEM] * 2 + [ANY] + [VMEM] * 7,
        out_specs=VMEM,
        scratch_shapes=[pltpu.VMEM((width, lat), BF16), pltpu.SemaphoreType.DMA((CHUNKS,))],
        compiler_params=pltpu.CompilerParams(vmem_limit_bytes=LIMIT),
        cost_estimate=COST,
        name="second_step",
    )(y0, y1, weights, h, c0, c1, ab0, ab1, k0, k1)


def held_order(parts):
    far = list(range(parts - 2, 0, -2))
    return [0] + far + [p ^ 1 for p in [0] + far]


def gather_pieces(block, axis):
    parts = lax.axis_size(axis)

    def across(held, apart):
        return lax.ppermute(held, axis, [(i, i ^ apart) for i in range(parts)])

    pieces = [block] + [across(block, apart) for apart in range(parts - 2, 0, -2)]
    return pieces + [across(jnp.concatenate(pieces, 0), 1)]


def restore(j, pieces, out):
    parts, rows = out.shape[:2]
    order, at = held_order(parts), 0
    for piece in pieces:
        for i in range(piece.shape[0] // rows):
            out[j ^ order[at]] = piece[i * rows : (i + 1) * rows, :]
            at += 1


def columns_of(x, y, narrow, down, g):
    parts, rows, share = x.shape
    lat = down.shape[3]
    narrow = narrow.reshape(parts * rows, narrow.shape[2])
    s = narrow[:, lat : lat + 1].astype(F32) + narrow[:, lat + 1 : lat + 2].astype(F32)
    m = dot_t(narrow[:, :lat], down[0, 0])
    x = x.reshape(parts * rows, share).astype(F32)
    y = y.reshape(parts * rows, share).astype(F32)
    return (y + m * g[...].astype(F32) - x * s).astype(BF16)


def columns_first_kernel(j_ref, d_ref, down_ref, g_ref, *rest):
    pieces, z_ref, narrow_ref = rest[:-2], rest[-2], rest[-1]
    restore(j_ref[0], pieces, narrow_ref)
    rows = d_ref.shape[2]
    z_ref[...] = columns_of(d_ref[:, 0], d_ref[:, 1], narrow_ref[:, :rows, :], down_ref, g_ref)


def columns_next_kernel(u_ref, down_ref, g_ref, narrow_ref, z_ref):
    rows = u_ref.shape[2]
    z_ref[...] = columns_of(u_ref[:, 0], u_ref[:, 1], narrow_ref[:, rows:, :], down_ref, g_ref)


def columns_first(j, d, down, g, pieces):
    parts, two, rows, share = d.shape
    lat = down.shape[3]
    return pl.pallas_call(
        columns_first_kernel,
        out_shape=[shape(parts * rows, share), shape(parts, *pieces[0].shape)],
        in_specs=[SMEM] + [VMEM] * (3 + len(pieces)),
        out_specs=[VMEM, VMEM],
        compiler_params=pltpu.CompilerParams(vmem_limit_bytes=LIMIT),
        cost_estimate=COST,
        name="columns_first",
    )(j, d, down, g, *pieces)


def columns_next(u, down, g, narrow):
    parts, two, rows, share = u.shape
    lat = down.shape[3]
    return pl.pallas_call(
        columns_next_kernel,
        out_shape=shape(parts * rows, share),
        in_specs=[VMEM] * 4,
        out_specs=VMEM,
        compiler_params=pltpu.CompilerParams(vmem_limit_bytes=LIMIT),
        cost_estimate=COST,
        name="columns_next",
    )(u, down, g, narrow)


def terms_kernel(j_ref, d_ref, u_ref, y1d_ref, y1u_ref, first_ref, g_ref, *rest):
    pieces, out_ref, second_ref = rest[:-2], rest[-2], rest[-1]
    parts, two, rows, share = d_ref.shape
    lat = second_ref.shape[2] // 2
    total = parts * rows
    restore(j_ref[0], pieces, second_ref)

    def half(ref, i, start):
        return ref[:, i * rows : (i + 1) * rows, start : start + lat].reshape(total, lat)

    def wide(ref, i):
        return ref[:, i].reshape(total, share)

    first = rows_dot(wide(d_ref, 0), half(first_ref, 0, 0))
    first += rows_dot(wide(u_ref, 0), half(first_ref, 1, 0))
    first += rows_dot(wide(d_ref, 2), half(second_ref, 0, 0))
    first += rows_dot(wide(u_ref, 2), half(second_ref, 1, 0))
    out_ref[0, 0] = (first * g_ref[...].astype(F32)).astype(BF16)
    second = rows_dot(wide(d_ref, 1), half(first_ref, 0, lat + LANES))
    second += rows_dot(wide(u_ref, 1), half(first_ref, 1, lat + LANES))
    second += rows_dot(y1d_ref[...], half(second_ref, 0, lat))
    second += rows_dot(y1u_ref[...], half(second_ref, 1, lat))
    out_ref[0, 1] = second.astype(BF16)


def terms(j, d, u, y1d, y1u, first, g, pieces):
    parts, two, rows, share = d.shape
    narrow = pieces[0].shape
    lat = narrow[1] // 2
    return pl.pallas_call(
        terms_kernel,
        out_shape=shape(1, 2, share, lat),
        in_specs=[SMEM] + [VMEM] * (6 + len(pieces)),
        out_specs=VMEM,
        scratch_shapes=[pltpu.VMEM((parts,) + narrow, BF16)],
        compiler_params=pltpu.CompilerParams(vmem_limit_bytes=LIMIT),
        cost_estimate=COST,
        name="terms",
    )(j, d, u, y1d, y1u, first, g, *pieces)


def per_device(weights, gain_model, gain_latent, saved_down, saved_up, grad_start):
    ranks = lax.axis_size("pipe")
    replicas = lax.axis_size("dp")
    j = lax.axis_index("dp")
    share = weights.shape[2] // replicas
    own_down = lax.dynamic_slice(weights, (0, 0, j * share, 0), (1, 1, share, weights.shape[3]))
    own_g = lax.dynamic_slice_in_dim(gain_model, j * share, share, 1)

    def mirror(block):
        return lax.ppermute(block, "pipe", [(i, ranks - 1 - i) for i in range(ranks)])

    def to_before(block):
        return lax.ppermute(block, "pipe", [(i + 1, i) for i in range(ranks - 1)])

    def exchange(blocks):
        return lax.all_to_all(blocks, "dp", 0, 0, tiled=True)

    packed, x0u, y0u, x1u = prepare(saved_down, saved_up, grad_start, replicas)
    packed, x0u, y0u, x1u, saved_down, grad_start = lax.optimization_barrier((packed, x0u, y0u, x1u, saved_down, grad_start))
    x0u, y0u, x1u = mirror(x0u), mirror(y0u), mirror(x1u)
    d_s = exchange(packed)
    z0d, before, k1d, c1d, ab1d = first_step(saved_down, grad_start, weights, gain_model, gain_latent)
    y1d = to_before(z0d)
    x0u, before = lax.optimization_barrier((x0u, before))
    k0u, c0u, ab0u = latent_side(x0u, weights, gain_model, gain_latent)
    y0u, c0u = lax.optimization_barrier((y0u, c0u))
    z0u, narrow = gradient_step(x0u, y0u, weights, gain_model, gain_latent, k0u, c0u, ab0u, before)
    z0u, narrow, y1d = lax.optimization_barrier((z0u, narrow, y1d))
    y1u = to_before(z0u)
    first_pieces = gather_pieces(narrow, "dp")
    far = len(first_pieces) - 1
    u_packed = pack([x0u, y0u, x1u], replicas)
    u_packed, y1u, x1u, d_s, *first_pieces[1:far] = lax.optimization_barrier((u_packed, y1u, x1u, d_s, *first_pieces[1:far]))
    u_s = exchange(u_packed)
    k1u, c1u, ab1u = latent_side(x1u, weights, gain_model, gain_latent)
    second = second_step(y1d, y1u, weights, gain_latent, c1d, c1u, ab1d, ab1u, k1d, k1u)
    second_pieces = gather_pieces(second, "dp")
    z0d_s, first = columns_first(j[None], d_s, own_down, own_g, first_pieces)
    y1d_s = to_before(z0d_s)
    u_s, first, *second_pieces[1:far] = lax.optimization_barrier((u_s, first, *second_pieces[1:far]))
    y1u_s = to_before(columns_next(u_s, own_down, own_g, first))
    return terms(j[None], d_s, u_s, y1d_s, y1u_s, first, own_g.reshape(share, 1), second_pieces)


def solution(mesh):
    placed = (
        P("pipe", None, None, None),
        P("pipe", None),
        P("pipe", None),
        P("pipe", None, "dp", None),
        P("pipe", None, "dp", None),
        P(None, "pipe", "dp", None),
    )
    return jax.shard_map(
        per_device,
        mesh=mesh,
        in_specs=placed,
        out_specs=P("pipe", None, "dp", None),
        check_vma=False,
    )
```

time: 137 us -> 119 us (0.87)
  waiting for transfers between devices: 58.8 us -> 28.7 us
  Pallas kernels: 25.2 us -> 45.4 us
  local copies, waits for them, and re-layouts: 16.7 us -> 9.02 us
  starting transfers between devices: 32.6 us -> 34 us
    all_to_all x3 -> x2, waiting for transfers between devices: 15.8 us -> 0.01 us  [exchange(): return lax.all_to_all(blocks, 'dp', 0, 0, tiled=True)]
    pallas_call x4 -> x5, Pallas kernels: 3.68 us -> 19.4 us  [the longest x1 7.52 us: gradient_step(): pl.pallas_call(gradient_kernel, out_shape=[shape(rows, width), shape(2 *...]
    ppermute x3, waiting for transfers between devices: 11 us -> 3.71 us  [mirror(): lax.ppermute(block, 'pipe', [(i, ranks - 1 - i) for i in range(ranks)])]
    ppermute x6 -> x8, waiting for transfers between devices: 31.9 us -> 25 us  [across(): return lax.ppermute(held, axis, [(i, i ^ apart) for i in range(parts)])]
    pallas_call x1 -> x2, Pallas kernels: 2.62 us -> 8.83 us  [latent_side(): pl.pallas_call(latent_kernel, out_shape=outs, in_specs=[VMEM, ANY, VMEM,...]
    squeeze x2 -> x0, local copies, waits for them, and re-layouts: 4.3 us -> none  [the longest x1 2.32 us: per_device(): y0u = mirror(grad_start[1, 0])]
    slice x1 -> x0, local copies, waits for them, and re-layouts: 4.07 us -> none  [per_device(): own_down = lax.dynamic_slice_in_dim(weights[0, 0], j * share, share, 0)]
    pallas_call x2 -> x1, Pallas kernels: 11.9 us -> 7.9 us  [first_step(): pl.pallas_call(functools.partial(first_kernel, before is None), out_shape...]
  transfers between devices with their start and end apart: 15 -> 17, of which waited for: 8 -> 5; matrix products, arithmetic and copies ran while one was open for 7% -> 5% of each run, Pallas kernels for 16% -> 31%
where the time goes in v4:
time: 119 us; the launch traced here: 118 us
  Pallas kernels  45.4 us (38%)
  starting transfers between devices  34 us (29%)
  waiting for transfers between devices  28.7 us (24%)
  local copies, waits for them, and re-layouts  9.02 us (8%)
    ppermute x8, waiting for transfers between devices, across(): return lax.ppermute(held, axis, [(i, i ^ apart) for i in range(parts)])  25 us
    ppermute x8, starting transfers between devices, across(): return lax.ppermute(held, axis, [(i, i ^ apart) for i in range(parts)])  12.5 us
    all_to_all x2, starting transfers between devices, exchange(): return lax.all_to_all(blocks, 'dp', 0, 0, tiled=True)  11.5 us
    pallas_call x2, Pallas kernels, latent_side(): pl.pallas_call(latent_kernel, out_shape=outs, in_specs=[VMEM, ANY, VMEM,...  8.83 us
    pallas_call x1, Pallas kernels, first_step(): pl.pallas_call(functools.partial(first_kernel, before is None), out_shape...  7.9 us
    pallas_call x1, Pallas kernels, gradient_step(): pl.pallas_call(gradient_kernel, out_shape=[shape(rows, width), shape(2 *...  7.52 us
    ppermute x4, starting transfers between devices, to_before(): return lax.ppermute(block, 'pipe', [(i + 1, i) for i in range(ranks - 1)])  5.14 us
    ppermute x3, starting transfers between devices, mirror(): lax.ppermute(block, 'pipe', [(i, ranks - 1 - i) for i in range(ranks)])  4.78 us
  transfers between devices with their start and end apart: 17, of which 5 were waited for; matrix products, arithmetic and copies ran while one was open for 5% of the time, Pallas kernels for 31%

profile of v4, /device:TPU:0, one launch (start us, length us, event | category | flops | bytes accessed | tf_op | source)
XLA Modules:
  0.0 118.3 jit_solution(2875282004263882020)
XLA Ops:
  0.0 3.6 %prepare.1 = (bf16[8,3,32,896]{3,2,1,0:T(8,128)(2,1)}, bf16[32,7168]{1,0:T(8,128)(2,1)}, bf16[32,7168]{1,0:T(8,128)(2,1)}, bf16[32,7168]{1,0:T(8,128)(2,1)}) custom-call(bf16[1,2,32,7168]{3,2,1,0:T(8,128)(2,1)} %x_ref, bf16[1,2,32,7168]{3,2,1,0:T(8,128)(2,1)} %up_ref.1, bf16[2,1,32,7168]{3,2,1,0:T(8,128)(2,1)} %y_ref), custom_call_target="tpu_custom_call" | custom-call | flops 1 | bytes 1 | tf_op jit(solution)/shard_map/prepare/pallas_call | solution.py:93
  3.6 7.3 %all-to-all-start = ((bf16[8,3,32,896]{3,2,1,0:T(8,128)(2,1)}), bf16[8,3,32,896]{3,2,1,0:T(8,128)(2,1)S(1)}, u32[]{:S(2)}, u32[]{:S(2)}) async-start(bf16[8,3,32,896]{3,2,1,0:T(8,128)(2,1)} %get-tuple-element.70), calls=%async_computation | async-start | bytes 2752512 | tf_op jit(solution)/shard_map/all_to_all | solution.py:427
  10.9 0.7 collective-permute-start
  11.6 1.1 collective-permute-start.1
  12.7 7.9 %first_step.1 = (bf16[32,7168]{1,0:T(8,128)(2,1)}, bf16[32,640]{1,0:T(8,128)(2,1)}, bf16[32,256]{1,0:T(8,128)(2,1)}, f32[32,256]{1,0:T(8,128)}, f32[32,128]{1,0:T(8,128)}) custom-call(bf16[1,2,32,7168]{3,2,1,0:T(8,128)(2,1)} %x_ref, bf16[2,1,32,7168]{3,2,1,0:T(8,128)(2,1)} %y_ref, bf16[1,2,7168,256]{3,2,1,0:T(8,128)(2,1)} %w_ref.9, bf16[1,7168]{1,0:T(2,128)(2,1)} %g_ref.7, ...), custom_call_target="tpu_custom_call" | custom-call | flops 1 | bytes 1 | tf_op jit(solution)/shard_map/first_step/pallas_call | solution.py:198
  20.6 1.3 %collective-permute-start.3 = (bf16[32,7168]{1,0:T(8,128)(2,1)}, bf16[32,7168]{1,0:T(8,128)(2,1)}, u32[]{:S(2)}, u32[]{:S(2)}) collective-permute-start(bf16[32,7168]{1,0:T(8,128)(2,1)} %get-tuple-element.68), channel_id=1, source_target_pairs={{8,0},{16,8},{24,16},{9,1},{17,9},{25,17},{10,2},{18,10},{26,18},{... | collective-permute-start | bytes 1376264 | tf_op jit(solution)/shard_map/ppermute | solution.py:424
  21.9 3.0 %collective-permute-start.2 = (bf16[32,7168]{1,0:T(8,128)(2,1)}, bf16[32,7168]{1,0:T(8,128)(2,1)}, u32[]{:S(2)}, u32[]{:S(2)}) collective-permute-start(bf16[32,7168]{1,0:T(8,128)(2,1)} %get-tuple-element.61), channel_id=1, source_target_pairs={{0,24},{8,16},{16,8},{24,0},{1,25},{9,17},{17,9},{25,1},{2,26},{10... | collective-permute-start | bytes 1376264 | tf_op jit(solution)/shard_map/ppermute | solution.py:421
  24.9 0.0 collective-permute-done.x_ref.refs_0_
  24.9 0.8 copy-done.1
  25.7 4.4 %latent_side.2 = (bf16[32,256]{1,0:T(8,128)(2,1)}, f32[32,256]{1,0:T(8,128)}, f32[32,128]{1,0:T(8,128)}) custom-call(bf16[32,7168]{1,0:T(8,128)(2,1)} %copy-done.1, bf16[1,2,7168,256]{3,2,1,0:T(8,128)(2,1)} %w_ref.9, bf16[1,7168]{1,0:T(2,128)(2,1)} %g_ref.7, bf16[1,256]{1,0:T(2,128)(2,1)} %h_ref.9), custom_call_target="tpu_custom_call" | custom-call | flops 1 | bytes 1 | tf_op jit(solution)/shard_map/latent_side/pallas_call | solution.py:222
  30.1 3.7 %collective-permute-done.1.refs_1_.y_ref = bf16[32,7168]{1,0:T(8,128)(2,1)} collective-permute-done((bf16[32,7168]{1,0:T(8,128)(2,1)}, bf16[32,7168]{1,0:T(8,128)(2,1)}, u32[]{:S(2)}, u32[]{:S(2)}) %collective-permute-start.1) | collective-permute-done | bytes 458784 | tf_op jit(solution)/shard_map/ppermute | solution.py:421
  33.8 7.5 %gradient_step.1 = (bf16[32,7168]{1,0:T(8,128)(2,1)}, bf16[64,640]{1,0:T(8,128)(2,1)}) custom-call(bf16[32,7168]{1,0:T(8,128)(2,1)} %copy-done.1, bf16[32,7168]{1,0:T(8,128)(2,1)} %collective-permute-done.1.refs_1_.y_ref, bf16[1,2,7168,256]{3,2,1,0:T(8,128)(2,1)} %w_ref.9, bf16[1,7168]{1,0:T(2,128)(2,1)} %g_ref.7, bf16[1,256]{1,0:T(2,128)(2,1)} %h_ref.9, ...), custom_call_target="tpu_custom_call" | custom-call | flops 1 | bytes 1 | tf_op jit(solution)/shard_map/gradient_step/pallas_call | solution.py:257
  41.3 0.0 collective-permute-done.3.y0_ref
  41.3 1.3 %collective-permute-start.4 = (bf16[32,7168]{1,0:T(8,128)(2,1)}, bf16[32,7168]{1,0:T(8,128)(2,1)S(1)}, u32[]{:S(2)}, u32[]{:S(2)}) collective-permute-start(bf16[32,7168]{1,0:T(8,128)(2,1)} %get-tuple-element.69), channel_id=1, source_target_pairs={{8,0},{16,8},{24,16},{9,1},{17,9},{25,17},{10,2},{18,10},{26,18},{... | collective-permute-start | bytes 1376264 | tf_op jit(solution)/shard_map/ppermute | solution.py:424
  42.6 3.9 %collective-permute-start.5 = (bf16[64,640]{1,0:T(8,128)(2,1)}, bf16[64,640]{1,0:T(8,128)(2,1)S(1)}, u32[]{:S(2)}, u32[]{:S(2)}) collective-permute-start(bf16[64,640]{1,0:T(8,128)(2,1)} %get-tuple-element.71.rest_0_), channel_id=1, source_target_pairs={{0,6},{1,7},{2,4},{3,5},{4,2},{5,3},{6,0},{7,1},{8,14},{9,15},{10,... | collective-permute-start | bytes 245768 | tf_op jit(solution)/shard_map/ppermute | solution.py:305
  46.5 0.0 collective-permute-start.6
  46.5 0.6 collective-permute-start.7
  47.2 0.0 collective-permute-done.2.refs_2_.x_ref
  47.2 2.5 %pack.1 = bf16[8,3,32,896]{3,2,1,0:T(8,128)(2,1)} custom-call(bf16[32,7168]{1,0:T(8,128)(2,1)} %copy-done.1, bf16[32,7168]{1,0:T(8,128)(2,1)} %collective-permute-done.1.refs_1_.y_ref, bf16[32,7168]{1,0:T(8,128)(2,1)} %collective-permute-done.2.refs_2_.x_ref), custom_call_target="tpu_custom_call" | custom-call | flops 1 | bytes 1 | tf_op jit(solution)/shard_map/pack/pallas_call | solution.py:58
  49.7 0.0 collective-permute-done.5.rest_1_
  49.7 5.2 %collective-permute-done.6.rest_2_ = bf16[64,640]{1,0:T(8,128)(2,1)} collective-permute-done((bf16[64,640]{1,0:T(8,128)(2,1)}, bf16[64,640]{1,0:T(8,128)(2,1)}, u32[]{:S(2)}, u32[]{:S(2)}) %collective-permute-start.6) | collective-permute-done | bytes 81952 | tf_op jit(solution)/shard_map/ppermute | solution.py:305
  54.9 0.0 collective-permute-done.7.rest_3_
  54.9 0.0 collective-permute-done.4.y1_ref
  54.9 0.0 all-to-all-done.d_ref
  54.9 0.0 copy-start
  55.0 0.8 copy-done.5
  55.7 0.5 copy-done
  56.2 4.3 %all-to-all-start.1 = ((bf16[8,3,32,896]{3,2,1,0:T(8,128)(2,1)}), bf16[8,3,32,896]{3,2,1,0:T(8,128)(2,1)}, u32[]{:S(2)}, u32[]{:S(2)}) async-start(bf16[8,3,32,896]{3,2,1,0:T(8,128)(2,1)} %pack.1), calls=%async_computation.1 | async-start | bytes 2752512 | tf_op jit(solution)/shard_map/all_to_all | solution.py:427
  60.5 0.0 copy-done.7
  60.5 0.0 copy-done.6
  60.5 1.0 pad_maximum_fusion
  61.4 2.0 %collective-permute-start.8 = (bf16[256,640]{1,0:T(8,128)(2,1)S(1)}, bf16[256,640]{1,0:T(8,128)(2,1)S(1)}, u32[]{:S(2)}, u32[]{:S(2)}) collective-permute-start(bf16[256,640]{1,0:T(8,128)(2,1)S(1)} %pad_maximum_fusion), channel_id=1, source_target_pairs={{0,1},{1,0},{2,3},{3,2},{4,5},{5,4},{6,7},{7,6},{8,9},{9,8},{10,11... | collective-permute-start | bytes 983048 | tf_op jit(solution)/shard_map/ppermute | solution.py:305
  63.4 1.8 %constant_dynamic-slice_fusion.1.down_ref = bf16[1,1,896,256]{3,2,1,0:T(8,128)(2,1)} fusion(bf16[1,2,7168,256]{3,2,1,0:T(8,128)(2,1)} %w_ref.9, s32[]{:T(128)S(6)} %select_n.4), kind=kLoop, calls=%fused_computation.3 | loop fusion | bytes 917508 | tf_op jit(solution)/shard_map/dynamic_slice | solution.py:417
  65.2 4.4 %latent_side.3 = (bf16[32,256]{1,0:T(8,128)(2,1)}, f32[32,256]{1,0:T(8,128)}, f32[32,128]{1,0:T(8,128)}) custom-call(bf16[32,7168]{1,0:T(8,128)(2,1)} %collective-permute-done.2.refs_2_.x_ref, bf16[1,2,7168,256]{3,2,1,0:T(8,128)(2,1)} %w_ref.9, bf16[1,7168]{1,0:T(2,128)(2,1)} %g_ref.7, bf16[1,256]{1,0:T(2,128)(2,1)} %h_ref.9), custom_call_target="tpu_custom_call" | custom-call | flops 1 | bytes 1 | tf_op jit(solution)/shard_map/latent_side/pallas_call | solution.py:222
  69.6 4.7 %second_step.1.rest_0_ = bf16[64,512]{1,0:T(8,128)(2,1)} custom-call(bf16[32,7168]{1,0:T(8,128)(2,1)} %collective-permute-done.3.y0_ref, bf16[32,7168]{1,0:T(8,128)(2,1)} %copy-done.5, bf16[1,2,7168,256]{3,2,1,0:T(8,128)(2,1)} %w_ref.9, bf16[1,256]{1,0:T(2,128)(2,1)} %h_ref.9, f32[32,256]{1,0:T(8,128)} %get-tuple-element.80.c0_ref, ...), custom_call_target="tpu_custom_call" | custom-call | flops 1 | bytes 1 | tf_op jit(solution)/shard_map/second_step/pallas_call | solution.py:284
  74.4 2.4 %collective-permute-start.10 = (bf16[64,512]{1,0:T(8,128)(2,1)}, bf16[64,512]{1,0:T(8,128)(2,1)S(1)}, u32[]{:S(2)}, u32[]{:S(2)}) collective-permute-start(bf16[64,512]{1,0:T(8,128)(2,1)} %second_step.1.rest_0_), channel_id=1, source_target_pairs={{0,4},{1,5},{2,6},{3,7},{4,0},{5,1},{6,2},{7,3},{8,12},{9,13},{10,... | collective-permute-start | bytes 196616 | tf_op jit(solution)/shard_map/ppermute | solution.py:305
  76.8 1.5 %collective-permute-start.11 = (bf16[64,512]{1,0:T(8,128)(2,1)}, bf16[64,512]{1,0:T(8,128)(2,1)S(1)}, u32[]{:S(2)}, u32[]{:S(2)}) collective-permute-start(bf16[64,512]{1,0:T(8,128)(2,1)} %second_step.1.rest_0_), channel_id=1, source_target_pairs={{0,2},{1,3},{2,0},{3,1},{4,6},{5,7},{6,4},{7,5},{8,10},{9,11},{10,... | collective-permute-start | bytes 196616 | tf_op jit(solution)/shard_map/ppermute | solution.py:305
  78.3 0.5 collective-permute-start.9
  78.8 1.3 %constant_dynamic-slice_fusion.g_ref = bf16[1,896]{1,0:T(2,128)(2,1)} fusion(bf16[1,7168]{1,0:T(2,128)(2,1)} %g_ref.7, s32[]{:T(128)S(6)} %select_n.4), kind=kLoop, calls=%fused_computation.2 | loop fusion | bytes 3588 | tf_op jit(solution)/shard_map/dynamic_slice | solution.py:418
  80.1 5.4 %collective-permute-done.8.rest_4_ = bf16[256,640]{1,0:T(8,128)(2,1)S(1)} collective-permute-done((bf16[256,640]{1,0:T(8,128)(2,1)S(1)}, bf16[256,640]{1,0:T(8,128)(2,1)S(1)}, u32[]{:S(2)}, u32[]{:S(2)}) %collective-permute-start.8) | collective-permute-done | bytes 327712 | tf_op jit(solution)/shard_map/ppermute | solution.py:305
  85.6 0.7 copy-done.8
  86.3 2.8 %columns_first.1 = (bf16[256,896]{1,0:T(8,128)(2,1)}, bf16[8,64,640]{2,1,0:T(8,128)(2,1)}) custom-call(s32[1]{0:T(128)} %bitcast.j_ref, bf16[8,3,32,896]{3,2,1,0:T(8,128)(2,1)} %copy-done, bf16[1,1,896,256]{3,2,1,0:T(8,128)(2,1)} %constant_dynamic-slice_fusion.1.down_ref, bf16[1,896]{1,0:T(2,128)(2,1)} %constant_dynamic-slice_fusion.g_ref, ...), custom_call_target="tpu_custom_call" | custom-call | flops 1 | bytes 1 | tf_op jit(solution)/shard_map/columns_first/pallas_call | solution.py:346
  89.1 1.3 %collective-permute-start.12 = (bf16[256,896]{1,0:T(8,128)(2,1)}, bf16[256,896]{1,0:T(8,128)(2,1)S(1)}, u32[]{:S(2)}, u32[]{:S(2)}) collective-permute-start(bf16[256,896]{1,0:T(8,128)(2,1)} %get-tuple-element.88), channel_id=1, source_target_pairs={{8,0},{16,8},{24,16},{9,1},{17,9},{25,17},{10,2},{18,10},{26,18},{... | collective-permute-start | bytes 1376264 | tf_op jit(solution)/shard_map/ppermute | solution.py:424
  90.4 8.4 %collective-permute-done.10.rest_2_ = bf16[64,512]{1,0:T(8,128)(2,1)S(1)} collective-permute-done((bf16[64,512]{1,0:T(8,128)(2,1)}, bf16[64,512]{1,0:T(8,128)(2,1)S(1)}, u32[]{:S(2)}, u32[]{:S(2)}) %collective-permute-start.10) | collective-permute-done | bytes 65568 | tf_op jit(solution)/shard_map/ppermute | solution.py:305
  98.8 0.0 collective-permute-done.11.rest_3_
  98.8 0.0 collective-permute-done.9.rest_1_
  98.8 0.0 copy-start.11
  98.8 0.0 all-to-all-done.1.u_ref
  98.8 0.0 copy-start.2
  98.8 2.9 %columns_next.1 = bf16[256,896]{1,0:T(8,128)(2,1)} custom-call(bf16[8,3,32,896]{3,2,1,0:T(8,128)(2,1)} %all-to-all-done.1.u_ref, bf16[1,1,896,256]{3,2,1,0:T(8,128)(2,1)} %constant_dynamic-slice_fusion.1.down_ref, bf16[1,896]{1,0:T(2,128)(2,1)} %constant_dynamic-slice_fusion.g_ref, bf16[8,64,640]{2,1,0:T(8,128)(2,1)} %get-tuple-element.89.narrow_ref.first_ref), custom_call_target="tpu_custom_call" | custom-call | flops 1 | bytes 1 | tf_op jit(solution)/shard_map/columns_next/pallas_call | solution.py:360
  101.7 1.3 %collective-permute-start.13 = (bf16[256,896]{1,0:T(8,128)(2,1)}, bf16[256,896]{1,0:T(8,128)(2,1)S(1)}, u32[]{:S(2)}, u32[]{:S(2)}) collective-permute-start(bf16[256,896]{1,0:T(8,128)(2,1)} %columns_next.1), channel_id=1, source_target_pairs={{8,0},{16,8},{24,16},{9,1},{17,9},{25,17},{10,2},{18,10},{26,18},{... | collective-permute-start | bytes 1376264 | tf_op jit(solution)/shard_map/ppermute | solution.py:424
  103.0 0.0 copy-done.9
  103.0 0.0 copy-done.10
  103.0 0.0 copy-done.11
  103.0 1.6 %collective-permute-start.14 = (bf16[256,512]{1,0:T(8,128)(2,1)S(1)}, bf16[256,512]{1,0:T(8,128)(2,1)S(1)}, u32[]{:S(2)}, u32[]{:S(2)}) collective-permute-start(bf16[256,512]{1,0:T(8,128)(2,1)S(1)} %pad_maximum_fusion.1), channel_id=1, source_target_pairs={{0,1},{1,0},{2,3},{3,2},{4,5},{5,4},{6,7},{7,6},{8,9},{9,8},{10,11... | collective-permute-start | bytes 786440 | tf_op jit(solution)/shard_map/ppermute | solution.py:305
  104.6 0.7 fusion
  105.3 0.9 copy.7.g_ref
  106.2 5.9 %collective-permute-done.14.rest_4_ = bf16[256,512]{1,0:T(8,128)(2,1)S(1)} collective-permute-done((bf16[256,512]{1,0:T(8,128)(2,1)S(1)}, bf16[256,512]{1,0:T(8,128)(2,1)S(1)}, u32[]{:S(2)}, u32[]{:S(2)}) %collective-permute-start.14) | collective-permute-done | bytes 262176 | tf_op jit(solution)/shard_map/ppermute | solution.py:305
  112.1 0.0 collective-permute-done.12.y1d_ref
  112.1 0.0 collective-permute-done.13.y1u_ref
  112.1 0.7 copy-done.12
  112.8 0.2 copy-done.3
  113.0 0.8 copy-done.4
  113.8 4.6 %terms.1 = bf16[1,2,896,256]{3,2,1,0:T(8,128)(2,1)} custom-call(s32[1]{0:T(128)} %bitcast.j_ref, bf16[8,3,32,896]{3,2,1,0:T(8,128)(2,1)} %copy-done, bf16[8,3,32,896]{3,2,1,0:T(8,128)(2,1)} %all-to-all-done.1.u_ref, bf16[256,896]{1,0:T(8,128)(2,1)} %copy-done.3, bf16[256,896]{1,0:T(8,128)(2,1)} %copy-done.4, ...), custom_call_target="tpu_custom_call" | custom-call | flops 1 | bytes 1 | tf_op jit(solution)/shard_map/terms/pallas_call | solution.py:400
  (12 shorter events, 0.0 us)
Async XLA Ops:
  3.6 51.3 %all-to-all-start = ((bf16[8,3,32,896]{3,2,1,0:T(8,128)(2,1)}), bf16[8,3,32,896]{3,2,1,0:T(8,128)(2,1)S(1)}, u32[]{:S(2)}, u32[]{:S(2)}) async-start(bf16[8,3,32,896]{3,2,1,0:T(8,128)(2,1)} %get-tuple-element.70), calls=%async_computation | async-start | bytes 2752512 | tf_op jit(solution)/shard_map/all_to_all | solution.py:427
  10.9 14.0 %collective-permute-start = (bf16[32,7168]{1,0:T(8,128)(2,1)}, bf16[32,7168]{1,0:T(8,128)(2,1)S(1)}, u32[]{:S(2)}, u32[]{:S(2)}) collective-permute-start(bf16[32,7168]{1,0:T(8,128)(2,1)} %get-tuple-element.53), channel_id=1, source_target_pairs={{0,24},{8,16},{16,8},{24,0},{1,25},{9,17},{17,9},{25,1},{2,26},{10... | collective-permute-start | bytes 1376264 | tf_op jit(solution)/shard_map/ppermute | solution.py:421
  11.6 22.2 %collective-permute-start.1 = (bf16[32,7168]{1,0:T(8,128)(2,1)}, bf16[32,7168]{1,0:T(8,128)(2,1)}, u32[]{:S(2)}, u32[]{:S(2)}) collective-permute-start(bf16[32,7168]{1,0:T(8,128)(2,1)} %get-tuple-element.58), channel_id=1, source_target_pairs={{0,24},{8,16},{16,8},{24,0},{1,25},{9,17},{17,9},{25,1},{2,26},{10... | collective-permute-start | bytes 1376264 | tf_op jit(solution)/shard_map/ppermute | solution.py:421
  20.6 20.8 %collective-permute-start.3 = (bf16[32,7168]{1,0:T(8,128)(2,1)}, bf16[32,7168]{1,0:T(8,128)(2,1)}, u32[]{:S(2)}, u32[]{:S(2)}) collective-permute-start(bf16[32,7168]{1,0:T(8,128)(2,1)} %get-tuple-element.68), channel_id=1, source_target_pairs={{8,0},{16,8},{24,16},{9,1},{17,9},{25,17},{10,2},{18,10},{26,18},{... | collective-permute-start | bytes 1376264 | tf_op jit(solution)/shard_map/ppermute | solution.py:424
  21.9 25.3 %collective-permute-start.2 = (bf16[32,7168]{1,0:T(8,128)(2,1)}, bf16[32,7168]{1,0:T(8,128)(2,1)}, u32[]{:S(2)}, u32[]{:S(2)}) collective-permute-start(bf16[32,7168]{1,0:T(8,128)(2,1)} %get-tuple-element.61), channel_id=1, source_target_pairs={{0,24},{8,16},{16,8},{24,0},{1,25},{9,17},{17,9},{25,1},{2,26},{10... | collective-permute-start | bytes 1376264 | tf_op jit(solution)/shard_map/ppermute | solution.py:421
  24.9 0.8 copy-start.1
  41.3 13.6 %collective-permute-start.4 = (bf16[32,7168]{1,0:T(8,128)(2,1)}, bf16[32,7168]{1,0:T(8,128)(2,1)S(1)}, u32[]{:S(2)}, u32[]{:S(2)}) collective-permute-start(bf16[32,7168]{1,0:T(8,128)(2,1)} %get-tuple-element.69), channel_id=1, source_target_pairs={{8,0},{16,8},{24,16},{9,1},{17,9},{25,17},{10,2},{18,10},{26,18},{... | collective-permute-start | bytes 1376264 | tf_op jit(solution)/shard_map/ppermute | solution.py:424
  42.6 7.0 %collective-permute-start.5 = (bf16[64,640]{1,0:T(8,128)(2,1)}, bf16[64,640]{1,0:T(8,128)(2,1)S(1)}, u32[]{:S(2)}, u32[]{:S(2)}) collective-permute-start(bf16[64,640]{1,0:T(8,128)(2,1)} %get-tuple-element.71.rest_0_), channel_id=1, source_target_pairs={{0,6},{1,7},{2,4},{3,5},{4,2},{5,3},{6,0},{7,1},{8,14},{9,15},{10,... | collective-permute-start | bytes 245768 | tf_op jit(solution)/shard_map/ppermute | solution.py:305
  46.5 8.4 %collective-permute-start.6 = (bf16[64,640]{1,0:T(8,128)(2,1)}, bf16[64,640]{1,0:T(8,128)(2,1)}, u32[]{:S(2)}, u32[]{:S(2)}) collective-permute-start(bf16[64,640]{1,0:T(8,128)(2,1)} %get-tuple-element.71.rest_0_), channel_id=1, source_target_pairs={{0,4},{1,5},{2,6},{3,7},{4,0},{5,1},{6,2},{7,3},{8,12},{9,13},{10,... | collective-permute-start | bytes 245768 | tf_op jit(solution)/shard_map/ppermute | solution.py:305
  46.5 8.4 %collective-permute-start.7 = (bf16[64,640]{1,0:T(8,128)(2,1)}, bf16[64,640]{1,0:T(8,128)(2,1)}, u32[]{:S(2)}, u32[]{:S(2)}) collective-permute-start(bf16[64,640]{1,0:T(8,128)(2,1)} %get-tuple-element.71.rest_0_), channel_id=1, source_target_pairs={{0,2},{1,3},{2,0},{3,1},{4,6},{5,7},{6,4},{7,5},{8,10},{9,11},{10,... | collective-permute-start | bytes 245768 | tf_op jit(solution)/shard_map/ppermute | solution.py:305
  49.7 10.8 %copy-start.6 = (bf16[64,640]{1,0:T(8,128)(2,1)S(1)}, bf16[64,640]{1,0:T(8,128)(2,1)}, u32[]{:S(2)}) copy-start(bf16[64,640]{1,0:T(8,128)(2,1)} %get-tuple-element.71.rest_0_) | copy-start | bytes 245764
  49.7 10.8 %copy-start.7 = (bf16[64,640]{1,0:T(8,128)(2,1)}, bf16[64,640]{1,0:T(8,128)(2,1)S(1)}, u32[]{:S(2)}) copy-start(bf16[64,640]{1,0:T(8,128)(2,1)S(1)} %collective-permute-done.5.rest_1_) | copy-start | bytes 245764
  54.9 0.8 copy-start.5
  54.9 1.2 %copy-start = (bf16[8,3,32,896]{3,2,1,0:T(8,128)(2,1)}, bf16[8,3,32,896]{3,2,1,0:T(8,128)(2,1)S(1)}, u32[]{:S(2)}) copy-start(bf16[8,3,32,896]{3,2,1,0:T(8,128)(2,1)S(1)} %all-to-all-done.d_ref) | copy-start | bytes 4128772
  56.2 42.6 %all-to-all-start.1 = ((bf16[8,3,32,896]{3,2,1,0:T(8,128)(2,1)}), bf16[8,3,32,896]{3,2,1,0:T(8,128)(2,1)}, u32[]{:S(2)}, u32[]{:S(2)}) async-start(bf16[8,3,32,896]{3,2,1,0:T(8,128)(2,1)} %pack.1), calls=%async_computation.1 | async-start | bytes 2752512 | tf_op jit(solution)/shard_map/all_to_all | solution.py:427
  61.4 24.1 %collective-permute-start.8 = (bf16[256,640]{1,0:T(8,128)(2,1)S(1)}, bf16[256,640]{1,0:T(8,128)(2,1)S(1)}, u32[]{:S(2)}, u32[]{:S(2)}) collective-permute-start(bf16[256,640]{1,0:T(8,128)(2,1)S(1)} %pad_maximum_fusion), channel_id=1, source_target_pairs={{0,1},{1,0},{2,3},{3,2},{4,5},{5,4},{6,7},{7,6},{8,9},{9,8},{10,11... | collective-permute-start | bytes 983048 | tf_op jit(solution)/shard_map/ppermute | solution.py:305
  74.4 24.4 %collective-permute-start.10 = (bf16[64,512]{1,0:T(8,128)(2,1)}, bf16[64,512]{1,0:T(8,128)(2,1)S(1)}, u32[]{:S(2)}, u32[]{:S(2)}) collective-permute-start(bf16[64,512]{1,0:T(8,128)(2,1)} %second_step.1.rest_0_), channel_id=1, source_target_pairs={{0,4},{1,5},{2,6},{3,7},{4,0},{5,1},{6,2},{7,3},{8,12},{9,13},{10,... | collective-permute-start | bytes 196616 | tf_op jit(solution)/shard_map/ppermute | solution.py:305
  76.8 22.0 %collective-permute-start.11 = (bf16[64,512]{1,0:T(8,128)(2,1)}, bf16[64,512]{1,0:T(8,128)(2,1)S(1)}, u32[]{:S(2)}, u32[]{:S(2)}) collective-permute-start(bf16[64,512]{1,0:T(8,128)(2,1)} %second_step.1.rest_0_), channel_id=1, source_target_pairs={{0,2},{1,3},{2,0},{3,1},{4,6},{5,7},{6,4},{7,5},{8,10},{9,11},{10,... | collective-permute-start | bytes 196616 | tf_op jit(solution)/shard_map/ppermute | solution.py:305
  78.3 20.5 %collective-permute-start.9 = (bf16[64,512]{1,0:T(8,128)(2,1)}, bf16[64,512]{1,0:T(8,128)(2,1)S(1)}, u32[]{:S(2)}, u32[]{:S(2)}) collective-permute-start(bf16[64,512]{1,0:T(8,128)(2,1)} %second_step.1.rest_0_), channel_id=1, source_target_pairs={{0,6},{1,7},{2,4},{3,5},{4,2},{5,3},{6,0},{7,1},{8,14},{9,15},{10,... | collective-permute-start | bytes 196616 | tf_op jit(solution)/shard_map/ppermute | solution.py:305
  85.5 0.7 copy-start.8
  89.1 23.0 %collective-permute-start.12 = (bf16[256,896]{1,0:T(8,128)(2,1)}, bf16[256,896]{1,0:T(8,128)(2,1)S(1)}, u32[]{:S(2)}, u32[]{:S(2)}) collective-permute-start(bf16[256,896]{1,0:T(8,128)(2,1)} %get-tuple-element.88), channel_id=1, source_target_pairs={{8,0},{16,8},{24,16},{9,1},{17,9},{25,17},{10,2},{18,10},{26,18},{... | collective-permute-start | bytes 1376264 | tf_op jit(solution)/shard_map/ppermute | solution.py:424
  98.8 4.2 %copy-start.9 = (bf16[64,512]{1,0:T(8,128)(2,1)}, bf16[64,512]{1,0:T(8,128)(2,1)S(1)}, u32[]{:S(2)}) copy-start(bf16[64,512]{1,0:T(8,128)(2,1)S(1)} %collective-permute-done.10.rest_2_) | copy-start | bytes 196612
  98.8 4.2 %copy-start.10 = (bf16[64,512]{1,0:T(8,128)(2,1)}, bf16[64,512]{1,0:T(8,128)(2,1)S(1)}, u32[]{:S(2)}) copy-start(bf16[64,512]{1,0:T(8,128)(2,1)S(1)} %collective-permute-done.11.rest_3_) | copy-start | bytes 196612
  98.8 4.2 %copy-start.11 = (bf16[64,512]{1,0:T(8,128)(2,1)}, bf16[64,512]{1,0:T(8,128)(2,1)S(1)}, u32[]{:S(2)}) copy-start(bf16[64,512]{1,0:T(8,128)(2,1)S(1)} %collective-permute-done.9.rest_1_) | copy-start | bytes 196612
  98.8 4.2 %copy-start.2 = (bf16[64,512]{1,0:T(8,128)(2,1)S(1)}, bf16[64,512]{1,0:T(8,128)(2,1)}, u32[]{:S(2)}) copy-start(bf16[64,512]{1,0:T(8,128)(2,1)} %second_step.1.rest_0_) | copy-start | bytes 196612
  101.7 10.5 %collective-permute-start.13 = (bf16[256,896]{1,0:T(8,128)(2,1)}, bf16[256,896]{1,0:T(8,128)(2,1)S(1)}, u32[]{:S(2)}, u32[]{:S(2)}) collective-permute-start(bf16[256,896]{1,0:T(8,128)(2,1)} %columns_next.1), channel_id=1, source_target_pairs={{8,0},{16,8},{24,16},{9,1},{17,9},{25,17},{10,2},{18,10},{26,18},{... | collective-permute-start | bytes 1376264 | tf_op jit(solution)/shard_map/ppermute | solution.py:424
  103.0 9.1 %collective-permute-start.14 = (bf16[256,512]{1,0:T(8,128)(2,1)S(1)}, bf16[256,512]{1,0:T(8,128)(2,1)S(1)}, u32[]{:S(2)}, u32[]{:S(2)}) collective-permute-start(bf16[256,512]{1,0:T(8,128)(2,1)S(1)} %pad_maximum_fusion.1), channel_id=1, source_target_pairs={{0,1},{1,0},{2,3},{3,2},{4,5},{5,4},{6,7},{7,6},{8,9},{9,8},{10,11... | collective-permute-start | bytes 786440 | tf_op jit(solution)/shard_map/ppermute | solution.py:305
  112.1 0.7 copy-start.12
  112.1 0.8 copy-start.3
  113.0 0.8 copy-start.4

commit v5 on v4

--- a/solution.py
+++ b/solution.py
@@ -13,6 +13,7 @@
 VMEM = pl.BlockSpec(memory_space=pltpu.VMEM)
 SMEM = pl.BlockSpec(memory_space=pltpu.SMEM)
 LIMIT = 62 * 1024 * 1024
+LATE = 32 * 1024 * 1024
 COST = pl.CostEstimate(flops=1, bytes_accessed=1, transcendentals=0)
 F32 = jnp.float32
 BF16 = jnp.bfloat16
@@ -231,19 +232,42 @@
     )(x, weights, g, h)
 
 
-def gradient_kernel(x_ref, y_ref, w_ref, g_ref, h_ref, k_ref, c_ref, ab_ref, before_ref, z_ref, narrow_ref, down, up, sem0, sem1):
-    copies1 = load_chunks(w_ref.at[0, 1], up, sem1)
-    copies0 = load_chunks(w_ref.at[0, 0], down, sem0)
-    rows, width = x_ref.shape
+def narrow_kernel(y_ref, w_ref, h_ref, k_ref, c_ref, ab_ref, before_ref, narrow_ref, up, sem):
+    copies = load_chunks(w_ref.at[0, 1], up, sem)
+    rows, width = y_ref.shape
     lat = h_ref.shape[1]
-    chunk = width // CHUNKS
     c, a, b = c_ref[...], ab_ref[:, 0:1], ab_ref[:, 1:2]
     narrow_ref[:rows] = before_ref[...]
     narrow_ref[rows:, lat + LANES :] = k_ref[...]
-    aq = latent_gradient(chunked_dot(y_ref[...], copies1, up) * h_ref[...].astype(F32), c, a, b)
+    aq = latent_gradient(chunked_dot(y_ref[...], copies, up) * h_ref[...].astype(F32), c, a, b)
     s = a * jnp.sum(aq.astype(F32) * c, axis=-1, keepdims=True) / width
     narrow_ref[rows:, : lat + LANES] = with_scalar(aq, s)
-    for i, copy in enumerate(copies0):
+
+
+def narrow_step(y, weights, h, k, c, ab, before):
+    rows, width = y.shape
+    lat = h.shape[1]
+    return pl.pallas_call(
+        narrow_kernel,
+        out_shape=shape(2 * rows, 2 * lat + LANES),
+        in_specs=[VMEM, ANY] + [VMEM] * 5,
+        out_specs=VMEM,
+        scratch_shapes=[pltpu.VMEM((width, lat), BF16), pltpu.SemaphoreType.DMA((CHUNKS,))],
+        compiler_params=pltpu.CompilerParams(vmem_limit_bytes=LIMIT),
+        cost_estimate=COST,
+        name="narrow_step",
+    )(y, weights, h, k, c, ab, before)
+
+
+def input_kernel(x_ref, y_ref, w_ref, g_ref, narrow_ref, z_ref, packed_ref, down, sem):
+    copies = load_chunks(w_ref.at[0, 0], down, sem)
+    rows, width = x_ref.shape
+    lat = down.shape[1]
+    chunk = width // CHUNKS
+    pack_into(packed_ref, [x_ref, y_ref])
+    aq = narrow_ref[rows:, :lat]
+    s = narrow_ref[rows:, lat : lat + 1].astype(F32) + narrow_ref[rows:, lat + 1 : lat + 2].astype(F32)
+    for i, copy in enumerate(copies):
         copy.wait()
         cols = slice(i * chunk, (i + 1) * chunk)
         m = dot_t(aq, down[cols, :])
@@ -251,46 +275,52 @@
         z_ref[:, cols] = z.astype(BF16)
 
 
-def gradient_step(x, y, weights, g, h, k, c, ab, before):
+def input_step(x, y, weights, g, narrow, parts):
+    rows, width = x.shape
+    lat = weights.shape[3]
+    return pl.pallas_call(
+        input_kernel,
+        out_shape=[shape(rows, width), shape(parts, 2, rows, width // parts)],
+        in_specs=[VMEM] * 2 + [ANY] + [VMEM] * 2,
+        out_specs=[VMEM] * 2,
+        scratch_shapes=[pltpu.VMEM((width, lat), BF16), pltpu.SemaphoreType.DMA((CHUNKS,))],
+        compiler_params=pltpu.CompilerParams(vmem_limit_bytes=LIMIT),
+        cost_estimate=COST,
+        name="input_step",
+    )(x, y, weights, g, narrow)
+
+
+def second_kernel(x_ref, y0_ref, y1_ref, w_ref, g_ref, h_ref, c0_ref, ab0_ref, k0_ref, out_ref, packed_ref, down, up, sem0, sem1):
+    copies0 = load_chunks(w_ref.at[0, 0], down, sem0)
+    copies1 = load_chunks(w_ref.at[0, 1], up, sem1)
+    rows, width = x_ref.shape
+    lat = h_ref.shape[1]
+    pack_into(packed_ref, [x_ref])
+    h = h_ref[...].astype(F32)
+    x = x_ref[...].astype(F32)
+    a = norm_scale(x)
+    c = chunked_dot((x * a * g_ref[...].astype(F32)).astype(BF16), copies0, down)
+    b = norm_scale(c)
+    out_ref[:rows, lat:] = k0_ref[...]
+    out_ref[rows:, lat:] = (c * b * h).astype(BF16)
+    u = chunked_dot(jnp.concatenate([y0_ref[...], y1_ref[...]], 0), copies1, up) * h
+    out_ref[:rows, :lat] = latent_gradient(u[:rows], c0_ref[...], ab0_ref[:, 0:1], ab0_ref[:, 1:2])
+    out_ref[rows:, :lat] = latent_gradient(u[rows:], c, a, b)
+
+
+def second_step(x, y0, y1, weights, g, h, c0, ab0, k0, parts):
     rows, width = x.shape
     lat = h.shape[1]
     return pl.pallas_call(
-        gradient_kernel,
-        out_shape=[shape(rows, width), shape(2 * rows, 2 * lat + LANES)],
-        in_specs=[VMEM] * 2 + [ANY] + [VMEM] * 6,
+        second_kernel,
+        out_shape=[shape(2 * rows, 2 * lat), shape(parts, 1, rows, width // parts)],
+        in_specs=[VMEM] * 3 + [ANY] + [VMEM] * 5,
         out_specs=[VMEM] * 2,
         scratch_shapes=[pltpu.VMEM((width, lat), BF16)] * 2 + [pltpu.SemaphoreType.DMA((CHUNKS,))] * 2,
         compiler_params=pltpu.CompilerParams(vmem_limit_bytes=LIMIT),
         cost_estimate=COST,
-        name="gradient_step",
-    )(x, y, weights, g, h, k, c, ab, before)
-
-
-def second_kernel(y0_ref, y1_ref, w_ref, h_ref, c0_ref, c1_ref, ab0_ref, ab1_ref, k0_ref, k1_ref, out_ref, up, sem):
-    copies = load_chunks(w_ref.at[0, 1], up, sem)
-    rows, width = y0_ref.shape
-    lat = h_ref.shape[1]
-    out_ref[:rows, lat:] = k0_ref[...]
-    out_ref[rows:, lat:] = k1_ref[...]
-    y = jnp.concatenate([y0_ref[...], y1_ref[...]], 0)
-    u = chunked_dot(y, copies, up) * h_ref[...].astype(F32)
-    out_ref[:rows, :lat] = latent_gradient(u[:rows], c0_ref[...], ab0_ref[:, 0:1], ab0_ref[:, 1:2])
-    out_ref[rows:, :lat] = latent_gradient(u[rows:], c1_ref[...], ab1_ref[:, 0:1], ab1_ref[:, 1:2])
-
-
-def second_step(y0, y1, weights, h, c0, c1, ab0, ab1, k0, k1):
-    rows, width = y0.shape
-    lat = h.shape[1]
-    return pl.pallas_call(
-        second_kernel,
-        out_shape=shape(2 * rows, 2 * lat),
-        in_specs=[VMEM] * 2 + [ANY] + [VMEM] * 7,
-        out_specs=VMEM,
-        scratch_shapes=[pltpu.VMEM((width, lat), BF16), pltpu.SemaphoreType.DMA((CHUNKS,))],
-        compiler_params=pltpu.CompilerParams(vmem_limit_bytes=LIMIT),
-        cost_estimate=COST,
         name="second_step",
-    )(y0, y1, weights, h, c0, c1, ab0, ab1, k0, k1)
+    )(x, y0, y1, weights, g, h, c0, ab0, k0)
 
 
 def held_order(parts):
@@ -348,7 +378,7 @@
         out_shape=[shape(parts * rows, share), shape(parts, *pieces[0].shape)],
         in_specs=[SMEM] + [VMEM] * (3 + len(pieces)),
         out_specs=[VMEM, VMEM],
-        compiler_params=pltpu.CompilerParams(vmem_limit_bytes=LIMIT),
+        compiler_params=pltpu.CompilerParams(vmem_limit_bytes=LATE),
         cost_estimate=COST,
         name="columns_first",
     )(j, d, down, g, *pieces)
@@ -362,51 +392,66 @@
         out_shape=shape(parts * rows, share),
         in_specs=[VMEM] * 4,
         out_specs=VMEM,
-        compiler_params=pltpu.CompilerParams(vmem_limit_bytes=LIMIT),
+        compiler_params=pltpu.CompilerParams(vmem_limit_bytes=LATE),
         cost_estimate=COST,
         name="columns_next",
     )(u, down, g, narrow)
 
 
-def terms_kernel(j_ref, d_ref, u_ref, y1d_ref, y1u_ref, first_ref, g_ref, *rest):
+def first_terms_kernel(d_ref, u_ref, first_ref, out_ref):
+    parts, three, rows, share = d_ref.shape
+    lat = out_ref.shape[2]
+    total = parts * rows
+    for at, start in ((0, 0), (1, lat + LANES)):
+        down = first_ref[:, :rows, start : start + lat].reshape(total, lat)
+        up = first_ref[:, rows:, start : start + lat].reshape(total, lat)
+        out_ref[at] = rows_dot(d_ref[:, at].reshape(total, share), down) + rows_dot(u_ref[:, at].reshape(total, share), up)
+
+
+def first_terms(d, u, first, lat):
+    share = d.shape[3]
+    return pl.pallas_call(
+        first_terms_kernel,
+        out_shape=shape(2, share, lat, dtype=F32),
+        in_specs=[VMEM] * 3,
+        out_specs=VMEM,
+        compiler_params=pltpu.CompilerParams(vmem_limit_bytes=LATE),
+        cost_estimate=COST,
+        name="first_terms",
+    )(d, u, first)
+
+
+def terms_kernel(j_ref, d_ref, x1_ref, y1d_ref, y1u_ref, part_ref, g_ref, *rest):
     pieces, out_ref, second_ref = rest[:-2], rest[-2], rest[-1]
-    parts, two, rows, share = d_ref.shape
+    parts, three, rows, share = d_ref.shape
     lat = second_ref.shape[2] // 2
     total = parts * rows
     restore(j_ref[0], pieces, second_ref)
 
-    def half(ref, i, start):
-        return ref[:, i * rows : (i + 1) * rows, start : start + lat].reshape(total, lat)
-
-    def wide(ref, i):
-        return ref[:, i].reshape(total, share)
-
-    first = rows_dot(wide(d_ref, 0), half(first_ref, 0, 0))
-    first += rows_dot(wide(u_ref, 0), half(first_ref, 1, 0))
-    first += rows_dot(wide(d_ref, 2), half(second_ref, 0, 0))
-    first += rows_dot(wide(u_ref, 2), half(second_ref, 1, 0))
+    def half(i, start):
+        return second_ref[:, i * rows : (i + 1) * rows, start : start + lat].reshape(total, lat)
+
+    first = part_ref[0] + rows_dot(d_ref[:, 2].reshape(total, share), half(0, 0))
+    first += rows_dot(x1_ref[:, 0].reshape(total, share), half(1, 0))
     out_ref[0, 0] = (first * g_ref[...].astype(F32)).astype(BF16)
-    second = rows_dot(wide(d_ref, 1), half(first_ref, 0, lat + LANES))
-    second += rows_dot(wide(u_ref, 1), half(first_ref, 1, lat + LANES))
-    second += rows_dot(y1d_ref[...], half(second_ref, 0, lat))
-    second += rows_dot(y1u_ref[...], half(second_ref, 1, lat))
+    second = part_ref[1] + rows_dot(y1d_ref[...], half(0, lat))
+    second += rows_dot(y1u_ref[...], half(1, lat))
     out_ref[0, 1] = second.astype(BF16)
 
 
-def terms(j, d, u, y1d, y1u, first, g, pieces):
-    parts, two, rows, share = d.shape
+def terms(j, d, x1, y1d, y1u, part, g, pieces):
+    parts, three, rows, share = d.shape
     narrow = pieces[0].shape
-    lat = narrow[1] // 2
     return pl.pallas_call(
         terms_kernel,
-        out_shape=shape(1, 2, share, lat),
+        out_shape=shape(1, 2, share, narrow[1] // 2),
         in_specs=[SMEM] + [VMEM] * (6 + len(pieces)),
         out_specs=VMEM,
         scratch_shapes=[pltpu.VMEM((parts,) + narrow, BF16)],
-        compiler_params=pltpu.CompilerParams(vmem_limit_bytes=LIMIT),
+        compiler_params=pltpu.CompilerParams(vmem_limit_bytes=LATE),
         cost_estimate=COST,
         name="terms",
-    )(j, d, u, y1d, y1u, first, g, *pieces)
+    )(j, d, x1, y1d, y1u, part, g, *pieces)
 
 
 def per_device(weights, gain_model, gain_latent, saved_down, saved_up, grad_start):
@@ -432,25 +477,27 @@
     d_s = exchange(packed)
     z0d, before, k1d, c1d, ab1d = first_step(saved_down, grad_start, weights, gain_model, gain_latent)
     y1d = to_before(z0d)
-    x0u, before = lax.optimization_barrier((x0u, before))
+    column_g = own_g.reshape(share, 1)
+    x0u, before, own_down, own_g, column_g = lax.optimization_barrier((x0u, before, own_down, own_g, column_g))
     k0u, c0u, ab0u = latent_side(x0u, weights, gain_model, gain_latent)
-    y0u, c0u = lax.optimization_barrier((y0u, c0u))
-    z0u, narrow = gradient_step(x0u, y0u, weights, gain_model, gain_latent, k0u, c0u, ab0u, before)
-    z0u, narrow, y1d = lax.optimization_barrier((z0u, narrow, y1d))
-    y1u = to_before(z0u)
+    narrow = narrow_step(y0u, weights, gain_latent, k0u, c0u, ab0u, before)
+    narrow, y1d = lax.optimization_barrier((narrow, y1d))
     first_pieces = gather_pieces(narrow, "dp")
     far = len(first_pieces) - 1
-    u_packed = pack([x0u, y0u, x1u], replicas)
-    u_packed, y1u, x1u, d_s, *first_pieces[1:far] = lax.optimization_barrier((u_packed, y1u, x1u, d_s, *first_pieces[1:far]))
+    z0u, u_packed = input_step(x0u, y0u, weights, gain_model, narrow, replicas)
+    y1u = to_before(z0u)
+    u_packed, x1u, d_s, *first_pieces[1:far] = lax.optimization_barrier((u_packed, x1u, d_s, *first_pieces[1:far]))
     u_s = exchange(u_packed)
-    k1u, c1u, ab1u = latent_side(x1u, weights, gain_model, gain_latent)
-    second = second_step(y1d, y1u, weights, gain_latent, c1d, c1u, ab1d, ab1u, k1d, k1u)
+    second, x1_packed = second_step(x1u, y1d, y1u, weights, gain_model, gain_latent, c1d, ab1d, k1d, replicas)
     second_pieces = gather_pieces(second, "dp")
     z0d_s, first = columns_first(j[None], d_s, own_down, own_g, first_pieces)
     y1d_s = to_before(z0d_s)
-    u_s, first, *second_pieces[1:far] = lax.optimization_barrier((u_s, first, *second_pieces[1:far]))
-    y1u_s = to_before(columns_next(u_s, own_down, own_g, first))
-    return terms(j[None], d_s, u_s, y1d_s, y1u_s, first, own_g.reshape(share, 1), second_pieces)
+    u_s, first, x1_packed, *second_pieces[1:far] = lax.optimization_barrier((u_s, first, x1_packed, *second_pieces[1:far]))
+    x1_s = exchange(x1_packed)
+    z0u_s = columns_next(u_s, own_down, own_g, first)
+    y1u_s = to_before(z0u_s)
+    part = first_terms(d_s, u_s, first, gain_latent.shape[1])
+    return terms(j[None], d_s, x1_s, y1d_s, y1u_s, part, column_g, second_pieces)
 
 
 def solution(mesh):

time: 119 us -> 109 us (0.916)
  waiting for transfers between devices: 28.7 us -> 16.4 us
  starting transfers between devices: 34 us -> 41.2 us
  Pallas kernels: 45.4 us -> 40.6 us
  local copies, waits for them, and re-layouts: 9.02 us -> 6.14 us
  other arithmetic: 0.98 us -> 3.29 us
    ppermute x8, waiting for transfers between devices: 25 us -> 11.8 us  [across(): return lax.ppermute(held, axis, [(i, i ^ apart) for i in range(parts)])]
    all_to_all x2 -> x3, starting transfers between devices: 11.5 us -> 18.3 us  [exchange(): return lax.all_to_all(blocks, 'dp', 0, 0, tiled=True)]
    pallas_call x2 -> x1, Pallas kernels: 8.83 us -> 4.41 us  [latent_side(): pl.pallas_call(latent_kernel, out_shape=outs, in_specs=[VMEM, ANY, VMEM,...]
    ppermute x4, waiting for transfers between devices: 0.01 us -> 2.48 us  [to_before(): return lax.ppermute(block, 'pipe', [(i + 1, i) for i in range(ranks - 1)])]
    concatenate x2, other arithmetic: 0.98 us -> 3.29 us  [gather_pieces(): return pieces + [across(jnp.concatenate(pieces, 0), 1)]]
    ppermute x3, waiting for transfers between devices: 3.71 us -> 2.06 us  [mirror(): lax.ppermute(block, 'pipe', [(i, ranks - 1 - i) for i in range(ranks)])]
    pallas_call x4 -> x5, Pallas kernels: 19.3 us -> 20.9 us  [the longest x1 6.7 us: second_step(): pl.pallas_call(second_kernel, out_shape=[shape(2 * rows, 2 * lat), shape(...]
    pallas_call x1, Pallas kernels: 2.85 us -> 1.47 us  [columns_first(): pl.pallas_call(columns_first_kernel, out_shape=[shape(parts * rows, share...]
  transfers between devices with their start and end apart: 17 -> 18, of which waited for: 5 -> 7; matrix products, arithmetic and copies ran while one was open for 5% -> 5% of each run, Pallas kernels for 31% -> 32%
where the time goes in v5:
time: 109 us; the launch traced here: 108 us
  starting transfers between devices  41.2 us (38%)
  Pallas kernels  40.6 us (37%)
  waiting for transfers between devices  16.4 us (15%)
  local copies, waits for them, and re-layouts  6.14 us (6%)
  other arithmetic  3.29 us (3%)
    all_to_all x3, starting transfers between devices, exchange(): return lax.all_to_all(blocks, 'dp', 0, 0, tiled=True)  18.3 us
    ppermute x8, starting transfers between devices, across(): return lax.ppermute(held, axis, [(i, i ^ apart) for i in range(parts)])  13 us
    ppermute x8, waiting for transfers between devices, across(): return lax.ppermute(held, axis, [(i, i ^ apart) for i in range(parts)])  11.8 us
    pallas_call x1, Pallas kernels, first_step(): pl.pallas_call(functools.partial(first_kernel, before is None), out_shape...  7.89 us
    pallas_call x1, Pallas kernels, second_step(): pl.pallas_call(second_kernel, out_shape=[shape(2 * rows, 2 * lat), shape(...  6.7 us
    ppermute x4, starting transfers between devices, to_before(): return lax.ppermute(block, 'pipe', [(i + 1, i) for i in range(ranks - 1)])  5.14 us
    pallas_call x1, Pallas kernels, input_step(): pl.pallas_call(input_kernel, out_shape=[shape(rows, width), shape(parts,...  4.88 us
    ppermute x3, starting transfers between devices, mirror(): lax.ppermute(block, 'pipe', [(i, ranks - 1 - i) for i in range(ranks)])  4.77 us
  transfers between devices with their start and end apart: 18, of which 7 were waited for; matrix products, arithmetic and copies ran while one was open for 5% of the time, Pallas kernels for 32%

profile of v5, /device:TPU:0, one launch (start us, length us, event | category | flops | bytes accessed | tf_op | source)
XLA Modules:
  0.0 107.8 jit_solution(10111319280610293723)
XLA Ops:
  0.0 3.6 %prepare.1 = (bf16[8,3,32,896]{3,2,1,0:T(8,128)(2,1)}, bf16[32,7168]{1,0:T(8,128)(2,1)}, bf16[32,7168]{1,0:T(8,128)(2,1)}, bf16[32,7168]{1,0:T(8,128)(2,1)}) custom-call(bf16[1,2,32,7168]{3,2,1,0:T(8,128)(2,1)} %x_ref, bf16[1,2,32,7168]{3,2,1,0:T(8,128)(2,1)} %up_ref.1, bf16[2,1,32,7168]{3,2,1,0:T(8,128)(2,1)} %y_ref), custom_call_target="tpu_custom_call" | custom-call | flops 1 | bytes 1 | tf_op jit(solution)/shard_map/prepare/pallas_call | solution.py:94
  3.6 7.3 %all-to-all-start = ((bf16[8,3,32,896]{3,2,1,0:T(8,128)(2,1)}), bf16[8,3,32,896]{3,2,1,0:T(8,128)(2,1)S(1)}, u32[]{:S(2)}, u32[]{:S(2)}) async-start(bf16[8,3,32,896]{3,2,1,0:T(8,128)(2,1)} %get-tuple-element.66), calls=%async_computation | async-start | bytes 2752512 | tf_op jit(solution)/shard_map/all_to_all | solution.py:472
  10.9 0.7 collective-permute-start
  11.6 1.1 collective-permute-start.1
  12.6 7.9 %first_step.1 = (bf16[32,7168]{1,0:T(8,128)(2,1)}, bf16[32,640]{1,0:T(8,128)(2,1)}, bf16[32,256]{1,0:T(8,128)(2,1)}, f32[32,256]{1,0:T(8,128)}, f32[32,128]{1,0:T(8,128)}) custom-call(bf16[1,2,32,7168]{3,2,1,0:T(8,128)(2,1)} %x_ref, bf16[2,1,32,7168]{3,2,1,0:T(8,128)(2,1)} %y_ref, bf16[1,2,7168,256]{3,2,1,0:T(8,128)(2,1)} %w_ref.9, bf16[1,7168]{1,0:T(2,128)(2,1)} %g_ref.7, ...), custom_call_target="tpu_custom_call" | custom-call | flops 1 | bytes 1 | tf_op jit(solution)/shard_map/first_step/pallas_call | solution.py:199
  20.5 1.3 %collective-permute-start.2 = (bf16[32,7168]{1,0:T(8,128)(2,1)}, bf16[32,7168]{1,0:T(8,128)(2,1)}, u32[]{:S(2)}, u32[]{:S(2)}) collective-permute-start(bf16[32,7168]{1,0:T(8,128)(2,1)} %get-tuple-element.62), channel_id=1, source_target_pairs={{8,0},{16,8},{24,16},{9,1},{17,9},{25,17},{10,2},{18,10},{26,18},{... | collective-permute-start | bytes 1376264 | tf_op jit(solution)/shard_map/ppermute | solution.py:469
  21.8 3.0 %collective-permute-start.3 = (bf16[32,7168]{1,0:T(8,128)(2,1)}, bf16[32,7168]{1,0:T(8,128)(2,1)}, u32[]{:S(2)}, u32[]{:S(2)}) collective-permute-start(bf16[32,7168]{1,0:T(8,128)(2,1)} %get-tuple-element.65), channel_id=1, source_target_pairs={{0,24},{8,16},{16,8},{24,0},{1,25},{9,17},{17,9},{25,1},{2,26},{10... | collective-permute-start | bytes 1376264 | tf_op jit(solution)/shard_map/ppermute | solution.py:466
  24.9 0.7 constant_dynamic-slice_fusion.g_ref
  25.6 0.7 fusion
  26.2 1.0 constant_dynamic-slice_fusion.1.down_ref
  27.3 0.0 collective-permute-done.x_ref
  27.3 4.4 %latent_side.1 = (bf16[32,256]{1,0:T(8,128)(2,1)}, f32[32,256]{1,0:T(8,128)}, f32[32,128]{1,0:T(8,128)}) custom-call(bf16[32,7168]{1,0:T(8,128)(2,1)} %collective-permute-done.x_ref, bf16[1,2,7168,256]{3,2,1,0:T(8,128)(2,1)} %w_ref.9, bf16[1,7168]{1,0:T(2,128)(2,1)} %g_ref.7, bf16[1,256]{1,0:T(2,128)(2,1)} %h_ref.7), custom_call_target="tpu_custom_call" | custom-call | flops 1 | bytes 1 | tf_op jit(solution)/shard_map/latent_side/pallas_call | solution.py:223
  31.7 2.1 %collective-permute-done.1.y_ref = bf16[32,7168]{1,0:T(8,128)(2,1)} collective-permute-done((bf16[32,7168]{1,0:T(8,128)(2,1)}, bf16[32,7168]{1,0:T(8,128)(2,1)}, u32[]{:S(2)}, u32[]{:S(2)}) %collective-permute-start.1) | collective-permute-done | bytes 458784 | tf_op jit(solution)/shard_map/ppermute | solution.py:466
  33.8 4.6 %narrow_step.1.narrow_ref.rest_0_ = bf16[64,640]{1,0:T(8,128)(2,1)} custom-call(bf16[32,7168]{1,0:T(8,128)(2,1)} %collective-permute-done.1.y_ref, bf16[1,2,7168,256]{3,2,1,0:T(8,128)(2,1)} %w_ref.9, bf16[1,256]{1,0:T(2,128)(2,1)} %h_ref.7, bf16[32,256]{1,0:T(8,128)(2,1)} %get-tuple-element.58.k_ref, f32[32,256]{1,0:T(8,128)} %get-tuple-element.59.c_ref, ...), custom_call_target="tpu_custom_call" | custom-call | flops 1 | bytes 1 | tf_op jit(solution)/shard_map/narrow_step/pallas_call | solution.py:250
  38.4 0.0 collective-permute-done.2.y0_ref
  38.4 3.9 %collective-permute-start.4 = (bf16[64,640]{1,0:T(8,128)(2,1)}, bf16[64,640]{1,0:T(8,128)(2,1)S(1)}, u32[]{:S(2)}, u32[]{:S(2)}) collective-permute-start(bf16[64,640]{1,0:T(8,128)(2,1)} %narrow_step.1.narrow_ref.rest_0_), channel_id=1, source_target_pairs={{0,6},{1,7},{2,4},{3,5},{4,2},{5,3},{6,0},{7,1},{8,14},{9,15},{10,... | collective-permute-start | bytes 245768 | tf_op jit(solution)/shard_map/ppermute | solution.py:335
  42.3 0.0 collective-permute-start.5
  42.3 0.6 collective-permute-start.6
  43.0 4.9 %input_step.1 = (bf16[32,7168]{1,0:T(8,128)(2,1)}, bf16[8,2,32,896]{3,2,1,0:T(8,128)(2,1)}) custom-call(bf16[32,7168]{1,0:T(8,128)(2,1)} %collective-permute-done.x_ref, bf16[32,7168]{1,0:T(8,128)(2,1)} %collective-permute-done.1.y_ref, bf16[1,2,7168,256]{3,2,1,0:T(8,128)(2,1)} %w_ref.9, bf16[1,7168]{1,0:T(2,128)(2,1)} %g_ref.7, ...), custom_call_target="tpu_custom_call" | custom-call | flops 1 | bytes 1 | tf_op jit(solution)/shard_map/input_step/pallas_call | solution.py:281
  47.9 0.0 copy-start.5
  47.9 0.0 copy-start.2
  47.9 0.0 collective-permute-done.3.x_ref
  47.9 0.0 collective-permute-done.4.rest_1_
  47.9 0.1 collective-permute-done.5.rest_2_
  48.0 0.0 collective-permute-done.6.rest_3_
  48.0 0.0 all-to-all-done.d_ref
  48.0 6.0 %all-to-all-start.1 = ((bf16[8,2,32,896]{3,2,1,0:T(8,128)(2,1)}), bf16[8,2,32,896]{3,2,1,0:T(8,128)(2,1)}, u32[]{:S(2)}, u32[]{:S(2)}) async-start(bf16[8,2,32,896]{3,2,1,0:T(8,128)(2,1)} %get-tuple-element.68), calls=%async_computation.1 | async-start | bytes 1835008 | tf_op jit(solution)/shard_map/all_to_all | solution.py:472
  54.0 0.0 copy-done.5
  54.0 1.3 %collective-permute-start.8 = (bf16[32,7168]{1,0:T(8,128)(2,1)S(1)}, bf16[32,7168]{1,0:T(8,128)(2,1)}, u32[]{:S(2)}, u32[]{:S(2)}) collective-permute-start(bf16[32,7168]{1,0:T(8,128)(2,1)S(1)} %copy-done.5), channel_id=1, source_target_pairs={{8,0},{16,8},{24,16},{9,1},{17,9},{25,17},{10,2},{18,10},{26,18},{... | collective-permute-start | bytes 1376264 | tf_op jit(solution)/shard_map/ppermute | solution.py:469
  55.3 0.0 copy-done.2
  55.3 1.7 %pad_maximum_fusion = bf16[256,640]{1,0:T(8,128)(2,1)} fusion(bf16[64,640]{1,0:T(8,128)(2,1)} %collective-permute-done.6.rest_3_, bf16[64,640]{1,0:T(8,128)(2,1)} %collective-permute-done.5.rest_2_, bf16[64,640]{1,0:T(8,128)(2,1)S(1)} %collective-permute-done.4.rest_1_, bf16[64,640]{1,0:T(8,128)(2,1)S(1)} %copy-done.2), kind=kLoop, calls=%fused_computation | loop fusion | flops 1310720 | bytes 655360 | tf_op jit(solution)/shard_map/concatenate | solution.py:338
  57.0 2.0 %collective-permute-start.7 = (bf16[256,640]{1,0:T(8,128)(2,1)}, bf16[256,640]{1,0:T(8,128)(2,1)}, u32[]{:S(2)}, u32[]{:S(2)}) collective-permute-start(bf16[256,640]{1,0:T(8,128)(2,1)} %pad_maximum_fusion), channel_id=1, source_target_pairs={{0,1},{1,0},{2,3},{3,2},{4,5},{5,4},{6,7},{7,6},{8,9},{9,8},{10,11... | collective-permute-start | bytes 983048 | tf_op jit(solution)/shard_map/ppermute | solution.py:335
  59.0 2.5 %collective-permute-done.8.y1_ref = bf16[32,7168]{1,0:T(8,128)(2,1)} collective-permute-done((bf16[32,7168]{1,0:T(8,128)(2,1)S(1)}, bf16[32,7168]{1,0:T(8,128)(2,1)}, u32[]{:S(2)}, u32[]{:S(2)}) %collective-permute-start.8) | collective-permute-done | bytes 458784 | tf_op jit(solution)/shard_map/ppermute | solution.py:469
  61.5 6.7 %second_step.1 = (bf16[64,512]{1,0:T(8,128)(2,1)}, bf16[8,1,32,896]{3,2,1,0:T(8,128)(2,1)}) custom-call(bf16[32,7168]{1,0:T(8,128)(2,1)} %collective-permute-done.3.x_ref, bf16[32,7168]{1,0:T(8,128)(2,1)} %collective-permute-done.2.y0_ref, bf16[32,7168]{1,0:T(8,128)(2,1)} %collective-permute-done.8.y1_ref, bf16[1,2,7168,256]{3,2,1,0:T(8,128)(2,1)} %w_ref.9, ...), custom_call_target="tpu_custom_call" | custom-call | flops 1 | bytes 1 | tf_op jit(solution)/shard_map/second_step/pallas_call | solution.py:314
  68.2 3.6 %collective-permute-start.9 = (bf16[64,512]{1,0:T(8,128)(2,1)}, bf16[64,512]{1,0:T(8,128)(2,1)}, u32[]{:S(2)}, u32[]{:S(2)}) collective-permute-start(bf16[64,512]{1,0:T(8,128)(2,1)} %get-tuple-element.82.rest_0_), channel_id=1, source_target_pairs={{0,6},{1,7},{2,4},{3,5},{4,2},{5,3},{6,0},{7,1},{8,14},{9,15},{10,... | collective-permute-start | bytes 196616 | tf_op jit(solution)/shard_map/ppermute | solution.py:335
  71.8 0.0 collective-permute-start.10
  71.8 0.9 collective-permute-start.11
  72.6 0.3 collective-permute-done.7.rest_4_
  72.9 1.5 %columns_first.1 = (bf16[256,896]{1,0:T(8,128)(2,1)S(1)}, bf16[8,64,640]{2,1,0:T(8,128)(2,1)S(1)}) custom-call(s32[1]{0:T(128)} %bitcast.j_ref, bf16[8,3,32,896]{3,2,1,0:T(8,128)(2,1)S(1)} %all-to-all-done.d_ref, bf16[1,1,896,256]{3,2,1,0:T(8,128)(2,1)S(1)} %constant_dynamic-slice_fusion.1.down_ref, bf16[1,896]{1,0:T(2,128)(2,1)S(1)} %constant_dynamic-slice_fusion.g_ref, ...), custom_call_target="tpu_custom_call" | custom-call | flops 1 | bytes 1 | tf_op jit(solution)/shard_map/columns_first/pallas_call | solution.py:376
  74.4 0.0 copy-start.4
  74.4 0.8 copy-done.4
  75.1 0.0 copy-start.3
  75.1 0.3 collective-permute-done.9.rest_1_
  75.4 6.6 %collective-permute-done.10.rest_2_ = bf16[64,512]{1,0:T(8,128)(2,1)} collective-permute-done((bf16[64,512]{1,0:T(8,128)(2,1)}, bf16[64,512]{1,0:T(8,128)(2,1)}, u32[]{:S(2)}, u32[]{:S(2)}) %collective-permute-start.10) | collective-permute-done | bytes 65568 | tf_op jit(solution)/shard_map/ppermute | solution.py:335
  82.1 0.0 collective-permute-done.11.rest_3_
  82.1 0.0 all-to-all-done.1.u_ref
  82.1 5.0 %all-to-all-start.2 = ((bf16[8,1,32,896]{3,2,1,0:T(8,128)(2,1)}), bf16[8,1,32,896]{3,2,1,0:T(8,128)(2,1)S(1)}, u32[]{:S(2)}, u32[]{:S(2)}) async-start(bf16[8,1,32,896]{3,2,1,0:T(8,128)(2,1)} %get-tuple-element.83), calls=%async_computation.2 | async-start | bytes 917504 | tf_op jit(solution)/shard_map/all_to_all | solution.py:472
  87.1 1.3 %collective-permute-start.12 = (bf16[256,896]{1,0:T(8,128)(2,1)}, bf16[256,896]{1,0:T(8,128)(2,1)}, u32[]{:S(2)}, u32[]{:S(2)}) collective-permute-start(bf16[256,896]{1,0:T(8,128)(2,1)} %copy-done.4), channel_id=1, source_target_pairs={{8,0},{16,8},{24,16},{9,1},{17,9},{25,17},{10,2},{18,10},{26,18},{... | collective-permute-start | bytes 1376264 | tf_op jit(solution)/shard_map/ppermute | solution.py:469
  88.4 2.3 %columns_next.1 = bf16[256,896]{1,0:T(8,128)(2,1)} custom-call(bf16[8,2,32,896]{3,2,1,0:T(8,128)(2,1)} %all-to-all-done.1.u_ref, bf16[1,1,896,256]{3,2,1,0:T(8,128)(2,1)S(1)} %constant_dynamic-slice_fusion.1.down_ref, bf16[1,896]{1,0:T(2,128)(2,1)S(1)} %constant_dynamic-slice_fusion.g_ref, bf16[8,64,640]{2,1,0:T(8,128)(2,1)S(1)} %get-tuple-element.86.narrow_ref.first_ref), custom_call_target="tpu_custom_call" | custom-call | flops 1 | bytes 1 | tf_op jit(solution)/shard_map/columns_next/pallas_call | solution.py:390
  90.7 1.3 %collective-permute-start.13 = (bf16[256,896]{1,0:T(8,128)(2,1)}, bf16[256,896]{1,0:T(8,128)(2,1)S(1)}, u32[]{:S(2)}, u32[]{:S(2)}) collective-permute-start(bf16[256,896]{1,0:T(8,128)(2,1)} %columns_next.1), channel_id=1, source_target_pairs={{8,0},{16,8},{24,16},{9,1},{17,9},{25,17},{10,2},{18,10},{26,18},{... | collective-permute-start | bytes 1376264 | tf_op jit(solution)/shard_map/ppermute | solution.py:469
  92.0 0.0 copy-done.3
  92.0 1.6 %pad_maximum_fusion.1 = bf16[256,512]{1,0:T(8,128)(2,1)} fusion(bf16[64,512]{1,0:T(8,128)(2,1)} %collective-permute-done.11.rest_3_, bf16[64,512]{1,0:T(8,128)(2,1)} %collective-permute-done.10.rest_2_, bf16[64,512]{1,0:T(8,128)(2,1)} %collective-permute-done.9.rest_1_, bf16[64,512]{1,0:T(8,128)(2,1)S(1)} %copy-done.3), kind=kLoop, calls=%fused_computation.1 | loop fusion | flops 1048576 | bytes 524288 | tf_op jit(solution)/shard_map/concatenate | solution.py:338
  93.6 2.0 %collective-permute-start.14 = (bf16[256,512]{1,0:T(8,128)(2,1)}, bf16[256,512]{1,0:T(8,128)(2,1)S(1)}, u32[]{:S(2)}, u32[]{:S(2)}) collective-permute-start(bf16[256,512]{1,0:T(8,128)(2,1)} %pad_maximum_fusion.1), channel_id=1, source_target_pairs={{0,1},{1,0},{2,3},{3,2},{4,5},{5,4},{6,7},{7,6},{8,9},{9,8},{10,11... | collective-permute-start | bytes 786440 | tf_op jit(solution)/shard_map/ppermute | solution.py:335
  95.6 0.2 copy.7.g_ref
  95.8 1.9 %first_terms.1.part_ref = f32[2,896,256]{2,1,0:T(8,128)S(1)} custom-call(bf16[8,3,32,896]{3,2,1,0:T(8,128)(2,1)S(1)} %all-to-all-done.d_ref, bf16[8,2,32,896]{3,2,1,0:T(8,128)(2,1)} %all-to-all-done.1.u_ref, bf16[8,64,640]{2,1,0:T(8,128)(2,1)S(1)} %get-tuple-element.86.narrow_ref.first_ref), custom_call_target="tpu_custom_call" | custom-call | flops 1 | bytes 1 | tf_op jit(solution)/shard_map/first_terms/pallas_call | solution.py:413
  97.7 0.0 copy-start
  97.7 1.2 %copy-done = f32[2,896,256]{2,1,0:T(8,128)} copy-done((f32[2,896,256]{2,1,0:T(8,128)}, f32[2,896,256]{2,1,0:T(8,128)S(1)}, u32[]{:S(2)}) %copy-start) | copy-done | bytes 1835032
  99.0 4.5 %collective-permute-done.14.rest_4_ = bf16[256,512]{1,0:T(8,128)(2,1)S(1)} collective-permute-done((bf16[256,512]{1,0:T(8,128)(2,1)}, bf16[256,512]{1,0:T(8,128)(2,1)S(1)}, u32[]{:S(2)}, u32[]{:S(2)}) %collective-permute-start.14) | collective-permute-done | bytes 262176 | tf_op jit(solution)/shard_map/ppermute | solution.py:335
  103.5 0.0 collective-permute-done.12.y1d_ref
  103.5 0.0 collective-permute-done.13.y1u_ref
  103.5 0.0 all-to-all-done.2.x1_ref
  103.5 0.0 copy-start.1
  103.5 1.5 %copy-done.1 = f32[2,896,256]{2,1,0:T(8,128)S(1)} copy-done((f32[2,896,256]{2,1,0:T(8,128)S(1)}, f32[2,896,256]{2,1,0:T(8,128)}, u32[]{:S(2)}) %copy-start.1) | copy-done | bytes 1835032
  105.0 2.8 %terms.1 = bf16[1,2,896,256]{3,2,1,0:T(8,128)(2,1)} custom-call(s32[1]{0:T(128)} %bitcast.j_ref, bf16[8,3,32,896]{3,2,1,0:T(8,128)(2,1)S(1)} %all-to-all-done.d_ref, bf16[8,1,32,896]{3,2,1,0:T(8,128)(2,1)S(1)} %all-to-all-done.2.x1_ref, bf16[256,896]{1,0:T(8,128)(2,1)} %collective-permute-done.12.y1d_ref, ...), custom_call_target="tpu_custom_call" | custom-call | flops 1 | bytes 1 | tf_op jit(solution)/shard_map/terms/pallas_call | solution.py:445
Async XLA Ops:
  3.6 44.4 %all-to-all-start = ((bf16[8,3,32,896]{3,2,1,0:T(8,128)(2,1)}), bf16[8,3,32,896]{3,2,1,0:T(8,128)(2,1)S(1)}, u32[]{:S(2)}, u32[]{:S(2)}) async-start(bf16[8,3,32,896]{3,2,1,0:T(8,128)(2,1)} %get-tuple-element.66), calls=%async_computation | async-start | bytes 2752512 | tf_op jit(solution)/shard_map/all_to_all | solution.py:472
  10.9 16.4 %collective-permute-start = (bf16[32,7168]{1,0:T(8,128)(2,1)}, bf16[32,7168]{1,0:T(8,128)(2,1)}, u32[]{:S(2)}, u32[]{:S(2)}) collective-permute-start(bf16[32,7168]{1,0:T(8,128)(2,1)} %get-tuple-element.52), channel_id=1, source_target_pairs={{0,24},{8,16},{16,8},{24,0},{1,25},{9,17},{17,9},{25,1},{2,26},{10... | collective-permute-start | bytes 1376264 | tf_op jit(solution)/shard_map/ppermute | solution.py:466
  11.6 22.2 %collective-permute-start.1 = (bf16[32,7168]{1,0:T(8,128)(2,1)}, bf16[32,7168]{1,0:T(8,128)(2,1)}, u32[]{:S(2)}, u32[]{:S(2)}) collective-permute-start(bf16[32,7168]{1,0:T(8,128)(2,1)} %get-tuple-element.57), channel_id=1, source_target_pairs={{0,24},{8,16},{16,8},{24,0},{1,25},{9,17},{17,9},{25,1},{2,26},{10... | collective-permute-start | bytes 1376264 | tf_op jit(solution)/shard_map/ppermute | solution.py:466
  20.5 17.9 %collective-permute-start.2 = (bf16[32,7168]{1,0:T(8,128)(2,1)}, bf16[32,7168]{1,0:T(8,128)(2,1)}, u32[]{:S(2)}, u32[]{:S(2)}) collective-permute-start(bf16[32,7168]{1,0:T(8,128)(2,1)} %get-tuple-element.62), channel_id=1, source_target_pairs={{8,0},{16,8},{24,16},{9,1},{17,9},{25,17},{10,2},{18,10},{26,18},{... | collective-permute-start | bytes 1376264 | tf_op jit(solution)/shard_map/ppermute | solution.py:469
  21.8 26.0 %collective-permute-start.3 = (bf16[32,7168]{1,0:T(8,128)(2,1)}, bf16[32,7168]{1,0:T(8,128)(2,1)}, u32[]{:S(2)}, u32[]{:S(2)}) collective-permute-start(bf16[32,7168]{1,0:T(8,128)(2,1)} %get-tuple-element.65), channel_id=1, source_target_pairs={{0,24},{8,16},{16,8},{24,0},{1,25},{9,17},{17,9},{25,1},{2,26},{10... | collective-permute-start | bytes 1376264 | tf_op jit(solution)/shard_map/ppermute | solution.py:466
  38.4 9.5 %collective-permute-start.4 = (bf16[64,640]{1,0:T(8,128)(2,1)}, bf16[64,640]{1,0:T(8,128)(2,1)S(1)}, u32[]{:S(2)}, u32[]{:S(2)}) collective-permute-start(bf16[64,640]{1,0:T(8,128)(2,1)} %narrow_step.1.narrow_ref.rest_0_), channel_id=1, source_target_pairs={{0,6},{1,7},{2,4},{3,5},{4,2},{5,3},{6,0},{7,1},{8,14},{9,15},{10,... | collective-permute-start | bytes 245768 | tf_op jit(solution)/shard_map/ppermute | solution.py:335
  42.3 5.7 %collective-permute-start.5 = (bf16[64,640]{1,0:T(8,128)(2,1)}, bf16[64,640]{1,0:T(8,128)(2,1)}, u32[]{:S(2)}, u32[]{:S(2)}) collective-permute-start(bf16[64,640]{1,0:T(8,128)(2,1)} %narrow_step.1.narrow_ref.rest_0_), channel_id=1, source_target_pairs={{0,4},{1,5},{2,6},{3,7},{4,0},{5,1},{6,2},{7,3},{8,12},{9,13},{10,... | collective-permute-start | bytes 245768 | tf_op jit(solution)/shard_map/ppermute | solution.py:335
  42.3 5.7 %collective-permute-start.6 = (bf16[64,640]{1,0:T(8,128)(2,1)}, bf16[64,640]{1,0:T(8,128)(2,1)}, u32[]{:S(2)}, u32[]{:S(2)}) collective-permute-start(bf16[64,640]{1,0:T(8,128)(2,1)} %narrow_step.1.narrow_ref.rest_0_), channel_id=1, source_target_pairs={{0,2},{1,3},{2,0},{3,1},{4,6},{5,7},{6,4},{7,5},{8,10},{9,11},{10,... | collective-permute-start | bytes 245768 | tf_op jit(solution)/shard_map/ppermute | solution.py:335
  47.9 6.1 %copy-start.5 = (bf16[32,7168]{1,0:T(8,128)(2,1)S(1)}, bf16[32,7168]{1,0:T(8,128)(2,1)}, u32[]{:S(2)}) copy-start(bf16[32,7168]{1,0:T(8,128)(2,1)} %get-tuple-element.77) | copy-start | bytes 1376260
  47.9 7.4 %copy-start.2 = (bf16[64,640]{1,0:T(8,128)(2,1)S(1)}, bf16[64,640]{1,0:T(8,128)(2,1)}, u32[]{:S(2)}) copy-start(bf16[64,640]{1,0:T(8,128)(2,1)} %narrow_step.1.narrow_ref.rest_0_) | copy-start | bytes 245764
  48.0 34.1 %all-to-all-start.1 = ((bf16[8,2,32,896]{3,2,1,0:T(8,128)(2,1)}), bf16[8,2,32,896]{3,2,1,0:T(8,128)(2,1)}, u32[]{:S(2)}, u32[]{:S(2)}) async-start(bf16[8,2,32,896]{3,2,1,0:T(8,128)(2,1)} %get-tuple-element.68), calls=%async_computation.1 | async-start | bytes 1835008 | tf_op jit(solution)/shard_map/all_to_all | solution.py:472
  54.0 7.5 %collective-permute-start.8 = (bf16[32,7168]{1,0:T(8,128)(2,1)S(1)}, bf16[32,7168]{1,0:T(8,128)(2,1)}, u32[]{:S(2)}, u32[]{:S(2)}) collective-permute-start(bf16[32,7168]{1,0:T(8,128)(2,1)S(1)} %copy-done.5), channel_id=1, source_target_pairs={{8,0},{16,8},{24,16},{9,1},{17,9},{25,17},{10,2},{18,10},{26,18},{... | collective-permute-start | bytes 1376264 | tf_op jit(solution)/shard_map/ppermute | solution.py:469
  57.0 15.9 %collective-permute-start.7 = (bf16[256,640]{1,0:T(8,128)(2,1)}, bf16[256,640]{1,0:T(8,128)(2,1)}, u32[]{:S(2)}, u32[]{:S(2)}) collective-permute-start(bf16[256,640]{1,0:T(8,128)(2,1)} %pad_maximum_fusion), channel_id=1, source_target_pairs={{0,1},{1,0},{2,3},{3,2},{4,5},{5,4},{6,7},{7,6},{8,9},{9,8},{10,11... | collective-permute-start | bytes 983048 | tf_op jit(solution)/shard_map/ppermute | solution.py:335
  68.2 7.3 %collective-permute-start.9 = (bf16[64,512]{1,0:T(8,128)(2,1)}, bf16[64,512]{1,0:T(8,128)(2,1)}, u32[]{:S(2)}, u32[]{:S(2)}) collective-permute-start(bf16[64,512]{1,0:T(8,128)(2,1)} %get-tuple-element.82.rest_0_), channel_id=1, source_target_pairs={{0,6},{1,7},{2,4},{3,5},{4,2},{5,3},{6,0},{7,1},{8,14},{9,15},{10,... | collective-permute-start | bytes 196616 | tf_op jit(solution)/shard_map/ppermute | solution.py:335
  71.8 10.3 %collective-permute-start.10 = (bf16[64,512]{1,0:T(8,128)(2,1)}, bf16[64,512]{1,0:T(8,128)(2,1)}, u32[]{:S(2)}, u32[]{:S(2)}) collective-permute-start(bf16[64,512]{1,0:T(8,128)(2,1)} %get-tuple-element.82.rest_0_), channel_id=1, source_target_pairs={{0,4},{1,5},{2,6},{3,7},{4,0},{5,1},{6,2},{7,3},{8,12},{9,13},{10,... | collective-permute-start | bytes 196616 | tf_op jit(solution)/shard_map/ppermute | solution.py:335
  71.8 10.3 %collective-permute-start.11 = (bf16[64,512]{1,0:T(8,128)(2,1)}, bf16[64,512]{1,0:T(8,128)(2,1)}, u32[]{:S(2)}, u32[]{:S(2)}) collective-permute-start(bf16[64,512]{1,0:T(8,128)(2,1)} %get-tuple-element.82.rest_0_), channel_id=1, source_target_pairs={{0,2},{1,3},{2,0},{3,1},{4,6},{5,7},{6,4},{7,5},{8,10},{9,11},{10,... | collective-permute-start | bytes 196616 | tf_op jit(solution)/shard_map/ppermute | solution.py:335
  74.4 0.8 copy-start.4
  75.1 16.9 %copy-start.3 = (bf16[64,512]{1,0:T(8,128)(2,1)S(1)}, bf16[64,512]{1,0:T(8,128)(2,1)}, u32[]{:S(2)}) copy-start(bf16[64,512]{1,0:T(8,128)(2,1)} %get-tuple-element.82.rest_0_) | copy-start | bytes 196612
  82.1 21.5 %all-to-all-start.2 = ((bf16[8,1,32,896]{3,2,1,0:T(8,128)(2,1)}), bf16[8,1,32,896]{3,2,1,0:T(8,128)(2,1)S(1)}, u32[]{:S(2)}, u32[]{:S(2)}) async-start(bf16[8,1,32,896]{3,2,1,0:T(8,128)(2,1)} %get-tuple-element.83), calls=%async_computation.2 | async-start | bytes 917504 | tf_op jit(solution)/shard_map/all_to_all | solution.py:472
  87.1 16.5 %collective-permute-start.12 = (bf16[256,896]{1,0:T(8,128)(2,1)}, bf16[256,896]{1,0:T(8,128)(2,1)}, u32[]{:S(2)}, u32[]{:S(2)}) collective-permute-start(bf16[256,896]{1,0:T(8,128)(2,1)} %copy-done.4), channel_id=1, source_target_pairs={{8,0},{16,8},{24,16},{9,1},{17,9},{25,17},{10,2},{18,10},{26,18},{... | collective-permute-start | bytes 1376264 | tf_op jit(solution)/shard_map/ppermute | solution.py:469
  90.7 12.8 %collective-permute-start.13 = (bf16[256,896]{1,0:T(8,128)(2,1)}, bf16[256,896]{1,0:T(8,128)(2,1)S(1)}, u32[]{:S(2)}, u32[]{:S(2)}) collective-permute-start(bf16[256,896]{1,0:T(8,128)(2,1)} %columns_next.1), channel_id=1, source_target_pairs={{8,0},{16,8},{24,16},{9,1},{17,9},{25,17},{10,2},{18,10},{26,18},{... | collective-permute-start | bytes 1376264 | tf_op jit(solution)/shard_map/ppermute | solution.py:469
  93.6 9.9 %collective-permute-start.14 = (bf16[256,512]{1,0:T(8,128)(2,1)}, bf16[256,512]{1,0:T(8,128)(2,1)S(1)}, u32[]{:S(2)}, u32[]{:S(2)}) collective-permute-start(bf16[256,512]{1,0:T(8,128)(2,1)} %pad_maximum_fusion.1), channel_id=1, source_target_pairs={{0,1},{1,0},{2,3},{3,2},{4,5},{5,4},{6,7},{7,6},{8,9},{9,8},{10,11... | collective-permute-start | bytes 786440 | tf_op jit(solution)/shard_map/ppermute | solution.py:335
  97.7 1.3 %copy-start = (f32[2,896,256]{2,1,0:T(8,128)}, f32[2,896,256]{2,1,0:T(8,128)S(1)}, u32[]{:S(2)}) copy-start(f32[2,896,256]{2,1,0:T(8,128)S(1)} %first_terms.1.part_ref) | copy-start | bytes 5505028
  103.5 1.5 %copy-start.1 = (f32[2,896,256]{2,1,0:T(8,128)S(1)}, f32[2,896,256]{2,1,0:T(8,128)}, u32[]{:S(2)}) copy-start(f32[2,896,256]{2,1,0:T(8,128)} %copy-done) | copy-start | bytes 5505028

commit v6 on v5

--- a/solution.py
+++ b/solution.py
@@ -481,20 +481,19 @@
     x0u, before, own_down, own_g, column_g = lax.optimization_barrier((x0u, before, own_down, own_g, column_g))
     k0u, c0u, ab0u = latent_side(x0u, weights, gain_model, gain_latent)
     narrow = narrow_step(y0u, weights, gain_latent, k0u, c0u, ab0u, before)
-    narrow, y1d = lax.optimization_barrier((narrow, y1d))
     first_pieces = gather_pieces(narrow, "dp")
     far = len(first_pieces) - 1
     z0u, u_packed = input_step(x0u, y0u, weights, gain_model, narrow, replicas)
     y1u = to_before(z0u)
-    u_packed, x1u, d_s, *first_pieces[1:far] = lax.optimization_barrier((u_packed, x1u, d_s, *first_pieces[1:far]))
+    u_packed, x1u, y1d, d_s, *first_pieces[1:far] = lax.optimization_barrier((u_packed, x1u, y1d, d_s, *first_pieces[1:far]))
     u_s = exchange(u_packed)
     second, x1_packed = second_step(x1u, y1d, y1u, weights, gain_model, gain_latent, c1d, ab1d, k1d, replicas)
     second_pieces = gather_pieces(second, "dp")
     z0d_s, first = columns_first(j[None], d_s, own_down, own_g, first_pieces)
     y1d_s = to_before(z0d_s)
-    u_s, first, x1_packed, *second_pieces[1:far] = lax.optimization_barrier((u_s, first, x1_packed, *second_pieces[1:far]))
+    z0u_s = columns_next(u_s, own_down, own_g, first)
+    z0u_s, x1_packed, *second_pieces[1:far] = lax.optimization_barrier((z0u_s, x1_packed, *second_pieces[1:far]))
     x1_s = exchange(x1_packed)
-    z0u_s = columns_next(u_s, own_down, own_g, first)
     y1u_s = to_before(z0u_s)
     part = first_terms(d_s, u_s, first, gain_latent.shape[1])
     return terms(j[None], d_s, x1_s, y1d_s, y1u_s, part, column_g, second_pieces)

time: 109 us -> 107 us (0.982)
  starting transfers between devices: 41.2 us -> 35.4 us
  waiting for transfers between devices: 16.4 us -> 21.4 us
    all_to_all x3, waiting for transfers between devices: 0.01 us -> 5.59 us  [exchange(): return lax.all_to_all(blocks, 'dp', 0, 0, tiled=True)]
    all_to_all x3, starting transfers between devices: 18.3 us -> 15 us  [exchange(): return lax.all_to_all(blocks, 'dp', 0, 0, tiled=True)]
    ppermute x4, waiting for transfers between devices: 2.48 us -> 0.01 us  [to_before(): return lax.ppermute(block, 'pipe', [(i + 1, i) for i in range(ranks - 1)])]
    ppermute x3, waiting for transfers between devices: 2.06 us -> 4.43 us  [mirror(): lax.ppermute(block, 'pipe', [(i, ranks - 1 - i) for i in range(ranks)])]
    ppermute x3, starting transfers between devices: 4.77 us -> 2.42 us  [mirror(): lax.ppermute(block, 'pipe', [(i, ranks - 1 - i) for i in range(ranks)])]
    unnamed x12 -> x14, local copies, waits for them, and re-layouts: 3.51 us -> 4.29 us
  transfers between devices with their start and end apart: 18 -> 18, of which waited for: 7 -> 5; matrix products, arithmetic and copies ran while one was open for 5% -> 5% of each run, Pallas kernels for 32% -> 31%
where the time goes in v6:
time: 107 us
  Pallas kernels  39.9 us (37%)
  starting transfers between devices  35.4 us (33%)
  waiting for transfers between devices  21.4 us (20%)
  local copies, waits for them, and re-layouts  6.93 us (6%)
  other arithmetic  2.59 us (2%)
    all_to_all x3, starting transfers between devices, exchange(): return lax.all_to_all(blocks, 'dp', 0, 0, tiled=True)  15 us
    ppermute x8, starting transfers between devices, across(): return lax.ppermute(held, axis, [(i, i ^ apart) for i in range(parts)])  12.8 us
    ppermute x8, waiting for transfers between devices, across(): return lax.ppermute(held, axis, [(i, i ^ apart) for i in range(parts)])  11.4 us
    pallas_call x1, Pallas kernels, first_step(): pl.pallas_call(functools.partial(first_kernel, before is None), out_shape...  7.87 us
    pallas_call x1, Pallas kernels, second_step(): pl.pallas_call(second_kernel, out_shape=[shape(2 * rows, 2 * lat), shape(...  6.7 us
    all_to_all x3, waiting for transfers between devices, exchange(): return lax.all_to_all(blocks, 'dp', 0, 0, tiled=True)  5.59 us
    ppermute x4, starting transfers between devices, to_before(): return lax.ppermute(block, 'pipe', [(i + 1, i) for i in range(ranks - 1)])  5.17 us
    pallas_call x1, Pallas kernels, input_step(): pl.pallas_call(input_kernel, out_shape=[shape(rows, width), shape(parts,...  4.89 us
  transfers between devices with their start and end apart: 18, of which 5 were waited for; matrix products, arithmetic and copies ran while one was open for 5% of the time, Pallas kernels for 31%

profile of v6, /device:TPU:0, one launch (start us, length us, event | category | flops | bytes accessed | tf_op | source)
XLA Modules:
  0.0 106.5 jit_solution(2289960909778242849)
XLA Ops:
  0.0 3.6 %prepare.1 = (bf16[8,3,32,896]{3,2,1,0:T(8,128)(2,1)}, bf16[32,7168]{1,0:T(8,128)(2,1)}, bf16[32,7168]{1,0:T(8,128)(2,1)}, bf16[32,7168]{1,0:T(8,128)(2,1)}) custom-call(bf16[1,2,32,7168]{3,2,1,0:T(8,128)(2,1)} %x_ref, bf16[1,2,32,7168]{3,2,1,0:T(8,128)(2,1)} %up_ref.1, bf16[2,1,32,7168]{3,2,1,0:T(8,128)(2,1)} %y_ref), custom_call_target="tpu_custom_call" | custom-call | flops 1 | bytes 1 | tf_op jit(solution)/shard_map/prepare/pallas_call | solution.py:94
  3.6 7.3 %all-to-all-start = ((bf16[8,3,32,896]{3,2,1,0:T(8,128)(2,1)}), bf16[8,3,32,896]{3,2,1,0:T(8,128)(2,1)S(1)}, u32[]{:S(2)}, u32[]{:S(2)}) async-start(bf16[8,3,32,896]{3,2,1,0:T(8,128)(2,1)} %get-tuple-element.63), calls=%async_computation | async-start | bytes 2752512 | tf_op jit(solution)/shard_map/all_to_all | solution.py:472
  10.9 0.7 collective-permute-start
  11.6 1.1 %collective-permute-start.1 = (bf16[32,7168]{1,0:T(8,128)(2,1)}, bf16[32,7168]{1,0:T(8,128)(2,1)}, u32[]{:S(2)}, u32[]{:S(2)}) collective-permute-start(bf16[32,7168]{1,0:T(8,128)(2,1)} %get-tuple-element.55), channel_id=1, source_target_pairs={{0,24},{8,16},{16,8},{24,0},{1,25},{9,17},{17,9},{25,1},{2,26},{10... | collective-permute-start | bytes 1376264 | tf_op jit(solution)/shard_map/ppermute | solution.py:466
  12.6 0.7 collective-permute-start.2
  13.3 7.9 %first_step.1 = (bf16[32,7168]{1,0:T(8,128)(2,1)}, bf16[32,640]{1,0:T(8,128)(2,1)}, bf16[32,256]{1,0:T(8,128)(2,1)}, f32[32,256]{1,0:T(8,128)}, f32[32,128]{1,0:T(8,128)}) custom-call(bf16[1,2,32,7168]{3,2,1,0:T(8,128)(2,1)} %x_ref, bf16[2,1,32,7168]{3,2,1,0:T(8,128)(2,1)} %y_ref, bf16[1,2,7168,256]{3,2,1,0:T(8,128)(2,1)} %w_ref.9, bf16[1,7168]{1,0:T(2,128)(2,1)} %g_ref.7, ...), custom_call_target="tpu_custom_call" | custom-call | flops 1 | bytes 1 | tf_op jit(solution)/shard_map/first_step/pallas_call | solution.py:199
  21.2 1.3 %collective-permute-start.3 = (bf16[32,7168]{1,0:T(8,128)(2,1)}, bf16[32,7168]{1,0:T(8,128)(2,1)}, u32[]{:S(2)}, u32[]{:S(2)}) collective-permute-start(bf16[32,7168]{1,0:T(8,128)(2,1)} %get-tuple-element.62), channel_id=1, source_target_pairs={{8,0},{16,8},{24,16},{9,1},{17,9},{25,17},{10,2},{18,10},{26,18},{... | collective-permute-start | bytes 1376264 | tf_op jit(solution)/shard_map/ppermute | solution.py:469
  22.5 0.7 constant_dynamic-slice_fusion.g_ref
  23.2 0.7 fusion
  23.9 1.0 constant_dynamic-slice_fusion.1.down_ref
  24.9 0.0 collective-permute-done.x_ref
  24.9 4.4 %latent_side.1 = (bf16[32,256]{1,0:T(8,128)(2,1)}, f32[32,256]{1,0:T(8,128)}, f32[32,128]{1,0:T(8,128)}) custom-call(bf16[32,7168]{1,0:T(8,128)(2,1)} %collective-permute-done.x_ref, bf16[1,2,7168,256]{3,2,1,0:T(8,128)(2,1)} %w_ref.9, bf16[1,7168]{1,0:T(2,128)(2,1)} %g_ref.7, bf16[1,256]{1,0:T(2,128)(2,1)} %h_ref.7), custom_call_target="tpu_custom_call" | custom-call | flops 1 | bytes 1 | tf_op jit(solution)/shard_map/latent_side/pallas_call | solution.py:223
  29.4 4.4 %collective-permute-done.1.y_ref = bf16[32,7168]{1,0:T(8,128)(2,1)} collective-permute-done((bf16[32,7168]{1,0:T(8,128)(2,1)}, bf16[32,7168]{1,0:T(8,128)(2,1)}, u32[]{:S(2)}, u32[]{:S(2)}) %collective-permute-start.1) | collective-permute-done | bytes 458784 | tf_op jit(solution)/shard_map/ppermute | solution.py:466
  33.8 4.6 %narrow_step.1.narrow_ref.rest_0_ = bf16[64,640]{1,0:T(8,128)(2,1)} custom-call(bf16[32,7168]{1,0:T(8,128)(2,1)} %collective-permute-done.1.y_ref, bf16[1,2,7168,256]{3,2,1,0:T(8,128)(2,1)} %w_ref.9, bf16[1,256]{1,0:T(2,128)(2,1)} %h_ref.7, bf16[32,256]{1,0:T(8,128)(2,1)} %get-tuple-element.56.k_ref, f32[32,256]{1,0:T(8,128)} %get-tuple-element.57.c_ref, ...), custom_call_target="tpu_custom_call" | custom-call | flops 1 | bytes 1 | tf_op jit(solution)/shard_map/narrow_step/pallas_call | solution.py:250
  38.4 3.9 %collective-permute-start.4 = (bf16[64,640]{1,0:T(8,128)(2,1)}, bf16[64,640]{1,0:T(8,128)(2,1)S(1)}, u32[]{:S(2)}, u32[]{:S(2)}) collective-permute-start(bf16[64,640]{1,0:T(8,128)(2,1)} %narrow_step.1.narrow_ref.rest_0_), channel_id=1, source_target_pairs={{0,6},{1,7},{2,4},{3,5},{4,2},{5,3},{6,0},{7,1},{8,14},{9,15},{10,... | collective-permute-start | bytes 245768 | tf_op jit(solution)/shard_map/ppermute | solution.py:335
  42.3 0.0 collective-permute-start.5
  42.3 0.6 collective-permute-start.6
  42.9 4.9 %input_step.1 = (bf16[32,7168]{1,0:T(8,128)(2,1)}, bf16[8,2,32,896]{3,2,1,0:T(8,128)(2,1)}) custom-call(bf16[32,7168]{1,0:T(8,128)(2,1)} %collective-permute-done.x_ref, bf16[32,7168]{1,0:T(8,128)(2,1)} %collective-permute-done.1.y_ref, bf16[1,2,7168,256]{3,2,1,0:T(8,128)(2,1)} %w_ref.9, bf16[1,7168]{1,0:T(2,128)(2,1)} %g_ref.7, ...), custom_call_target="tpu_custom_call" | custom-call | flops 1 | bytes 1 | tf_op jit(solution)/shard_map/input_step/pallas_call | solution.py:281
  47.8 0.0 copy-start.6
  47.9 0.0 copy-start.2
  47.9 0.0 collective-permute-done.2.x_ref
  47.9 0.0 collective-permute-done.3.y0_ref
  47.9 0.0 collective-permute-done.4.rest_1_
  47.9 2.9 %collective-permute-done.5.rest_2_ = bf16[64,640]{1,0:T(8,128)(2,1)} collective-permute-done((bf16[64,640]{1,0:T(8,128)(2,1)}, bf16[64,640]{1,0:T(8,128)(2,1)}, u32[]{:S(2)}, u32[]{:S(2)}) %collective-permute-start.5) | collective-permute-done | bytes 81952 | tf_op jit(solution)/shard_map/ppermute | solution.py:335
  50.8 0.0 collective-permute-done.6.rest_3_
  50.8 0.0 all-to-all-done.d_ref
  50.8 4.2 %all-to-all-start.1 = ((bf16[8,2,32,896]{3,2,1,0:T(8,128)(2,1)}), bf16[8,2,32,896]{3,2,1,0:T(8,128)(2,1)}, u32[]{:S(2)}, u32[]{:S(2)}) async-start(bf16[8,2,32,896]{3,2,1,0:T(8,128)(2,1)} %get-tuple-element.65), calls=%async_computation.1 | async-start | bytes 1835008 | tf_op jit(solution)/shard_map/all_to_all | solution.py:472
  55.1 0.0 copy-done.6
  55.1 1.3 %collective-permute-start.8 = (bf16[32,7168]{1,0:T(8,128)(2,1)S(1)}, bf16[32,7168]{1,0:T(8,128)(2,1)}, u32[]{:S(2)}, u32[]{:S(2)}) collective-permute-start(bf16[32,7168]{1,0:T(8,128)(2,1)S(1)} %copy-done.6), channel_id=1, source_target_pairs={{8,0},{16,8},{24,16},{9,1},{17,9},{25,17},{10,2},{18,10},{26,18},{... | collective-permute-start | bytes 1376264 | tf_op jit(solution)/shard_map/ppermute | solution.py:469
  56.4 0.0 copy-done.2
  56.4 1.7 %pad_maximum_fusion = bf16[256,640]{1,0:T(8,128)(2,1)} fusion(bf16[64,640]{1,0:T(8,128)(2,1)} %collective-permute-done.6.rest_3_, bf16[64,640]{1,0:T(8,128)(2,1)} %collective-permute-done.5.rest_2_, bf16[64,640]{1,0:T(8,128)(2,1)S(1)} %collective-permute-done.4.rest_1_, bf16[64,640]{1,0:T(8,128)(2,1)S(1)} %copy-done.2), kind=kLoop, calls=%fused_computation | loop fusion | flops 1310720 | bytes 655360 | tf_op jit(solution)/shard_map/concatenate | solution.py:338
  58.1 1.9 %collective-permute-start.7 = (bf16[256,640]{1,0:T(8,128)(2,1)}, bf16[256,640]{1,0:T(8,128)(2,1)}, u32[]{:S(2)}, u32[]{:S(2)}) collective-permute-start(bf16[256,640]{1,0:T(8,128)(2,1)} %pad_maximum_fusion), channel_id=1, source_target_pairs={{0,1},{1,0},{2,3},{3,2},{4,5},{5,4},{6,7},{7,6},{8,9},{9,8},{10,11... | collective-permute-start | bytes 983048 | tf_op jit(solution)/shard_map/ppermute | solution.py:335
  59.9 0.0 collective-permute-done.8.y1_ref
  59.9 6.7 %second_step.1 = (bf16[64,512]{1,0:T(8,128)(2,1)}, bf16[8,1,32,896]{3,2,1,0:T(8,128)(2,1)}) custom-call(bf16[32,7168]{1,0:T(8,128)(2,1)} %collective-permute-done.2.x_ref, bf16[32,7168]{1,0:T(8,128)(2,1)} %collective-permute-done.3.y0_ref, bf16[32,7168]{1,0:T(8,128)(2,1)} %collective-permute-done.8.y1_ref, bf16[1,2,7168,256]{3,2,1,0:T(8,128)(2,1)} %w_ref.9, ...), custom_call_target="tpu_custom_call" | custom-call | flops 1 | bytes 1 | tf_op jit(solution)/shard_map/second_step/pallas_call | solution.py:314
  66.6 3.4 %collective-permute-start.9 = (bf16[64,512]{1,0:T(8,128)(2,1)}, bf16[64,512]{1,0:T(8,128)(2,1)}, u32[]{:S(2)}, u32[]{:S(2)}) collective-permute-start(bf16[64,512]{1,0:T(8,128)(2,1)} %get-tuple-element.79.rest_0_), channel_id=1, source_target_pairs={{0,6},{1,7},{2,4},{3,5},{4,2},{5,3},{6,0},{7,1},{8,14},{9,15},{10,... | collective-permute-start | bytes 196616 | tf_op jit(solution)/shard_map/ppermute | solution.py:335
  70.0 0.0 collective-permute-start.10
  70.0 1.1 %collective-permute-start.11 = (bf16[64,512]{1,0:T(8,128)(2,1)}, bf16[64,512]{1,0:T(8,128)(2,1)}, u32[]{:S(2)}, u32[]{:S(2)}) collective-permute-start(bf16[64,512]{1,0:T(8,128)(2,1)} %get-tuple-element.79.rest_0_), channel_id=1, source_target_pairs={{0,2},{1,3},{2,0},{3,1},{4,6},{5,7},{6,4},{7,5},{8,10},{9,11},{10,... | collective-permute-start | bytes 196616 | tf_op jit(solution)/shard_map/ppermute | solution.py:335
  71.1 3.3 %collective-permute-done.7.rest_4_ = bf16[256,640]{1,0:T(8,128)(2,1)} collective-permute-done((bf16[256,640]{1,0:T(8,128)(2,1)}, bf16[256,640]{1,0:T(8,128)(2,1)}, u32[]{:S(2)}, u32[]{:S(2)}) %collective-permute-start.7) | collective-permute-done | bytes 327712 | tf_op jit(solution)/shard_map/ppermute | solution.py:335
  74.4 1.5 %columns_first.1 = (bf16[256,896]{1,0:T(8,128)(2,1)S(1)}, bf16[8,64,640]{2,1,0:T(8,128)(2,1)S(1)}) custom-call(s32[1]{0:T(128)} %bitcast.j_ref, bf16[8,3,32,896]{3,2,1,0:T(8,128)(2,1)S(1)} %all-to-all-done.d_ref, bf16[1,1,896,256]{3,2,1,0:T(8,128)(2,1)S(1)} %constant_dynamic-slice_fusion.1.down_ref, bf16[1,896]{1,0:T(2,128)(2,1)S(1)} %constant_dynamic-slice_fusion.g_ref, ...), custom_call_target="tpu_custom_call" | custom-call | flops 1 | bytes 1 | tf_op jit(solution)/shard_map/columns_first/pallas_call | solution.py:376
  75.9 0.0 copy-start.5
  75.9 0.8 copy-done.5
  76.7 5.6 %all-to-all-done.1.u_ref = bf16[8,2,32,896]{3,2,1,0:T(8,128)(2,1)} async-done(((bf16[8,2,32,896]{3,2,1,0:T(8,128)(2,1)}), bf16[8,2,32,896]{3,2,1,0:T(8,128)(2,1)}, u32[]{:S(2)}, u32[]{:S(2)}) %all-to-all-start.1) | async-done | bytes 917536 | tf_op jit(solution)/shard_map/all_to_all | solution.py:472
  82.3 1.6 %columns_next.1 = bf16[256,896]{1,0:T(8,128)(2,1)S(1)} custom-call(bf16[8,2,32,896]{3,2,1,0:T(8,128)(2,1)} %all-to-all-done.1.u_ref, bf16[1,1,896,256]{3,2,1,0:T(8,128)(2,1)S(1)} %constant_dynamic-slice_fusion.1.down_ref, bf16[1,896]{1,0:T(2,128)(2,1)S(1)} %constant_dynamic-slice_fusion.g_ref, bf16[8,64,640]{2,1,0:T(8,128)(2,1)S(1)} %get-tuple-element.71.narrow_ref.first_ref), custom_call_target="tpu_custom_call" | custom-call | flops 1 | bytes 1 | tf_op jit(solution)/shard_map/columns_next/pallas_call | solution.py:390
  83.8 0.0 copy-start.3
  83.8 0.8 copy-done.3
  84.6 0.0 collective-permute-done.9.rest_1_
  84.6 0.0 collective-permute-done.10.rest_2_
  84.6 0.0 collective-permute-done.11.rest_3_
  84.6 3.5 %all-to-all-start.2 = ((bf16[8,1,32,896]{3,2,1,0:T(8,128)(2,1)}), bf16[8,1,32,896]{3,2,1,0:T(8,128)(2,1)S(1)}, u32[]{:S(2)}, u32[]{:S(2)}) async-start(bf16[8,1,32,896]{3,2,1,0:T(8,128)(2,1)} %get-tuple-element.80), calls=%async_computation.2 | async-start | bytes 917504 | tf_op jit(solution)/shard_map/all_to_all | solution.py:472
  88.1 1.3 %collective-permute-start.12 = (bf16[256,896]{1,0:T(8,128)(2,1)}, bf16[256,896]{1,0:T(8,128)(2,1)S(1)}, u32[]{:S(2)}, u32[]{:S(2)}) collective-permute-start(bf16[256,896]{1,0:T(8,128)(2,1)} %copy-done.5), channel_id=1, source_target_pairs={{8,0},{16,8},{24,16},{9,1},{17,9},{25,17},{10,2},{18,10},{26,18},{... | collective-permute-start | bytes 1376264 | tf_op jit(solution)/shard_map/ppermute | solution.py:469
  89.4 1.3 %collective-permute-start.13 = (bf16[256,896]{1,0:T(8,128)(2,1)}, bf16[256,896]{1,0:T(8,128)(2,1)}, u32[]{:S(2)}, u32[]{:S(2)}) collective-permute-start(bf16[256,896]{1,0:T(8,128)(2,1)} %copy-done.3), channel_id=1, source_target_pairs={{8,0},{16,8},{24,16},{9,1},{17,9},{25,17},{10,2},{18,10},{26,18},{... | collective-permute-start | bytes 1376264 | tf_op jit(solution)/shard_map/ppermute | solution.py:469
  90.7 0.0 copy-done.4
  90.7 0.9 pad_maximum_fusion.1
  91.6 2.0 %collective-permute-start.14 = (bf16[256,512]{1,0:T(8,128)(2,1)S(1)}, bf16[256,512]{1,0:T(8,128)(2,1)}, u32[]{:S(2)}, u32[]{:S(2)}) collective-permute-start(bf16[256,512]{1,0:T(8,128)(2,1)S(1)} %pad_maximum_fusion.1), channel_id=1, source_target_pairs={{0,1},{1,0},{2,3},{3,2},{4,5},{5,4},{6,7},{7,6},{8,9},{9,8},{10,11... | collective-permute-start | bytes 786440 | tf_op jit(solution)/shard_map/ppermute | solution.py:335
  93.6 0.2 copy.7.g_ref
  93.8 1.9 %first_terms.1.part_ref = f32[2,896,256]{2,1,0:T(8,128)S(1)} custom-call(bf16[8,3,32,896]{3,2,1,0:T(8,128)(2,1)S(1)} %all-to-all-done.d_ref, bf16[8,2,32,896]{3,2,1,0:T(8,128)(2,1)} %all-to-all-done.1.u_ref, bf16[8,64,640]{2,1,0:T(8,128)(2,1)S(1)} %get-tuple-element.71.narrow_ref.first_ref), custom_call_target="tpu_custom_call" | custom-call | flops 1 | bytes 1 | tf_op jit(solution)/shard_map/first_terms/pallas_call | solution.py:413
  95.7 0.0 copy-start
  95.7 1.3 %copy-done = f32[2,896,256]{2,1,0:T(8,128)} copy-done((f32[2,896,256]{2,1,0:T(8,128)}, f32[2,896,256]{2,1,0:T(8,128)S(1)}, u32[]{:S(2)}) %copy-start) | copy-done | bytes 1835032
  97.0 5.2 %collective-permute-done.14.rest_4_ = bf16[256,512]{1,0:T(8,128)(2,1)} collective-permute-done((bf16[256,512]{1,0:T(8,128)(2,1)S(1)}, bf16[256,512]{1,0:T(8,128)(2,1)}, u32[]{:S(2)}, u32[]{:S(2)}) %collective-permute-start.14) | collective-permute-done | bytes 262176 | tf_op jit(solution)/shard_map/ppermute | solution.py:335
  102.1 0.0 collective-permute-done.12.y1d_ref
  102.1 0.0 collective-permute-done.13.y1u_ref
  102.1 0.0 all-to-all-done.2.x1_ref
  102.1 1.5 %copy-done.1 = f32[2,896,256]{2,1,0:T(8,128)S(1)} copy-done((f32[2,896,256]{2,1,0:T(8,128)S(1)}, f32[2,896,256]{2,1,0:T(8,128)}, u32[]{:S(2)}) %copy-start.1) | copy-done | bytes 1835032
  103.6 2.9 %terms.1 = bf16[1,2,896,256]{3,2,1,0:T(8,128)(2,1)} custom-call(s32[1]{0:T(128)} %bitcast.j_ref, bf16[8,3,32,896]{3,2,1,0:T(8,128)(2,1)S(1)} %all-to-all-done.d_ref, bf16[8,1,32,896]{3,2,1,0:T(8,128)(2,1)S(1)} %all-to-all-done.2.x1_ref, bf16[256,896]{1,0:T(8,128)(2,1)S(1)} %collective-permute-done.12.y1d_ref, ...), custom_call_target="tpu_custom_call" | custom-call | flops 1 | bytes 1 | tf_op jit(solution)/shard_map/terms/pallas_call | solution.py:445
  (2 shorter events, 0.0 us)
Async XLA Ops:
  3.6 47.2 %all-to-all-start = ((bf16[8,3,32,896]{3,2,1,0:T(8,128)(2,1)}), bf16[8,3,32,896]{3,2,1,0:T(8,128)(2,1)S(1)}, u32[]{:S(2)}, u32[]{:S(2)}) async-start(bf16[8,3,32,896]{3,2,1,0:T(8,128)(2,1)} %get-tuple-element.63), calls=%async_computation | async-start | bytes 2752512 | tf_op jit(solution)/shard_map/all_to_all | solution.py:472
  10.9 14.0 %collective-permute-start = (bf16[32,7168]{1,0:T(8,128)(2,1)}, bf16[32,7168]{1,0:T(8,128)(2,1)}, u32[]{:S(2)}, u32[]{:S(2)}) collective-permute-start(bf16[32,7168]{1,0:T(8,128)(2,1)} %get-tuple-element.50), channel_id=1, source_target_pairs={{0,24},{8,16},{16,8},{24,0},{1,25},{9,17},{17,9},{25,1},{2,26},{10... | collective-permute-start | bytes 1376264 | tf_op jit(solution)/shard_map/ppermute | solution.py:466
  11.6 22.2 %collective-permute-start.1 = (bf16[32,7168]{1,0:T(8,128)(2,1)}, bf16[32,7168]{1,0:T(8,128)(2,1)}, u32[]{:S(2)}, u32[]{:S(2)}) collective-permute-start(bf16[32,7168]{1,0:T(8,128)(2,1)} %get-tuple-element.55), channel_id=1, source_target_pairs={{0,24},{8,16},{16,8},{24,0},{1,25},{9,17},{17,9},{25,1},{2,26},{10... | collective-permute-start | bytes 1376264 | tf_op jit(solution)/shard_map/ppermute | solution.py:466
  12.6 35.2 %collective-permute-start.2 = (bf16[32,7168]{1,0:T(8,128)(2,1)}, bf16[32,7168]{1,0:T(8,128)(2,1)}, u32[]{:S(2)}, u32[]{:S(2)}) collective-permute-start(bf16[32,7168]{1,0:T(8,128)(2,1)} %get-tuple-element.61), channel_id=1, source_target_pairs={{0,24},{8,16},{16,8},{24,0},{1,25},{9,17},{17,9},{25,1},{2,26},{10... | collective-permute-start | bytes 1376264 | tf_op jit(solution)/shard_map/ppermute | solution.py:466
  21.2 26.7 %collective-permute-start.3 = (bf16[32,7168]{1,0:T(8,128)(2,1)}, bf16[32,7168]{1,0:T(8,128)(2,1)}, u32[]{:S(2)}, u32[]{:S(2)}) collective-permute-start(bf16[32,7168]{1,0:T(8,128)(2,1)} %get-tuple-element.62), channel_id=1, source_target_pairs={{8,0},{16,8},{24,16},{9,1},{17,9},{25,17},{10,2},{18,10},{26,18},{... | collective-permute-start | bytes 1376264 | tf_op jit(solution)/shard_map/ppermute | solution.py:469
  38.4 9.5 %collective-permute-start.4 = (bf16[64,640]{1,0:T(8,128)(2,1)}, bf16[64,640]{1,0:T(8,128)(2,1)S(1)}, u32[]{:S(2)}, u32[]{:S(2)}) collective-permute-start(bf16[64,640]{1,0:T(8,128)(2,1)} %narrow_step.1.narrow_ref.rest_0_), channel_id=1, source_target_pairs={{0,6},{1,7},{2,4},{3,5},{4,2},{5,3},{6,0},{7,1},{8,14},{9,15},{10,... | collective-permute-start | bytes 245768 | tf_op jit(solution)/shard_map/ppermute | solution.py:335
  42.3 8.5 %collective-permute-start.5 = (bf16[64,640]{1,0:T(8,128)(2,1)}, bf16[64,640]{1,0:T(8,128)(2,1)}, u32[]{:S(2)}, u32[]{:S(2)}) collective-permute-start(bf16[64,640]{1,0:T(8,128)(2,1)} %narrow_step.1.narrow_ref.rest_0_), channel_id=1, source_target_pairs={{0,4},{1,5},{2,6},{3,7},{4,0},{5,1},{6,2},{7,3},{8,12},{9,13},{10,... | collective-permute-start | bytes 245768 | tf_op jit(solution)/shard_map/ppermute | solution.py:335
  42.3 8.5 %collective-permute-start.6 = (bf16[64,640]{1,0:T(8,128)(2,1)}, bf16[64,640]{1,0:T(8,128)(2,1)}, u32[]{:S(2)}, u32[]{:S(2)}) collective-permute-start(bf16[64,640]{1,0:T(8,128)(2,1)} %narrow_step.1.narrow_ref.rest_0_), channel_id=1, source_target_pairs={{0,2},{1,3},{2,0},{3,1},{4,6},{5,7},{6,4},{7,5},{8,10},{9,11},{10,... | collective-permute-start | bytes 245768 | tf_op jit(solution)/shard_map/ppermute | solution.py:335
  47.8 7.2 %copy-start.6 = (bf16[32,7168]{1,0:T(8,128)(2,1)S(1)}, bf16[32,7168]{1,0:T(8,128)(2,1)}, u32[]{:S(2)}) copy-start(bf16[32,7168]{1,0:T(8,128)(2,1)} %get-tuple-element.74) | copy-start | bytes 1376260
  47.9 8.5 %copy-start.2 = (bf16[64,640]{1,0:T(8,128)(2,1)S(1)}, bf16[64,640]{1,0:T(8,128)(2,1)}, u32[]{:S(2)}) copy-start(bf16[64,640]{1,0:T(8,128)(2,1)} %narrow_step.1.narrow_ref.rest_0_) | copy-start | bytes 245764
  50.8 31.4 %all-to-all-start.1 = ((bf16[8,2,32,896]{3,2,1,0:T(8,128)(2,1)}), bf16[8,2,32,896]{3,2,1,0:T(8,128)(2,1)}, u32[]{:S(2)}, u32[]{:S(2)}) async-start(bf16[8,2,32,896]{3,2,1,0:T(8,128)(2,1)} %get-tuple-element.65), calls=%async_computation.1 | async-start | bytes 1835008 | tf_op jit(solution)/shard_map/all_to_all | solution.py:472
  55.1 4.9 %collective-permute-start.8 = (bf16[32,7168]{1,0:T(8,128)(2,1)S(1)}, bf16[32,7168]{1,0:T(8,128)(2,1)}, u32[]{:S(2)}, u32[]{:S(2)}) collective-permute-start(bf16[32,7168]{1,0:T(8,128)(2,1)S(1)} %copy-done.6), channel_id=1, source_target_pairs={{8,0},{16,8},{24,16},{9,1},{17,9},{25,17},{10,2},{18,10},{26,18},{... | collective-permute-start | bytes 1376264 | tf_op jit(solution)/shard_map/ppermute | solution.py:469
  58.1 16.4 %collective-permute-start.7 = (bf16[256,640]{1,0:T(8,128)(2,1)}, bf16[256,640]{1,0:T(8,128)(2,1)}, u32[]{:S(2)}, u32[]{:S(2)}) collective-permute-start(bf16[256,640]{1,0:T(8,128)(2,1)} %pad_maximum_fusion), channel_id=1, source_target_pairs={{0,1},{1,0},{2,3},{3,2},{4,5},{5,4},{6,7},{7,6},{8,9},{9,8},{10,11... | collective-permute-start | bytes 983048 | tf_op jit(solution)/shard_map/ppermute | solution.py:335
  66.6 18.0 %collective-permute-start.9 = (bf16[64,512]{1,0:T(8,128)(2,1)}, bf16[64,512]{1,0:T(8,128)(2,1)}, u32[]{:S(2)}, u32[]{:S(2)}) collective-permute-start(bf16[64,512]{1,0:T(8,128)(2,1)} %get-tuple-element.79.rest_0_), channel_id=1, source_target_pairs={{0,6},{1,7},{2,4},{3,5},{4,2},{5,3},{6,0},{7,1},{8,14},{9,15},{10,... | collective-permute-start | bytes 196616 | tf_op jit(solution)/shard_map/ppermute | solution.py:335
  70.0 14.6 %collective-permute-start.10 = (bf16[64,512]{1,0:T(8,128)(2,1)}, bf16[64,512]{1,0:T(8,128)(2,1)}, u32[]{:S(2)}, u32[]{:S(2)}) collective-permute-start(bf16[64,512]{1,0:T(8,128)(2,1)} %get-tuple-element.79.rest_0_), channel_id=1, source_target_pairs={{0,4},{1,5},{2,6},{3,7},{4,0},{5,1},{6,2},{7,3},{8,12},{9,13},{10,... | collective-permute-start | bytes 196616 | tf_op jit(solution)/shard_map/ppermute | solution.py:335
  70.0 14.6 %collective-permute-start.11 = (bf16[64,512]{1,0:T(8,128)(2,1)}, bf16[64,512]{1,0:T(8,128)(2,1)}, u32[]{:S(2)}, u32[]{:S(2)}) collective-permute-start(bf16[64,512]{1,0:T(8,128)(2,1)} %get-tuple-element.79.rest_0_), channel_id=1, source_target_pairs={{0,2},{1,3},{2,0},{3,1},{4,6},{5,7},{6,4},{7,5},{8,10},{9,11},{10,... | collective-permute-start | bytes 196616 | tf_op jit(solution)/shard_map/ppermute | solution.py:335
  75.9 0.8 copy-start.5
  76.7 14.0 %copy-start.4 = (bf16[64,512]{1,0:T(8,128)(2,1)S(1)}, bf16[64,512]{1,0:T(8,128)(2,1)}, u32[]{:S(2)}) copy-start(bf16[64,512]{1,0:T(8,128)(2,1)} %get-tuple-element.79.rest_0_) | copy-start | bytes 196612
  83.8 0.8 copy-start.3
  84.6 17.5 %all-to-all-start.2 = ((bf16[8,1,32,896]{3,2,1,0:T(8,128)(2,1)}), bf16[8,1,32,896]{3,2,1,0:T(8,128)(2,1)S(1)}, u32[]{:S(2)}, u32[]{:S(2)}) async-start(bf16[8,1,32,896]{3,2,1,0:T(8,128)(2,1)} %get-tuple-element.80), calls=%async_computation.2 | async-start | bytes 917504 | tf_op jit(solution)/shard_map/all_to_all | solution.py:472
  88.1 14.0 %collective-permute-start.12 = (bf16[256,896]{1,0:T(8,128)(2,1)}, bf16[256,896]{1,0:T(8,128)(2,1)S(1)}, u32[]{:S(2)}, u32[]{:S(2)}) collective-permute-start(bf16[256,896]{1,0:T(8,128)(2,1)} %copy-done.5), channel_id=1, source_target_pairs={{8,0},{16,8},{24,16},{9,1},{17,9},{25,17},{10,2},{18,10},{26,18},{... | collective-permute-start | bytes 1376264 | tf_op jit(solution)/shard_map/ppermute | solution.py:469
  89.4 12.7 %collective-permute-start.13 = (bf16[256,896]{1,0:T(8,128)(2,1)}, bf16[256,896]{1,0:T(8,128)(2,1)}, u32[]{:S(2)}, u32[]{:S(2)}) collective-permute-start(bf16[256,896]{1,0:T(8,128)(2,1)} %copy-done.3), channel_id=1, source_target_pairs={{8,0},{16,8},{24,16},{9,1},{17,9},{25,17},{10,2},{18,10},{26,18},{... | collective-permute-start | bytes 1376264 | tf_op jit(solution)/shard_map/ppermute | solution.py:469
  91.6 10.5 %collective-permute-start.14 = (bf16[256,512]{1,0:T(8,128)(2,1)S(1)}, bf16[256,512]{1,0:T(8,128)(2,1)}, u32[]{:S(2)}, u32[]{:S(2)}) collective-permute-start(bf16[256,512]{1,0:T(8,128)(2,1)S(1)} %pad_maximum_fusion.1), channel_id=1, source_target_pairs={{0,1},{1,0},{2,3},{3,2},{4,5},{5,4},{6,7},{7,6},{8,9},{9,8},{10,11... | collective-permute-start | bytes 786440 | tf_op jit(solution)/shard_map/ppermute | solution.py:335
  95.7 1.3 %copy-start = (f32[2,896,256]{2,1,0:T(8,128)}, f32[2,896,256]{2,1,0:T(8,128)S(1)}, u32[]{:S(2)}) copy-start(f32[2,896,256]{2,1,0:T(8,128)S(1)} %first_terms.1.part_ref) | copy-start | bytes 5505028
  102.1 1.5 %copy-start.1 = (f32[2,896,256]{2,1,0:T(8,128)S(1)}, f32[2,896,256]{2,1,0:T(8,128)}, u32[]{:S(2)}) copy-start(f32[2,896,256]{2,1,0:T(8,128)} %copy-done) | copy-start | bytes 5505028

commit v7 on v6

--- a/solution.py
+++ b/solution.py
@@ -338,6 +338,16 @@
     return pieces + [across(jnp.concatenate(pieces, 0), 1)]
 
 
+def gather_split(block, axis):
+    parts = lax.axis_size(axis)
+
+    def across(held, apart):
+        return lax.ppermute(held, axis, [(i, i ^ apart) for i in range(parts)])
+
+    far = [across(block, apart) for apart in range(parts - 2, 0, -2)]
+    return [block, *far, across(block, 1), across(jnp.concatenate(far, 0), 1)]
+
+
 def restore(j, pieces, out):
     parts, rows = out.shape[:2]
     order, at = held_order(parts), 0
@@ -488,11 +498,11 @@
     u_packed, x1u, y1d, d_s, *first_pieces[1:far] = lax.optimization_barrier((u_packed, x1u, y1d, d_s, *first_pieces[1:far]))
     u_s = exchange(u_packed)
     second, x1_packed = second_step(x1u, y1d, y1u, weights, gain_model, gain_latent, c1d, ab1d, k1d, replicas)
-    second_pieces = gather_pieces(second, "dp")
+    second_pieces = gather_split(second, "dp")
     z0d_s, first = columns_first(j[None], d_s, own_down, own_g, first_pieces)
     y1d_s = to_before(z0d_s)
     z0u_s = columns_next(u_s, own_down, own_g, first)
-    z0u_s, x1_packed, *second_pieces[1:far] = lax.optimization_barrier((z0u_s, x1_packed, *second_pieces[1:far]))
+    z0u_s, x1_packed, *second_pieces[1 : far + 1] = lax.optimization_barrier((z0u_s, x1_packed, *second_pieces[1 : far + 1]))
     x1_s = exchange(x1_packed)
     y1u_s = to_before(z0u_s)
     part = first_terms(d_s, u_s, first, gain_latent.shape[1])

time: 107 us -> 107 us (level); the launches traced: 107 us -> 105 us
  waiting for transfers between devices: 21.4 us -> 18.6 us
    ppermute x8 -> x9, waiting for transfers between devices: 11.4 us -> 8.62 us  [across(): return lax.ppermute(held, axis, [(i, i ^ apart) for i in range(parts)])]
    concatenate x0 -> x1, other arithmetic: none -> 1.6 us  [gather_split(): return [block, *far, across(block, 1), across(jnp.concatenate(far, 0), 1)]]
    concatenate x2 -> x1, other arithmetic: 2.59 us -> 1.7 us  [gather_pieces(): return pieces + [across(jnp.concatenate(pieces, 0), 1)]]
    ppermute x8 -> x9, starting transfers between devices: 12.8 us -> 13.6 us  [across(): return lax.ppermute(held, axis, [(i, i ^ apart) for i in range(parts)])]
  transfers between devices with their start and end apart: 18 -> 19, of which waited for: 5 -> 5; matrix products, arithmetic and copies ran while one was open for 5% -> 6% of each run, Pallas kernels for 31% -> 32%
where the time goes in v7:
time: 107 us; the launch traced here: 105 us
  Pallas kernels  39.9 us (37%)
  starting transfers between devices  36.2 us (34%)
  waiting for transfers between devices  18.6 us (17%)
  local copies, waits for them, and re-layouts  6.92 us (6%)
  other arithmetic  3.3 us (3%)
    all_to_all x3, starting transfers between devices, exchange(): return lax.all_to_all(blocks, 'dp', 0, 0, tiled=True)  15 us
    ppermute x9, starting transfers between devices, across(): return lax.ppermute(held, axis, [(i, i ^ apart) for i in range(parts)])  13.6 us
    ppermute x9, waiting for transfers between devices, across(): return lax.ppermute(held, axis, [(i, i ^ apart) for i in range(parts)])  8.62 us
    pallas_call x1, Pallas kernels, first_step(): pl.pallas_call(functools.partial(first_kernel, before is None), out_shape...  7.88 us
    pallas_call x1, Pallas kernels, second_step(): pl.pallas_call(second_kernel, out_shape=[shape(2 * rows, 2 * lat), shape(...  6.7 us
    all_to_all x3, waiting for transfers between devices, exchange(): return lax.all_to_all(blocks, 'dp', 0, 0, tiled=True)  5.59 us
    ppermute x4, starting transfers between devices, to_before(): return lax.ppermute(block, 'pipe', [(i + 1, i) for i in range(ranks - 1)])  5.17 us
    pallas_call x1, Pallas kernels, input_step(): pl.pallas_call(input_kernel, out_shape=[shape(rows, width), shape(parts,...  4.9 us
  transfers between devices with their start and end apart: 19, of which 5 were waited for; matrix products, arithmetic and copies ran while one was open for 6% of the time, Pallas kernels for 32%

profile of v7, /device:TPU:0, one launch (start us, length us, event | category | flops | bytes accessed | tf_op | source)
XLA Modules:
  0.0 105.1 jit_solution(12583871501362302898)
XLA Ops:
  0.0 3.6 %prepare.1 = (bf16[8,3,32,896]{3,2,1,0:T(8,128)(2,1)}, bf16[32,7168]{1,0:T(8,128)(2,1)}, bf16[32,7168]{1,0:T(8,128)(2,1)}, bf16[32,7168]{1,0:T(8,128)(2,1)}) custom-call(bf16[1,2,32,7168]{3,2,1,0:T(8,128)(2,1)} %x_ref, bf16[1,2,32,7168]{3,2,1,0:T(8,128)(2,1)} %up_ref.1, bf16[2,1,32,7168]{3,2,1,0:T(8,128)(2,1)} %y_ref), custom_call_target="tpu_custom_call" | custom-call | flops 1 | bytes 1 | tf_op jit(solution)/shard_map/prepare/pallas_call | solution.py:94
  3.6 7.3 %all-to-all-start = ((bf16[8,3,32,896]{3,2,1,0:T(8,128)(2,1)}), bf16[8,3,32,896]{3,2,1,0:T(8,128)(2,1)S(1)}, u32[]{:S(2)}, u32[]{:S(2)}) async-start(bf16[8,3,32,896]{3,2,1,0:T(8,128)(2,1)} %get-tuple-element.64), calls=%async_computation | async-start | bytes 2752512 | tf_op jit(solution)/shard_map/all_to_all | solution.py:482
  10.9 0.7 collective-permute-start
  11.6 1.1 %collective-permute-start.1 = (bf16[32,7168]{1,0:T(8,128)(2,1)}, bf16[32,7168]{1,0:T(8,128)(2,1)}, u32[]{:S(2)}, u32[]{:S(2)}) collective-permute-start(bf16[32,7168]{1,0:T(8,128)(2,1)} %get-tuple-element.56), channel_id=1, source_target_pairs={{0,24},{8,16},{16,8},{24,0},{1,25},{9,17},{17,9},{25,1},{2,26},{10... | collective-permute-start | bytes 1376264 | tf_op jit(solution)/shard_map/ppermute | solution.py:476
  12.6 0.7 collective-permute-start.2
  13.3 7.9 %first_step.1 = (bf16[32,7168]{1,0:T(8,128)(2,1)}, bf16[32,640]{1,0:T(8,128)(2,1)}, bf16[32,256]{1,0:T(8,128)(2,1)}, f32[32,256]{1,0:T(8,128)}, f32[32,128]{1,0:T(8,128)}) custom-call(bf16[1,2,32,7168]{3,2,1,0:T(8,128)(2,1)} %x_ref, bf16[2,1,32,7168]{3,2,1,0:T(8,128)(2,1)} %y_ref, bf16[1,2,7168,256]{3,2,1,0:T(8,128)(2,1)} %w_ref.9, bf16[1,7168]{1,0:T(2,128)(2,1)} %g_ref.7, ...), custom_call_target="tpu_custom_call" | custom-call | flops 1 | bytes 1 | tf_op jit(solution)/shard_map/first_step/pallas_call | solution.py:199
  21.2 1.3 %collective-permute-start.3 = (bf16[32,7168]{1,0:T(8,128)(2,1)}, bf16[32,7168]{1,0:T(8,128)(2,1)}, u32[]{:S(2)}, u32[]{:S(2)}) collective-permute-start(bf16[32,7168]{1,0:T(8,128)(2,1)} %get-tuple-element.63), channel_id=1, source_target_pairs={{8,0},{16,8},{24,16},{9,1},{17,9},{25,17},{10,2},{18,10},{26,18},{... | collective-permute-start | bytes 1376264 | tf_op jit(solution)/shard_map/ppermute | solution.py:479
  22.5 0.7 constant_dynamic-slice_fusion.g_ref
  23.2 0.7 fusion
  23.9 1.0 constant_dynamic-slice_fusion.1.down_ref
  24.9 0.0 collective-permute-done.x_ref
  25.0 4.4 %latent_side.1 = (bf16[32,256]{1,0:T(8,128)(2,1)}, f32[32,256]{1,0:T(8,128)}, f32[32,128]{1,0:T(8,128)}) custom-call(bf16[32,7168]{1,0:T(8,128)(2,1)} %collective-permute-done.x_ref, bf16[1,2,7168,256]{3,2,1,0:T(8,128)(2,1)} %w_ref.9, bf16[1,7168]{1,0:T(2,128)(2,1)} %g_ref.7, bf16[1,256]{1,0:T(2,128)(2,1)} %h_ref.7), custom_call_target="tpu_custom_call" | custom-call | flops 1 | bytes 1 | tf_op jit(solution)/shard_map/latent_side/pallas_call | solution.py:223
  29.4 4.4 %collective-permute-done.1.y_ref = bf16[32,7168]{1,0:T(8,128)(2,1)} collective-permute-done((bf16[32,7168]{1,0:T(8,128)(2,1)}, bf16[32,7168]{1,0:T(8,128)(2,1)}, u32[]{:S(2)}, u32[]{:S(2)}) %collective-permute-start.1) | collective-permute-done | bytes 458784 | tf_op jit(solution)/shard_map/ppermute | solution.py:476
  33.8 4.6 %narrow_step.1.narrow_ref.rest_0_ = bf16[64,640]{1,0:T(8,128)(2,1)} custom-call(bf16[32,7168]{1,0:T(8,128)(2,1)} %collective-permute-done.1.y_ref, bf16[1,2,7168,256]{3,2,1,0:T(8,128)(2,1)} %w_ref.9, bf16[1,256]{1,0:T(2,128)(2,1)} %h_ref.7, bf16[32,256]{1,0:T(8,128)(2,1)} %get-tuple-element.57.k_ref, f32[32,256]{1,0:T(8,128)} %get-tuple-element.58.c_ref, ...), custom_call_target="tpu_custom_call" | custom-call | flops 1 | bytes 1 | tf_op jit(solution)/shard_map/narrow_step/pallas_call | solution.py:250
  38.4 3.9 %collective-permute-start.4 = (bf16[64,640]{1,0:T(8,128)(2,1)}, bf16[64,640]{1,0:T(8,128)(2,1)S(1)}, u32[]{:S(2)}, u32[]{:S(2)}) collective-permute-start(bf16[64,640]{1,0:T(8,128)(2,1)} %narrow_step.1.narrow_ref.rest_0_), channel_id=1, source_target_pairs={{0,6},{1,7},{2,4},{3,5},{4,2},{5,3},{6,0},{7,1},{8,14},{9,15},{10,... | collective-permute-start | bytes 245768 | tf_op jit(solution)/shard_map/ppermute | solution.py:335
  42.3 0.0 collective-permute-start.5
  42.3 0.6 collective-permute-start.6
  42.9 4.9 %input_step.1 = (bf16[32,7168]{1,0:T(8,128)(2,1)}, bf16[8,2,32,896]{3,2,1,0:T(8,128)(2,1)}) custom-call(bf16[32,7168]{1,0:T(8,128)(2,1)} %collective-permute-done.x_ref, bf16[32,7168]{1,0:T(8,128)(2,1)} %collective-permute-done.1.y_ref, bf16[1,2,7168,256]{3,2,1,0:T(8,128)(2,1)} %w_ref.9, bf16[1,7168]{1,0:T(2,128)(2,1)} %g_ref.7, ...), custom_call_target="tpu_custom_call" | custom-call | flops 1 | bytes 1 | tf_op jit(solution)/shard_map/input_step/pallas_call | solution.py:281
  47.9 0.0 copy-start.6
  47.9 0.0 copy-start.2
  47.9 0.0 collective-permute-done.2.x_ref
  47.9 0.0 collective-permute-done.3.y0_ref
  47.9 0.0 collective-permute-done.4.rest_1_
  47.9 2.9 %collective-permute-done.5.rest_2_ = bf16[64,640]{1,0:T(8,128)(2,1)} collective-permute-done((bf16[64,640]{1,0:T(8,128)(2,1)}, bf16[64,640]{1,0:T(8,128)(2,1)}, u32[]{:S(2)}, u32[]{:S(2)}) %collective-permute-start.5) | collective-permute-done | bytes 81952 | tf_op jit(solution)/shard_map/ppermute | solution.py:335
  50.8 0.0 collective-permute-done.6.rest_3_
  50.8 0.0 all-to-all-done.d_ref
  50.8 4.2 %all-to-all-start.1 = ((bf16[8,2,32,896]{3,2,1,0:T(8,128)(2,1)}), bf16[8,2,32,896]{3,2,1,0:T(8,128)(2,1)}, u32[]{:S(2)}, u32[]{:S(2)}) async-start(bf16[8,2,32,896]{3,2,1,0:T(8,128)(2,1)} %get-tuple-element.66), calls=%async_computation.1 | async-start | bytes 1835008 | tf_op jit(solution)/shard_map/all_to_all | solution.py:482
  55.1 1.3 %collective-permute-start.8 = (bf16[32,7168]{1,0:T(8,128)(2,1)S(1)}, bf16[32,7168]{1,0:T(8,128)(2,1)}, u32[]{:S(2)}, u32[]{:S(2)}) collective-permute-start(bf16[32,7168]{1,0:T(8,128)(2,1)S(1)} %copy-done.6), channel_id=1, source_target_pairs={{8,0},{16,8},{24,16},{9,1},{17,9},{25,17},{10,2},{18,10},{26,18},{... | collective-permute-start | bytes 1376264 | tf_op jit(solution)/shard_map/ppermute | solution.py:479
  56.4 1.7 %pad_maximum_fusion = bf16[256,640]{1,0:T(8,128)(2,1)} fusion(bf16[64,640]{1,0:T(8,128)(2,1)} %collective-permute-done.6.rest_3_, bf16[64,640]{1,0:T(8,128)(2,1)} %collective-permute-done.5.rest_2_, bf16[64,640]{1,0:T(8,128)(2,1)S(1)} %collective-permute-done.4.rest_1_, bf16[64,640]{1,0:T(8,128)(2,1)S(1)} %copy-done.2), kind=kLoop, calls=%fused_computation | loop fusion | flops 1310720 | bytes 655360 | tf_op jit(solution)/shard_map/concatenate | solution.py:338
  58.1 1.9 %collective-permute-start.7 = (bf16[256,640]{1,0:T(8,128)(2,1)}, bf16[256,640]{1,0:T(8,128)(2,1)}, u32[]{:S(2)}, u32[]{:S(2)}) collective-permute-start(bf16[256,640]{1,0:T(8,128)(2,1)} %pad_maximum_fusion), channel_id=1, source_target_pairs={{0,1},{1,0},{2,3},{3,2},{4,5},{5,4},{6,7},{7,6},{8,9},{9,8},{10,11... | collective-permute-start | bytes 983048 | tf_op jit(solution)/shard_map/ppermute | solution.py:335
  59.9 0.0 collective-permute-done.8.y1_ref
  60.0 6.7 %second_step.1 = (bf16[64,512]{1,0:T(8,128)(2,1)}, bf16[8,1,32,896]{3,2,1,0:T(8,128)(2,1)}) custom-call(bf16[32,7168]{1,0:T(8,128)(2,1)} %collective-permute-done.2.x_ref, bf16[32,7168]{1,0:T(8,128)(2,1)} %collective-permute-done.3.y0_ref, bf16[32,7168]{1,0:T(8,128)(2,1)} %collective-permute-done.8.y1_ref, bf16[1,2,7168,256]{3,2,1,0:T(8,128)(2,1)} %w_ref.9, ...), custom_call_target="tpu_custom_call" | custom-call | flops 1 | bytes 1 | tf_op jit(solution)/shard_map/second_step/pallas_call | solution.py:314
  66.7 3.4 %collective-permute-start.9 = (bf16[64,512]{1,0:T(8,128)(2,1)}, bf16[64,512]{1,0:T(8,128)(2,1)}, u32[]{:S(2)}, u32[]{:S(2)}) collective-permute-start(bf16[64,512]{1,0:T(8,128)(2,1)} %get-tuple-element.80.rest_0_), channel_id=1, source_target_pairs={{0,6},{1,7},{2,4},{3,5},{4,2},{5,3},{6,0},{7,1},{8,14},{9,15},{10,... | collective-permute-start | bytes 196616 | tf_op jit(solution)/shard_map/ppermute | solution.py:345
  70.0 0.0 collective-permute-start.10
  70.0 1.1 %collective-permute-start.11 = (bf16[64,512]{1,0:T(8,128)(2,1)}, bf16[64,512]{1,0:T(8,128)(2,1)}, u32[]{:S(2)}, u32[]{:S(2)}) collective-permute-start(bf16[64,512]{1,0:T(8,128)(2,1)} %get-tuple-element.80.rest_0_), channel_id=1, source_target_pairs={{0,2},{1,3},{2,0},{3,1},{4,6},{5,7},{6,4},{7,5},{8,10},{9,11},{10,... | collective-permute-start | bytes 196616 | tf_op jit(solution)/shard_map/ppermute | solution.py:345
  71.1 0.8 collective-permute-start.12
  71.9 2.5 %collective-permute-done.7.rest_4_ = bf16[256,640]{1,0:T(8,128)(2,1)} collective-permute-done((bf16[256,640]{1,0:T(8,128)(2,1)}, bf16[256,640]{1,0:T(8,128)(2,1)}, u32[]{:S(2)}, u32[]{:S(2)}) %collective-permute-start.7) | collective-permute-done | bytes 327712 | tf_op jit(solution)/shard_map/ppermute | solution.py:335
  74.4 1.5 %columns_first.1 = (bf16[256,896]{1,0:T(8,128)(2,1)S(1)}, bf16[8,64,640]{2,1,0:T(8,128)(2,1)S(1)}) custom-call(s32[1]{0:T(128)} %bitcast.j_ref, bf16[8,3,32,896]{3,2,1,0:T(8,128)(2,1)S(1)} %all-to-all-done.d_ref, bf16[1,1,896,256]{3,2,1,0:T(8,128)(2,1)S(1)} %constant_dynamic-slice_fusion.1.down_ref, bf16[1,896]{1,0:T(2,128)(2,1)S(1)} %constant_dynamic-slice_fusion.g_ref, ...), custom_call_target="tpu_custom_call" | custom-call | flops 1 | bytes 1 | tf_op jit(solution)/shard_map/columns_first/pallas_call | solution.py:386
  75.9 0.8 copy-done.5
  76.7 5.6 %all-to-all-done.1.u_ref = bf16[8,2,32,896]{3,2,1,0:T(8,128)(2,1)} async-done(((bf16[8,2,32,896]{3,2,1,0:T(8,128)(2,1)}), bf16[8,2,32,896]{3,2,1,0:T(8,128)(2,1)}, u32[]{:S(2)}, u32[]{:S(2)}) %all-to-all-start.1) | async-done | bytes 917536 | tf_op jit(solution)/shard_map/all_to_all | solution.py:482
  82.2 1.6 %columns_next.1 = bf16[256,896]{1,0:T(8,128)(2,1)S(1)} custom-call(bf16[8,2,32,896]{3,2,1,0:T(8,128)(2,1)} %all-to-all-done.1.u_ref, bf16[1,1,896,256]{3,2,1,0:T(8,128)(2,1)S(1)} %constant_dynamic-slice_fusion.1.down_ref, bf16[1,896]{1,0:T(2,128)(2,1)S(1)} %constant_dynamic-slice_fusion.g_ref, bf16[8,64,640]{2,1,0:T(8,128)(2,1)S(1)} %get-tuple-element.72.narrow_ref.first_ref), custom_call_target="tpu_custom_call" | custom-call | flops 1 | bytes 1 | tf_op jit(solution)/shard_map/columns_next/pallas_call | solution.py:400
  83.8 0.0 copy-start.3
  83.8 0.8 copy-done.3
  84.6 0.0 collective-permute-done.9.rest_1_
  84.6 0.0 collective-permute-done.10.rest_2_
  84.6 0.0 collective-permute-done.11.rest_3_
  84.6 0.0 collective-permute-done.12.rest_4_
  84.6 3.5 %all-to-all-start.2 = ((bf16[8,1,32,896]{3,2,1,0:T(8,128)(2,1)}), bf16[8,1,32,896]{3,2,1,0:T(8,128)(2,1)S(1)}, u32[]{:S(2)}, u32[]{:S(2)}) async-start(bf16[8,1,32,896]{3,2,1,0:T(8,128)(2,1)} %get-tuple-element.81), calls=%async_computation.2 | async-start | bytes 917504 | tf_op jit(solution)/shard_map/all_to_all | solution.py:482
  88.1 1.3 %collective-permute-start.13 = (bf16[256,896]{1,0:T(8,128)(2,1)}, bf16[256,896]{1,0:T(8,128)(2,1)S(1)}, u32[]{:S(2)}, u32[]{:S(2)}) collective-permute-start(bf16[256,896]{1,0:T(8,128)(2,1)} %copy-done.5), channel_id=1, source_target_pairs={{8,0},{16,8},{24,16},{9,1},{17,9},{25,17},{10,2},{18,10},{26,18},{... | collective-permute-start | bytes 1376264 | tf_op jit(solution)/shard_map/ppermute | solution.py:479
  89.4 1.3 %collective-permute-start.14 = (bf16[256,896]{1,0:T(8,128)(2,1)}, bf16[256,896]{1,0:T(8,128)(2,1)}, u32[]{:S(2)}, u32[]{:S(2)}) collective-permute-start(bf16[256,896]{1,0:T(8,128)(2,1)} %copy-done.3), channel_id=1, source_target_pairs={{8,0},{16,8},{24,16},{9,1},{17,9},{25,17},{10,2},{18,10},{26,18},{... | collective-permute-start | bytes 1376264 | tf_op jit(solution)/shard_map/ppermute | solution.py:479
  90.7 1.6 %pad_maximum_fusion.1 = bf16[192,512]{1,0:T(8,128)(2,1)} fusion(bf16[64,512]{1,0:T(8,128)(2,1)} %collective-permute-done.11.rest_3_, bf16[64,512]{1,0:T(8,128)(2,1)} %collective-permute-done.10.rest_2_, bf16[64,512]{1,0:T(8,128)(2,1)} %collective-permute-done.9.rest_1_), kind=kLoop, calls=%fused_computation.1 | loop fusion | flops 589824 | bytes 393216 | tf_op jit(solution)/shard_map/concatenate | solution.py:348
  92.3 1.9 %collective-permute-start.15 = (bf16[192,512]{1,0:T(8,128)(2,1)}, bf16[192,512]{1,0:T(8,128)(2,1)S(1)}, u32[]{:S(2)}, u32[]{:S(2)}) collective-permute-start(bf16[192,512]{1,0:T(8,128)(2,1)} %pad_maximum_fusion.1), channel_id=1, source_target_pairs={{0,1},{1,0},{2,3},{3,2},{4,5},{5,4},{6,7},{7,6},{8,9},{9,8},{10,11... | collective-permute-start | bytes 589832 | tf_op jit(solution)/shard_map/ppermute | solution.py:345
  94.2 0.2 copy.7.g_ref
  94.4 1.9 %first_terms.1.part_ref = f32[2,896,256]{2,1,0:T(8,128)S(1)} custom-call(bf16[8,3,32,896]{3,2,1,0:T(8,128)(2,1)S(1)} %all-to-all-done.d_ref, bf16[8,2,32,896]{3,2,1,0:T(8,128)(2,1)} %all-to-all-done.1.u_ref, bf16[8,64,640]{2,1,0:T(8,128)(2,1)S(1)} %get-tuple-element.72.narrow_ref.first_ref), custom_call_target="tpu_custom_call" | custom-call | flops 1 | bytes 1 | tf_op jit(solution)/shard_map/first_terms/pallas_call | solution.py:423
  96.3 0.0 copy-start
  96.3 1.3 %copy-done = f32[2,896,256]{2,1,0:T(8,128)} copy-done((f32[2,896,256]{2,1,0:T(8,128)}, f32[2,896,256]{2,1,0:T(8,128)S(1)}, u32[]{:S(2)}) %copy-start) | copy-done | bytes 1835032
  97.6 3.2 %collective-permute-done.15.rest_5_ = bf16[192,512]{1,0:T(8,128)(2,1)S(1)} collective-permute-done((bf16[192,512]{1,0:T(8,128)(2,1)}, bf16[192,512]{1,0:T(8,128)(2,1)S(1)}, u32[]{:S(2)}, u32[]{:S(2)}) %collective-permute-start.15) | collective-permute-done | bytes 196640 | tf_op jit(solution)/shard_map/ppermute | solution.py:345
  100.8 0.0 collective-permute-done.13.y1d_ref
  100.8 0.0 collective-permute-done.14.y1u_ref
  100.8 0.0 all-to-all-done.2.x1_ref
  100.8 0.0 copy-done.4
  100.8 0.0 copy-start.1
  100.8 1.5 %copy-done.1 = f32[2,896,256]{2,1,0:T(8,128)S(1)} copy-done((f32[2,896,256]{2,1,0:T(8,128)S(1)}, f32[2,896,256]{2,1,0:T(8,128)}, u32[]{:S(2)}) %copy-start.1) | copy-done | bytes 1835032
  102.3 2.8 %terms.1 = bf16[1,2,896,256]{3,2,1,0:T(8,128)(2,1)} custom-call(s32[1]{0:T(128)} %bitcast.j_ref, bf16[8,3,32,896]{3,2,1,0:T(8,128)(2,1)S(1)} %all-to-all-done.d_ref, bf16[8,1,32,896]{3,2,1,0:T(8,128)(2,1)S(1)} %all-to-all-done.2.x1_ref, bf16[256,896]{1,0:T(8,128)(2,1)S(1)} %collective-permute-done.13.y1d_ref, ...), custom_call_target="tpu_custom_call" | custom-call | flops 1 | bytes 1 | tf_op jit(solution)/shard_map/terms/pallas_call | solution.py:455
  (4 shorter events, 0.0 us)
Async XLA Ops:
  3.6 47.2 %all-to-all-start = ((bf16[8,3,32,896]{3,2,1,0:T(8,128)(2,1)}), bf16[8,3,32,896]{3,2,1,0:T(8,128)(2,1)S(1)}, u32[]{:S(2)}, u32[]{:S(2)}) async-start(bf16[8,3,32,896]{3,2,1,0:T(8,128)(2,1)} %get-tuple-element.64), calls=%async_computation | async-start | bytes 2752512 | tf_op jit(solution)/shard_map/all_to_all | solution.py:482
  10.9 14.1 %collective-permute-start = (bf16[32,7168]{1,0:T(8,128)(2,1)}, bf16[32,7168]{1,0:T(8,128)(2,1)}, u32[]{:S(2)}, u32[]{:S(2)}) collective-permute-start(bf16[32,7168]{1,0:T(8,128)(2,1)} %get-tuple-element.51), channel_id=1, source_target_pairs={{0,24},{8,16},{16,8},{24,0},{1,25},{9,17},{17,9},{25,1},{2,26},{10... | collective-permute-start | bytes 1376264 | tf_op jit(solution)/shard_map/ppermute | solution.py:476
  11.6 22.2 %collective-permute-start.1 = (bf16[32,7168]{1,0:T(8,128)(2,1)}, bf16[32,7168]{1,0:T(8,128)(2,1)}, u32[]{:S(2)}, u32[]{:S(2)}) collective-permute-start(bf16[32,7168]{1,0:T(8,128)(2,1)} %get-tuple-element.56), channel_id=1, source_target_pairs={{0,24},{8,16},{16,8},{24,0},{1,25},{9,17},{17,9},{25,1},{2,26},{10... | collective-permute-start | bytes 1376264 | tf_op jit(solution)/shard_map/ppermute | solution.py:476
  12.6 35.2 %collective-permute-start.2 = (bf16[32,7168]{1,0:T(8,128)(2,1)}, bf16[32,7168]{1,0:T(8,128)(2,1)}, u32[]{:S(2)}, u32[]{:S(2)}) collective-permute-start(bf16[32,7168]{1,0:T(8,128)(2,1)} %get-tuple-element.62), channel_id=1, source_target_pairs={{0,24},{8,16},{16,8},{24,0},{1,25},{9,17},{17,9},{25,1},{2,26},{10... | collective-permute-start | bytes 1376264 | tf_op jit(solution)/shard_map/ppermute | solution.py:476
  21.2 26.7 %collective-permute-start.3 = (bf16[32,7168]{1,0:T(8,128)(2,1)}, bf16[32,7168]{1,0:T(8,128)(2,1)}, u32[]{:S(2)}, u32[]{:S(2)}) collective-permute-start(bf16[32,7168]{1,0:T(8,128)(2,1)} %get-tuple-element.63), channel_id=1, source_target_pairs={{8,0},{16,8},{24,16},{9,1},{17,9},{25,17},{10,2},{18,10},{26,18},{... | collective-permute-start | bytes 1376264 | tf_op jit(solution)/shard_map/ppermute | solution.py:479
  38.4 9.5 %collective-permute-start.4 = (bf16[64,640]{1,0:T(8,128)(2,1)}, bf16[64,640]{1,0:T(8,128)(2,1)S(1)}, u32[]{:S(2)}, u32[]{:S(2)}) collective-permute-start(bf16[64,640]{1,0:T(8,128)(2,1)} %narrow_step.1.narrow_ref.rest_0_), channel_id=1, source_target_pairs={{0,6},{1,7},{2,4},{3,5},{4,2},{5,3},{6,0},{7,1},{8,14},{9,15},{10,... | collective-permute-start | bytes 245768 | tf_op jit(solution)/shard_map/ppermute | solution.py:335
  42.3 8.5 %collective-permute-start.5 = (bf16[64,640]{1,0:T(8,128)(2,1)}, bf16[64,640]{1,0:T(8,128)(2,1)}, u32[]{:S(2)}, u32[]{:S(2)}) collective-permute-start(bf16[64,640]{1,0:T(8,128)(2,1)} %narrow_step.1.narrow_ref.rest_0_), channel_id=1, source_target_pairs={{0,4},{1,5},{2,6},{3,7},{4,0},{5,1},{6,2},{7,3},{8,12},{9,13},{10,... | collective-permute-start | bytes 245768 | tf_op jit(solution)/shard_map/ppermute | solution.py:335
  42.3 8.5 %collective-permute-start.6 = (bf16[64,640]{1,0:T(8,128)(2,1)}, bf16[64,640]{1,0:T(8,128)(2,1)}, u32[]{:S(2)}, u32[]{:S(2)}) collective-permute-start(bf16[64,640]{1,0:T(8,128)(2,1)} %narrow_step.1.narrow_ref.rest_0_), channel_id=1, source_target_pairs={{0,2},{1,3},{2,0},{3,1},{4,6},{5,7},{6,4},{7,5},{8,10},{9,11},{10,... | collective-permute-start | bytes 245768 | tf_op jit(solution)/shard_map/ppermute | solution.py:335
  47.9 7.2 %copy-start.6 = (bf16[32,7168]{1,0:T(8,128)(2,1)S(1)}, bf16[32,7168]{1,0:T(8,128)(2,1)}, u32[]{:S(2)}) copy-start(bf16[32,7168]{1,0:T(8,128)(2,1)} %get-tuple-element.75) | copy-start | bytes 1376260
  47.9 8.5 %copy-start.2 = (bf16[64,640]{1,0:T(8,128)(2,1)S(1)}, bf16[64,640]{1,0:T(8,128)(2,1)}, u32[]{:S(2)}) copy-start(bf16[64,640]{1,0:T(8,128)(2,1)} %narrow_step.1.narrow_ref.rest_0_) | copy-start | bytes 245764
  50.8 31.4 %all-to-all-start.1 = ((bf16[8,2,32,896]{3,2,1,0:T(8,128)(2,1)}), bf16[8,2,32,896]{3,2,1,0:T(8,128)(2,1)}, u32[]{:S(2)}, u32[]{:S(2)}) async-start(bf16[8,2,32,896]{3,2,1,0:T(8,128)(2,1)} %get-tuple-element.66), calls=%async_computation.1 | async-start | bytes 1835008 | tf_op jit(solution)/shard_map/all_to_all | solution.py:482
  55.1 4.9 %collective-permute-start.8 = (bf16[32,7168]{1,0:T(8,128)(2,1)S(1)}, bf16[32,7168]{1,0:T(8,128)(2,1)}, u32[]{:S(2)}, u32[]{:S(2)}) collective-permute-start(bf16[32,7168]{1,0:T(8,128)(2,1)S(1)} %copy-done.6), channel_id=1, source_target_pairs={{8,0},{16,8},{24,16},{9,1},{17,9},{25,17},{10,2},{18,10},{26,18},{... | collective-permute-start | bytes 1376264 | tf_op jit(solution)/shard_map/ppermute | solution.py:479
  58.1 16.4 %collective-permute-start.7 = (bf16[256,640]{1,0:T(8,128)(2,1)}, bf16[256,640]{1,0:T(8,128)(2,1)}, u32[]{:S(2)}, u32[]{:S(2)}) collective-permute-start(bf16[256,640]{1,0:T(8,128)(2,1)} %pad_maximum_fusion), channel_id=1, source_target_pairs={{0,1},{1,0},{2,3},{3,2},{4,5},{5,4},{6,7},{7,6},{8,9},{9,8},{10,11... | collective-permute-start | bytes 983048 | tf_op jit(solution)/shard_map/ppermute | solution.py:335
  66.7 17.9 %collective-permute-start.9 = (bf16[64,512]{1,0:T(8,128)(2,1)}, bf16[64,512]{1,0:T(8,128)(2,1)}, u32[]{:S(2)}, u32[]{:S(2)}) collective-permute-start(bf16[64,512]{1,0:T(8,128)(2,1)} %get-tuple-element.80.rest_0_), channel_id=1, source_target_pairs={{0,6},{1,7},{2,4},{3,5},{4,2},{5,3},{6,0},{7,1},{8,14},{9,15},{10,... | collective-permute-start | bytes 196616 | tf_op jit(solution)/shard_map/ppermute | solution.py:345
  70.0 14.6 %collective-permute-start.10 = (bf16[64,512]{1,0:T(8,128)(2,1)}, bf16[64,512]{1,0:T(8,128)(2,1)}, u32[]{:S(2)}, u32[]{:S(2)}) collective-permute-start(bf16[64,512]{1,0:T(8,128)(2,1)} %get-tuple-element.80.rest_0_), channel_id=1, source_target_pairs={{0,4},{1,5},{2,6},{3,7},{4,0},{5,1},{6,2},{7,3},{8,12},{9,13},{10,... | collective-permute-start | bytes 196616 | tf_op jit(solution)/shard_map/ppermute | solution.py:345
  70.0 14.6 %collective-permute-start.11 = (bf16[64,512]{1,0:T(8,128)(2,1)}, bf16[64,512]{1,0:T(8,128)(2,1)}, u32[]{:S(2)}, u32[]{:S(2)}) collective-permute-start(bf16[64,512]{1,0:T(8,128)(2,1)} %get-tuple-element.80.rest_0_), channel_id=1, source_target_pairs={{0,2},{1,3},{2,0},{3,1},{4,6},{5,7},{6,4},{7,5},{8,10},{9,11},{10,... | collective-permute-start | bytes 196616 | tf_op jit(solution)/shard_map/ppermute | solution.py:345
  71.1 13.5 %collective-permute-start.12 = (bf16[64,512]{1,0:T(8,128)(2,1)}, bf16[64,512]{1,0:T(8,128)(2,1)}, u32[]{:S(2)}, u32[]{:S(2)}) collective-permute-start(bf16[64,512]{1,0:T(8,128)(2,1)} %get-tuple-element.80.rest_0_), channel_id=1, source_target_pairs={{0,1},{1,0},{2,3},{3,2},{4,5},{5,4},{6,7},{7,6},{8,9},{9,8},{10,11... | collective-permute-start | bytes 196616 | tf_op jit(solution)/shard_map/ppermute | solution.py:345
  75.9 0.8 copy-start.5
  83.8 0.8 copy-start.3
  84.6 16.2 %all-to-all-start.2 = ((bf16[8,1,32,896]{3,2,1,0:T(8,128)(2,1)}), bf16[8,1,32,896]{3,2,1,0:T(8,128)(2,1)S(1)}, u32[]{:S(2)}, u32[]{:S(2)}) async-start(bf16[8,1,32,896]{3,2,1,0:T(8,128)(2,1)} %get-tuple-element.81), calls=%async_computation.2 | async-start | bytes 917504 | tf_op jit(solution)/shard_map/all_to_all | solution.py:482
  88.1 12.7 %collective-permute-start.13 = (bf16[256,896]{1,0:T(8,128)(2,1)}, bf16[256,896]{1,0:T(8,128)(2,1)S(1)}, u32[]{:S(2)}, u32[]{:S(2)}) collective-permute-start(bf16[256,896]{1,0:T(8,128)(2,1)} %copy-done.5), channel_id=1, source_target_pairs={{8,0},{16,8},{24,16},{9,1},{17,9},{25,17},{10,2},{18,10},{26,18},{... | collective-permute-start | bytes 1376264 | tf_op jit(solution)/shard_map/ppermute | solution.py:479
  89.4 11.4 %collective-permute-start.14 = (bf16[256,896]{1,0:T(8,128)(2,1)}, bf16[256,896]{1,0:T(8,128)(2,1)}, u32[]{:S(2)}, u32[]{:S(2)}) collective-permute-start(bf16[256,896]{1,0:T(8,128)(2,1)} %copy-done.3), channel_id=1, source_target_pairs={{8,0},{16,8},{24,16},{9,1},{17,9},{25,17},{10,2},{18,10},{26,18},{... | collective-permute-start | bytes 1376264 | tf_op jit(solution)/shard_map/ppermute | solution.py:479
  92.3 8.5 %collective-permute-start.15 = (bf16[192,512]{1,0:T(8,128)(2,1)}, bf16[192,512]{1,0:T(8,128)(2,1)S(1)}, u32[]{:S(2)}, u32[]{:S(2)}) collective-permute-start(bf16[192,512]{1,0:T(8,128)(2,1)} %pad_maximum_fusion.1), channel_id=1, source_target_pairs={{0,1},{1,0},{2,3},{3,2},{4,5},{5,4},{6,7},{7,6},{8,9},{9,8},{10,11... | collective-permute-start | bytes 589832 | tf_op jit(solution)/shard_map/ppermute | solution.py:345
  94.4 6.4 %copy-start.4 = (bf16[64,512]{1,0:T(8,128)(2,1)S(1)}, bf16[64,512]{1,0:T(8,128)(2,1)}, u32[]{:S(2)}) copy-start(bf16[64,512]{1,0:T(8,128)(2,1)} %get-tuple-element.80.rest_0_) | copy-start | bytes 196612
  96.3 1.3 %copy-start = (f32[2,896,256]{2,1,0:T(8,128)}, f32[2,896,256]{2,1,0:T(8,128)S(1)}, u32[]{:S(2)}) copy-start(f32[2,896,256]{2,1,0:T(8,128)S(1)} %first_terms.1.part_ref) | copy-start | bytes 5505028
  100.8 1.5 %copy-start.1 = (f32[2,896,256]{2,1,0:T(8,128)S(1)}, f32[2,896,256]{2,1,0:T(8,128)}, u32[]{:S(2)}) copy-start(f32[2,896,256]{2,1,0:T(8,128)} %copy-done) | copy-start | bytes 5505028

commit v8 on v7

--- a/solution.py
+++ b/solution.py
@@ -415,14 +415,15 @@
     for at, start in ((0, 0), (1, lat + LANES)):
         down = first_ref[:, :rows, start : start + lat].reshape(total, lat)
         up = first_ref[:, rows:, start : start + lat].reshape(total, lat)
-        out_ref[at] = rows_dot(d_ref[:, at].reshape(total, share), down) + rows_dot(u_ref[:, at].reshape(total, share), up)
+        both = rows_dot(d_ref[:, at].reshape(total, share), down)
+        out_ref[at] = (both + rows_dot(u_ref[:, at].reshape(total, share), up)).astype(BF16)
 
 
 def first_terms(d, u, first, lat):
     share = d.shape[3]
     return pl.pallas_call(
         first_terms_kernel,
-        out_shape=shape(2, share, lat, dtype=F32),
+        out_shape=shape(2, share, lat),
         in_specs=[VMEM] * 3,
         out_specs=VMEM,
         compiler_params=pltpu.CompilerParams(vmem_limit_bytes=LATE),
@@ -441,10 +442,10 @@
     def half(i, start):
         return second_ref[:, i * rows : (i + 1) * rows, start : start + lat].reshape(total, lat)
 
-    first = part_ref[0] + rows_dot(d_ref[:, 2].reshape(total, share), half(0, 0))
+    first = part_ref[0].astype(F32) + rows_dot(d_ref[:, 2].reshape(total, share), half(0, 0))
     first += rows_dot(x1_ref[:, 0].reshape(total, share), half(1, 0))
     out_ref[0, 0] = (first * g_ref[...].astype(F32)).astype(BF16)
-    second = part_ref[1] + rows_dot(y1d_ref[...], half(0, lat))
+    second = part_ref[1].astype(F32) + rows_dot(y1d_ref[...], half(0, lat))
     second += rows_dot(y1u_ref[...], half(1, lat))
     out_ref[0, 1] = second.astype(BF16)
 

time: 107 us -> 107 us (level)
    unnamed x14 -> x18, local copies, waits for them, and re-layouts: 4.28 us -> 4.4 us
where the time goes in v8:
time: 107 us; the launch traced here: 106 us
  Pallas kernels  40.1 us (37%)
  starting transfers between devices  36.4 us (34%)
  waiting for transfers between devices  18.1 us (17%)
  local copies, waits for them, and re-layouts  7.71 us (7%)
  other arithmetic  3.23 us (3%)
    all_to_all x3, starting transfers between devices, exchange(): return lax.all_to_all(blocks, 'dp', 0, 0, tiled=True)  15 us
    ppermute x9, starting transfers between devices, across(): return lax.ppermute(held, axis, [(i, i ^ apart) for i in range(parts)])  13.8 us
    ppermute x9, waiting for transfers between devices, across(): return lax.ppermute(held, axis, [(i, i ^ apart) for i in range(parts)])  8.07 us
    pallas_call x1, Pallas kernels, first_step(): pl.pallas_call(functools.partial(first_kernel, before is None), out_shape...  7.87 us
    pallas_call x1, Pallas kernels, second_step(): pl.pallas_call(second_kernel, out_shape=[shape(2 * rows, 2 * lat), shape(...  6.72 us
    all_to_all x3, waiting for transfers between devices, exchange(): return lax.all_to_all(blocks, 'dp', 0, 0, tiled=True)  5.57 us
    ppermute x4, starting transfers between devices, to_before(): return lax.ppermute(block, 'pipe', [(i + 1, i) for i in range(ranks - 1)])  5.17 us
    pallas_call x1, Pallas kernels, input_step(): pl.pallas_call(input_kernel, out_shape=[shape(rows, width), shape(parts,...  4.92 us
  transfers between devices with their start and end apart: 19, of which 5 were waited for; matrix products, arithmetic and copies ran while one was open for 6% of the time, Pallas kernels for 32%

profile of v8, /device:TPU:0, one launch (start us, length us, event | category | flops | bytes accessed | tf_op | source)
XLA Modules:
  0.0 105.7 jit_solution(5226907926337967056)
XLA Ops:
  0.0 3.6 %prepare.1 = (bf16[8,3,32,896]{3,2,1,0:T(8,128)(2,1)}, bf16[32,7168]{1,0:T(8,128)(2,1)}, bf16[32,7168]{1,0:T(8,128)(2,1)}, bf16[32,7168]{1,0:T(8,128)(2,1)}) custom-call(bf16[1,2,32,7168]{3,2,1,0:T(8,128)(2,1)} %x_ref, bf16[1,2,32,7168]{3,2,1,0:T(8,128)(2,1)} %up_ref.1, bf16[2,1,32,7168]{3,2,1,0:T(8,128)(2,1)} %y_ref), custom_call_target="tpu_custom_call" | custom-call | flops 1 | bytes 1 | tf_op jit(solution)/shard_map/prepare/pallas_call | solution.py:94
  3.6 7.3 %all-to-all-start = ((bf16[8,3,32,896]{3,2,1,0:T(8,128)(2,1)}), bf16[8,3,32,896]{3,2,1,0:T(8,128)(2,1)S(1)}, u32[]{:S(2)}, u32[]{:S(2)}) async-start(bf16[8,3,32,896]{3,2,1,0:T(8,128)(2,1)} %get-tuple-element.64), calls=%async_computation | async-start | bytes 2752512 | tf_op jit(solution)/shard_map/all_to_all | solution.py:483
  10.9 0.7 collective-permute-start
  11.6 1.1 %collective-permute-start.1 = (bf16[32,7168]{1,0:T(8,128)(2,1)}, bf16[32,7168]{1,0:T(8,128)(2,1)}, u32[]{:S(2)}, u32[]{:S(2)}) collective-permute-start(bf16[32,7168]{1,0:T(8,128)(2,1)} %get-tuple-element.56), channel_id=1, source_target_pairs={{0,24},{8,16},{16,8},{24,0},{1,25},{9,17},{17,9},{25,1},{2,26},{10... | collective-permute-start | bytes 1376264 | tf_op jit(solution)/shard_map/ppermute | solution.py:477
  12.7 0.7 collective-permute-start.2
  13.3 7.9 %first_step.1 = (bf16[32,7168]{1,0:T(8,128)(2,1)}, bf16[32,640]{1,0:T(8,128)(2,1)}, bf16[32,256]{1,0:T(8,128)(2,1)}, f32[32,256]{1,0:T(8,128)}, f32[32,128]{1,0:T(8,128)}) custom-call(bf16[1,2,32,7168]{3,2,1,0:T(8,128)(2,1)} %x_ref, bf16[2,1,32,7168]{3,2,1,0:T(8,128)(2,1)} %y_ref, bf16[1,2,7168,256]{3,2,1,0:T(8,128)(2,1)} %w_ref.9, bf16[1,7168]{1,0:T(2,128)(2,1)} %g_ref.7, ...), custom_call_target="tpu_custom_call" | custom-call | flops 1 | bytes 1 | tf_op jit(solution)/shard_map/first_step/pallas_call | solution.py:199
  21.2 1.3 %collective-permute-start.3 = (bf16[32,7168]{1,0:T(8,128)(2,1)}, bf16[32,7168]{1,0:T(8,128)(2,1)}, u32[]{:S(2)}, u32[]{:S(2)}) collective-permute-start(bf16[32,7168]{1,0:T(8,128)(2,1)} %get-tuple-element.63), channel_id=1, source_target_pairs={{8,0},{16,8},{24,16},{9,1},{17,9},{25,17},{10,2},{18,10},{26,18},{... | collective-permute-start | bytes 1376264 | tf_op jit(solution)/shard_map/ppermute | solution.py:480
  22.5 0.7 constant_dynamic-slice_fusion.g_ref
  23.2 0.7 fusion
  23.9 1.0 constant_dynamic-slice_fusion.1.down_ref
  25.0 0.0 collective-permute-done.x_ref
  25.0 4.4 %latent_side.1 = (bf16[32,256]{1,0:T(8,128)(2,1)}, f32[32,256]{1,0:T(8,128)}, f32[32,128]{1,0:T(8,128)}) custom-call(bf16[32,7168]{1,0:T(8,128)(2,1)} %collective-permute-done.x_ref, bf16[1,2,7168,256]{3,2,1,0:T(8,128)(2,1)} %w_ref.9, bf16[1,7168]{1,0:T(2,128)(2,1)} %g_ref.7, bf16[1,256]{1,0:T(2,128)(2,1)} %h_ref.7), custom_call_target="tpu_custom_call" | custom-call | flops 1 | bytes 1 | tf_op jit(solution)/shard_map/latent_side/pallas_call | solution.py:223
  29.4 4.4 %collective-permute-done.1.y_ref = bf16[32,7168]{1,0:T(8,128)(2,1)} collective-permute-done((bf16[32,7168]{1,0:T(8,128)(2,1)}, bf16[32,7168]{1,0:T(8,128)(2,1)}, u32[]{:S(2)}, u32[]{:S(2)}) %collective-permute-start.1) | collective-permute-done | bytes 458784 | tf_op jit(solution)/shard_map/ppermute | solution.py:477
  33.8 4.6 %narrow_step.1.narrow_ref.rest_0_ = bf16[64,640]{1,0:T(8,128)(2,1)} custom-call(bf16[32,7168]{1,0:T(8,128)(2,1)} %collective-permute-done.1.y_ref, bf16[1,2,7168,256]{3,2,1,0:T(8,128)(2,1)} %w_ref.9, bf16[1,256]{1,0:T(2,128)(2,1)} %h_ref.7, bf16[32,256]{1,0:T(8,128)(2,1)} %get-tuple-element.57.k_ref, f32[32,256]{1,0:T(8,128)} %get-tuple-element.58.c_ref, ...), custom_call_target="tpu_custom_call" | custom-call | flops 1 | bytes 1 | tf_op jit(solution)/shard_map/narrow_step/pallas_call | solution.py:250
  38.4 0.0 copy-start.2
  38.4 3.9 %collective-permute-start.4 = (bf16[64,640]{1,0:T(8,128)(2,1)}, bf16[64,640]{1,0:T(8,128)(2,1)S(1)}, u32[]{:S(2)}, u32[]{:S(2)}) collective-permute-start(bf16[64,640]{1,0:T(8,128)(2,1)} %narrow_step.1.narrow_ref.rest_0_), channel_id=1, source_target_pairs={{0,6},{1,7},{2,4},{3,5},{4,2},{5,3},{6,0},{7,1},{8,14},{9,15},{10,... | collective-permute-start | bytes 245768 | tf_op jit(solution)/shard_map/ppermute | solution.py:335
  42.3 0.0 collective-permute-start.5
  42.3 0.6 collective-permute-start.6
  43.0 4.9 %input_step.1 = (bf16[32,7168]{1,0:T(8,128)(2,1)}, bf16[8,2,32,896]{3,2,1,0:T(8,128)(2,1)}) custom-call(bf16[32,7168]{1,0:T(8,128)(2,1)} %collective-permute-done.x_ref, bf16[32,7168]{1,0:T(8,128)(2,1)} %collective-permute-done.1.y_ref, bf16[1,2,7168,256]{3,2,1,0:T(8,128)(2,1)} %w_ref.9, bf16[1,7168]{1,0:T(2,128)(2,1)} %g_ref.7, ...), custom_call_target="tpu_custom_call" | custom-call | flops 1 | bytes 1 | tf_op jit(solution)/shard_map/input_step/pallas_call | solution.py:281
  47.9 0.0 collective-permute-done.2.x_ref
  47.9 0.0 collective-permute-done.3.y0_ref
  47.9 0.0 collective-permute-done.4.rest_1_
  47.9 2.9 %collective-permute-done.5.rest_2_ = bf16[64,640]{1,0:T(8,128)(2,1)} collective-permute-done((bf16[64,640]{1,0:T(8,128)(2,1)}, bf16[64,640]{1,0:T(8,128)(2,1)}, u32[]{:S(2)}, u32[]{:S(2)}) %collective-permute-start.5) | collective-permute-done | bytes 81952 | tf_op jit(solution)/shard_map/ppermute | solution.py:335
  50.8 0.0 collective-permute-done.6.rest_3_
  50.8 0.0 all-to-all-done.d_ref
  50.8 4.2 %all-to-all-start.1 = ((bf16[8,2,32,896]{3,2,1,0:T(8,128)(2,1)}), bf16[8,2,32,896]{3,2,1,0:T(8,128)(2,1)}, u32[]{:S(2)}, u32[]{:S(2)}) async-start(bf16[8,2,32,896]{3,2,1,0:T(8,128)(2,1)} %get-tuple-element.66), calls=%async_computation.1 | async-start | bytes 1835008 | tf_op jit(solution)/shard_map/all_to_all | solution.py:483
  55.1 1.3 %collective-permute-start.8 = (bf16[32,7168]{1,0:T(8,128)(2,1)}, bf16[32,7168]{1,0:T(8,128)(2,1)}, u32[]{:S(2)}, u32[]{:S(2)}) collective-permute-start(bf16[32,7168]{1,0:T(8,128)(2,1)} %get-tuple-element.75), channel_id=1, source_target_pairs={{8,0},{16,8},{24,16},{9,1},{17,9},{25,17},{10,2},{18,10},{26,18},{... | collective-permute-start | bytes 1376264 | tf_op jit(solution)/shard_map/ppermute | solution.py:480
  56.4 1.7 %pad_maximum_fusion = bf16[256,640]{1,0:T(8,128)(2,1)} fusion(bf16[64,640]{1,0:T(8,128)(2,1)} %collective-permute-done.6.rest_3_, bf16[64,640]{1,0:T(8,128)(2,1)} %collective-permute-done.5.rest_2_, bf16[64,640]{1,0:T(8,128)(2,1)S(1)} %collective-permute-done.4.rest_1_, bf16[64,640]{1,0:T(8,128)(2,1)S(1)} %copy-done.2), kind=kLoop, calls=%fused_computation | loop fusion | flops 1310720 | bytes 655360 | tf_op jit(solution)/shard_map/concatenate | solution.py:338
  58.0 1.9 %collective-permute-start.7 = (bf16[256,640]{1,0:T(8,128)(2,1)}, bf16[256,640]{1,0:T(8,128)(2,1)}, u32[]{:S(2)}, u32[]{:S(2)}) collective-permute-start(bf16[256,640]{1,0:T(8,128)(2,1)} %pad_maximum_fusion), channel_id=1, source_target_pairs={{0,1},{1,0},{2,3},{3,2},{4,5},{5,4},{6,7},{7,6},{8,9},{9,8},{10,11... | collective-permute-start | bytes 983048 | tf_op jit(solution)/shard_map/ppermute | solution.py:335
  59.9 0.0 collective-permute-done.8.y1_ref
  59.9 6.7 %second_step.1 = (bf16[64,512]{1,0:T(8,128)(2,1)}, bf16[8,1,32,896]{3,2,1,0:T(8,128)(2,1)}) custom-call(bf16[32,7168]{1,0:T(8,128)(2,1)} %collective-permute-done.2.x_ref, bf16[32,7168]{1,0:T(8,128)(2,1)} %collective-permute-done.3.y0_ref, bf16[32,7168]{1,0:T(8,128)(2,1)} %collective-permute-done.8.y1_ref, bf16[1,2,7168,256]{3,2,1,0:T(8,128)(2,1)} %w_ref.9, ...), custom_call_target="tpu_custom_call" | custom-call | flops 1 | bytes 1 | tf_op jit(solution)/shard_map/second_step/pallas_call | solution.py:314
  66.7 3.4 %collective-permute-start.9 = (bf16[64,512]{1,0:T(8,128)(2,1)}, bf16[64,512]{1,0:T(8,128)(2,1)S(1)}, u32[]{:S(2)}, u32[]{:S(2)}) collective-permute-start(bf16[64,512]{1,0:T(8,128)(2,1)} %get-tuple-element.80.rest_0_), channel_id=1, source_target_pairs={{0,6},{1,7},{2,4},{3,5},{4,2},{5,3},{6,0},{7,1},{8,14},{9,15},{10,... | collective-permute-start | bytes 196616 | tf_op jit(solution)/shard_map/ppermute | solution.py:345
  70.0 0.0 collective-permute-start.10
  70.0 1.1 %collective-permute-start.11 = (bf16[64,512]{1,0:T(8,128)(2,1)}, bf16[64,512]{1,0:T(8,128)(2,1)}, u32[]{:S(2)}, u32[]{:S(2)}) collective-permute-start(bf16[64,512]{1,0:T(8,128)(2,1)} %get-tuple-element.80.rest_0_), channel_id=1, source_target_pairs={{0,2},{1,3},{2,0},{3,1},{4,6},{5,7},{6,4},{7,5},{8,10},{9,11},{10,... | collective-permute-start | bytes 196616 | tf_op jit(solution)/shard_map/ppermute | solution.py:345
  71.1 1.1 %collective-permute-start.12 = (bf16[64,512]{1,0:T(8,128)(2,1)}, bf16[64,512]{1,0:T(8,128)(2,1)}, u32[]{:S(2)}, u32[]{:S(2)}) collective-permute-start(bf16[64,512]{1,0:T(8,128)(2,1)} %get-tuple-element.80.rest_0_), channel_id=1, source_target_pairs={{0,1},{1,0},{2,3},{3,2},{4,5},{5,4},{6,7},{7,6},{8,9},{9,8},{10,11... | collective-permute-start | bytes 196616 | tf_op jit(solution)/shard_map/ppermute | solution.py:345
  72.2 2.2 %collective-permute-done.7.rest_4_ = bf16[256,640]{1,0:T(8,128)(2,1)} collective-permute-done((bf16[256,640]{1,0:T(8,128)(2,1)}, bf16[256,640]{1,0:T(8,128)(2,1)}, u32[]{:S(2)}, u32[]{:S(2)}) %collective-permute-start.7) | collective-permute-done | bytes 327712 | tf_op jit(solution)/shard_map/ppermute | solution.py:335
  74.4 1.5 %columns_first.1 = (bf16[256,896]{1,0:T(8,128)(2,1)S(1)}, bf16[8,64,640]{2,1,0:T(8,128)(2,1)S(1)}) custom-call(s32[1]{0:T(128)} %bitcast.j_ref, bf16[8,3,32,896]{3,2,1,0:T(8,128)(2,1)S(1)} %all-to-all-done.d_ref, bf16[1,1,896,256]{3,2,1,0:T(8,128)(2,1)S(1)} %constant_dynamic-slice_fusion.1.down_ref, bf16[1,896]{1,0:T(2,128)(2,1)S(1)} %constant_dynamic-slice_fusion.g_ref, ...), custom_call_target="tpu_custom_call" | custom-call | flops 1 | bytes 1 | tf_op jit(solution)/shard_map/columns_first/pallas_call | solution.py:386
  75.9 0.0 copy-start.8
  75.9 0.8 copy-done.8
  76.7 5.6 %all-to-all-done.1.u_ref = bf16[8,2,32,896]{3,2,1,0:T(8,128)(2,1)} async-done(((bf16[8,2,32,896]{3,2,1,0:T(8,128)(2,1)}), bf16[8,2,32,896]{3,2,1,0:T(8,128)(2,1)}, u32[]{:S(2)}, u32[]{:S(2)}) %all-to-all-start.1) | async-done | bytes 917536 | tf_op jit(solution)/shard_map/all_to_all | solution.py:483
  82.3 1.6 %columns_next.1 = bf16[256,896]{1,0:T(8,128)(2,1)S(1)} custom-call(bf16[8,2,32,896]{3,2,1,0:T(8,128)(2,1)} %all-to-all-done.1.u_ref, bf16[1,1,896,256]{3,2,1,0:T(8,128)(2,1)S(1)} %constant_dynamic-slice_fusion.1.down_ref, bf16[1,896]{1,0:T(2,128)(2,1)S(1)} %constant_dynamic-slice_fusion.g_ref, bf16[8,64,640]{2,1,0:T(8,128)(2,1)S(1)} %get-tuple-element.72.narrow_ref.first_ref), custom_call_target="tpu_custom_call" | custom-call | flops 1 | bytes 1 | tf_op jit(solution)/shard_map/columns_next/pallas_call | solution.py:400
  83.8 0.0 copy-start.4
  83.8 0.8 copy-done.4
  84.6 0.0 collective-permute-done.9.rest_1_
  84.6 0.0 collective-permute-done.10.rest_2_
  84.6 0.0 collective-permute-done.11.rest_3_
  84.6 0.0 collective-permute-done.12.rest_4_
  84.6 3.5 %all-to-all-start.2 = ((bf16[8,1,32,896]{3,2,1,0:T(8,128)(2,1)}), bf16[8,1,32,896]{3,2,1,0:T(8,128)(2,1)S(1)}, u32[]{:S(2)}, u32[]{:S(2)}) async-start(bf16[8,1,32,896]{3,2,1,0:T(8,128)(2,1)} %get-tuple-element.81), calls=%async_computation.2 | async-start | bytes 917504 | tf_op jit(solution)/shard_map/all_to_all | solution.py:483
  88.1 1.3 %collective-permute-start.13 = (bf16[256,896]{1,0:T(8,128)(2,1)}, bf16[256,896]{1,0:T(8,128)(2,1)}, u32[]{:S(2)}, u32[]{:S(2)}) collective-permute-start(bf16[256,896]{1,0:T(8,128)(2,1)} %copy-done.8), channel_id=1, source_target_pairs={{8,0},{16,8},{24,16},{9,1},{17,9},{25,17},{10,2},{18,10},{26,18},{... | collective-permute-start | bytes 1376264 | tf_op jit(solution)/shard_map/ppermute | solution.py:480
  89.4 1.3 %collective-permute-start.14 = (bf16[256,896]{1,0:T(8,128)(2,1)}, bf16[256,896]{1,0:T(8,128)(2,1)}, u32[]{:S(2)}, u32[]{:S(2)}) collective-permute-start(bf16[256,896]{1,0:T(8,128)(2,1)} %copy-done.4), channel_id=1, source_target_pairs={{8,0},{16,8},{24,16},{9,1},{17,9},{25,17},{10,2},{18,10},{26,18},{... | collective-permute-start | bytes 1376264 | tf_op jit(solution)/shard_map/ppermute | solution.py:480
  90.7 1.6 %pad_maximum_fusion.1 = bf16[192,512]{1,0:T(8,128)(2,1)} fusion(bf16[64,512]{1,0:T(8,128)(2,1)} %collective-permute-done.11.rest_3_, bf16[64,512]{1,0:T(8,128)(2,1)} %collective-permute-done.10.rest_2_, bf16[64,512]{1,0:T(8,128)(2,1)S(1)} %collective-permute-done.9.rest_1_), kind=kLoop, calls=%fused_computation.1 | loop fusion | flops 589824 | bytes 393216 | tf_op jit(solution)/shard_map/concatenate | solution.py:348
  92.3 1.9 %collective-permute-start.15 = (bf16[192,512]{1,0:T(8,128)(2,1)}, bf16[192,512]{1,0:T(8,128)(2,1)}, u32[]{:S(2)}, u32[]{:S(2)}) collective-permute-start(bf16[192,512]{1,0:T(8,128)(2,1)} %pad_maximum_fusion.1), channel_id=1, source_target_pairs={{0,1},{1,0},{2,3},{3,2},{4,5},{5,4},{6,7},{7,6},{8,9},{9,8},{10,11... | collective-permute-start | bytes 589832 | tf_op jit(solution)/shard_map/ppermute | solution.py:345
  94.2 0.9 copy.7.g_ref
  95.1 1.1 %copy-done.1 = bf16[8,64,640]{2,1,0:T(8,128)(2,1)S(1)} copy-done((bf16[8,64,640]{2,1,0:T(8,128)(2,1)S(1)}, bf16[8,64,640]{2,1,0:T(8,128)(2,1)}, u32[]{:S(2)}) %copy-start.1) | copy-done | bytes 655384
  96.2 1.9 %first_terms.1.part_ref = bf16[2,896,256]{2,1,0:T(8,128)(2,1)S(1)} custom-call(bf16[8,3,32,896]{3,2,1,0:T(8,128)(2,1)S(1)} %all-to-all-done.d_ref, bf16[8,2,32,896]{3,2,1,0:T(8,128)(2,1)} %all-to-all-done.1.u_ref, bf16[8,64,640]{2,1,0:T(8,128)(2,1)S(1)} %copy-done.1), custom_call_target="tpu_custom_call" | custom-call | flops 1 | bytes 1 | tf_op jit(solution)/shard_map/first_terms/pallas_call | solution.py:424
  98.0 2.9 %collective-permute-done.15.rest_5_ = bf16[192,512]{1,0:T(8,128)(2,1)} collective-permute-done((bf16[192,512]{1,0:T(8,128)(2,1)}, bf16[192,512]{1,0:T(8,128)(2,1)}, u32[]{:S(2)}, u32[]{:S(2)}) %collective-permute-start.15) | collective-permute-done | bytes 196640 | tf_op jit(solution)/shard_map/ppermute | solution.py:345
  100.9 0.0 collective-permute-done.13.y1d_ref
  100.9 0.0 collective-permute-done.14.y1u_ref
  100.9 0.0 all-to-all-done.2.x1_ref
  100.9 0.0 copy-done.7
  101.0 0.0 copy-start.3
  101.0 0.9 copy-done.3
  101.9 0.8 copy-done.6
  102.7 3.0 %terms.1 = bf16[1,2,896,256]{3,2,1,0:T(8,128)(2,1)} custom-call(s32[1]{0:T(128)} %bitcast.j_ref, bf16[8,3,32,896]{3,2,1,0:T(8,128)(2,1)S(1)} %all-to-all-done.d_ref, bf16[8,1,32,896]{3,2,1,0:T(8,128)(2,1)S(1)} %all-to-all-done.2.x1_ref, bf16[256,896]{1,0:T(8,128)(2,1)} %collective-permute-done.13.y1d_ref, bf16[256,896]{1,0:T(8,128)(2,1)} %collective-permute-done.14.y1u_ref, ...), custom_call_target="tpu_custom_call" | custom-call | flops 1 | bytes 1 | tf_op jit(solution)/shard_map/terms/pallas_call | solution.py:456
  (8 shorter events, 0.0 us)
Async XLA Ops:
  3.6 47.2 %all-to-all-start = ((bf16[8,3,32,896]{3,2,1,0:T(8,128)(2,1)}), bf16[8,3,32,896]{3,2,1,0:T(8,128)(2,1)S(1)}, u32[]{:S(2)}, u32[]{:S(2)}) async-start(bf16[8,3,32,896]{3,2,1,0:T(8,128)(2,1)} %get-tuple-element.64), calls=%async_computation | async-start | bytes 2752512 | tf_op jit(solution)/shard_map/all_to_all | solution.py:483
  10.9 14.1 %collective-permute-start = (bf16[32,7168]{1,0:T(8,128)(2,1)}, bf16[32,7168]{1,0:T(8,128)(2,1)}, u32[]{:S(2)}, u32[]{:S(2)}) collective-permute-start(bf16[32,7168]{1,0:T(8,128)(2,1)} %get-tuple-element.51), channel_id=1, source_target_pairs={{0,24},{8,16},{16,8},{24,0},{1,25},{9,17},{17,9},{25,1},{2,26},{10... | collective-permute-start | bytes 1376264 | tf_op jit(solution)/shard_map/ppermute | solution.py:477
  11.6 22.2 %collective-permute-start.1 = (bf16[32,7168]{1,0:T(8,128)(2,1)}, bf16[32,7168]{1,0:T(8,128)(2,1)}, u32[]{:S(2)}, u32[]{:S(2)}) collective-permute-start(bf16[32,7168]{1,0:T(8,128)(2,1)} %get-tuple-element.56), channel_id=1, source_target_pairs={{0,24},{8,16},{16,8},{24,0},{1,25},{9,17},{17,9},{25,1},{2,26},{10... | collective-permute-start | bytes 1376264 | tf_op jit(solution)/shard_map/ppermute | solution.py:477
  12.7 35.2 %collective-permute-start.2 = (bf16[32,7168]{1,0:T(8,128)(2,1)}, bf16[32,7168]{1,0:T(8,128)(2,1)}, u32[]{:S(2)}, u32[]{:S(2)}) collective-permute-start(bf16[32,7168]{1,0:T(8,128)(2,1)} %get-tuple-element.62), channel_id=1, source_target_pairs={{0,24},{8,16},{16,8},{24,0},{1,25},{9,17},{17,9},{25,1},{2,26},{10... | collective-permute-start | bytes 1376264 | tf_op jit(solution)/shard_map/ppermute | solution.py:477
  21.2 26.7 %collective-permute-start.3 = (bf16[32,7168]{1,0:T(8,128)(2,1)}, bf16[32,7168]{1,0:T(8,128)(2,1)}, u32[]{:S(2)}, u32[]{:S(2)}) collective-permute-start(bf16[32,7168]{1,0:T(8,128)(2,1)} %get-tuple-element.63), channel_id=1, source_target_pairs={{8,0},{16,8},{24,16},{9,1},{17,9},{25,17},{10,2},{18,10},{26,18},{... | collective-permute-start | bytes 1376264 | tf_op jit(solution)/shard_map/ppermute | solution.py:480
  38.4 17.9 %copy-start.2 = (bf16[64,640]{1,0:T(8,128)(2,1)S(1)}, bf16[64,640]{1,0:T(8,128)(2,1)}, u32[]{:S(2)}) copy-start(bf16[64,640]{1,0:T(8,128)(2,1)} %narrow_step.1.narrow_ref.rest_0_) | copy-start | bytes 245764
  38.4 9.5 %collective-permute-start.4 = (bf16[64,640]{1,0:T(8,128)(2,1)}, bf16[64,640]{1,0:T(8,128)(2,1)S(1)}, u32[]{:S(2)}, u32[]{:S(2)}) collective-permute-start(bf16[64,640]{1,0:T(8,128)(2,1)} %narrow_step.1.narrow_ref.rest_0_), channel_id=1, source_target_pairs={{0,6},{1,7},{2,4},{3,5},{4,2},{5,3},{6,0},{7,1},{8,14},{9,15},{10,... | collective-permute-start | bytes 245768 | tf_op jit(solution)/shard_map/ppermute | solution.py:335
  42.3 8.5 %collective-permute-start.5 = (bf16[64,640]{1,0:T(8,128)(2,1)}, bf16[64,640]{1,0:T(8,128)(2,1)}, u32[]{:S(2)}, u32[]{:S(2)}) collective-permute-start(bf16[64,640]{1,0:T(8,128)(2,1)} %narrow_step.1.narrow_ref.rest_0_), channel_id=1, source_target_pairs={{0,4},{1,5},{2,6},{3,7},{4,0},{5,1},{6,2},{7,3},{8,12},{9,13},{10,... | collective-permute-start | bytes 245768 | tf_op jit(solution)/shard_map/ppermute | solution.py:335
  42.3 8.5 %collective-permute-start.6 = (bf16[64,640]{1,0:T(8,128)(2,1)}, bf16[64,640]{1,0:T(8,128)(2,1)}, u32[]{:S(2)}, u32[]{:S(2)}) collective-permute-start(bf16[64,640]{1,0:T(8,128)(2,1)} %narrow_step.1.narrow_ref.rest_0_), channel_id=1, source_target_pairs={{0,2},{1,3},{2,0},{3,1},{4,6},{5,7},{6,4},{7,5},{8,10},{9,11},{10,... | collective-permute-start | bytes 245768 | tf_op jit(solution)/shard_map/ppermute | solution.py:335
  50.8 31.4 %all-to-all-start.1 = ((bf16[8,2,32,896]{3,2,1,0:T(8,128)(2,1)}), bf16[8,2,32,896]{3,2,1,0:T(8,128)(2,1)}, u32[]{:S(2)}, u32[]{:S(2)}) async-start(bf16[8,2,32,896]{3,2,1,0:T(8,128)(2,1)} %get-tuple-element.66), calls=%async_computation.1 | async-start | bytes 1835008 | tf_op jit(solution)/shard_map/all_to_all | solution.py:483
  55.1 4.9 %collective-permute-start.8 = (bf16[32,7168]{1,0:T(8,128)(2,1)}, bf16[32,7168]{1,0:T(8,128)(2,1)}, u32[]{:S(2)}, u32[]{:S(2)}) collective-permute-start(bf16[32,7168]{1,0:T(8,128)(2,1)} %get-tuple-element.75), channel_id=1, source_target_pairs={{8,0},{16,8},{24,16},{9,1},{17,9},{25,17},{10,2},{18,10},{26,18},{... | collective-permute-start | bytes 1376264 | tf_op jit(solution)/shard_map/ppermute | solution.py:480
  58.0 16.4 %collective-permute-start.7 = (bf16[256,640]{1,0:T(8,128)(2,1)}, bf16[256,640]{1,0:T(8,128)(2,1)}, u32[]{:S(2)}, u32[]{:S(2)}) collective-permute-start(bf16[256,640]{1,0:T(8,128)(2,1)} %pad_maximum_fusion), channel_id=1, source_target_pairs={{0,1},{1,0},{2,3},{3,2},{4,5},{5,4},{6,7},{7,6},{8,9},{9,8},{10,11... | collective-permute-start | bytes 983048 | tf_op jit(solution)/shard_map/ppermute | solution.py:335
  66.7 17.9 %collective-permute-start.9 = (bf16[64,512]{1,0:T(8,128)(2,1)}, bf16[64,512]{1,0:T(8,128)(2,1)S(1)}, u32[]{:S(2)}, u32[]{:S(2)}) collective-permute-start(bf16[64,512]{1,0:T(8,128)(2,1)} %get-tuple-element.80.rest_0_), channel_id=1, source_target_pairs={{0,6},{1,7},{2,4},{3,5},{4,2},{5,3},{6,0},{7,1},{8,14},{9,15},{10,... | collective-permute-start | bytes 196616 | tf_op jit(solution)/shard_map/ppermute | solution.py:345
  70.0 14.6 %collective-permute-start.10 = (bf16[64,512]{1,0:T(8,128)(2,1)}, bf16[64,512]{1,0:T(8,128)(2,1)}, u32[]{:S(2)}, u32[]{:S(2)}) collective-permute-start(bf16[64,512]{1,0:T(8,128)(2,1)} %get-tuple-element.80.rest_0_), channel_id=1, source_target_pairs={{0,4},{1,5},{2,6},{3,7},{4,0},{5,1},{6,2},{7,3},{8,12},{9,13},{10,... | collective-permute-start | bytes 196616 | tf_op jit(solution)/shard_map/ppermute | solution.py:345
  70.0 14.6 %collective-permute-start.11 = (bf16[64,512]{1,0:T(8,128)(2,1)}, bf16[64,512]{1,0:T(8,128)(2,1)}, u32[]{:S(2)}, u32[]{:S(2)}) collective-permute-start(bf16[64,512]{1,0:T(8,128)(2,1)} %get-tuple-element.80.rest_0_), channel_id=1, source_target_pairs={{0,2},{1,3},{2,0},{3,1},{4,6},{5,7},{6,4},{7,5},{8,10},{9,11},{10,... | collective-permute-start | bytes 196616 | tf_op jit(solution)/shard_map/ppermute | solution.py:345
  71.1 13.5 %collective-permute-start.12 = (bf16[64,512]{1,0:T(8,128)(2,1)}, bf16[64,512]{1,0:T(8,128)(2,1)}, u32[]{:S(2)}, u32[]{:S(2)}) collective-permute-start(bf16[64,512]{1,0:T(8,128)(2,1)} %get-tuple-element.80.rest_0_), channel_id=1, source_target_pairs={{0,1},{1,0},{2,3},{3,2},{4,5},{5,4},{6,7},{7,6},{8,9},{9,8},{10,11... | collective-permute-start | bytes 196616 | tf_op jit(solution)/shard_map/ppermute | solution.py:345
  75.9 0.8 copy-start.8
  76.7 17.5 %copy-start = (bf16[8,64,640]{2,1,0:T(8,128)(2,1)}, bf16[8,64,640]{2,1,0:T(8,128)(2,1)S(1)}, u32[]{:S(2)}) copy-start(bf16[8,64,640]{2,1,0:T(8,128)(2,1)S(1)} %get-tuple-element.72.narrow_ref.first_ref) | copy-start | bytes 1966084
  76.7 24.3 %copy-start.7 = (bf16[64,512]{1,0:T(8,128)(2,1)S(1)}, bf16[64,512]{1,0:T(8,128)(2,1)}, u32[]{:S(2)}) copy-start(bf16[64,512]{1,0:T(8,128)(2,1)} %get-tuple-element.80.rest_0_) | copy-start | bytes 196612
  83.8 0.8 copy-start.4
  84.6 9.6 %copy-start.5 = (bf16[64,512]{1,0:T(8,128)(2,1)}, bf16[64,512]{1,0:T(8,128)(2,1)S(1)}, u32[]{:S(2)}) copy-start(bf16[64,512]{1,0:T(8,128)(2,1)S(1)} %collective-permute-done.9.rest_1_) | copy-start | bytes 196612
  84.6 16.3 %all-to-all-start.2 = ((bf16[8,1,32,896]{3,2,1,0:T(8,128)(2,1)}), bf16[8,1,32,896]{3,2,1,0:T(8,128)(2,1)S(1)}, u32[]{:S(2)}, u32[]{:S(2)}) async-start(bf16[8,1,32,896]{3,2,1,0:T(8,128)(2,1)} %get-tuple-element.81), calls=%async_computation.2 | async-start | bytes 917504 | tf_op jit(solution)/shard_map/all_to_all | solution.py:483
  88.1 12.8 %collective-permute-start.13 = (bf16[256,896]{1,0:T(8,128)(2,1)}, bf16[256,896]{1,0:T(8,128)(2,1)}, u32[]{:S(2)}, u32[]{:S(2)}) collective-permute-start(bf16[256,896]{1,0:T(8,128)(2,1)} %copy-done.8), channel_id=1, source_target_pairs={{8,0},{16,8},{24,16},{9,1},{17,9},{25,17},{10,2},{18,10},{26,18},{... | collective-permute-start | bytes 1376264 | tf_op jit(solution)/shard_map/ppermute | solution.py:480
  89.4 11.5 %collective-permute-start.14 = (bf16[256,896]{1,0:T(8,128)(2,1)}, bf16[256,896]{1,0:T(8,128)(2,1)}, u32[]{:S(2)}, u32[]{:S(2)}) collective-permute-start(bf16[256,896]{1,0:T(8,128)(2,1)} %copy-done.4), channel_id=1, source_target_pairs={{8,0},{16,8},{24,16},{9,1},{17,9},{25,17},{10,2},{18,10},{26,18},{... | collective-permute-start | bytes 1376264 | tf_op jit(solution)/shard_map/ppermute | solution.py:480
  92.3 8.7 %collective-permute-start.15 = (bf16[192,512]{1,0:T(8,128)(2,1)}, bf16[192,512]{1,0:T(8,128)(2,1)}, u32[]{:S(2)}, u32[]{:S(2)}) collective-permute-start(bf16[192,512]{1,0:T(8,128)(2,1)} %pad_maximum_fusion.1), channel_id=1, source_target_pairs={{0,1},{1,0},{2,3},{3,2},{4,5},{5,4},{6,7},{7,6},{8,9},{9,8},{10,11... | collective-permute-start | bytes 589832 | tf_op jit(solution)/shard_map/ppermute | solution.py:345
  95.1 1.1 %copy-start.1 = (bf16[8,64,640]{2,1,0:T(8,128)(2,1)S(1)}, bf16[8,64,640]{2,1,0:T(8,128)(2,1)}, u32[]{:S(2)}) copy-start(bf16[8,64,640]{2,1,0:T(8,128)(2,1)} %copy-done) | copy-start | bytes 1966084
  101.0 0.9 copy-start.3
  101.9 0.8 copy-start.6
